TPU v7x, 32 devices: a whole 2x2x4 slice. The times are simulated.
32 devices in a mesh: groups: 2 (over x), expert: 8 (over z, y), context: 2 (over core).
Axes of the slice: x: 2, y: 2, z: 4, core: 2. Of those that a mesh axis runs over, the one named last changes fastest.
Arguments:
- query_heads: bfloat16 [16, 256, 2048], P(('groups', 'expert'), 'context'), parts along dimension 0, may hold values from -4.5 to 4.5
- key_heads: bfloat16 [16, 256, 2048], P(('groups', 'expert'), 'context'), parts along dimension 0, may hold values from -4.5 to 4.5
- value_heads: bfloat16 [16, 256, 2048], P(('groups', 'expert'), 'context'), parts along dimension 0, may hold values from -6 to 6
- latent: bfloat16 [16, 256, 1024], P(('groups', 'expert'), 'context'), parts along dimension 0, may hold values from -6 to 6
- router: bfloat16 [1024, 16], replicated, may hold values from -0.1875 to 0.1875
- expert_in: bfloat16 [16, 1024, 2048], P(('expert', 'context')), may hold values from -0.1875 to 0.1875
- expert_out: bfloat16 [16, 2048, 1024], P(('expert', 'context')), may hold values from -0.125 to 0.125
- routes: int32 [16, 256, 6], P(('groups', 'expert'), 'context'), parts along dimension 0, may hold values from 0 to 15, all different within a row; in each aligned block of 128 rows (0 to 127, 128 to 255, ..., all dimensions but the last counted through in order) at most 96 rows name the same one
- segments: int32 [16, 256], P(('groups', 'expert'), 'context'), parts along dimension 0, may hold values from 0 to 3, never falling along the last dimension, each value on 1 to 128 neighbouring positions
- offsets: int32 [16, 256], P(('groups', 'expert'), 'context'), parts along dimension 0, may hold values from 0 to 3
- capacity: int32 [16], replicated, may hold values from 512 to 1024, as said below
Outputs:
- attn_out: bfloat16 [16, 256, 2048], P(('groups', 'expert'), 'context'), parts along dimension 0
- moe_out: bfloat16 [16, 256, 1024], P(('groups', 'expert'), 'context'), parts along dimension 0
There are 2 independent parts, one for each index of `groups`. A program takes and returns all parts, laid end to end along the dimension named above; an argument that names none is the same for every part. Nothing has to cross between parts.
Inputs may be any that keep to these rules, and one draw needn't show every extreme that they name: `routes`: each row names 6 different experts; among the rows of one device (aligned blocks of 128 tokens) no expert is named more than 96 times, a bound that some block reaches. Some expert's capacity is exactly 1024. `segments`: document numbers never fall along a window; each document spans 1 to 128 positions, one exactly that many.
All inputs are finite; a program needn't handle non-finite values.
Results may differ from a plain program's by a relative error of at most 0.008.
Values may be sent and summed in bfloat16 or wider, within the bound.
No kernel may reach another device: no remote copies, remote signals or barrier semaphores. Data moves between devices by JAX's collectives and lax.ppermute only.
A program may use at most 128 MiB of HBM per device.

v0:
```python
import functools

import jax
import jax.numpy as jnp
from jax import lax
from jax.experimental import pallas as pl
from jax.experimental.pallas import tpu as pltpu
from jax.sharding import PartitionSpec as P

HEAD_DIM = 128
LATENT = 1024
TOPK = 6
DENSE_EXPERTS = 16
VMEM_LIMIT = 56 * 1024 * 1024


def run_expert(rows_in, w_first, w_second):
    hidden = jax.nn.relu(jnp.dot(rows_in, w_first, preferred_element_type=jnp.float32))
    hidden = (hidden * hidden).astype(jnp.bfloat16)
    return jnp.dot(hidden, w_second, preferred_element_type=jnp.float32).astype(jnp.bfloat16)


def column_of(row):
    n = row.shape[1]
    square = jnp.broadcast_to(row.astype(jnp.float32), (n, n)).T
    return square[:, :1].astype(jnp.int32)


def attend_kernel(
    place_ref, q_ref, k_own, k_far, v_own, v_far, doc_own, doc_far, ahead_ref, out_ref
):
    rows = q_ref.shape[0]
    heads = q_ref.shape[1] // HEAD_DIM
    here = place_ref[0] * rows
    there = (1 - place_ref[0]) * rows
    doc_query = column_of(doc_own[...])
    reach = here + lax.broadcasted_iota(jnp.int32, (rows, 1), 0) + column_of(ahead_ref[...])
    lane = lax.broadcasted_iota(jnp.int32, (1, rows), 1)
    see_own = (doc_own[...] == doc_query) & (here + lane <= reach)
    see_far = (doc_far[...] == doc_query) & (there + lane <= reach)
    scale = HEAD_DIM ** (-0.5)
    across = (((1,), (1,)), ((), ()))
    for head in range(heads):
        cols = slice(head * HEAD_DIM, (head + 1) * HEAD_DIM)
        q = q_ref[:, cols]
        near = lax.dot_general(q, k_own[:, cols], across, preferred_element_type=jnp.float32)
        far = lax.dot_general(q, k_far[:, cols], across, preferred_element_type=jnp.float32)
        near = jnp.where(see_own, near * scale, -1e30)
        far = jnp.where(see_far, far * scale, -1e30)
        top = jnp.max(jnp.maximum(near, far), axis=1, keepdims=True)
        near = jnp.exp(near - top)
        far = jnp.exp(far - top)
        share = 1.0 / jnp.sum(near + far, axis=1, keepdims=True)
        near = (near * share).astype(jnp.bfloat16)
        far = (far * share).astype(jnp.bfloat16)
        mixed = jnp.dot(near, v_own[:, cols], preferred_element_type=jnp.float32)
        mixed += jnp.dot(far, v_far[:, cols], preferred_element_type=jnp.float32)
        out_ref[:, cols] = mixed.astype(jnp.bfloat16)


def attend(place, q, k_own, k_far, v_own, v_far, doc_own, doc_far, ahead):
    vmem = pl.BlockSpec(memory_space=pltpu.VMEM)
    return pl.pallas_call(
        attend_kernel,
        out_shape=jax.ShapeDtypeStruct(q.shape, jnp.bfloat16),
        in_specs=[pl.BlockSpec(memory_space=pltpu.SMEM)] + [vmem] * 8,
        out_specs=vmem,
        compiler_params=pltpu.CompilerParams(vmem_limit_bytes=VMEM_LIMIT),
        cost_estimate=pl.CostEstimate(
            flops=4 * q.shape[0] * 2 * q.shape[0] * q.shape[1],
            bytes_accessed=6 * q.size * 2,
            transcendentals=2 * q.shape[0] * q.size // HEAD_DIM,
        ),
    )(place, q, k_own, k_far, v_own, v_far, doc_own, doc_far, ahead)


def gate_kernel(latent_ref, router_ref, routes_ref, out_ref):
    logits = jnp.dot(latent_ref[...], router_ref[...], preferred_element_type=jnp.float32)
    rows, experts = logits.shape
    lane = lax.broadcasted_iota(jnp.int32, (rows, experts), 1)
    named = lane == routes_ref[:, 0:1]
    for k in range(1, TOPK):
        named |= lane == routes_ref[:, k : k + 1]
    sigma = jnp.where(named, jax.nn.sigmoid(logits), 0.0)
    gates = sigma / jnp.sum(sigma, axis=1, keepdims=True)
    out_ref[...] = jnp.where(named, gates, -1.0).T


def gate_table(latent, router, routes):
    vmem = pl.BlockSpec(memory_space=pltpu.VMEM)
    return pl.pallas_call(
        gate_kernel,
        out_shape=jax.ShapeDtypeStruct((router.shape[1], latent.shape[0]), jnp.float32),
        in_specs=[vmem] * 3,
        out_specs=vmem,
    )(latent, router, routes)


def kept_gates(table, limit):
    sources, rows = table.shape
    named = table != -1.0
    flags = jnp.where(named, 1.0, 0.0)
    upto = lax.broadcasted_iota(jnp.int32, (rows, rows), 0) <= lax.broadcasted_iota(
        jnp.int32, (rows, rows), 1
    )
    running = jnp.dot(
        flags.astype(jnp.bfloat16),
        jnp.where(upto, 1.0, 0.0).astype(jnp.bfloat16),
        preferred_element_type=jnp.float32,
    )
    earlier = lax.broadcasted_iota(jnp.int32, (sources, sources), 1) < lax.broadcasted_iota(
        jnp.int32, (sources, sources), 0
    )
    totals = jnp.broadcast_to(running[:, rows - 1 :], (sources, rows))
    before = jnp.dot(
        jnp.where(earlier, 1.0, 0.0).astype(jnp.bfloat16),
        totals.astype(jnp.bfloat16),
        preferred_element_type=jnp.float32,
    )
    slots = before + running - flags
    return jnp.where(named & (slots < limit), table, 0.0).T


def expert_kernel(tile, own_ref, capacity_ref, table_ref, x_ref, w1_ref, w2_ref, out_ref, gates):
    step = pl.program_id(0)

    @pl.when(step == 0)
    def _():
        own = own_ref[0]
        limit = capacity_ref[own].astype(jnp.float32)
        gates[...] = kept_gates(table_ref[:, own, :], limit)

    rows = gates.shape[0]
    hidden = jnp.maximum(
        jnp.dot(x_ref[...], w1_ref[...], preferred_element_type=jnp.float32), 0.0
    )
    hidden = (hidden * hidden).astype(jnp.bfloat16)
    result = jnp.dot(hidden, w2_ref[...], preferred_element_type=jnp.float32)
    result = result.astype(jnp.bfloat16).astype(jnp.float32)
    lane = lax.broadcasted_iota(jnp.int32, gates.shape, 1)
    for part in range(tile // rows):
        source = step * (tile // rows) + part
        gate = jnp.sum(jnp.where(lane == source, gates[...], 0.0), axis=1, keepdims=True)
        place = slice(part * rows, (part + 1) * rows)
        out_ref[place, :] = (result[place, :] * gate).astype(jnp.bfloat16)


def expert_all(own, capacity, table, x, w_first, w_second):
    tile = 256
    total, width = x.shape
    sources, _, rows = table.shape
    smem = pl.BlockSpec(memory_space=pltpu.SMEM)

    def whole(shape):
        return pl.BlockSpec(shape, lambda i: (0,) * len(shape), pipeline_mode=pl.Buffered(1))

    return pl.pallas_call(
        functools.partial(expert_kernel, tile),
        grid=(total // tile,),
        out_shape=jax.ShapeDtypeStruct((total, width), jnp.bfloat16),
        in_specs=[
            smem,
            smem,
            whole(table.shape),
            pl.BlockSpec((tile, width), lambda i: (i, 0)),
            whole(w_first.shape),
            whole(w_second.shape),
        ],
        out_specs=pl.BlockSpec((tile, width), lambda i: (i, 0)),
        scratch_shapes=[pltpu.VMEM((rows, sources), jnp.float32)],
        compiler_params=pltpu.CompilerParams(vmem_limit_bytes=VMEM_LIMIT),
        cost_estimate=pl.CostEstimate(
            flops=4 * total * w_first.size,
            bytes_accessed=4 * total * width + 4 * w_first.size,
            transcendentals=0,
        ),
    )(own, capacity, table, x, w_first, w_second)


def dense_moe(latent, router, expert_in, expert_out, routes, capacity):
    axes = ("expert", "context")
    gates = gate_table(latent[0], router, routes[0])
    table = lax.all_gather(gates, axes, axis=0, tiled=False)
    everyone = lax.all_gather(latent[0], axes, axis=0, tiled=True)
    own = lax.axis_index(axes).astype(jnp.int32).reshape(1)
    partial = expert_all(own, capacity, table, everyone, expert_in[0], expert_out[0])
    return lax.psum_scatter(partial, axes, scatter_dimension=0, tiled=True)[None]


def routed_moe(latent, router, expert_in, expert_out, routes, capacity):
    tok_count = latent.shape[1]
    token_rows = latent[0]
    expert_count = router.shape[1]
    per_peer = max(2, 2 * tok_count * TOPK // expert_count)
    logits = jnp.dot(token_rows, router, preferred_element_type=jnp.float32)
    chosen_ids = routes[0]
    expert_ids = jnp.arange(expert_count, dtype=jnp.int32)
    one_hot = chosen_ids[:, :, None] == expert_ids[None, None, :]
    picked = jnp.sum(jnp.where(one_hot, logits[:, None, :], 0.0), axis=2)
    sigmas = jax.nn.sigmoid(picked)
    gates = sigmas / jnp.sum(sigmas, axis=1, keepdims=True)
    flat_hot = one_hot.reshape(tok_count * TOPK, expert_count).astype(jnp.int32)
    counts = jnp.sum(flat_hot, axis=0)
    ranks = jnp.sum((jnp.cumsum(flat_hot, axis=0) - flat_hot) * flat_hot, axis=1)
    count_rows = lax.all_gather(counts[None, :], ("expert", "context"), axis=0, tiled=True)
    own_index = lax.axis_index(("expert", "context"))
    lower_rows = jnp.arange(count_rows.shape[0], dtype=jnp.int32)[:, None] < own_index
    before = jnp.sum(jnp.where(lower_rows, count_rows, 0), axis=0)
    slots = jnp.sum(flat_hot * before[None, :], axis=1) + ranks
    limits = jnp.sum(flat_hot * capacity[None, :], axis=1)
    kept = slots < limits
    flat_ids = chosen_ids.reshape(-1)
    places = flat_ids * per_peer + ranks
    owners = jnp.arange(tok_count * TOPK, dtype=jnp.int32) // TOPK
    send_rows = (
        jnp.zeros((expert_count * per_peer, LATENT), jnp.bfloat16)
        .at[places]
        .set(token_rows[owners])
    )
    recv_rows = lax.all_to_all(
        send_rows.reshape(expert_count, per_peer, LATENT),
        ("expert", "context"),
        split_axis=0,
        concat_axis=0,
        tiled=True,
    ).reshape(expert_count * per_peer, LATENT)
    results = run_expert(recv_rows, expert_in[0], expert_out[0])
    returned = lax.all_to_all(
        results.reshape(expert_count, per_peer, LATENT),
        ("expert", "context"),
        split_axis=0,
        concat_axis=0,
        tiled=True,
    ).reshape(expert_count * per_peer, LATENT)
    gate_kept = jnp.where(kept, gates.reshape(-1), 0.0).reshape(tok_count, TOPK)
    back_rows = returned[places].reshape(tok_count, TOPK, LATENT).astype(jnp.float32)
    mixture = jnp.sum(gate_kept[:, :, None] * back_rows, axis=1)
    return mixture.astype(jnp.bfloat16).reshape(1, tok_count, LATENT)


def shards(
    query_heads,
    key_heads,
    value_heads,
    latent,
    router,
    expert_in,
    expert_out,
    routes,
    segments,
    offsets,
    capacity,
):
    swap = [(0, 1), (1, 0)]
    k_far = lax.ppermute(key_heads[0], "context", swap)
    v_far = lax.ppermute(value_heads[0], "context", swap)
    doc_far = lax.ppermute(segments, "context", swap)
    place = lax.axis_index("context").astype(jnp.int32).reshape(1)
    attn_out = attend(
        place, query_heads[0], key_heads[0], k_far, value_heads[0], v_far, segments, doc_far, offsets
    )[None]
    moe = dense_moe if router.shape[1] <= DENSE_EXPERTS else routed_moe
    moe_out = moe(latent, router, expert_in, expert_out, routes, capacity)
    return (attn_out, moe_out)


def solution(mesh):
    rows = P(("groups", "expert"), "context", None)
    placed = (
        rows,
        rows,
        rows,
        rows,
        P(),
        P(("expert", "context"), None, None),
        P(("expert", "context"), None, None),
        rows,
        P(("groups", "expert"), "context"),
        P(("groups", "expert"), "context"),
        P(),
    )
    return jax.shard_map(
        shards,
        mesh=mesh,
        in_specs=placed,
        out_specs=(rows, rows),
        check_vma=False,
    )
```

profile of v0, /device:TPU:0, one launch (start us, length us, event | category | flops | bytes accessed | tf_op | source)
XLA Modules:
  0.0 165.8 jit_solution(6552399748755472277)
XLA Ops:
  7.2 0.0 all-gather.4.cloned.1.call-start
  7.2 0.7 all-gather.4.cloned.1.call-update
  7.9 0.0 reduce-scatter.2.cloned.1.call-start
  7.9 1.4 copy.13
  9.4 1.6 copy.14.router_ref
  11.0 2.0 %shard_map.123 = f32[16,128]{1,0:T(8,128)} custom-call(bf16[128,1024]{1,0:T(8,128)(2,1)} %bitcast.13, bf16[1024,16]{1,0:T(8,128)(2,1)} %copy.14.router_ref, s32[128,6]{1,0:T(8,128)} %bitcast.20), custom_call_target="tpu_custom_call" | custom-call | tf_op jit(solution)/shard_map/pallas_call | solution.py:91
  12.9 25.2 %all-gather = f32[256,128]{1,0:T(8,128)} all-gather(f32[16,128]{1,0:T(8,128)} %shard_map.123), channel_id=2, replica_groups=mesh['groups'=2,'expert'=8,'context'=2] {'expert','context'}, dimensions={0}, use_global_device_ids=true | all-gather | bytes 139264 | tf_op jit(solution)/shard_map/all_gather | solution.py:183
  38.1 25.6 %all-gather.4.cloned.1.call-done = bf16[1,2048,1024]{2,1,0:T(8,128)(2,1)} async-done(((bf16[1,128,1024]{2,1,0:T(8,128)(2,1)}), bf16[1,2048,1024]{2,1,0:T(8,128)(2,1)}) %all-gather.4.cloned.1.call-update) | async-done | bytes 4194320 | tf_op jit(solution)/shard_map/all_gather | solution.py:184
  63.7 23.9 %shard_map.124 = bf16[2048,1024]{1,0:T(8,128)(2,1)} custom-call(s32[1]{0:T(128)} %bitcast.5.own_ref, s32[16]{0:T(128)} %capacity_ref.1, f32[16,16,128]{2,1,0:T(8,128)} %bitcast.21, bf16[2048,1024]{1,0:T(8,128)(2,1)} %bitcast.24, bf16[1024,2048]{1,0:T(8,128)(2,1)} %bitcast.22, bf16[2048,1024]{1,0:T(8,128)(2,1)} %bitcast.23), custom_call_target="tpu_custom_call" | custom-call | flops 17179869184 | bytes 16777216 | tf_op jit(solution)/shard_map/pallas_call | solution.py:157
  87.6 0.0 copy-start
  87.6 0.0 copy-start.1
  87.6 0.0 copy-start.4
  87.6 0.0 reduce-scatter.2.cloned.1.call-update
  87.6 1.0 copy-done
  88.6 0.3 collective-permute-start
  88.9 0.0 copy-done.1
  88.9 0.3 collective-permute-start.1
  89.2 0.0 copy-done.4
  89.2 0.3 collective-permute-start.2
  89.4 1.9 %collective-permute-done.2.doc_far = s32[1,128]{1,0:T(1,128)S(1)} collective-permute-done((s32[1,128]{1,0:T(1,128)S(1)}, s32[1,128]{1,0:T(1,128)S(1)}, u32[]{:S(2)}, u32[]{:S(2)}) %collective-permute-start.2) | collective-permute-done | bytes 544 | tf_op jit(solution)/shard_map/ppermute | solution.py:257
  91.3 0.0 copy-start.5
  91.3 0.0 collective-permute-done.k_far
  91.3 0.0 copy-start.2
  91.3 0.0 collective-permute-done.1.v_far
  91.3 0.0 copy-start.3
  91.3 0.5 copy-done.5
  91.8 0.3 copy-done.2
  92.1 0.2 copy-done.3
  92.3 8.3 %shard_map.122 = bf16[128,2048]{1,0:T(8,128)(2,1)} custom-call(s32[1]{0:T(128)} %bitcast.place_ref, bf16[128,2048]{1,0:T(8,128)(2,1)} %bitcast.14, bf16[128,2048]{1,0:T(8,128)(2,1)} %bitcast.15, bf16[128,2048]{1,0:T(8,128)(2,1)} %copy-done.2, bf16[128,2048]{1,0:T(8,128)(2,1)} %bitcast.17, bf16[128,2048]{1,0:T(8,128)(2,1)} %copy-done.3, s32[1,128]{1,0:T(1,128)} %doc_own.1, ...), custom_call_target="tpu_custom_call" | custom-call | flops 268435456 | bytes 3145728 | tf_op jit(solution)/shard_map/pallas_call | solution.py:63
  100.6 58.4 %reduce-scatter.2.cloned.1.call-done = bf16[128,1024]{1,0:T(8,128)(2,1)} async-done(((bf16[2048,1024]{1,0:T(8,128)(2,1)}), bf16[128,1024]{1,0:T(8,128)(2,1)}) %reduce-scatter.2.cloned.1.call-update) | async-done | bytes 262160 | tf_op jit(solution)/shard_map/reduce_scatter | solution.py:187
Async XLA Ops:
  7.2 56.6 %all-gather.4.cloned.1.call-start = ((), (), s32[]{:S(2)}) async-start(), calls=%async_computation.2 | async-start | bytes 4456448 | tf_op jit(solution)/shard_map/all_gather | solution.py:184
  7.9 151.1 %reduce-scatter.2.cloned.1.call-start = ((), (), s32[]{:S(2)}) async-start(), calls=%async_computation.1 | async-start | bytes 4456448 | tf_op jit(solution)/shard_map/reduce_scatter | solution.py:187
  87.6 1.0 copy-start
  87.6 1.3 copy-start.1
  87.6 1.6 copy-start.4
  88.6 2.7 %collective-permute-start = (bf16[128,2048]{1,0:T(8,128)(2,1)S(1)}, bf16[128,2048]{1,0:T(8,128)(2,1)S(1)}, u32[]{:S(2)}, u32[]{:S(2)}) collective-permute-start(bf16[128,2048]{1,0:T(8,128)(2,1)S(1)} %bitcast.16), channel_id=1, source_target_pairs={{0,1},{1,0},{2,3},{3,2},{4,5},{5,4},{6,7},{7,6},{8,9},{9,8},{10,11... | collective-permute-start | bytes 1572872 | tf_op jit(solution)/shard_map/ppermute | solution.py:255
  88.9 2.4 %collective-permute-start.1 = (bf16[128,2048]{1,0:T(8,128)(2,1)S(1)}, bf16[128,2048]{1,0:T(8,128)(2,1)S(1)}, u32[]{:S(2)}, u32[]{:S(2)}) collective-permute-start(bf16[128,2048]{1,0:T(8,128)(2,1)S(1)} %bitcast.18), channel_id=1, source_target_pairs={{0,1},{1,0},{2,3},{3,2},{4,5},{5,4},{6,7},{7,6},{8,9},{9,8},{10,11... | collective-permute-start | bytes 1572872 | tf_op jit(solution)/shard_map/ppermute | solution.py:256
  89.2 2.1 %collective-permute-start.2 = (s32[1,128]{1,0:T(1,128)S(1)}, s32[1,128]{1,0:T(1,128)S(1)}, u32[]{:S(2)}, u32[]{:S(2)}) collective-permute-start(s32[1,128]{1,0:T(1,128)S(1)} %copy-done.4), channel_id=1, source_target_pairs={{0,1},{1,0},{2,3},{3,2},{4,5},{5,4},{6,7},{7,6},{8,9},{9,8},{10,11... | collective-permute-start | bytes 1544 | tf_op jit(solution)/shard_map/ppermute | solution.py:257
  91.3 0.5 copy-start.5
  91.3 0.8 copy-start.2
  91.3 1.0 copy-start.3
Sparse Core Ops, SparseCore 0:
  10.2 53.5 all-gather.3
  87.8 71.1 reduce-scatter.1
where the time goes:
time: 166 us
  waiting for transfers between devices  86.6 us (52%)
  Pallas kernels  34.1 us (21%)
  blocking collectives  25.2 us (15%)
  between operations  14.1 us (8%)
  local copies, waits for them, and re-layouts  4.99 us (3%)
    reduce_scatter x1, waiting for transfers between devices, dense_moe(): lax.psum_scatter(partial, axes, scatter_dimension=0, tiled=True)[None]  58.4 us
    all_gather x1, waiting for transfers between devices, dense_moe(): everyone = lax.all_gather(latent[0], axes, axis=0, tiled=True)  25.6 us
    all_gather x1, blocking collectives, dense_moe(): table = lax.all_gather(gates, axes, axis=0, tiled=False)  25.2 us
    pallas_call x1, Pallas kernels, expert_all(): pl.pallas_call(functools.partial(expert_kernel, tile), grid=(total // til...  23.9 us
    pallas_call x1, Pallas kernels, attend(): pl.pallas_call(attend_kernel, out_shape=jax.ShapeDtypeStruct(q.shape, jnp...  8.28 us
    unnamed x14, local copies, waits for them, and re-layouts  4.99 us
  transfers between devices with their start and end apart: 5, of which 3 were waited for; matrix products, arithmetic and copies ran while one was open for 2% of the time, Pallas kernels for 6%

commit v1 on v0

--- a/solution.py
+++ b/solution.py
@@ -12,6 +12,7 @@
 TOPK = 6
 DENSE_EXPERTS = 16
 VMEM_LIMIT = 56 * 1024 * 1024
+EXPERT_VMEM = 28 * 1024 * 1024
 
 
 def run_expert(rows_in, w_first, w_second):
@@ -75,15 +76,16 @@
 
 
 def gate_kernel(latent_ref, router_ref, routes_ref, out_ref):
-    logits = jnp.dot(latent_ref[...], router_ref[...], preferred_element_type=jnp.float32)
-    rows, experts = logits.shape
-    lane = lax.broadcasted_iota(jnp.int32, (rows, experts), 1)
-    named = lane == routes_ref[:, 0:1]
+    logits = lax.dot_general(
+        router_ref[...], latent_ref[...], (((1,), (1,)), ((), ())), preferred_element_type=jnp.float32
+    )
+    number = lax.broadcasted_iota(jnp.int32, logits.shape, 0)
+    named = number == routes_ref[0]
     for k in range(1, TOPK):
-        named |= lane == routes_ref[:, k : k + 1]
+        named |= number == routes_ref[k]
     sigma = jnp.where(named, jax.nn.sigmoid(logits), 0.0)
-    gates = sigma / jnp.sum(sigma, axis=1, keepdims=True)
-    out_ref[...] = jnp.where(named, gates, -1.0).T
+    gates = sigma / jnp.sum(sigma, axis=0, keepdims=True)
+    out_ref[...] = jnp.where(named, gates, -1.0)
 
 
 def gate_table(latent, router, routes):
@@ -93,10 +95,12 @@
         out_shape=jax.ShapeDtypeStruct((router.shape[1], latent.shape[0]), jnp.float32),
         in_specs=[vmem] * 3,
         out_specs=vmem,
-    )(latent, router, routes)
-
-
-def kept_gates(table, limit):
+    )(latent, router.T, routes.transpose(2, 0, 1))
+
+
+def kept_kernel(own_ref, order_ref, capacity_ref, table_ref, out_ref):
+    own = own_ref[0]
+    table = table_ref[:, own, :]
     sources, rows = table.shape
     named = table != -1.0
     flags = jnp.where(named, 1.0, 0.0)
@@ -108,83 +112,140 @@
         jnp.where(upto, 1.0, 0.0).astype(jnp.bfloat16),
         preferred_element_type=jnp.float32,
     )
-    earlier = lax.broadcasted_iota(jnp.int32, (sources, sources), 1) < lax.broadcasted_iota(
-        jnp.int32, (sources, sources), 0
-    )
+    device = lax.broadcasted_iota(jnp.int32, (sources, sources), 0) ^ own
+    other = lax.broadcasted_iota(jnp.int32, (sources, sources), 1) ^ own
     totals = jnp.broadcast_to(running[:, rows - 1 :], (sources, rows))
     before = jnp.dot(
-        jnp.where(earlier, 1.0, 0.0).astype(jnp.bfloat16),
+        jnp.where(other < device, 1.0, 0.0).astype(jnp.bfloat16),
         totals.astype(jnp.bfloat16),
         preferred_element_type=jnp.float32,
     )
     slots = before + running - flags
-    return jnp.where(named & (slots < limit), table, 0.0).T
-
-
-def expert_kernel(tile, own_ref, capacity_ref, table_ref, x_ref, w1_ref, w2_ref, out_ref, gates):
-    step = pl.program_id(0)
-
-    @pl.when(step == 0)
-    def _():
-        own = own_ref[0]
-        limit = capacity_ref[own].astype(jnp.float32)
-        gates[...] = kept_gates(table_ref[:, own, :], limit)
-
-    rows = gates.shape[0]
-    hidden = jnp.maximum(
-        jnp.dot(x_ref[...], w1_ref[...], preferred_element_type=jnp.float32), 0.0
-    )
-    hidden = (hidden * hidden).astype(jnp.bfloat16)
-    result = jnp.dot(hidden, w2_ref[...], preferred_element_type=jnp.float32)
-    result = result.astype(jnp.bfloat16).astype(jnp.float32)
-    lane = lax.broadcasted_iota(jnp.int32, gates.shape, 1)
-    for part in range(tile // rows):
-        source = step * (tile // rows) + part
-        gate = jnp.sum(jnp.where(lane == source, gates[...], 0.0), axis=1, keepdims=True)
-        place = slice(part * rows, (part + 1) * rows)
-        out_ref[place, :] = (result[place, :] * gate).astype(jnp.bfloat16)
-
-
-def expert_all(own, capacity, table, x, w_first, w_second):
-    tile = 256
-    total, width = x.shape
-    sources, _, rows = table.shape
+    limit = capacity_ref[own].astype(jnp.float32)
+    kept = jnp.where(named & (slots < limit), table, 0.0)
+    entry = lax.broadcasted_iota(jnp.int32, table.shape, 0)
+    ordered = [
+        jnp.sum(jnp.where(entry == order_ref[place], kept, 0.0), axis=0, keepdims=True)
+        for place in range(sources)
+    ]
+    out_ref[...] = jnp.concatenate(ordered, axis=0).T
+
+
+def kept_gates(own, order, capacity, table):
     smem = pl.BlockSpec(memory_space=pltpu.SMEM)
-
-    def whole(shape):
-        return pl.BlockSpec(shape, lambda i: (0,) * len(shape), pipeline_mode=pl.Buffered(1))
-
+    vmem = pl.BlockSpec(memory_space=pltpu.VMEM)
     return pl.pallas_call(
-        functools.partial(expert_kernel, tile),
-        grid=(total // tile,),
-        out_shape=jax.ShapeDtypeStruct((total, width), jnp.bfloat16),
-        in_specs=[
-            smem,
-            smem,
-            whole(table.shape),
-            pl.BlockSpec((tile, width), lambda i: (i, 0)),
-            whole(w_first.shape),
-            whole(w_second.shape),
-        ],
-        out_specs=pl.BlockSpec((tile, width), lambda i: (i, 0)),
-        scratch_shapes=[pltpu.VMEM((rows, sources), jnp.float32)],
-        compiler_params=pltpu.CompilerParams(vmem_limit_bytes=VMEM_LIMIT),
+        kept_kernel,
+        out_shape=jax.ShapeDtypeStruct((table.shape[2], table.shape[0]), jnp.float32),
+        in_specs=[smem, smem, smem, vmem],
+        out_specs=vmem,
+    )(own, order, capacity, table)
+
+
+def expert_kernel(columns, gates_ref, *refs):
+    count = len(columns)
+    blocks, (w1_ref, w2_ref, keep_ref, give_ref, hidden_ref) = refs[:count], refs[count:]
+    rows = blocks[0].shape[0]
+    x = jnp.concatenate([block[...] for block in blocks], axis=0)
+    step = 512
+    for first in range(0, w1_ref.shape[1], step):
+        cols = slice(first, first + step)
+        hidden = jnp.maximum(jnp.dot(x, w1_ref[:, cols], preferred_element_type=jnp.float32), 0.0)
+        hidden_ref[:, cols] = (hidden * hidden).astype(jnp.bfloat16)
+    for first in range(0, w2_ref.shape[1], step):
+        cols = slice(first, first + step)
+        result = jnp.dot(hidden_ref[...], w2_ref[:, cols], preferred_element_type=jnp.float32)
+        for index, column in enumerate(columns):
+            gate = gates_ref[:, column : column + 1]
+            part = result[index * rows : (index + 1) * rows]
+            out = give_ref if index % 2 else keep_ref
+            out[index // 2, :, cols] = (part * gate).astype(jnp.bfloat16)
+
+
+def run_pieces(gates, pieces, w_first, w_second):
+    columns, blocks = [], []
+    for place, mine, theirs in pieces:
+        columns += [2 * place, 2 * place + 1]
+        blocks += [mine, theirs]
+    rows, width = blocks[0].shape
+    vmem = pl.BlockSpec(memory_space=pltpu.VMEM)
+    half = jax.ShapeDtypeStruct((len(pieces), rows, width), jnp.bfloat16)
+    return pl.pallas_call(
+        functools.partial(expert_kernel, tuple(columns)),
+        out_shape=(half, half),
+        in_specs=[vmem] * (3 + len(blocks)),
+        out_specs=(vmem, vmem),
+        scratch_shapes=[pltpu.VMEM((rows * len(blocks), w_first.shape[1]), jnp.bfloat16)],
+        compiler_params=pltpu.CompilerParams(vmem_limit_bytes=EXPERT_VMEM),
         cost_estimate=pl.CostEstimate(
-            flops=4 * total * w_first.size,
-            bytes_accessed=4 * total * width + 4 * w_first.size,
+            flops=4 * rows * len(blocks) * w_first.size,
+            bytes_accessed=4 * rows * len(blocks) * width + 4 * w_first.size,
             transcendentals=0,
         ),
-    )(own, capacity, table, x, w_first, w_second)
+    )(gates, *blocks, w_first, w_second)
 
 
 def dense_moe(latent, router, expert_in, expert_out, routes, capacity):
-    axes = ("expert", "context")
-    gates = gate_table(latent[0], router, routes[0])
-    table = lax.all_gather(gates, axes, axis=0, tiled=False)
-    everyone = lax.all_gather(latent[0], axes, axis=0, tiled=True)
-    own = lax.axis_index(axes).astype(jnp.int32).reshape(1)
-    partial = expert_all(own, capacity, table, everyone, expert_in[0], expert_out[0])
-    return lax.psum_scatter(partial, axes, scatter_dimension=0, tiled=True)[None]
+    f32 = jnp.float32
+    line = router.shape[1] // 4
+    spots = [(z, y) for z in range(line) for y in range(2)]
+    sibling = [(0, 1), (1, 0)]
+    across = [(2 * z + y, 2 * z + 1 - y) for z, y in spots]
+
+    def toward(step):
+        return [(2 * z + y, 2 * ((z + step) % line) + y) for z, y in spots]
+
+    def swap_core(x):
+        return lax.ppermute(x, "context", sibling)
+
+    def swap_side(x):
+        return lax.ppermute(x, "expert", across)
+
+    def along(x, step):
+        return lax.ppermute(x, "expert", toward(step))
+
+    own = lax.axis_index(("expert", "context")).astype(jnp.int32)
+    z = own // 4
+    order = jnp.stack(
+        [4 * (z ^ ((z - step) % line)) + rest for step in range(line) for rest in range(4)]
+    )
+
+    table = gate_table(latent[0], router, routes)[None]
+    table = jnp.concatenate([table, swap_core(table)], axis=0)
+    table = jnp.concatenate([table, swap_side(table)], axis=0)
+    span = 1
+    while span < line:
+        flip = [(2 * z + y, 2 * (z ^ span) + y) for z, y in spots]
+        table = jnp.concatenate([table, lax.ppermute(table, "expert", flip)], axis=0)
+        span *= 2
+    gates = kept_gates(own.reshape(1), order, capacity, table)
+
+    chunk = latent[0]
+    ahead, side = [], []
+    for step in range(line):
+        if step:
+            chunk = along(chunk, 1)
+        beside = swap_side(chunk)
+        ahead.append((2 * step, chunk, swap_core(chunk)))
+        side.append((2 * step + 1, beside, swap_core(beside)))
+
+    total = None
+    waiting = None
+    for step in range(line + 1):
+        pieces = ([side[step - 1]] if step else []) + ([ahead[step]] if step < line else [])
+        keep, give = run_pieces(gates, pieces, expert_in[0], expert_out[0])
+        got = swap_core(give)
+        if step:
+            crossing = (keep[0].astype(f32) + got[0].astype(f32)).astype(jnp.bfloat16)
+            arrived = swap_side(crossing)
+            column = waiting[0].astype(f32) + waiting[1].astype(f32) + arrived.astype(f32)
+            if step == 1:
+                total = column
+            else:
+                sent = along(column.astype(jnp.bfloat16), line - (step - 1))
+                total = total + sent.astype(f32)
+        waiting = (keep[-1], got[-1])
+    return total.astype(jnp.bfloat16)[None]
 
 
 def routed_moe(latent, router, expert_in, expert_out, routes, capacity):

time: 166 us -> 114 us (0.69)
  waiting for transfers between devices: 86.6 us -> 50.2 us
  blocking collectives: 25.2 us -> 0 us
  starting transfers between devices: 0.84 us -> 20 us
  between operations: 14.1 us -> 0.89 us
  Pallas kernels: 34.1 us -> 30.1 us
  other arithmetic: 0 us -> 3.91 us
  local copies, waits for them, and re-layouts: 4.99 us -> 8.23 us
    reduce_scatter x1 -> x0, waiting for transfers between devices: 58.4 us -> none  [dense_moe(): lax.psum_scatter(partial, axes, scatter_dimension=0, tiled=True)[None]]
    ppermute x0 -> x31, waiting for transfers between devices: none -> 50.2 us  [the longest x9 22.6 us: swap_side(): return lax.ppermute(x, 'expert', across)]
    all_gather x1 -> x0, waiting for transfers between devices: 25.6 us -> none  [dense_moe(): everyone = lax.all_gather(latent[0], axes, axis=0, tiled=True)]
    all_gather x1 -> x0, blocking collectives: 25.2 us -> none  [dense_moe(): table = lax.all_gather(gates, axes, axis=0, tiled=False)]
    ppermute x0 -> x31, starting transfers between devices: none -> 19.9 us  [the longest x9 6.46 us: swap_side(): return lax.ppermute(x, 'expert', across)]
    pallas_call x1 -> x6, Pallas kernels: 23.9 us -> 20.2 us  [the longest x5 18.2 us: run_pieces(): pl.pallas_call(functools.partial(expert_kernel, tuple(columns)), out_shap...]
    unnamed x14 -> x30, local copies, waits for them, and re-layouts: 4.99 us -> 7.56 us
    concatenate x0 -> x3, other arithmetic: none -> 2.1 us  [the longest x1 0.7 us: dense_moe(): jnp.concatenate([table, lax.ppermute(table, 'expert', flip)], axis=0)]
  transfers between devices with their start and end apart: 5 -> 34, of which waited for: 3 -> 10; matrix products, arithmetic and copies ran while one was open for 2% -> 4% of each run, Pallas kernels for 6% -> 27%
where the time goes in v1:
time: 114 us; the launch traced here: 113 us
  waiting for transfers between devices  50.2 us (44%)
  Pallas kernels  30.1 us (26%)
  starting transfers between devices  20 us (18%)
  local copies, waits for them, and re-layouts  8.23 us (7%)
  other arithmetic  3.91 us (3%)
    ppermute x9, waiting for transfers between devices, swap_side(): return lax.ppermute(x, 'expert', across)  22.6 us
    pallas_call x5, Pallas kernels, run_pieces(): pl.pallas_call(functools.partial(expert_kernel, tuple(columns)), out_shap...  18.2 us
    ppermute x6, waiting for transfers between devices, along(): return lax.ppermute(x, 'expert', toward(step))  16.6 us
    ppermute x2, waiting for transfers between devices, dense_moe(): lax.ppermute(table, 'expert', flip)  10.6 us
    pallas_call x1, Pallas kernels, attend(): pl.pallas_call(attend_kernel, out_shape=jax.ShapeDtypeStruct(q.shape, jnp...  8.13 us
    unnamed x30, local copies, waits for them, and re-layouts  7.56 us
    ppermute x9, starting transfers between devices, swap_side(): return lax.ppermute(x, 'expert', across)  6.46 us
    ppermute x6, starting transfers between devices, along(): return lax.ppermute(x, 'expert', toward(step))  5.67 us
  transfers between devices with their start and end apart: 34, of which 10 were waited for; matrix products, arithmetic and copies ran while one was open for 4% of the time, Pallas kernels for 27%

profile of v1, /device:TPU:0, one launch (start us, length us, event | category | flops | bytes accessed | tf_op | source)
XLA Modules:
  0.0 113.3 jit_solution(12152290043070425878)
XLA Ops:
  0.6 3.1 %collective-permute-start.11 = (bf16[128,1024]{1,0:T(8,128)(2,1)}, bf16[128,1024]{1,0:T(8,128)(2,1)S(1)}, u32[]{:S(2)}, u32[]{:S(2)}) collective-permute-start(bf16[128,1024]{1,0:T(8,128)(2,1)} %bitcast.73), channel_id=1, source_target_pairs={{0,4},{2,6},{4,8},{6,10},{8,12},{10,14},{12,0},{14,2},{1,5},{3,7},... | collective-permute-start | bytes 786440 | tf_op jit(solution)/shard_map/ppermute | solution.py:205
  3.7 1.5 %collective-permute-start.9 = (bf16[128,1024]{1,0:T(8,128)(2,1)}, bf16[128,1024]{1,0:T(8,128)(2,1)S(1)}, u32[]{:S(2)}, u32[]{:S(2)}) collective-permute-start(bf16[128,1024]{1,0:T(8,128)(2,1)} %bitcast.74), channel_id=1, source_target_pairs={{0,2},{2,0},{4,6},{6,4},{8,10},{10,8},{12,14},{14,12},{1,3},{3,1},... | collective-permute-start | bytes 786440 | tf_op jit(solution)/shard_map/ppermute | solution.py:202
  5.2 1.8 %shard_map.123 = f32[16,128]{1,0:T(8,128)} custom-call(bf16[128,1024]{1,0:T(8,128)(2,1)} %bitcast.76, bf16[16,1024]{1,0:T(8,128)(2,1)} %bitcast.88, s32[6,1,128]{2,1,0:T(1,128)} %bitcast.89), custom_call_target="tpu_custom_call" | custom-call | tf_op jit(solution)/shard_map/pallas_call | solution.py:93
  7.0 0.5 collective-permute-start.3
  7.5 0.7 constant_dynamic-update-slice_fusion.4
  8.2 0.7 stack.67.order_ref
  8.9 0.7 pad_maximum_fusion.2
  9.6 0.5 collective-permute-start.4
  10.1 3.2 %collective-permute-done.4 = f32[2,16,128]{2,1,0:T(8,128)S(1)} collective-permute-done((f32[2,16,128]{2,1,0:T(8,128)S(1)}, f32[2,16,128]{2,1,0:T(8,128)S(1)}, u32[]{:S(2)}, u32[]{:S(2)}) %collective-permute-start.4) | collective-permute-done | bytes 16416 | tf_op jit(solution)/shard_map/ppermute | solution.py:202
  13.3 0.7 pad_maximum_fusion.1
  14.0 1.6 %collective-permute-start.5 = (f32[4,16,128]{2,1,0:T(8,128)S(1)}, f32[4,16,128]{2,1,0:T(8,128)S(1)}, u32[]{:S(2)}, u32[]{:S(2)}) collective-permute-start(f32[4,16,128]{2,1,0:T(8,128)S(1)} %pad_maximum_fusion.1), channel_id=1, source_target_pairs={{0,4},{2,6},{4,0},{6,2},{8,12},{10,14},{12,8},{14,10},{1,5},{3,7},... | collective-permute-start | bytes 98312 | tf_op jit(solution)/shard_map/ppermute | solution.py:219
  15.6 2.3 %collective-permute-done.5 = f32[4,16,128]{2,1,0:T(8,128)S(1)} collective-permute-done((f32[4,16,128]{2,1,0:T(8,128)S(1)}, f32[4,16,128]{2,1,0:T(8,128)S(1)}, u32[]{:S(2)}, u32[]{:S(2)}) %collective-permute-start.5) | collective-permute-done | bytes 32800 | tf_op jit(solution)/shard_map/ppermute | solution.py:219
  17.9 0.7 pad_maximum_fusion
  18.6 2.6 %collective-permute-start.6 = (f32[8,16,128]{2,1,0:T(8,128)S(1)}, f32[8,16,128]{2,1,0:T(8,128)S(1)}, u32[]{:S(2)}, u32[]{:S(2)}) collective-permute-start(f32[8,16,128]{2,1,0:T(8,128)S(1)} %pad_maximum_fusion), channel_id=1, source_target_pairs={{0,8},{2,10},{4,12},{6,14},{8,0},{10,2},{12,4},{14,6},{1,9},{3,11}... | collective-permute-start | bytes 196616 | tf_op jit(solution)/shard_map/ppermute | solution.py:219
  21.2 0.2 collective-permute-start.17
  21.5 0.4 collective-permute-start.15
  21.8 8.3 %collective-permute-done.6 = f32[8,16,128]{2,1,0:T(8,128)S(1)} collective-permute-done((f32[8,16,128]{2,1,0:T(8,128)S(1)}, f32[8,16,128]{2,1,0:T(8,128)S(1)}, u32[]{:S(2)}, u32[]{:S(2)}) %collective-permute-start.6) | collective-permute-done | bytes 65568 | tf_op jit(solution)/shard_map/ppermute | solution.py:219
  30.1 0.5 collective-permute-start.10
  30.6 0.7 copy-done.10
  31.3 2.0 %shard_map.124.gates_ref = f32[128,16]{1,0:T(8,128)} custom-call(s32[1]{0:T(128)} %bitcast.5.own_ref, s32[16]{0:T(128)} %stack.67.order_ref, s32[16]{0:T(128)} %capacity_ref.1, f32[16,16,128]{2,1,0:T(8,128)} %copy-done.10), custom_call_target="tpu_custom_call" | custom-call | tf_op jit(solution)/shard_map/pallas_call | solution.py:137
  33.3 0.0 collective-permute-start
  33.3 2.2 %copy-done = bf16[1,1024,2048]{2,1,0:T(8,128)(2,1)S(1)} copy-done((bf16[1,1024,2048]{2,1,0:T(8,128)(2,1)S(1)}, bf16[1,1024,2048]{2,1,0:T(8,128)(2,1)}, u32[]{:S(2)}) %copy-start) | copy-done | bytes 4194328
  35.5 2.2 %copy-done.2 = bf16[1,2048,1024]{2,1,0:T(8,128)(2,1)S(1)} copy-done((bf16[1,2048,1024]{2,1,0:T(8,128)(2,1)S(1)}, bf16[1,2048,1024]{2,1,0:T(8,128)(2,1)}, u32[]{:S(2)}) %copy-start.2) | copy-done | bytes 4194328
  37.6 0.9 copy-done.4
  38.6 0.8 copy-done.5
  39.4 2.3 %shard_map.125 = (bf16[1,128,1024]{2,1,0:T(8,128)(2,1)S(1)}, bf16[1,128,1024]{2,1,0:T(8,128)(2,1)S(1)}) custom-call(f32[128,16]{1,0:T(8,128)S(1)} %copy-done.5, bf16[128,1024]{1,0:T(8,128)(2,1)S(1)} %bitcast.77, bf16[128,1024]{1,0:T(8,128)(2,1)S(1)} %collective-permute-done.7.refs_1_, bf16[1024,2048]{1,0:T(8,128)(2,1)S(1)} %bitcast.63, ...), custom_call_target="tpu_custom_call" | custom-call | flops 2147483648 | bytes 9437184 | tf_op jit(solution)/shard_map/pallas_call | solution.py:173
  41.8 0.2 collective-permute-start.24
  42.1 0.6 collective-permute-start.22
  42.7 0.2 collective-permute-start.18
  42.9 0.3 collective-permute-start.16
  43.2 4.5 %shard_map.126 = (bf16[2,128,1024]{2,1,0:T(8,128)(2,1)S(1)}, bf16[2,128,1024]{2,1,0:T(8,128)(2,1)S(1)}) custom-call(f32[128,16]{1,0:T(8,128)S(1)} %copy-done.5, bf16[128,1024]{1,0:T(8,128)(2,1)S(1)} %collective-permute-done.9.refs_0_, bf16[128,1024]{1,0:T(8,128)(2,1)S(1)} %collective-permute-done.10.refs_1_, ...), custom_call_target="tpu_custom_call" | custom-call | flops 4294967296 | bytes 10485760 | tf_op jit(solution)/shard_map/pallas_call | solution.py:173
  47.7 4.8 %collective-permute-done.24.refs_2_ = bf16[128,1024]{1,0:T(8,128)(2,1)S(1)} collective-permute-done((bf16[128,1024]{1,0:T(8,128)(2,1)S(1)}, bf16[128,1024]{1,0:T(8,128)(2,1)S(1)}, u32[]{:S(2)}, u32[]{:S(2)}) %collective-permute-start.24) | collective-permute-done | bytes 262176 | tf_op jit(solution)/shard_map/ppermute | solution.py:205
  52.5 0.6 collective-permute-start.29
  53.2 0.2 collective-permute-start.25
  53.3 0.4 collective-permute-start.23
  53.7 4.5 %shard_map.127 = (bf16[2,128,1024]{2,1,0:T(8,128)(2,1)S(1)}, bf16[2,128,1024]{2,1,0:T(8,128)(2,1)S(1)}) custom-call(f32[128,16]{1,0:T(8,128)S(1)} %copy-done.5, bf16[128,1024]{1,0:T(8,128)(2,1)S(1)} %collective-permute-done.15.refs_0_, bf16[128,1024]{1,0:T(8,128)(2,1)S(1)} %collective-permute-done.16.refs_1_, ...), custom_call_target="tpu_custom_call" | custom-call | flops 4294967296 | bytes 10485760 | tf_op jit(solution)/shard_map/pallas_call | solution.py:173
  58.2 3.1 %collective-permute-done.29.refs_0_ = bf16[128,1024]{1,0:T(8,128)(2,1)S(1)} collective-permute-done((bf16[128,1024]{1,0:T(8,128)(2,1)S(1)}, bf16[128,1024]{1,0:T(8,128)(2,1)S(1)}, u32[]{:S(2)}, u32[]{:S(2)}) %collective-permute-start.29) | collective-permute-done | bytes 262176 | tf_op jit(solution)/shard_map/ppermute | solution.py:202
  61.3 0.5 collective-permute-start.19
  61.8 0.1 collective-permute-start.30
  61.9 4.5 %shard_map.128 = (bf16[2,128,1024]{2,1,0:T(8,128)(2,1)S(1)}, bf16[2,128,1024]{2,1,0:T(8,128)(2,1)S(1)}) custom-call(f32[128,16]{1,0:T(8,128)S(1)} %copy-done.5, bf16[128,1024]{1,0:T(8,128)(2,1)S(1)} %collective-permute-done.22.refs_0_, bf16[128,1024]{1,0:T(8,128)(2,1)S(1)} %collective-permute-done.23.refs_1_, ...), custom_call_target="tpu_custom_call" | custom-call | flops 4294967296 | bytes 10485760 | tf_op jit(solution)/shard_map/pallas_call | solution.py:173
  66.4 0.5 collective-permute-start.26
  66.9 0.1 fusion.7
  67.0 0.2 collective-permute-start.2
  67.1 2.3 %shard_map.129 = (bf16[1,128,1024]{2,1,0:T(8,128)(2,1)S(1)}, bf16[1,128,1024]{2,1,0:T(8,128)(2,1)S(1)}) custom-call(f32[128,16]{1,0:T(8,128)S(1)} %copy-done.6, bf16[128,1024]{1,0:T(8,128)(2,1)S(1)} %collective-permute-done.29.refs_0_, bf16[128,1024]{1,0:T(8,128)(2,1)S(1)} %collective-permute-done.30.refs_1_, bf16[1024,2048]{1,0:T(8,128)(2,1)S(1)} %bitcast.67, ...), custom_call_target="tpu_custom_call" | custom-call | flops 2147483648 | bytes 9437184 | tf_op jit(solution)/shard_map/pallas_call | solution.py:173
  69.5 0.5 collective-permute-start.31
  70.0 0.1 fusion.8
  70.1 0.6 collective-permute-start.20
  70.7 0.1 fusion.9
  70.7 0.4 collective-permute-done.31
  71.1 1.2 %collective-permute-start.27 = (bf16[128,1024]{1,0:T(8,128)(2,1)S(1)}, bf16[128,1024]{1,0:T(8,128)(2,1)S(1)}, u32[]{:S(2)}, u32[]{:S(2)}) collective-permute-start(bf16[128,1024]{1,0:T(8,128)(2,1)S(1)} %fusion.9), channel_id=1, source_target_pairs={{0,2},{2,0},{4,6},{6,4},{8,10},{10,8},{12,14},{14,12},{1,3},{3,1},... | collective-permute-start | bytes 786440 | tf_op jit(solution)/shard_map/ppermute | solution.py:202
  72.3 0.3 fusion.10
  72.6 6.7 %collective-permute-done.20 = bf16[128,1024]{1,0:T(8,128)(2,1)S(1)} collective-permute-done((bf16[128,1024]{1,0:T(8,128)(2,1)S(1)}, bf16[128,1024]{1,0:T(8,128)(2,1)S(1)}, u32[]{:S(2)}, u32[]{:S(2)}) %collective-permute-start.20) | collective-permute-done | bytes 262176 | tf_op jit(solution)/shard_map/ppermute | solution.py:202
  79.3 0.5 collective-permute-start.32
  79.8 0.1 fusion.2
  79.9 5.0 %collective-permute-done.27 = bf16[128,1024]{1,0:T(8,128)(2,1)S(1)} collective-permute-done((bf16[128,1024]{1,0:T(8,128)(2,1)S(1)}, bf16[128,1024]{1,0:T(8,128)(2,1)S(1)}, u32[]{:S(2)}, u32[]{:S(2)}) %collective-permute-start.27) | collective-permute-done | bytes 262176 | tf_op jit(solution)/shard_map/ppermute | solution.py:202
  84.9 0.1 fusion.1
  85.0 4.6 %collective-permute-done.32 = bf16[128,1024]{1,0:T(8,128)(2,1)S(1)} collective-permute-done((bf16[128,1024]{1,0:T(8,128)(2,1)S(1)}, bf16[128,1024]{1,0:T(8,128)(2,1)S(1)}, u32[]{:S(2)}, u32[]{:S(2)}) %collective-permute-start.32) | collective-permute-done | bytes 262176 | tf_op jit(solution)/shard_map/ppermute | solution.py:202
  89.7 0.6 collective-permute-start.14
  90.2 0.1 fusion
  90.4 0.7 collective-permute-start.21
  91.1 1.5 %collective-permute-start.33 = (bf16[128,1024]{1,0:T(8,128)(2,1)S(1)}, bf16[128,1024]{1,0:T(8,128)(2,1)S(1)}, u32[]{:S(2)}, u32[]{:S(2)}) collective-permute-start(bf16[128,1024]{1,0:T(8,128)(2,1)S(1)} %fusion), channel_id=1, source_target_pairs={{0,4},{2,6},{4,8},{6,10},{8,12},{10,14},{12,0},{14,2},{1,5},{3,7},... | collective-permute-start | bytes 786440 | tf_op jit(solution)/shard_map/ppermute | solution.py:205
  92.5 8.1 %shard_map.122 = bf16[128,2048]{1,0:T(8,128)(2,1)} custom-call(s32[1]{0:T(128)} %bitcast.place_ref, bf16[128,2048]{1,0:T(8,128)(2,1)} %bitcast.78, bf16[128,2048]{1,0:T(8,128)(2,1)} %bitcast.80, bf16[128,2048]{1,0:T(8,128)(2,1)} %copy-done.8, bf16[128,2048]{1,0:T(8,128)(2,1)} %bitcast.81, bf16[128,2048]{1,0:T(8,128)(2,1)} %copy-done.9, s32[1,128]{1,0:T(1,128)} %doc_own.1, ...), custom_call_target="tpu_custom_call" | custom-call | flops 268435456 | bytes 3145728 | tf_op jit(solution)/shard_map/pallas_call | solution.py:64
  100.7 11.7 %collective-permute-done.28 = bf16[128,1024]{1,0:T(8,128)(2,1)S(1)} collective-permute-done((bf16[128,1024]{1,0:T(8,128)(2,1)S(1)}, bf16[128,1024]{1,0:T(8,128)(2,1)S(1)}, u32[]{:S(2)}, u32[]{:S(2)}) %collective-permute-start.28) | collective-permute-done | bytes 262176 | tf_op jit(solution)/shard_map/ppermute | solution.py:205
  112.4 1.0 fusion.11
  (55 shorter events, 0.1 us)
Async XLA Ops:
  0.6 20.6 %collective-permute-start.11 = (bf16[128,1024]{1,0:T(8,128)(2,1)}, bf16[128,1024]{1,0:T(8,128)(2,1)S(1)}, u32[]{:S(2)}, u32[]{:S(2)}) collective-permute-start(bf16[128,1024]{1,0:T(8,128)(2,1)} %bitcast.73), channel_id=1, source_target_pairs={{0,4},{2,6},{4,8},{6,10},{8,12},{10,14},{12,0},{14,2},{1,5},{3,7},... | collective-permute-start | bytes 786440 | tf_op jit(solution)/shard_map/ppermute | solution.py:205
  3.7 26.4 %collective-permute-start.9 = (bf16[128,1024]{1,0:T(8,128)(2,1)}, bf16[128,1024]{1,0:T(8,128)(2,1)S(1)}, u32[]{:S(2)}, u32[]{:S(2)}) collective-permute-start(bf16[128,1024]{1,0:T(8,128)(2,1)} %bitcast.74), channel_id=1, source_target_pairs={{0,2},{2,0},{4,6},{6,4},{8,10},{10,8},{12,14},{14,12},{1,3},{3,1},... | collective-permute-start | bytes 786440 | tf_op jit(solution)/shard_map/ppermute | solution.py:202
  5.2 28.0 %collective-permute-start.7 = (bf16[128,1024]{1,0:T(8,128)(2,1)}, bf16[128,1024]{1,0:T(8,128)(2,1)S(1)}, u32[]{:S(2)}, u32[]{:S(2)}) collective-permute-start(bf16[128,1024]{1,0:T(8,128)(2,1)} %bitcast.75), channel_id=1, source_target_pairs={{0,1},{1,0},{2,3},{3,2},{4,5},{5,4},{6,7},{7,6},{8,9},{9,8},{10,11... | collective-permute-start | bytes 786440 | tf_op jit(solution)/shard_map/ppermute | solution.py:199
  7.0 1.9 %collective-permute-start.3 = (f32[1,16,128]{2,1,0:T(8,128)}, f32[1,16,128]{2,1,0:T(8,128)S(1)}, u32[]{:S(2)}, u32[]{:S(2)}) collective-permute-start(f32[1,16,128]{2,1,0:T(8,128)} %bitcast.84), channel_id=1, source_target_pairs={{0,1},{1,0},{2,3},{3,2},{4,5},{5,4},{6,7},{7,6},{8,9},{9,8},{10,11... | collective-permute-start | bytes 24584 | tf_op jit(solution)/shard_map/ppermute | solution.py:199
  9.6 3.7 %collective-permute-start.4 = (f32[2,16,128]{2,1,0:T(8,128)S(1)}, f32[2,16,128]{2,1,0:T(8,128)S(1)}, u32[]{:S(2)}, u32[]{:S(2)}) collective-permute-start(f32[2,16,128]{2,1,0:T(8,128)S(1)} %pad_maximum_fusion.2), channel_id=1, source_target_pairs={{0,2},{2,0},{4,6},{6,4},{8,10},{10,8},{12,14},{14,12},{1,3},{3,1},... | collective-permute-start | bytes 49160 | tf_op jit(solution)/shard_map/ppermute | solution.py:202
  14.0 3.9 %collective-permute-start.5 = (f32[4,16,128]{2,1,0:T(8,128)S(1)}, f32[4,16,128]{2,1,0:T(8,128)S(1)}, u32[]{:S(2)}, u32[]{:S(2)}) collective-permute-start(f32[4,16,128]{2,1,0:T(8,128)S(1)} %pad_maximum_fusion.1), channel_id=1, source_target_pairs={{0,4},{2,6},{4,0},{6,2},{8,12},{10,14},{12,8},{14,10},{1,5},{3,7},... | collective-permute-start | bytes 98312 | tf_op jit(solution)/shard_map/ppermute | solution.py:219
  18.6 11.4 %collective-permute-start.6 = (f32[8,16,128]{2,1,0:T(8,128)S(1)}, f32[8,16,128]{2,1,0:T(8,128)S(1)}, u32[]{:S(2)}, u32[]{:S(2)}) collective-permute-start(f32[8,16,128]{2,1,0:T(8,128)S(1)} %pad_maximum_fusion), channel_id=1, source_target_pairs={{0,8},{2,10},{4,12},{6,14},{8,0},{10,2},{12,4},{14,6},{1,9},{3,11}... | collective-permute-start | bytes 196616 | tf_op jit(solution)/shard_map/ppermute | solution.py:219
  21.2 20.6 %collective-permute-start.17 = (bf16[128,1024]{1,0:T(8,128)(2,1)S(1)}, bf16[128,1024]{1,0:T(8,128)(2,1)S(1)}, u32[]{:S(2)}, u32[]{:S(2)}) collective-permute-start(bf16[128,1024]{1,0:T(8,128)(2,1)S(1)} %collective-permute-done.11.refs_2_), channel_id=1, source_target_pairs={{0,4},{2,6},{4,8},{6,10},{8,12},{10,14},{12,0},{14,2},{1,5},{3,7},... | collective-permute-start | bytes 786440 | tf_op jit(solution)/shard_map/ppermute | solution.py:205
  21.5 20.6 %collective-permute-start.15 = (bf16[128,1024]{1,0:T(8,128)(2,1)S(1)}, bf16[128,1024]{1,0:T(8,128)(2,1)S(1)}, u32[]{:S(2)}, u32[]{:S(2)}) collective-permute-start(bf16[128,1024]{1,0:T(8,128)(2,1)S(1)} %collective-permute-done.11.refs_2_), channel_id=1, source_target_pairs={{0,2},{2,0},{4,6},{6,4},{8,10},{10,8},{12,14},{14,12},{1,3},{3,1},... | collective-permute-start | bytes 786440 | tf_op jit(solution)/shard_map/ppermute | solution.py:202
  30.1 12.8 %collective-permute-start.12 = (bf16[128,1024]{1,0:T(8,128)(2,1)S(1)}, bf16[128,1024]{1,0:T(8,128)(2,1)S(1)}, u32[]{:S(2)}, u32[]{:S(2)}) collective-permute-start(bf16[128,1024]{1,0:T(8,128)(2,1)S(1)} %collective-permute-done.11.refs_2_), channel_id=1, source_target_pairs={{0,1},{1,0},{2,3},{3,2},{4,5},{5,4},{6,7},{7,6},{8,9},{9,8},{10,11... | collective-permute-start | bytes 786440 | tf_op jit(solution)/shard_map/ppermute | solution.py:199
  30.1 12.6 %collective-permute-start.10 = (bf16[128,1024]{1,0:T(8,128)(2,1)S(1)}, bf16[128,1024]{1,0:T(8,128)(2,1)S(1)}, u32[]{:S(2)}, u32[]{:S(2)}) collective-permute-start(bf16[128,1024]{1,0:T(8,128)(2,1)S(1)} %collective-permute-done.9.refs_0_), channel_id=1, source_target_pairs={{0,1},{1,0},{2,3},{3,2},{4,5},{5,4},{6,7},{7,6},{8,9},{9,8},{10,11... | collective-permute-start | bytes 786440 | tf_op jit(solution)/shard_map/ppermute | solution.py:199
  30.6 0.7 copy-start.10
  33.3 57.8 %collective-permute-start = (bf16[128,2048]{1,0:T(8,128)(2,1)}, bf16[128,2048]{1,0:T(8,128)(2,1)S(1)}, u32[]{:S(2)}, u32[]{:S(2)}) collective-permute-start(bf16[128,2048]{1,0:T(8,128)(2,1)} %bitcast.79), channel_id=1, source_target_pairs={{0,1},{1,0},{2,3},{3,2},{4,5},{5,4},{6,7},{7,6},{8,9},{9,8},{10,11... | collective-permute-start | bytes 1572872 | tf_op jit(solution)/shard_map/ppermute | solution.py:316
  33.3 2.2 %copy-start = (bf16[1,1024,2048]{2,1,0:T(8,128)(2,1)S(1)}, bf16[1,1024,2048]{2,1,0:T(8,128)(2,1)}, u32[]{:S(2)}) copy-start(bf16[1,1024,2048]{2,1,0:T(8,128)(2,1)} %param.16) | copy-start | bytes 12582916
  35.5 2.2 %copy-start.2 = (bf16[1,2048,1024]{2,1,0:T(8,128)(2,1)S(1)}, bf16[1,2048,1024]{2,1,0:T(8,128)(2,1)}, u32[]{:S(2)}) copy-start(bf16[1,2048,1024]{2,1,0:T(8,128)(2,1)} %param.17) | copy-start | bytes 12582916
  37.6 0.9 copy-start.4
  38.6 0.8 copy-start.5
  39.4 3.7 %copy-start.1 = (bf16[1,1024,2048]{2,1,0:T(8,128)(2,1)S(1)}, bf16[1,1024,2048]{2,1,0:T(8,128)(2,1)}, u32[]{:S(2)}) copy-start(bf16[1,1024,2048]{2,1,0:T(8,128)(2,1)} %param.16) | copy-start | bytes 12582916
  39.4 3.7 %copy-start.3 = (bf16[1,2048,1024]{2,1,0:T(8,128)(2,1)S(1)}, bf16[1,2048,1024]{2,1,0:T(8,128)(2,1)}, u32[]{:S(2)}) copy-start(bf16[1,2048,1024]{2,1,0:T(8,128)(2,1)} %param.17) | copy-start | bytes 12582916
  41.8 10.7 %collective-permute-start.24 = (bf16[128,1024]{1,0:T(8,128)(2,1)S(1)}, bf16[128,1024]{1,0:T(8,128)(2,1)S(1)}, u32[]{:S(2)}, u32[]{:S(2)}) collective-permute-start(bf16[128,1024]{1,0:T(8,128)(2,1)S(1)} %collective-permute-done.17.refs_2_), channel_id=1, source_target_pairs={{0,4},{2,6},{4,8},{6,10},{8,12},{10,14},{12,0},{14,2},{1,5},{3,7},... | collective-permute-start | bytes 786440 | tf_op jit(solution)/shard_map/ppermute | solution.py:205
  42.1 10.5 %collective-permute-start.22 = (bf16[128,1024]{1,0:T(8,128)(2,1)S(1)}, bf16[128,1024]{1,0:T(8,128)(2,1)S(1)}, u32[]{:S(2)}, u32[]{:S(2)}) collective-permute-start(bf16[128,1024]{1,0:T(8,128)(2,1)S(1)} %collective-permute-done.17.refs_2_), channel_id=1, source_target_pairs={{0,2},{2,0},{4,6},{6,4},{8,10},{10,8},{12,14},{14,12},{1,3},{3,1},... | collective-permute-start | bytes 786440 | tf_op jit(solution)/shard_map/ppermute | solution.py:202
  42.7 10.7 %collective-permute-start.18 = (bf16[128,1024]{1,0:T(8,128)(2,1)S(1)}, bf16[128,1024]{1,0:T(8,128)(2,1)S(1)}, u32[]{:S(2)}, u32[]{:S(2)}) collective-permute-start(bf16[128,1024]{1,0:T(8,128)(2,1)S(1)} %collective-permute-done.17.refs_2_), channel_id=1, source_target_pairs={{0,1},{1,0},{2,3},{3,2},{4,5},{5,4},{6,7},{7,6},{8,9},{9,8},{10,11... | collective-permute-start | bytes 786440 | tf_op jit(solution)/shard_map/ppermute | solution.py:199
  42.9 10.3 %collective-permute-start.16 = (bf16[128,1024]{1,0:T(8,128)(2,1)S(1)}, bf16[128,1024]{1,0:T(8,128)(2,1)S(1)}, u32[]{:S(2)}, u32[]{:S(2)}) collective-permute-start(bf16[128,1024]{1,0:T(8,128)(2,1)S(1)} %collective-permute-done.15.refs_0_), channel_id=1, source_target_pairs={{0,1},{1,0},{2,3},{3,2},{4,5},{5,4},{6,7},{7,6},{8,9},{9,8},{10,11... | collective-permute-start | bytes 786440 | tf_op jit(solution)/shard_map/ppermute | solution.py:199
  52.5 8.7 %copy-start.7 = (bf16[1,128,2048]{2,1,0:T(8,128)(2,1)S(1)}, bf16[1,128,2048]{2,1,0:T(8,128)(2,1)}, u32[]{:S(2)}) copy-start(bf16[1,128,2048]{2,1,0:T(8,128)(2,1)} %param.13) | copy-start | bytes 1572868
  52.5 13.8 %collective-permute-start.13 = (bf16[2,128,1024]{2,1,0:T(8,128)(2,1)S(1)}, bf16[2,128,1024]{2,1,0:T(8,128)(2,1)S(1)}, u32[]{:S(2)}, u32[]{:S(2)}) collective-permute-start(bf16[2,128,1024]{2,1,0:T(8,128)(2,1)S(1)} %get-tuple-element.15), channel_id=1, source_target_pairs={{0,1},{1,0},{2,3},{3,2},{4,5},{5,4},{6,7},{7,6},{8,9},{9,8},{10,11... | collective-permute-start | bytes 1572872 | tf_op jit(solution)/shard_map/ppermute | solution.py:199
  52.5 8.7 %collective-permute-start.29 = (bf16[128,1024]{1,0:T(8,128)(2,1)S(1)}, bf16[128,1024]{1,0:T(8,128)(2,1)S(1)}, u32[]{:S(2)}, u32[]{:S(2)}) collective-permute-start(bf16[128,1024]{1,0:T(8,128)(2,1)S(1)} %collective-permute-done.24.refs_2_), channel_id=1, source_target_pairs={{0,2},{2,0},{4,6},{6,4},{8,10},{10,8},{12,14},{14,12},{1,3},{3,1},... | collective-permute-start | bytes 786440 | tf_op jit(solution)/shard_map/ppermute | solution.py:202
  53.2 8.6 %collective-permute-start.25 = (bf16[128,1024]{1,0:T(8,128)(2,1)S(1)}, bf16[128,1024]{1,0:T(8,128)(2,1)S(1)}, u32[]{:S(2)}, u32[]{:S(2)}) collective-permute-start(bf16[128,1024]{1,0:T(8,128)(2,1)S(1)} %collective-permute-done.24.refs_2_), channel_id=1, source_target_pairs={{0,1},{1,0},{2,3},{3,2},{4,5},{5,4},{6,7},{7,6},{8,9},{9,8},{10,11... | collective-permute-start | bytes 786440 | tf_op jit(solution)/shard_map/ppermute | solution.py:199
  53.3 7.9 %collective-permute-start.23 = (bf16[128,1024]{1,0:T(8,128)(2,1)S(1)}, bf16[128,1024]{1,0:T(8,128)(2,1)S(1)}, u32[]{:S(2)}, u32[]{:S(2)}) collective-permute-start(bf16[128,1024]{1,0:T(8,128)(2,1)S(1)} %collective-permute-done.22.refs_0_), channel_id=1, source_target_pairs={{0,1},{1,0},{2,3},{3,2},{4,5},{5,4},{6,7},{7,6},{8,9},{9,8},{10,11... | collective-permute-start | bytes 786440 | tf_op jit(solution)/shard_map/ppermute | solution.py:199
  61.3 29.8 %collective-permute-start.1 = (bf16[128,2048]{1,0:T(8,128)(2,1)S(1)}, bf16[128,2048]{1,0:T(8,128)(2,1)S(1)}, u32[]{:S(2)}, u32[]{:S(2)}) collective-permute-start(bf16[128,2048]{1,0:T(8,128)(2,1)S(1)} %bitcast.82), channel_id=1, source_target_pairs={{0,1},{1,0},{2,3},{3,2},{4,5},{5,4},{6,7},{7,6},{8,9},{9,8},{10,11... | collective-permute-start | bytes 1572872 | tf_op jit(solution)/shard_map/ppermute | solution.py:317
  61.3 5.7 %copy-start.11 = (s32[1,128]{1,0:T(1,128)S(1)}, s32[1,128]{1,0:T(1,128)}, u32[]{:S(2)}) copy-start(s32[1,128]{1,0:T(1,128)} %doc_own.1) | copy-start | bytes 1540
  61.3 5.8 %copy-start.6 = (f32[128,16]{1,0:T(8,128)S(1)}, f32[128,16]{1,0:T(8,128)}, u32[]{:S(2)}) copy-start(f32[128,16]{1,0:T(8,128)} %shard_map.124.gates_ref) | copy-start | bytes 24580
  61.3 8.2 %collective-permute-start.19 = (bf16[2,128,1024]{2,1,0:T(8,128)(2,1)S(1)}, bf16[2,128,1024]{2,1,0:T(8,128)(2,1)S(1)}, u32[]{:S(2)}, u32[]{:S(2)}) collective-permute-start(bf16[2,128,1024]{2,1,0:T(8,128)(2,1)S(1)} %get-tuple-element.17), channel_id=1, source_target_pairs={{0,1},{1,0},{2,3},{3,2},{4,5},{5,4},{6,7},{7,6},{8,9},{9,8},{10,11... | collective-permute-start | bytes 1572872 | tf_op jit(solution)/shard_map/ppermute | solution.py:199
  61.8 5.2 %collective-permute-start.30 = (bf16[128,1024]{1,0:T(8,128)(2,1)S(1)}, bf16[128,1024]{1,0:T(8,128)(2,1)S(1)}, u32[]{:S(2)}, u32[]{:S(2)}) collective-permute-start(bf16[128,1024]{1,0:T(8,128)(2,1)S(1)} %collective-permute-done.29.refs_0_), channel_id=1, source_target_pairs={{0,1},{1,0},{2,3},{3,2},{4,5},{5,4},{6,7},{7,6},{8,9},{9,8},{10,11... | collective-permute-start | bytes 786440 | tf_op jit(solution)/shard_map/ppermute | solution.py:199
  66.4 3.6 %collective-permute-start.26 = (bf16[2,128,1024]{2,1,0:T(8,128)(2,1)S(1)}, bf16[2,128,1024]{2,1,0:T(8,128)(2,1)S(1)}, u32[]{:S(2)}, u32[]{:S(2)}) collective-permute-start(bf16[2,128,1024]{2,1,0:T(8,128)(2,1)S(1)} %get-tuple-element.19), channel_id=1, source_target_pairs={{0,1},{1,0},{2,3},{3,2},{4,5},{5,4},{6,7},{7,6},{8,9},{9,8},{10,11... | collective-permute-start | bytes 1572872 | tf_op jit(solution)/shard_map/ppermute | solution.py:199
  67.0 23.4 %collective-permute-start.2 = (s32[1,128]{1,0:T(1,128)S(1)}, s32[1,128]{1,0:T(1,128)S(1)}, u32[]{:S(2)}, u32[]{:S(2)}) collective-permute-start(s32[1,128]{1,0:T(1,128)S(1)} %copy-done.11), channel_id=1, source_target_pairs={{0,1},{1,0},{2,3},{3,2},{4,5},{5,4},{6,7},{7,6},{8,9},{9,8},{10,11... | collective-permute-start | bytes 1544 | tf_op jit(solution)/shard_map/ppermute | solution.py:318
  69.5 1.7 %collective-permute-start.31 = (bf16[1,128,1024]{2,1,0:T(8,128)(2,1)S(1)}, bf16[1,128,1024]{2,1,0:T(8,128)(2,1)S(1)}, u32[]{:S(2)}, u32[]{:S(2)}) collective-permute-start(bf16[1,128,1024]{2,1,0:T(8,128)(2,1)S(1)} %get-tuple-element.21), channel_id=1, source_target_pairs={{0,1},{1,0},{2,3},{3,2},{4,5},{5,4},{6,7},{7,6},{8,9},{9,8},{10,11... | collective-permute-start | bytes 786440 | tf_op jit(solution)/shard_map/ppermute | solution.py:199
  70.1 9.2 %collective-permute-start.20 = (bf16[128,1024]{1,0:T(8,128)(2,1)S(1)}, bf16[128,1024]{1,0:T(8,128)(2,1)S(1)}, u32[]{:S(2)}, u32[]{:S(2)}) collective-permute-start(bf16[128,1024]{1,0:T(8,128)(2,1)S(1)} %fusion.8), channel_id=1, source_target_pairs={{0,2},{2,0},{4,6},{6,4},{8,10},{10,8},{12,14},{14,12},{1,3},{3,1},... | collective-permute-start | bytes 786440 | tf_op jit(solution)/shard_map/ppermute | solution.py:202
  71.1 13.8 %collective-permute-start.27 = (bf16[128,1024]{1,0:T(8,128)(2,1)S(1)}, bf16[128,1024]{1,0:T(8,128)(2,1)S(1)}, u32[]{:S(2)}, u32[]{:S(2)}) collective-permute-start(bf16[128,1024]{1,0:T(8,128)(2,1)S(1)} %fusion.9), channel_id=1, source_target_pairs={{0,2},{2,0},{4,6},{6,4},{8,10},{10,8},{12,14},{14,12},{1,3},{3,1},... | collective-permute-start | bytes 786440 | tf_op jit(solution)/shard_map/ppermute | solution.py:202
  79.3 10.4 %collective-permute-start.32 = (bf16[128,1024]{1,0:T(8,128)(2,1)S(1)}, bf16[128,1024]{1,0:T(8,128)(2,1)S(1)}, u32[]{:S(2)}, u32[]{:S(2)}) collective-permute-start(bf16[128,1024]{1,0:T(8,128)(2,1)S(1)} %fusion.10), channel_id=1, source_target_pairs={{0,2},{2,0},{4,6},{6,4},{8,10},{10,8},{12,14},{14,12},{1,3},{3,1},... | collective-permute-start | bytes 786440 | tf_op jit(solution)/shard_map/ppermute | solution.py:202
  84.9 15.8 %collective-permute-start.8 = (bf16[1,128,1024]{2,1,0:T(8,128)(2,1)S(1)}, bf16[1,128,1024]{2,1,0:T(8,128)(2,1)S(1)}, u32[]{:S(2)}, u32[]{:S(2)}) collective-permute-start(bf16[1,128,1024]{2,1,0:T(8,128)(2,1)S(1)} %get-tuple-element.13), channel_id=1, source_target_pairs={{0,1},{1,0},{2,3},{3,2},{4,5},{5,4},{6,7},{7,6},{8,9},{9,8},{10,11... | collective-permute-start | bytes 786440 | tf_op jit(solution)/shard_map/ppermute | solution.py:199
  89.7 11.0 %collective-permute-start.14 = (bf16[128,1024]{1,0:T(8,128)(2,1)S(1)}, bf16[128,1024]{1,0:T(8,128)(2,1)S(1)}, u32[]{:S(2)}, u32[]{:S(2)}) collective-permute-start(bf16[128,1024]{1,0:T(8,128)(2,1)S(1)} %fusion.7), channel_id=1, source_target_pairs={{0,2},{2,0},{4,6},{6,4},{8,10},{10,8},{12,14},{14,12},{1,3},{3,1},... | collective-permute-start | bytes 786440 | tf_op jit(solution)/shard_map/ppermute | solution.py:202
  90.3 2.2 %copy-start.12 = (s32[1,128]{1,0:T(1,128)}, s32[1,128]{1,0:T(1,128)S(1)}, u32[]{:S(2)}) copy-start(s32[1,128]{1,0:T(1,128)S(1)} %collective-permute-done.2.doc_far) | copy-start | bytes 1540
  90.4 10.3 %collective-permute-start.21 = (bf16[128,1024]{1,0:T(8,128)(2,1)S(1)}, bf16[128,1024]{1,0:T(8,128)(2,1)S(1)}, u32[]{:S(2)}, u32[]{:S(2)}) collective-permute-start(bf16[128,1024]{1,0:T(8,128)(2,1)S(1)} %fusion.2), channel_id=1, source_target_pairs={{0,12},{2,14},{4,0},{6,2},{8,4},{10,6},{12,8},{14,10},{1,13},{3,15... | collective-permute-start | bytes 786440 | tf_op jit(solution)/shard_map/ppermute | solution.py:205
  91.0 1.5 %copy-start.8 = (bf16[128,2048]{1,0:T(8,128)(2,1)}, bf16[128,2048]{1,0:T(8,128)(2,1)S(1)}, u32[]{:S(2)}) copy-start(bf16[128,2048]{1,0:T(8,128)(2,1)S(1)} %collective-permute-done.k_far) | copy-start | bytes 1572868
  91.0 21.3 %collective-permute-start.28 = (bf16[128,1024]{1,0:T(8,128)(2,1)S(1)}, bf16[128,1024]{1,0:T(8,128)(2,1)S(1)}, u32[]{:S(2)}, u32[]{:S(2)}) collective-permute-start(bf16[128,1024]{1,0:T(8,128)(2,1)S(1)} %fusion.1), channel_id=1, source_target_pairs={{0,8},{2,10},{4,12},{6,14},{8,0},{10,2},{12,4},{14,6},{1,9},{3,11}... | collective-permute-start | bytes 786440 | tf_op jit(solution)/shard_map/ppermute | solution.py:205
  91.1 1.5 %copy-start.9 = (bf16[128,2048]{1,0:T(8,128)(2,1)}, bf16[128,2048]{1,0:T(8,128)(2,1)S(1)}, u32[]{:S(2)}) copy-start(bf16[128,2048]{1,0:T(8,128)(2,1)S(1)} %collective-permute-done.1.v_far) | copy-start | bytes 1572868
  91.1 21.3 %collective-permute-start.33 = (bf16[128,1024]{1,0:T(8,128)(2,1)S(1)}, bf16[128,1024]{1,0:T(8,128)(2,1)S(1)}, u32[]{:S(2)}, u32[]{:S(2)}) collective-permute-start(bf16[128,1024]{1,0:T(8,128)(2,1)S(1)} %fusion), channel_id=1, source_target_pairs={{0,4},{2,6},{4,8},{6,10},{8,12},{10,14},{12,0},{14,2},{1,5},{3,7},... | collective-permute-start | bytes 786440 | tf_op jit(solution)/shard_map/ppermute | solution.py:205

commit v2 on v1

--- a/solution.py
+++ b/solution.py
@@ -98,102 +98,106 @@
     )(latent, router.T, routes.transpose(2, 0, 1))
 
 
-def kept_kernel(own_ref, order_ref, capacity_ref, table_ref, out_ref):
+def kept_kernel(line, own_ref, capacity_ref, *refs):
+    tables, out_ref = refs[:-1], refs[-1]
     own = own_ref[0]
-    table = table_ref[:, own, :]
-    sources, rows = table.shape
-    named = table != -1.0
-    flags = jnp.where(named, 1.0, 0.0)
+    z = own // 4
+    rows = tables[0].shape[2]
+    sources = 4 * line
     upto = lax.broadcasted_iota(jnp.int32, (rows, rows), 0) <= lax.broadcasted_iota(
         jnp.int32, (rows, rows), 1
     )
-    running = jnp.dot(
-        flags.astype(jnp.bfloat16),
-        jnp.where(upto, 1.0, 0.0).astype(jnp.bfloat16),
-        preferred_element_type=jnp.float32,
-    )
+    upto = jnp.where(upto, 1.0, 0.0).astype(jnp.bfloat16)
     device = lax.broadcasted_iota(jnp.int32, (sources, sources), 0) ^ own
     other = lax.broadcasted_iota(jnp.int32, (sources, sources), 1) ^ own
-    totals = jnp.broadcast_to(running[:, rows - 1 :], (sources, rows))
-    before = jnp.dot(
-        jnp.where(other < device, 1.0, 0.0).astype(jnp.bfloat16),
-        totals.astype(jnp.bfloat16),
-        preferred_element_type=jnp.float32,
-    )
-    slots = before + running - flags
-    limit = capacity_ref[own].astype(jnp.float32)
-    kept = jnp.where(named & (slots < limit), table, 0.0)
-    entry = lax.broadcasted_iota(jnp.int32, table.shape, 0)
-    ordered = [
-        jnp.sum(jnp.where(entry == order_ref[place], kept, 0.0), axis=0, keepdims=True)
-        for place in range(sources)
-    ]
+    lower = jnp.where(other < device, 1.0, 0.0).astype(jnp.bfloat16)
+    entry = lax.broadcasted_iota(jnp.int32, (sources, rows), 0)
+    gates = []
+    for which in range(2):
+        expert = own ^ which
+        table = jnp.concatenate([part[:, expert, :] for part in tables], axis=0)
+        named = table != -1.0
+        flags = jnp.where(named, 1.0, 0.0)
+        running = jnp.dot(flags.astype(jnp.bfloat16), upto, preferred_element_type=jnp.float32)
+        totals = jnp.broadcast_to(running[:, rows - 1 :], (sources, rows)).astype(jnp.bfloat16)
+        before = jnp.dot(lower, totals, preferred_element_type=jnp.float32)
+        slots = before + running - flags
+        limit = capacity_ref[expert].astype(jnp.float32)
+        gates.append(jnp.where(named & (slots < limit), table, 0.0))
+    ordered = []
+    for step in range(line):
+        home = 4 * (z ^ lax.rem(z + line - step, line))
+        for side in range(2):
+            for kept in gates:
+                here = jnp.where(entry == home + 2 * side, kept, 0.0)
+                ordered.append(jnp.sum(here, axis=0, keepdims=True))
     out_ref[...] = jnp.concatenate(ordered, axis=0).T
 
 
-def kept_gates(own, order, capacity, table):
+def kept_gates(own, capacity, tables):
     smem = pl.BlockSpec(memory_space=pltpu.SMEM)
     vmem = pl.BlockSpec(memory_space=pltpu.VMEM)
+    line, rows = len(tables), tables[0].shape[2]
     return pl.pallas_call(
-        kept_kernel,
-        out_shape=jax.ShapeDtypeStruct((table.shape[2], table.shape[0]), jnp.float32),
-        in_specs=[smem, smem, smem, vmem],
+        functools.partial(kept_kernel, line),
+        out_shape=jax.ShapeDtypeStruct((rows, 4 * line), jnp.float32),
+        in_specs=[smem, smem] + [vmem] * line,
         out_specs=vmem,
-    )(own, order, capacity, table)
-
-
-def expert_kernel(columns, gates_ref, *refs):
-    count = len(columns)
-    blocks, (w1_ref, w2_ref, keep_ref, give_ref, hidden_ref) = refs[:count], refs[count:]
-    rows = blocks[0].shape[0]
-    x = jnp.concatenate([block[...] for block in blocks], axis=0)
+    )(own, capacity, *tables)
+
+
+def expert_kernel(place, gates_ref, xz_ref, xy_ref, w1a, w2a, w1b, w2b, z_ref, y_ref, hidden_ref):
+    rows = xz_ref.shape[0]
+    x = jnp.concatenate([xz_ref[...], xy_ref[...]], axis=0)
     step = 512
-    for first in range(0, w1_ref.shape[1], step):
+    for which, w1_ref in enumerate((w1a, w1b)):
+        for first in range(0, w1_ref.shape[1], step):
+            cols = slice(first, first + step)
+            hidden = jnp.dot(x, w1_ref[:, cols], preferred_element_type=jnp.float32)
+            hidden = jnp.maximum(hidden, 0.0)
+            hidden_ref[which, :, cols] = (hidden * hidden).astype(jnp.bfloat16)
+    for first in range(0, w2a.shape[1], step):
         cols = slice(first, first + step)
-        hidden = jnp.maximum(jnp.dot(x, w1_ref[:, cols], preferred_element_type=jnp.float32), 0.0)
-        hidden_ref[:, cols] = (hidden * hidden).astype(jnp.bfloat16)
-    for first in range(0, w2_ref.shape[1], step):
-        cols = slice(first, first + step)
-        result = jnp.dot(hidden_ref[...], w2_ref[:, cols], preferred_element_type=jnp.float32)
-        for index, column in enumerate(columns):
-            gate = gates_ref[:, column : column + 1]
-            part = result[index * rows : (index + 1) * rows]
-            out = give_ref if index % 2 else keep_ref
-            out[index // 2, :, cols] = (part * gate).astype(jnp.bfloat16)
-
-
-def run_pieces(gates, pieces, w_first, w_second):
-    columns, blocks = [], []
-    for place, mine, theirs in pieces:
-        columns += [2 * place, 2 * place + 1]
-        blocks += [mine, theirs]
-    rows, width = blocks[0].shape
+        results = [
+            jnp.dot(hidden_ref[which], w2_ref[:, cols], preferred_element_type=jnp.float32)
+            for which, w2_ref in enumerate((w2a, w2b))
+        ]
+        for side, out_ref in enumerate((z_ref, y_ref)):
+            column = 4 * place + 2 * side
+            part = slice(side * rows, (side + 1) * rows)
+            mixed = results[0][part] * gates_ref[:, column : column + 1]
+            mixed += results[1][part] * gates_ref[:, column + 1 : column + 2]
+            out_ref[:, cols] = mixed.astype(jnp.bfloat16)
+
+
+def run_piece(place, gates, from_line, from_side, weights):
+    rows, width = from_line.shape
+    hidden = weights[0].shape[1]
     vmem = pl.BlockSpec(memory_space=pltpu.VMEM)
-    half = jax.ShapeDtypeStruct((len(pieces), rows, width), jnp.bfloat16)
+    piece = jax.ShapeDtypeStruct((rows, width), jnp.bfloat16)
     return pl.pallas_call(
-        functools.partial(expert_kernel, tuple(columns)),
-        out_shape=(half, half),
-        in_specs=[vmem] * (3 + len(blocks)),
+        functools.partial(expert_kernel, place),
+        out_shape=(piece, piece),
+        in_specs=[vmem] * 7,
         out_specs=(vmem, vmem),
-        scratch_shapes=[pltpu.VMEM((rows * len(blocks), w_first.shape[1]), jnp.bfloat16)],
+        scratch_shapes=[pltpu.VMEM((2, 2 * rows, hidden), jnp.bfloat16)],
         compiler_params=pltpu.CompilerParams(vmem_limit_bytes=EXPERT_VMEM),
         cost_estimate=pl.CostEstimate(
-            flops=4 * rows * len(blocks) * w_first.size,
-            bytes_accessed=4 * rows * len(blocks) * width + 4 * w_first.size,
+            flops=16 * rows * width * hidden,
+            bytes_accessed=8 * rows * width + 8 * width * hidden,
             transcendentals=0,
         ),
-    )(gates, *blocks, w_first, w_second)
+    )(gates, from_line, from_side, *weights)
 
 
 def dense_moe(latent, router, expert_in, expert_out, routes, capacity):
     f32 = jnp.float32
+    axes = ("expert", "context")
     line = router.shape[1] // 4
     spots = [(z, y) for z in range(line) for y in range(2)]
     sibling = [(0, 1), (1, 0)]
     across = [(2 * z + y, 2 * z + 1 - y) for z, y in spots]
-
-    def toward(step):
-        return [(2 * z + y, 2 * ((z + step) % line) + y) for z, y in spots]
+    diagonal = [(4 * z + k, 4 * z + 3 - k) for z in range(line) for k in range(4)]
 
     def swap_core(x):
         return lax.ppermute(x, "context", sibling)
@@ -202,49 +206,32 @@
         return lax.ppermute(x, "expert", across)
 
     def along(x, step):
-        return lax.ppermute(x, "expert", toward(step))
-
-    own = lax.axis_index(("expert", "context")).astype(jnp.int32)
-    z = own // 4
-    order = jnp.stack(
-        [4 * (z ^ ((z - step) % line)) + rest for step in range(line) for rest in range(4)]
-    )
-
-    table = gate_table(latent[0], router, routes)[None]
-    table = jnp.concatenate([table, swap_core(table)], axis=0)
-    table = jnp.concatenate([table, swap_side(table)], axis=0)
-    span = 1
-    while span < line:
-        flip = [(2 * z + y, 2 * (z ^ span) + y) for z, y in spots]
-        table = jnp.concatenate([table, lax.ppermute(table, "expert", flip)], axis=0)
-        span *= 2
-    gates = kept_gates(own.reshape(1), order, capacity, table)
-
-    chunk = latent[0]
-    ahead, side = [], []
-    for step in range(line):
+        return lax.ppermute(x, "expert", [(2 * z + y, 2 * ((z + step) % line) + y) for z, y in spots])
+
+    def flipped(x, span):
+        return lax.ppermute(x, "expert", [(2 * z + y, 2 * (z ^ span) + y) for z, y in spots])
+
+    own = lax.axis_index(axes).astype(jnp.int32).reshape(1)
+    rows = latent[0]
+    from_line = [rows] + [along(rows, step) for step in range(1, line)]
+    from_side = [swap_side(x) for x in from_line]
+    w_first, w_second = expert_in[0], expert_out[0]
+    weights = (w_first, w_second, swap_core(w_first), swap_core(w_second))
+
+    table = gate_table(rows, router, routes)[None]
+    table = jnp.concatenate(
+        [table, swap_core(table), swap_side(table), lax.ppermute(table, axes, diagonal)], axis=0
+    )
+    tables = [table] + [flipped(table, span) for span in range(1, line)]
+    gates = kept_gates(own, capacity, tables)
+
+    total = None
+    for step in list(range(1, line)) + [0]:
+        mine, theirs = run_piece(step, gates, from_line[step], from_side[step], weights)
+        column = mine.astype(f32) + swap_side(theirs).astype(f32)
         if step:
-            chunk = along(chunk, 1)
-        beside = swap_side(chunk)
-        ahead.append((2 * step, chunk, swap_core(chunk)))
-        side.append((2 * step + 1, beside, swap_core(beside)))
-
-    total = None
-    waiting = None
-    for step in range(line + 1):
-        pieces = ([side[step - 1]] if step else []) + ([ahead[step]] if step < line else [])
-        keep, give = run_pieces(gates, pieces, expert_in[0], expert_out[0])
-        got = swap_core(give)
-        if step:
-            crossing = (keep[0].astype(f32) + got[0].astype(f32)).astype(jnp.bfloat16)
-            arrived = swap_side(crossing)
-            column = waiting[0].astype(f32) + waiting[1].astype(f32) + arrived.astype(f32)
-            if step == 1:
-                total = column
-            else:
-                sent = along(column.astype(jnp.bfloat16), line - (step - 1))
-                total = total + sent.astype(f32)
-        waiting = (keep[-1], got[-1])
+            column = along(column.astype(jnp.bfloat16), line - step).astype(f32)
+        total = column if total is None else total + column
     return total.astype(jnp.bfloat16)[None]
 
 

time: 114 us -> 124 us (1.088)
  Pallas kernels: 30.1 us -> 44.1 us
  starting transfers between devices: 20 us -> 30.6 us
  waiting for transfers between devices: 50.2 us -> 39.9 us
  local copies, waits for them, and re-layouts: 8.23 us -> 6.09 us
  other arithmetic: 3.91 us -> 1.82 us
    pallas_call x6 -> x5, Pallas kernels: 20.2 us -> 34.2 us  [the longest x4 32.1 us: run_piece(): pl.pallas_call(functools.partial(expert_kernel, place), out_shape=(piece,...]
    ppermute x9, waiting for transfers between devices: 22.6 us -> 10.8 us  [swap_side(): return lax.ppermute(x, 'expert', across)]
    ppermute x8 -> x10, starting transfers between devices: 9.84 us -> 20.2 us  [the longest x3 10.7 us: flipped(): lax.ppermute(x, 'expert', [(2 * z + y, 2 * (z ^ span) + y) for z, y in sp...]
    ppermute x14 -> x3, starting transfers between devices: 3.58 us -> 0.6 us  [swap_core(): return lax.ppermute(x, 'context', sibling)]
    ppermute x9, starting transfers between devices: 6.46 us -> 9.2 us  [swap_side(): return lax.ppermute(x, 'expert', across)]
    unnamed x30 -> x28, local copies, waits for them, and re-layouts: 7.56 us -> 6.09 us
    concatenate x3 -> x1, other arithmetic: 2.1 us -> 0.7 us  [dense_moe(): jnp.concatenate([table, swap_core(table), swap_side(table), lax.ppermute(...]
    ppermute x8 -> x10, waiting for transfers between devices: 27.1 us -> 27.8 us  [the longest x6 16.7 us: along(): lax.ppermute(x, 'expert', [(2 * z + y, 2 * ((z + step) % line) + y) for z...]
  transfers between devices with their start and end apart: 34 -> 25, of which waited for: 10 -> 10; matrix products, arithmetic and copies ran while one was open for 4% -> 1% of each run, Pallas kernels for 27% -> 36%
where the time goes in v2:
time: 124 us; the launch traced here: 123 us
  Pallas kernels  44.1 us (36%)
  waiting for transfers between devices  39.9 us (32%)
  starting transfers between devices  30.6 us (25%)
  local copies, waits for them, and re-layouts  6.09 us (5%)
  other arithmetic  1.82 us (1%)
    pallas_call x4, Pallas kernels, run_piece(): pl.pallas_call(functools.partial(expert_kernel, place), out_shape=(piece,...  32.1 us
    ppermute x6, waiting for transfers between devices, along(): lax.ppermute(x, 'expert', [(2 * z + y, 2 * ((z + step) % line) + y) for z...  16.7 us
    ppermute x9, waiting for transfers between devices, swap_side(): return lax.ppermute(x, 'expert', across)  10.8 us
    ppermute x3, starting transfers between devices, flipped(): lax.ppermute(x, 'expert', [(2 * z + y, 2 * (z ^ span) + y) for z, y in sp...  10.7 us
    ppermute x6, starting transfers between devices, along(): lax.ppermute(x, 'expert', [(2 * z + y, 2 * ((z + step) % line) + y) for z...  9.51 us
    ppermute x9, starting transfers between devices, swap_side(): return lax.ppermute(x, 'expert', across)  9.2 us
    pallas_call x1, Pallas kernels, attend(): pl.pallas_call(attend_kernel, out_shape=jax.ShapeDtypeStruct(q.shape, jnp...  8.12 us
    ppermute x3, waiting for transfers between devices, flipped(): lax.ppermute(x, 'expert', [(2 * z + y, 2 * (z ^ span) + y) for z, y in sp...  7.76 us
  transfers between devices with their start and end apart: 25, of which 10 were waited for; matrix products, arithmetic and copies ran while one was open for 1% of the time, Pallas kernels for 36%

profile of v2, /device:TPU:0, one launch (start us, length us, event | category | flops | bytes accessed | tf_op | source)
XLA Modules:
  0.0 123.3 jit_solution(16455443060369977077)
XLA Ops:
  0.6 0.5 collective-permute-start.11
  1.1 0.1 collective-permute-start.12
  1.2 3.0 %collective-permute-start.9 = (bf16[128,1024]{1,0:T(8,128)(2,1)}, bf16[128,1024]{1,0:T(8,128)(2,1)S(1)}, u32[]{:S(2)}, u32[]{:S(2)}) collective-permute-start(bf16[128,1024]{1,0:T(8,128)(2,1)} %bitcast.24), channel_id=1, source_target_pairs={{0,4},{2,6},{4,8},{6,10},{8,12},{10,14},{12,0},{14,2},{1,5},{3,7},... | collective-permute-start | bytes 786440 | tf_op jit(solution)/shard_map/ppermute | solution.py:209
  4.2 2.6 %collective-permute-start.15 = (bf16[128,1024]{1,0:T(8,128)(2,1)}, bf16[128,1024]{1,0:T(8,128)(2,1)S(1)}, u32[]{:S(2)}, u32[]{:S(2)}) collective-permute-start(bf16[128,1024]{1,0:T(8,128)(2,1)} %bitcast.25), channel_id=1, source_target_pairs={{0,8},{2,10},{4,12},{6,14},{8,0},{10,2},{12,4},{14,6},{1,9},{3,11}... | collective-permute-start | bytes 786440 | tf_op jit(solution)/shard_map/ppermute | solution.py:209
  6.8 6.8 %collective-permute-done.9.xz_ref = bf16[128,1024]{1,0:T(8,128)(2,1)S(1)} collective-permute-done((bf16[128,1024]{1,0:T(8,128)(2,1)}, bf16[128,1024]{1,0:T(8,128)(2,1)S(1)}, u32[]{:S(2)}, u32[]{:S(2)}) %collective-permute-start.9) | collective-permute-done | bytes 262176 | tf_op jit(solution)/shard_map/ppermute | solution.py:209
  13.7 1.8 %collective-permute-start.10 = (bf16[128,1024]{1,0:T(8,128)(2,1)S(1)}, bf16[128,1024]{1,0:T(8,128)(2,1)S(1)}, u32[]{:S(2)}, u32[]{:S(2)}) collective-permute-start(bf16[128,1024]{1,0:T(8,128)(2,1)S(1)} %collective-permute-done.9.xz_ref), channel_id=1, source_target_pairs={{0,2},{2,0},{4,6},{6,4},{8,10},{10,8},{12,14},{14,12},{1,3},{3,1},... | collective-permute-start | bytes 786440 | tf_op jit(solution)/shard_map/ppermute | solution.py:206
  15.4 1.8 %shard_map.123 = f32[16,128]{1,0:T(8,128)} custom-call(bf16[128,1024]{1,0:T(8,128)(2,1)} %bitcast.26, bf16[16,1024]{1,0:T(8,128)(2,1)} %bitcast.36, s32[6,1,128]{2,1,0:T(1,128)} %bitcast.41), custom_call_target="tpu_custom_call" | custom-call | tf_op jit(solution)/shard_map/pallas_call | solution.py:93
  17.2 0.0 collective-permute-start.3
  17.2 1.4 %collective-permute-done.3 = f32[1,16,128]{2,1,0:T(8,128)S(1)} collective-permute-done((f32[1,16,128]{2,1,0:T(8,128)}, f32[1,16,128]{2,1,0:T(8,128)S(1)}, u32[]{:S(2)}, u32[]{:S(2)}) %collective-permute-start.3) | collective-permute-done | bytes 8224 | tf_op jit(solution)/shard_map/ppermute | solution.py:203
  18.6 0.3 collective-permute-start.4
  18.9 3.6 %collective-permute-done.4 = f32[1,16,128]{2,1,0:T(8,128)S(1)} collective-permute-done((f32[1,16,128]{2,1,0:T(8,128)}, f32[1,16,128]{2,1,0:T(8,128)S(1)}, u32[]{:S(2)}, u32[]{:S(2)}) %collective-permute-start.4) | collective-permute-done | bytes 8224 | tf_op jit(solution)/shard_map/ppermute | solution.py:206
  22.5 0.0 collective-permute-start.5
  22.5 3.3 %collective-permute-done.5 = f32[1,16,128]{2,1,0:T(8,128)S(1)} collective-permute-done((f32[1,16,128]{2,1,0:T(8,128)}, f32[1,16,128]{2,1,0:T(8,128)S(1)}, u32[]{:S(2)}, u32[]{:S(2)}) %collective-permute-start.5) | collective-permute-done | bytes 8224 | tf_op jit(solution)/shard_map/ppermute | solution.py:223
  25.7 0.7 pad_maximum_fusion.refs_0_
  26.4 4.5 %collective-permute-start.6 = (f32[4,16,128]{2,1,0:T(8,128)S(1)}, f32[4,16,128]{2,1,0:T(8,128)S(1)}, u32[]{:S(2)}, u32[]{:S(2)}) collective-permute-start(f32[4,16,128]{2,1,0:T(8,128)S(1)} %pad_maximum_fusion.refs_0_), channel_id=1, source_target_pairs={{0,4},{2,6},{4,0},{6,2},{8,12},{10,14},{12,8},{14,10},{1,5},{3,7},... | collective-permute-start | bytes 98312 | tf_op jit(solution)/shard_map/ppermute | solution.py:212
  31.0 1.9 %collective-permute-done.6.refs_1_ = f32[4,16,128]{2,1,0:T(8,128)S(1)} collective-permute-done((f32[4,16,128]{2,1,0:T(8,128)S(1)}, f32[4,16,128]{2,1,0:T(8,128)S(1)}, u32[]{:S(2)}, u32[]{:S(2)}) %collective-permute-start.6) | collective-permute-done | bytes 32800 | tf_op jit(solution)/shard_map/ppermute | solution.py:212
  32.8 4.1 %collective-permute-start.7 = (f32[4,16,128]{2,1,0:T(8,128)S(1)}, f32[4,16,128]{2,1,0:T(8,128)S(1)}, u32[]{:S(2)}, u32[]{:S(2)}) collective-permute-start(f32[4,16,128]{2,1,0:T(8,128)S(1)} %pad_maximum_fusion.refs_0_), channel_id=1, source_target_pairs={{0,8},{2,10},{4,12},{6,14},{8,0},{10,2},{12,4},{14,6},{1,9},{3,11}... | collective-permute-start | bytes 98312 | tf_op jit(solution)/shard_map/ppermute | solution.py:212
  36.9 1.9 %collective-permute-done.7.refs_2_ = f32[4,16,128]{2,1,0:T(8,128)S(1)} collective-permute-done((f32[4,16,128]{2,1,0:T(8,128)S(1)}, f32[4,16,128]{2,1,0:T(8,128)S(1)}, u32[]{:S(2)}, u32[]{:S(2)}) %collective-permute-start.7) | collective-permute-done | bytes 32800 | tf_op jit(solution)/shard_map/ppermute | solution.py:212
  38.8 2.1 %collective-permute-start.8 = (f32[4,16,128]{2,1,0:T(8,128)S(1)}, f32[4,16,128]{2,1,0:T(8,128)S(1)}, u32[]{:S(2)}, u32[]{:S(2)}) collective-permute-start(f32[4,16,128]{2,1,0:T(8,128)S(1)} %pad_maximum_fusion.refs_0_), channel_id=1, source_target_pairs={{0,12},{2,14},{4,8},{6,10},{8,4},{10,6},{12,0},{14,2},{1,13},{3,15... | collective-permute-start | bytes 98312 | tf_op jit(solution)/shard_map/ppermute | solution.py:212
  40.9 4.0 %collective-permute-done.8.refs_3_ = f32[4,16,128]{2,1,0:T(8,128)S(1)} collective-permute-done((f32[4,16,128]{2,1,0:T(8,128)S(1)}, f32[4,16,128]{2,1,0:T(8,128)S(1)}, u32[]{:S(2)}, u32[]{:S(2)}) %collective-permute-start.8) | collective-permute-done | bytes 32800 | tf_op jit(solution)/shard_map/ppermute | solution.py:212
  44.9 1.8 %collective-permute-start.19 = (bf16[128,1024]{1,0:T(8,128)(2,1)}, bf16[128,1024]{1,0:T(8,128)(2,1)S(1)}, u32[]{:S(2)}, u32[]{:S(2)}) collective-permute-start(bf16[128,1024]{1,0:T(8,128)(2,1)} %bitcast.27), channel_id=1, source_target_pairs={{0,12},{2,14},{4,0},{6,2},{8,4},{10,6},{12,8},{14,10},{1,13},{3,15... | collective-permute-start | bytes 786440 | tf_op jit(solution)/shard_map/ppermute | solution.py:209
  46.7 2.1 %shard_map.124.gates_ref = f32[128,16]{1,0:T(8,128)} custom-call(s32[1]{0:T(128)} %bitcast.5.own_ref, s32[16]{0:T(128)} %capacity_ref.1, f32[4,16,128]{2,1,0:T(8,128)} %copy-done.8, f32[4,16,128]{2,1,0:T(8,128)} %copy-done.9, f32[4,16,128]{2,1,0:T(8,128)} %copy-done.10, f32[4,16,128]{2,1,0:T(8,128)} %copy-done.11), custom_call_target="tpu_custom_call" | custom-call | tf_op jit(solution)/shard_map/pallas_call | solution.py:141
  48.8 0.0 collective-permute-done.15.xz_ref
  48.8 0.5 collective-permute-start.23
  49.3 0.0 collective-permute-done.10.xy_ref
  49.3 0.0 collective-permute-start
  49.3 0.0 collective-permute-done.11.w1b
  49.3 0.0 copy-start.12
  49.3 0.5 collective-permute-start.1
  49.8 0.0 collective-permute-done.12.w2b
  49.8 1.5 %collective-permute-start.16 = (bf16[128,1024]{1,0:T(8,128)(2,1)S(1)}, bf16[128,1024]{1,0:T(8,128)(2,1)S(1)}, u32[]{:S(2)}, u32[]{:S(2)}) collective-permute-start(bf16[128,1024]{1,0:T(8,128)(2,1)S(1)} %collective-permute-done.15.xz_ref), channel_id=1, source_target_pairs={{0,2},{2,0},{4,6},{6,4},{8,10},{10,8},{12,14},{14,12},{1,3},{3,1},... | collective-permute-start | bytes 786440 | tf_op jit(solution)/shard_map/ppermute | solution.py:206
  51.3 2.2 %copy-done = bf16[1,1024,2048]{2,1,0:T(8,128)(2,1)S(1)} copy-done((bf16[1,1024,2048]{2,1,0:T(8,128)(2,1)S(1)}, bf16[1,1024,2048]{2,1,0:T(8,128)(2,1)}, u32[]{:S(2)}) %copy-start) | copy-done | bytes 4194328
  53.5 2.2 %copy-done.2 = bf16[1,2048,1024]{2,1,0:T(8,128)(2,1)S(1)} copy-done((bf16[1,2048,1024]{2,1,0:T(8,128)(2,1)S(1)}, bf16[1,2048,1024]{2,1,0:T(8,128)(2,1)}, u32[]{:S(2)}) %copy-start.2) | copy-done | bytes 4194328
  55.7 0.8 copy-done.3
  56.5 8.0 %shard_map.125 = (bf16[128,1024]{1,0:T(8,128)(2,1)S(1)}, bf16[128,1024]{1,0:T(8,128)(2,1)S(1)}) custom-call(f32[128,16]{1,0:T(8,128)S(1)} %copy-done.3, bf16[128,1024]{1,0:T(8,128)(2,1)S(1)} %collective-permute-done.9.xz_ref, bf16[128,1024]{1,0:T(8,128)(2,1)S(1)} %collective-permute-done.10.xy_ref, bf16[1024,2048]{1,0:T(8,128)(2,1)S(1)} %bitcast.15, ...), custom_call_target="tpu_custom_call" | custom-call | flops 4294967296 | bytes 17825792 | tf_op jit(solution)/shard_map/pallas_call | solution.py:178
  64.5 0.0 collective-permute-done.19.xz_ref
  64.5 0.1 collective-permute-start.2
  64.6 0.6 collective-permute-start.20
  65.2 8.0 %shard_map.126 = (bf16[128,1024]{1,0:T(8,128)(2,1)S(1)}, bf16[128,1024]{1,0:T(8,128)(2,1)S(1)}) custom-call(f32[128,16]{1,0:T(8,128)S(1)} %copy-done.3, bf16[128,1024]{1,0:T(8,128)(2,1)S(1)} %collective-permute-done.15.xz_ref, bf16[128,1024]{1,0:T(8,128)(2,1)S(1)} %collective-permute-done.16.xy_ref, bf16[1024,2048]{1,0:T(8,128)(2,1)S(1)} %bitcast.16, ...), custom_call_target="tpu_custom_call" | custom-call | flops 4294967296 | bytes 17825792 | tf_op jit(solution)/shard_map/pallas_call | solution.py:178
  73.2 0.2 collective-permute-done.20.xy_ref
  73.3 1.5 %collective-permute-start.13 = (bf16[128,1024]{1,0:T(8,128)(2,1)S(1)}, bf16[128,1024]{1,0:T(8,128)(2,1)S(1)}, u32[]{:S(2)}, u32[]{:S(2)}) collective-permute-start(bf16[128,1024]{1,0:T(8,128)(2,1)S(1)} %get-tuple-element.11), channel_id=1, source_target_pairs={{0,2},{2,0},{4,6},{6,4},{8,10},{10,8},{12,14},{14,12},{1,3},{3,1},... | collective-permute-start | bytes 786440 | tf_op jit(solution)/shard_map/ppermute | solution.py:206
  74.8 8.0 %shard_map.127 = (bf16[128,1024]{1,0:T(8,128)(2,1)S(1)}, bf16[128,1024]{1,0:T(8,128)(2,1)S(1)}) custom-call(f32[128,16]{1,0:T(8,128)S(1)} %copy-done.3, bf16[128,1024]{1,0:T(8,128)(2,1)S(1)} %collective-permute-done.19.xz_ref, bf16[128,1024]{1,0:T(8,128)(2,1)S(1)} %collective-permute-done.20.xy_ref, bf16[1024,2048]{1,0:T(8,128)(2,1)S(1)} %bitcast.17, ...), custom_call_target="tpu_custom_call" | custom-call | flops 4294967296 | bytes 17825792 | tf_op jit(solution)/shard_map/pallas_call | solution.py:178
  82.8 0.0 collective-permute-done.23.xy_ref
  82.8 0.9 collective-permute-start.17
  83.8 8.2 %shard_map.128 = (bf16[128,1024]{1,0:T(8,128)(2,1)S(1)}, bf16[128,1024]{1,0:T(8,128)(2,1)S(1)}) custom-call(f32[128,16]{1,0:T(8,128)S(1)} %copy-done.4, bf16[128,1024]{1,0:T(8,128)(2,1)S(1)} %bitcast.29, bf16[128,1024]{1,0:T(8,128)(2,1)S(1)} %collective-permute-done.23.xy_ref, bf16[1024,2048]{1,0:T(8,128)(2,1)S(1)} %bitcast.18, ...), custom_call_target="tpu_custom_call" | custom-call | flops 4294967296 | bytes 17825792 | tf_op jit(solution)/shard_map/pallas_call | solution.py:178
  91.9 1.2 collective-permute-start.21
  93.2 0.1 add_convert_fusion.3
  93.2 0.0 collective-permute-done.17
  93.2 0.9 collective-permute-start.24
  94.2 0.1 add_convert_fusion.2
  94.2 7.0 %collective-permute-done.21 = bf16[128,1024]{1,0:T(8,128)(2,1)S(1)} collective-permute-done((bf16[128,1024]{1,0:T(8,128)(2,1)S(1)}, bf16[128,1024]{1,0:T(8,128)(2,1)S(1)}, u32[]{:S(2)}, u32[]{:S(2)}) %collective-permute-start.21) | collective-permute-done | bytes 262176 | tf_op jit(solution)/shard_map/ppermute | solution.py:206
  101.2 0.9 collective-permute-start.14
  102.1 0.1 add_convert_fusion.1
  102.2 0.0 copy-start.13
  102.2 0.9 collective-permute-start.18
  103.1 0.0 collective-permute-done.k_far
  103.1 0.4 collective-permute-start.22
  103.5 0.0 collective-permute-done.1.v_far
  103.5 0.4 copy-done.6
  103.9 0.4 copy-done.7
  104.4 8.1 %shard_map.122 = bf16[128,2048]{1,0:T(8,128)(2,1)} custom-call(s32[1]{0:T(128)} %bitcast.place_ref, bf16[128,2048]{1,0:T(8,128)(2,1)} %bitcast.30, bf16[128,2048]{1,0:T(8,128)(2,1)} %bitcast.32, bf16[128,2048]{1,0:T(8,128)(2,1)} %copy-done.6, bf16[128,2048]{1,0:T(8,128)(2,1)} %bitcast.34, bf16[128,2048]{1,0:T(8,128)(2,1)} %copy-done.7, s32[1,128]{1,0:T(1,128)} %doc_own.1, ...), custom_call_target="tpu_custom_call" | custom-call | flops 268435456 | bytes 3145728 | tf_op jit(solution)/shard_map/pallas_call | solution.py:64
  112.5 0.0 collective-permute-done.14
  112.5 9.9 %collective-permute-done.18 = bf16[128,1024]{1,0:T(8,128)(2,1)S(1)} collective-permute-done((bf16[128,1024]{1,0:T(8,128)(2,1)S(1)}, bf16[128,1024]{1,0:T(8,128)(2,1)S(1)}, u32[]{:S(2)}, u32[]{:S(2)}) %collective-permute-start.18) | collective-permute-done | bytes 262176 | tf_op jit(solution)/shard_map/ppermute | solution.py:209
  122.4 0.9 fusion
  (26 shorter events, 0.1 us)
Async XLA Ops:
  0.6 48.7 %collective-permute-start.11 = (bf16[1024,2048]{1,0:T(8,128)(2,1)}, bf16[1024,2048]{1,0:T(8,128)(2,1)}, u32[]{:S(2)}, u32[]{:S(2)}) collective-permute-start(bf16[1024,2048]{1,0:T(8,128)(2,1)} %bitcast.14), channel_id=1, source_target_pairs={{0,1},{1,0},{2,3},{3,2},{4,5},{5,4},{6,7},{7,6},{8,9},{9,8},{10,11... | collective-permute-start | bytes 12582920 | tf_op jit(solution)/shard_map/ppermute | solution.py:203
  1.1 48.7 %collective-permute-start.12 = (bf16[2048,1024]{1,0:T(8,128)(2,1)}, bf16[2048,1024]{1,0:T(8,128)(2,1)}, u32[]{:S(2)}, u32[]{:S(2)}) collective-permute-start(bf16[2048,1024]{1,0:T(8,128)(2,1)} %bitcast.19), channel_id=1, source_target_pairs={{0,1},{1,0},{2,3},{3,2},{4,5},{5,4},{6,7},{7,6},{8,9},{9,8},{10,11... | collective-permute-start | bytes 12582920 | tf_op jit(solution)/shard_map/ppermute | solution.py:203
  1.2 12.4 %collective-permute-start.9 = (bf16[128,1024]{1,0:T(8,128)(2,1)}, bf16[128,1024]{1,0:T(8,128)(2,1)S(1)}, u32[]{:S(2)}, u32[]{:S(2)}) collective-permute-start(bf16[128,1024]{1,0:T(8,128)(2,1)} %bitcast.24), channel_id=1, source_target_pairs={{0,4},{2,6},{4,8},{6,10},{8,12},{10,14},{12,0},{14,2},{1,5},{3,7},... | collective-permute-start | bytes 786440 | tf_op jit(solution)/shard_map/ppermute | solution.py:209
  4.2 44.5 %collective-permute-start.15 = (bf16[128,1024]{1,0:T(8,128)(2,1)}, bf16[128,1024]{1,0:T(8,128)(2,1)S(1)}, u32[]{:S(2)}, u32[]{:S(2)}) collective-permute-start(bf16[128,1024]{1,0:T(8,128)(2,1)} %bitcast.25), channel_id=1, source_target_pairs={{0,8},{2,10},{4,12},{6,14},{8,0},{10,2},{12,4},{14,6},{1,9},{3,11}... | collective-permute-start | bytes 786440 | tf_op jit(solution)/shard_map/ppermute | solution.py:209
  13.7 35.6 %collective-permute-start.10 = (bf16[128,1024]{1,0:T(8,128)(2,1)S(1)}, bf16[128,1024]{1,0:T(8,128)(2,1)S(1)}, u32[]{:S(2)}, u32[]{:S(2)}) collective-permute-start(bf16[128,1024]{1,0:T(8,128)(2,1)S(1)} %collective-permute-done.9.xz_ref), channel_id=1, source_target_pairs={{0,2},{2,0},{4,6},{6,4},{8,10},{10,8},{12,14},{14,12},{1,3},{3,1},... | collective-permute-start | bytes 786440 | tf_op jit(solution)/shard_map/ppermute | solution.py:206
  17.2 1.4 %collective-permute-start.3 = (f32[1,16,128]{2,1,0:T(8,128)}, f32[1,16,128]{2,1,0:T(8,128)S(1)}, u32[]{:S(2)}, u32[]{:S(2)}) collective-permute-start(f32[1,16,128]{2,1,0:T(8,128)} %bitcast.37), channel_id=1, source_target_pairs={{0,1},{1,0},{2,3},{3,2},{4,5},{5,4},{6,7},{7,6},{8,9},{9,8},{10,11... | collective-permute-start | bytes 24584 | tf_op jit(solution)/shard_map/ppermute | solution.py:203
  18.6 3.9 %collective-permute-start.4 = (f32[1,16,128]{2,1,0:T(8,128)}, f32[1,16,128]{2,1,0:T(8,128)S(1)}, u32[]{:S(2)}, u32[]{:S(2)}) collective-permute-start(f32[1,16,128]{2,1,0:T(8,128)} %bitcast.38), channel_id=1, source_target_pairs={{0,2},{2,0},{4,6},{6,4},{8,10},{10,8},{12,14},{14,12},{1,3},{3,1},... | collective-permute-start | bytes 24584 | tf_op jit(solution)/shard_map/ppermute | solution.py:206
  22.5 3.3 %collective-permute-start.5 = (f32[1,16,128]{2,1,0:T(8,128)}, f32[1,16,128]{2,1,0:T(8,128)S(1)}, u32[]{:S(2)}, u32[]{:S(2)}) collective-permute-start(f32[1,16,128]{2,1,0:T(8,128)} %bitcast.39), channel_id=1, source_target_pairs={{0,3},{1,2},{2,1},{3,0},{4,7},{5,6},{6,5},{7,4},{8,11},{9,10},{10,... | collective-permute-start | bytes 24584 | tf_op jit(solution)/shard_map/ppermute | solution.py:223
  26.4 20.2 %copy-start.8 = (f32[4,16,128]{2,1,0:T(8,128)}, f32[4,16,128]{2,1,0:T(8,128)S(1)}, u32[]{:S(2)}) copy-start(f32[4,16,128]{2,1,0:T(8,128)S(1)} %pad_maximum_fusion.refs_0_) | copy-start | bytes 98308
  26.4 6.4 %collective-permute-start.6 = (f32[4,16,128]{2,1,0:T(8,128)S(1)}, f32[4,16,128]{2,1,0:T(8,128)S(1)}, u32[]{:S(2)}, u32[]{:S(2)}) collective-permute-start(f32[4,16,128]{2,1,0:T(8,128)S(1)} %pad_maximum_fusion.refs_0_), channel_id=1, source_target_pairs={{0,4},{2,6},{4,0},{6,2},{8,12},{10,14},{12,8},{14,10},{1,5},{3,7},... | collective-permute-start | bytes 98312 | tf_op jit(solution)/shard_map/ppermute | solution.py:212
  32.8 13.8 %copy-start.9 = (f32[4,16,128]{2,1,0:T(8,128)}, f32[4,16,128]{2,1,0:T(8,128)S(1)}, u32[]{:S(2)}) copy-start(f32[4,16,128]{2,1,0:T(8,128)S(1)} %collective-permute-done.6.refs_1_) | copy-start | bytes 98308
  32.8 6.0 %collective-permute-start.7 = (f32[4,16,128]{2,1,0:T(8,128)S(1)}, f32[4,16,128]{2,1,0:T(8,128)S(1)}, u32[]{:S(2)}, u32[]{:S(2)}) collective-permute-start(f32[4,16,128]{2,1,0:T(8,128)S(1)} %pad_maximum_fusion.refs_0_), channel_id=1, source_target_pairs={{0,8},{2,10},{4,12},{6,14},{8,0},{10,2},{12,4},{14,6},{1,9},{3,11}... | collective-permute-start | bytes 98312 | tf_op jit(solution)/shard_map/ppermute | solution.py:212
  38.8 7.8 %copy-start.10 = (f32[4,16,128]{2,1,0:T(8,128)}, f32[4,16,128]{2,1,0:T(8,128)S(1)}, u32[]{:S(2)}) copy-start(f32[4,16,128]{2,1,0:T(8,128)S(1)} %collective-permute-done.7.refs_2_) | copy-start | bytes 98308
  38.8 6.1 %collective-permute-start.8 = (f32[4,16,128]{2,1,0:T(8,128)S(1)}, f32[4,16,128]{2,1,0:T(8,128)S(1)}, u32[]{:S(2)}, u32[]{:S(2)}) collective-permute-start(f32[4,16,128]{2,1,0:T(8,128)S(1)} %pad_maximum_fusion.refs_0_), channel_id=1, source_target_pairs={{0,12},{2,14},{4,8},{6,10},{8,4},{10,6},{12,0},{14,2},{1,13},{3,15... | collective-permute-start | bytes 98312 | tf_op jit(solution)/shard_map/ppermute | solution.py:212
  44.9 1.8 %copy-start.11 = (f32[4,16,128]{2,1,0:T(8,128)}, f32[4,16,128]{2,1,0:T(8,128)S(1)}, u32[]{:S(2)}) copy-start(f32[4,16,128]{2,1,0:T(8,128)S(1)} %collective-permute-done.8.refs_3_) | copy-start | bytes 98308
  44.9 19.6 %collective-permute-start.19 = (bf16[128,1024]{1,0:T(8,128)(2,1)}, bf16[128,1024]{1,0:T(8,128)(2,1)S(1)}, u32[]{:S(2)}, u32[]{:S(2)}) collective-permute-start(bf16[128,1024]{1,0:T(8,128)(2,1)} %bitcast.27), channel_id=1, source_target_pairs={{0,12},{2,14},{4,0},{6,2},{8,4},{10,6},{12,8},{14,10},{1,13},{3,15... | collective-permute-start | bytes 786440 | tf_op jit(solution)/shard_map/ppermute | solution.py:209
  48.8 34.0 %collective-permute-start.23 = (bf16[128,1024]{1,0:T(8,128)(2,1)}, bf16[128,1024]{1,0:T(8,128)(2,1)S(1)}, u32[]{:S(2)}, u32[]{:S(2)}) collective-permute-start(bf16[128,1024]{1,0:T(8,128)(2,1)} %bitcast.28), channel_id=1, source_target_pairs={{0,2},{2,0},{4,6},{6,4},{8,10},{10,8},{12,14},{14,12},{1,3},{3,1},... | collective-permute-start | bytes 786440 | tf_op jit(solution)/shard_map/ppermute | solution.py:206
  49.3 53.9 %collective-permute-start = (bf16[128,2048]{1,0:T(8,128)(2,1)}, bf16[128,2048]{1,0:T(8,128)(2,1)S(1)}, u32[]{:S(2)}, u32[]{:S(2)}) collective-permute-start(bf16[128,2048]{1,0:T(8,128)(2,1)} %bitcast.31), channel_id=1, source_target_pairs={{0,1},{1,0},{2,3},{3,2},{4,5},{5,4},{6,7},{7,6},{8,9},{9,8},{10,11... | collective-permute-start | bytes 1572872 | tf_op jit(solution)/shard_map/ppermute | solution.py:303
  49.3 15.2 %copy-start.12 = (s32[1,128]{1,0:T(1,128)S(1)}, s32[1,128]{1,0:T(1,128)}, u32[]{:S(2)}) copy-start(s32[1,128]{1,0:T(1,128)} %doc_own.1) | copy-start | bytes 1540
  49.3 54.2 %collective-permute-start.1 = (bf16[128,2048]{1,0:T(8,128)(2,1)}, bf16[128,2048]{1,0:T(8,128)(2,1)S(1)}, u32[]{:S(2)}, u32[]{:S(2)}) collective-permute-start(bf16[128,2048]{1,0:T(8,128)(2,1)} %bitcast.33), channel_id=1, source_target_pairs={{0,1},{1,0},{2,3},{3,2},{4,5},{5,4},{6,7},{7,6},{8,9},{9,8},{10,11... | collective-permute-start | bytes 1572872 | tf_op jit(solution)/shard_map/ppermute | solution.py:304
  49.8 14.8 %collective-permute-start.16 = (bf16[128,1024]{1,0:T(8,128)(2,1)S(1)}, bf16[128,1024]{1,0:T(8,128)(2,1)S(1)}, u32[]{:S(2)}, u32[]{:S(2)}) collective-permute-start(bf16[128,1024]{1,0:T(8,128)(2,1)S(1)} %collective-permute-done.15.xz_ref), channel_id=1, source_target_pairs={{0,2},{2,0},{4,6},{6,4},{8,10},{10,8},{12,14},{14,12},{1,3},{3,1},... | collective-permute-start | bytes 786440 | tf_op jit(solution)/shard_map/ppermute | solution.py:206
  51.3 2.2 %copy-start = (bf16[1,1024,2048]{2,1,0:T(8,128)(2,1)S(1)}, bf16[1,1024,2048]{2,1,0:T(8,128)(2,1)}, u32[]{:S(2)}) copy-start(bf16[1,1024,2048]{2,1,0:T(8,128)(2,1)} %param.16) | copy-start | bytes 12582916
  53.5 2.2 %copy-start.2 = (bf16[1,2048,1024]{2,1,0:T(8,128)(2,1)S(1)}, bf16[1,2048,1024]{2,1,0:T(8,128)(2,1)}, u32[]{:S(2)}) copy-start(bf16[1,2048,1024]{2,1,0:T(8,128)(2,1)} %param.17) | copy-start | bytes 12582916
  55.7 0.8 copy-start.3
  64.5 37.7 %collective-permute-start.2 = (s32[1,128]{1,0:T(1,128)S(1)}, s32[1,128]{1,0:T(1,128)S(1)}, u32[]{:S(2)}, u32[]{:S(2)}) collective-permute-start(s32[1,128]{1,0:T(1,128)S(1)} %copy-done.12), channel_id=1, source_target_pairs={{0,1},{1,0},{2,3},{3,2},{4,5},{5,4},{6,7},{7,6},{8,9},{9,8},{10,11... | collective-permute-start | bytes 1544 | tf_op jit(solution)/shard_map/ppermute | solution.py:305
  64.6 8.7 %collective-permute-start.20 = (bf16[128,1024]{1,0:T(8,128)(2,1)S(1)}, bf16[128,1024]{1,0:T(8,128)(2,1)S(1)}, u32[]{:S(2)}, u32[]{:S(2)}) collective-permute-start(bf16[128,1024]{1,0:T(8,128)(2,1)S(1)} %collective-permute-done.19.xz_ref), channel_id=1, source_target_pairs={{0,2},{2,0},{4,6},{6,4},{8,10},{10,8},{12,14},{14,12},{1,3},{3,1},... | collective-permute-start | bytes 786440 | tf_op jit(solution)/shard_map/ppermute | solution.py:206
  73.3 10.4 %copy-start.1 = (bf16[1,1024,2048]{2,1,0:T(8,128)(2,1)S(1)}, bf16[1,1024,2048]{2,1,0:T(8,128)(2,1)}, u32[]{:S(2)}) copy-start(bf16[1,1024,2048]{2,1,0:T(8,128)(2,1)} %param.16) | copy-start | bytes 12582916
  73.3 10.4 %copy-start.4 = (f32[128,16]{1,0:T(8,128)S(1)}, f32[128,16]{1,0:T(8,128)}, u32[]{:S(2)}) copy-start(f32[128,16]{1,0:T(8,128)} %shard_map.124.gates_ref) | copy-start | bytes 24580
  73.3 10.4 %copy-start.5 = (bf16[1,128,1024]{2,1,0:T(8,128)(2,1)S(1)}, bf16[1,128,1024]{2,1,0:T(8,128)(2,1)}, u32[]{:S(2)}) copy-start(bf16[1,128,1024]{2,1,0:T(8,128)(2,1)} %param.14) | copy-start | bytes 786436
  73.3 18.6 %collective-permute-start.13 = (bf16[128,1024]{1,0:T(8,128)(2,1)S(1)}, bf16[128,1024]{1,0:T(8,128)(2,1)S(1)}, u32[]{:S(2)}, u32[]{:S(2)}) collective-permute-start(bf16[128,1024]{1,0:T(8,128)(2,1)S(1)} %get-tuple-element.11), channel_id=1, source_target_pairs={{0,2},{2,0},{4,6},{6,4},{8,10},{10,8},{12,14},{14,12},{1,3},{3,1},... | collective-permute-start | bytes 786440 | tf_op jit(solution)/shard_map/ppermute | solution.py:206
  82.8 10.4 %collective-permute-start.17 = (bf16[128,1024]{1,0:T(8,128)(2,1)S(1)}, bf16[128,1024]{1,0:T(8,128)(2,1)S(1)}, u32[]{:S(2)}, u32[]{:S(2)}) collective-permute-start(bf16[128,1024]{1,0:T(8,128)(2,1)S(1)} %get-tuple-element.13), channel_id=1, source_target_pairs={{0,2},{2,0},{4,6},{6,4},{8,10},{10,8},{12,14},{14,12},{1,3},{3,1},... | collective-permute-start | bytes 786440 | tf_op jit(solution)/shard_map/ppermute | solution.py:206
  91.9 9.3 %collective-permute-start.21 = (bf16[128,1024]{1,0:T(8,128)(2,1)S(1)}, bf16[128,1024]{1,0:T(8,128)(2,1)S(1)}, u32[]{:S(2)}, u32[]{:S(2)}) collective-permute-start(bf16[128,1024]{1,0:T(8,128)(2,1)S(1)} %get-tuple-element.15), channel_id=1, source_target_pairs={{0,2},{2,0},{4,6},{6,4},{8,10},{10,8},{12,14},{14,12},{1,3},{3,1},... | collective-permute-start | bytes 786440 | tf_op jit(solution)/shard_map/ppermute | solution.py:206
  93.2 19.3 %collective-permute-start.24 = (bf16[128,1024]{1,0:T(8,128)(2,1)S(1)}, bf16[128,1024]{1,0:T(8,128)(2,1)S(1)}, u32[]{:S(2)}, u32[]{:S(2)}) collective-permute-start(bf16[128,1024]{1,0:T(8,128)(2,1)S(1)} %get-tuple-element.17), channel_id=1, source_target_pairs={{0,2},{2,0},{4,6},{6,4},{8,10},{10,8},{12,14},{14,12},{1,3},{3,1},... | collective-permute-start | bytes 786440 | tf_op jit(solution)/shard_map/ppermute | solution.py:206
  101.2 11.2 %collective-permute-start.14 = (bf16[128,1024]{1,0:T(8,128)(2,1)S(1)}, bf16[128,1024]{1,0:T(8,128)(2,1)S(1)}, u32[]{:S(2)}, u32[]{:S(2)}) collective-permute-start(bf16[128,1024]{1,0:T(8,128)(2,1)S(1)} %add_convert_fusion.3), channel_id=1, source_target_pairs={{0,12},{2,14},{4,0},{6,2},{8,4},{10,6},{12,8},{14,10},{1,13},{3,15... | collective-permute-start | bytes 786440 | tf_op jit(solution)/shard_map/ppermute | solution.py:209
  102.2 1.3 %copy-start.13 = (s32[1,128]{1,0:T(1,128)}, s32[1,128]{1,0:T(1,128)S(1)}, u32[]{:S(2)}) copy-start(s32[1,128]{1,0:T(1,128)S(1)} %collective-permute-done.2.doc_far) | copy-start | bytes 1540
  102.2 20.1 %collective-permute-start.18 = (bf16[128,1024]{1,0:T(8,128)(2,1)S(1)}, bf16[128,1024]{1,0:T(8,128)(2,1)S(1)}, u32[]{:S(2)}, u32[]{:S(2)}) collective-permute-start(bf16[128,1024]{1,0:T(8,128)(2,1)S(1)} %add_convert_fusion.2), channel_id=1, source_target_pairs={{0,8},{2,10},{4,12},{6,14},{8,0},{10,2},{12,4},{14,6},{1,9},{3,11}... | collective-permute-start | bytes 786440 | tf_op jit(solution)/shard_map/ppermute | solution.py:209
  103.1 0.8 copy-start.6
  103.1 19.2 %collective-permute-start.22 = (bf16[128,1024]{1,0:T(8,128)(2,1)S(1)}, bf16[128,1024]{1,0:T(8,128)(2,1)S(1)}, u32[]{:S(2)}, u32[]{:S(2)}) collective-permute-start(bf16[128,1024]{1,0:T(8,128)(2,1)S(1)} %add_convert_fusion.1), channel_id=1, source_target_pairs={{0,4},{2,6},{4,8},{6,10},{8,12},{10,14},{12,0},{14,2},{1,5},{3,7},... | collective-permute-start | bytes 786440 | tf_op jit(solution)/shard_map/ppermute | solution.py:209
  103.5 0.8 copy-start.7

commit v3 on v2

v3 whole, which is shorter than its diff:
```python
import functools
import math

import jax
import jax.numpy as jnp
from jax import lax
from jax.experimental import pallas as pl
from jax.experimental.pallas import tpu as pltpu
from jax.sharding import PartitionSpec as P

HEAD_DIM = 128
LATENT = 1024
TOPK = 6
DENSE_EXPERTS = 16
EXPERT_VMEM = 28 * 1024 * 1024
ATTEND_VMEM = 16 * 1024 * 1024
EXPERT_COST = 1024
ATTEND_COST = 1024


def run_expert(rows_in, w_first, w_second):
    hidden = jax.nn.relu(jnp.dot(rows_in, w_first, preferred_element_type=jnp.float32))
    hidden = (hidden * hidden).astype(jnp.bfloat16)
    return jnp.dot(hidden, w_second, preferred_element_type=jnp.float32).astype(jnp.bfloat16)


def column_of(row):
    n = row.shape[1]
    square = jnp.broadcast_to(row.astype(jnp.float32), (n, n)).T
    return square[:, :1].astype(jnp.int32)


def attend_kernel(place_ref, q_ref, k_own, k_far, v_own, v_far, doc_own, doc_far, ahead_ref, *rest):
    out_ref = rest[-1]
    rows = q_ref.shape[0]
    heads = q_ref.shape[1] // HEAD_DIM
    here = place_ref[0] * rows
    there = (1 - place_ref[0]) * rows
    doc_query = column_of(doc_own[...])
    reach = here + lax.broadcasted_iota(jnp.int32, (rows, 1), 0) + column_of(ahead_ref[...])
    lane = lax.broadcasted_iota(jnp.int32, (1, rows), 1)
    doc_key = jnp.concatenate([doc_own[...], doc_far[...]], axis=1)
    spot = jnp.concatenate([here + lane, there + lane], axis=1)
    visible = (doc_key == doc_query) & (spot <= reach)
    scale = HEAD_DIM ** (-0.5) * math.log2(math.e)
    across = (((1,), (1,)), ((), ()))
    for head in range(heads):
        cols = slice(head * HEAD_DIM, (head + 1) * HEAD_DIM)
        keys = jnp.concatenate([k_own[:, cols], k_far[:, cols]], axis=0)
        values = jnp.concatenate([v_own[:, cols], v_far[:, cols]], axis=0)
        scores = lax.dot_general(q_ref[:, cols], keys, across, preferred_element_type=jnp.float32)
        scores = jnp.where(visible, scores * scale, -1e30)
        raw = jnp.exp2(scores - jnp.max(scores, axis=1, keepdims=True))
        share = 1.0 / jnp.sum(raw, axis=1, keepdims=True)
        mixed = jnp.dot(raw.astype(jnp.bfloat16), values, preferred_element_type=jnp.float32)
        out_ref[:, cols] = (mixed * share).astype(jnp.bfloat16)


def attend(half, place, q, k_own, k_far, v_own, v_far, doc_own, doc_far, ahead, before=None, after=()):
    rows, width = q.shape
    smem = pl.BlockSpec(memory_space=pltpu.SMEM)
    heads = pl.BlockSpec((rows, width // 2), lambda i: (0, half))
    line = pl.BlockSpec((1, rows), lambda i: (0, 0))
    extra = list(after) + ([] if before is None else [before])
    return pl.pallas_call(
        attend_kernel,
        grid=(1,),
        out_shape=jax.ShapeDtypeStruct(q.shape, jnp.bfloat16),
        in_specs=[smem] + [heads] * 5 + [line] * 3 + [pl.BlockSpec(memory_space=pl.ANY)] * len(extra),
        out_specs=heads,
        input_output_aliases={} if before is None else {8 + len(extra): 0},
        compiler_params=pltpu.CompilerParams(vmem_limit_bytes=ATTEND_VMEM),
        cost_estimate=pl.CostEstimate(flops=ATTEND_COST, bytes_accessed=ATTEND_COST, transcendentals=0),
    )(place, q, k_own, k_far, v_own, v_far, doc_own, doc_far, ahead, *extra)


def prep_kernel(latent_ref, *refs):
    parts, rows_ref, table_ref = refs[:-2], refs[-2], refs[-1]
    rows_ref[...] = latent_ref[...]
    for index, part in enumerate(parts):
        for k in range(TOPK):
            table_ref[index, k : k + 1, :] = part[k]
        table_ref[index, TOPK:, :] = jnp.full((8 - TOPK, part.shape[2]), -1, jnp.int32)


def prepare(latent, parts):
    vmem = pl.BlockSpec(memory_space=pltpu.VMEM)
    return pl.pallas_call(
        prep_kernel,
        out_shape=(
            jax.ShapeDtypeStruct(latent.shape, latent.dtype),
            jax.ShapeDtypeStruct((len(parts), 8, latent.shape[0]), jnp.int32),
        ),
        in_specs=[vmem] * (1 + len(parts)),
        out_specs=(vmem, vmem),
        cost_estimate=pl.CostEstimate(flops=1024, bytes_accessed=1024, transcendentals=0),
    )(latent, *parts)


def kept_kernel(line, own_ref, capacity_ref, *refs):
    tables, out_ref = refs[:-1], refs[-1]
    own = own_ref[0]
    z = own // 4
    rows = tables[0].shape[2]
    sources = 4 * line
    upto = lax.broadcasted_iota(jnp.int32, (rows, rows), 0) <= lax.broadcasted_iota(
        jnp.int32, (rows, rows), 1
    )
    upto = jnp.where(upto, 1.0, 0.0).astype(jnp.bfloat16)
    device = lax.broadcasted_iota(jnp.int32, (sources, sources), 0) ^ own
    other = lax.broadcasted_iota(jnp.int32, (sources, sources), 1) ^ own
    lower = jnp.where(other < device, 1.0, 0.0).astype(jnp.bfloat16)
    entry = lax.broadcasted_iota(jnp.int32, (sources, rows), 0)
    named = []
    for k in range(TOPK):
        named.append(jnp.concatenate([part[:, k, :] for part in tables], axis=0))
    kept = []
    for which in range(2):
        expert = own ^ which
        mine = named[0] == expert
        for k in range(1, TOPK):
            mine |= named[k] == expert
        flags = jnp.where(mine, 1.0, 0.0)
        running = jnp.dot(flags.astype(jnp.bfloat16), upto, preferred_element_type=jnp.float32)
        totals = jnp.broadcast_to(running[:, rows - 1 :], (sources, rows)).astype(jnp.bfloat16)
        before = jnp.dot(lower, totals, preferred_element_type=jnp.float32)
        slots = before + running - flags
        limit = capacity_ref[expert].astype(jnp.float32)
        kept.append(jnp.where(mine & (slots < limit), 1, 0))
    for step in range(line):
        home = 4 * (z ^ lax.rem(z + line - step, line))
        for side in range(2):
            here = entry == home + 2 * side
            for k, part in enumerate(named + kept):
                picked = jnp.sum(jnp.where(here, part, 0), axis=0, keepdims=True)
                out_ref[2 * step + side, k : k + 1, :] = picked


def kept_rows(own, capacity, tables):
    smem = pl.BlockSpec(memory_space=pltpu.SMEM)
    vmem = pl.BlockSpec(memory_space=pltpu.VMEM)
    line, rows = len(tables), tables[0].shape[2]
    return pl.pallas_call(
        functools.partial(kept_kernel, line),
        out_shape=jax.ShapeDtypeStruct((2 * line, 8, rows), jnp.int32),
        in_specs=[smem, smem] + [vmem] * line,
        out_specs=vmem,
        cost_estimate=pl.CostEstimate(flops=1024, bytes_accessed=1024, transcendentals=0),
    )(own, capacity, *tables)


def gate_columns(own, router_ref, x, kept):
    logits = lax.dot_general(
        router_ref[...], x, (((1,), (1,)), ((), ())), preferred_element_type=jnp.float32
    )
    number = lax.broadcasted_iota(jnp.int32, logits.shape, 0)
    named = number == kept[0:1]
    for k in range(1, TOPK):
        named |= number == kept[k : k + 1]
    sigma = jnp.where(named, jax.nn.sigmoid(logits), 0.0)
    gates = sigma / jnp.sum(sigma, axis=0, keepdims=True)
    lines = []
    for which in range(2):
        gate = jnp.sum(jnp.where(number == own ^ which, gates, 0.0), axis=0, keepdims=True)
        lines.append(jnp.where(kept[TOPK + which : TOPK + which + 1] > 0, gate, 0.0))
    square = jnp.concatenate(lines + [jnp.zeros((x.shape[0] - 2, x.shape[0]), jnp.float32)], axis=0)
    return square.T


def expert_kernel(
    place, own_ref, kept_ref, router_ref, xz_ref, xy_ref, w1a, w2a, w1b_any, w2b_any, *rest
):
    z_ref, y_ref, hidden_ref, w1b, w2b, sems = rest[-6:]
    loads = [
        pltpu.make_async_copy(w1b_any, w1b, sems.at[0]),
        pltpu.make_async_copy(w2b_any, w2b, sems.at[1]),
    ]
    for load in loads:
        load.start()
    own = own_ref[0]
    rows = xz_ref.shape[0]
    x = jnp.concatenate([xz_ref[...], xy_ref[...]], axis=0)
    step = 512

    def enter(which, w1_ref):
        for first in range(0, w1_ref.shape[1], step):
            cols = slice(first, first + step)
            hidden = jnp.dot(x, w1_ref[:, cols], preferred_element_type=jnp.float32)
            hidden = jnp.maximum(hidden, 0.0)
            hidden_ref[which, :, cols] = (hidden * hidden).astype(jnp.bfloat16)

    enter(0, w1a)
    gates = [
        gate_columns(own, router_ref, x_ref[...], kept_ref[2 * place + side])
        for side, x_ref in enumerate((xz_ref, xy_ref))
    ]
    loads[0].wait()
    enter(1, w1b)
    loads[1].wait()
    for first in range(0, w2a.shape[1], step):
        cols = slice(first, first + step)
        results = [
            jnp.dot(hidden_ref[which], w2_ref[:, cols], preferred_element_type=jnp.float32)
            for which, w2_ref in enumerate((w2a, w2b))
        ]
        for side, out_ref in enumerate((z_ref, y_ref)):
            part = slice(side * rows, (side + 1) * rows)
            mixed = results[0][part] * gates[side][:, 0:1] + results[1][part] * gates[side][:, 1:2]
            out_ref[:, cols] = mixed.astype(jnp.bfloat16)


def run_piece(place, own, kept, router, from_line, from_side, weights, after):
    rows, width = from_line.shape
    hidden = weights[0].shape[1]
    smem = pl.BlockSpec(memory_space=pltpu.SMEM)
    vmem = pl.BlockSpec(memory_space=pltpu.VMEM)
    anywhere = pl.BlockSpec(memory_space=pl.ANY)
    piece = jax.ShapeDtypeStruct((rows, width), jnp.bfloat16)
    return pl.pallas_call(
        functools.partial(expert_kernel, place),
        out_shape=(piece, piece),
        in_specs=[smem] + [vmem] * 6 + [anywhere] * (2 + len(after)),
        out_specs=(vmem, vmem),
        scratch_shapes=[
            pltpu.VMEM((2, 2 * rows, hidden), jnp.bfloat16),
            pltpu.VMEM(weights[2].shape, jnp.bfloat16),
            pltpu.VMEM(weights[3].shape, jnp.bfloat16),
            pltpu.SemaphoreType.DMA((2,)),
        ],
        compiler_params=pltpu.CompilerParams(vmem_limit_bytes=EXPERT_VMEM),
        cost_estimate=pl.CostEstimate(flops=EXPERT_COST, bytes_accessed=EXPERT_COST, transcendentals=0),
    )(own, kept, router, from_line, from_side, *weights, *after)


def dense_moe(latent, router, expert_in, expert_out, routes, capacity, attention):
    f32 = jnp.float32
    axes = ("expert", "context")
    line = router.shape[1] // 4
    spots = [(z, y) for z in range(line) for y in range(2)]
    sibling = [(0, 1), (1, 0)]
    across = [(2 * z + y, 2 * z + 1 - y) for z, y in spots]
    diagonal = [(4 * z + k, 4 * z + 3 - k) for z in range(line) for k in range(4)]

    def swap_core(x):
        return lax.ppermute(x, "context", sibling)

    def swap_side(x):
        return lax.ppermute(x, "expert", across)

    def along(x, step):
        return lax.ppermute(x, "expert", [(2 * z + y, 2 * ((z + step) % line) + y) for z, y in spots])

    def flipped(x, span):
        return lax.ppermute(x, "expert", [(2 * z + y, 2 * (z ^ span) + y) for z, y in spots])

    own = lax.axis_index(axes).astype(jnp.int32).reshape(1)
    named = routes[0].T[:, None, :]
    parts = [named, swap_core(named), swap_side(named), lax.ppermute(named, axes, diagonal)]
    rows, table = prepare(latent[0], parts)
    tables = [table] + [flipped(table, span) for span in range(1, line)]
    kept = kept_rows(own, capacity, tables)

    w_first, w_second = expert_in[0], expert_out[0]
    weights = (w_first, w_second, swap_core(w_first), swap_core(w_second))
    from_line = [rows] + [along(rows, step) for step in range(1, line)]
    from_side = [swap_side(x) for x in from_line]

    half = attention(0, after=(kept,))
    total = None
    after = ()
    for step in range(line):
        mine, theirs = run_piece(
            step, own, kept, router.T, from_line[step], from_side[step], weights, after
        )
        after = (mine,)
        column = mine.astype(f32) + swap_side(theirs).astype(f32)
        if step:
            column = along(column.astype(jnp.bfloat16), line - step).astype(f32)
        total = column if total is None else total + column
    return attention(1, before=half, after=after), total.astype(jnp.bfloat16)[None]


def routed_moe(latent, router, expert_in, expert_out, routes, capacity):
    tok_count = latent.shape[1]
    token_rows = latent[0]
    expert_count = router.shape[1]
    per_peer = max(2, 2 * tok_count * TOPK // expert_count)
    logits = jnp.dot(token_rows, router, preferred_element_type=jnp.float32)
    chosen_ids = routes[0]
    expert_ids = jnp.arange(expert_count, dtype=jnp.int32)
    one_hot = chosen_ids[:, :, None] == expert_ids[None, None, :]
    picked = jnp.sum(jnp.where(one_hot, logits[:, None, :], 0.0), axis=2)
    sigmas = jax.nn.sigmoid(picked)
    gates = sigmas / jnp.sum(sigmas, axis=1, keepdims=True)
    flat_hot = one_hot.reshape(tok_count * TOPK, expert_count).astype(jnp.int32)
    counts = jnp.sum(flat_hot, axis=0)
    ranks = jnp.sum((jnp.cumsum(flat_hot, axis=0) - flat_hot) * flat_hot, axis=1)
    count_rows = lax.all_gather(counts[None, :], ("expert", "context"), axis=0, tiled=True)
    own_index = lax.axis_index(("expert", "context"))
    lower_rows = jnp.arange(count_rows.shape[0], dtype=jnp.int32)[:, None] < own_index
    before = jnp.sum(jnp.where(lower_rows, count_rows, 0), axis=0)
    slots = jnp.sum(flat_hot * before[None, :], axis=1) + ranks
    limits = jnp.sum(flat_hot * capacity[None, :], axis=1)
    kept = slots < limits
    flat_ids = chosen_ids.reshape(-1)
    places = flat_ids * per_peer + ranks
    owners = jnp.arange(tok_count * TOPK, dtype=jnp.int32) // TOPK
    send_rows = (
        jnp.zeros((expert_count * per_peer, LATENT), jnp.bfloat16)
        .at[places]
        .set(token_rows[owners])
    )
    recv_rows = lax.all_to_all(
        send_rows.reshape(expert_count, per_peer, LATENT),
        ("expert", "context"),
        split_axis=0,
        concat_axis=0,
        tiled=True,
    ).reshape(expert_count * per_peer, LATENT)
    results = run_expert(recv_rows, expert_in[0], expert_out[0])
    returned = lax.all_to_all(
        results.reshape(expert_count, per_peer, LATENT),
        ("expert", "context"),
        split_axis=0,
        concat_axis=0,
        tiled=True,
    ).reshape(expert_count * per_peer, LATENT)
    gate_kept = jnp.where(kept, gates.reshape(-1), 0.0).reshape(tok_count, TOPK)
    back_rows = returned[places].reshape(tok_count, TOPK, LATENT).astype(jnp.float32)
    mixture = jnp.sum(gate_kept[:, :, None] * back_rows, axis=1)
    return mixture.astype(jnp.bfloat16).reshape(1, tok_count, LATENT)


def shards(
    query_heads,
    key_heads,
    value_heads,
    latent,
    router,
    expert_in,
    expert_out,
    routes,
    segments,
    offsets,
    capacity,
):
    swap = [(0, 1), (1, 0)]
    k_far = lax.ppermute(key_heads[0], "context", swap)
    v_far = lax.ppermute(value_heads[0], "context", swap)
    doc_far = lax.ppermute(segments, "context", swap)
    place = lax.axis_index("context").astype(jnp.int32).reshape(1)

    def attention(half, **order):
        return attend(
            half,
            place,
            query_heads[0],
            key_heads[0],
            k_far,
            value_heads[0],
            v_far,
            segments,
            doc_far,
            offsets,
            **order,
        )

    if router.shape[1] <= DENSE_EXPERTS:
        attn_out, moe_out = dense_moe(
            latent, router, expert_in, expert_out, routes, capacity, attention
        )
    else:
        attn_out = attention(1, before=attention(0))
        moe_out = routed_moe(latent, router, expert_in, expert_out, routes, capacity)
    return (attn_out[None], moe_out)


def solution(mesh):
    rows = P(("groups", "expert"), "context", None)
    placed = (
        rows,
        rows,
        rows,
        rows,
        P(),
        P(("expert", "context"), None, None),
        P(("expert", "context"), None, None),
        rows,
        P(("groups", "expert"), "context"),
        P(("groups", "expert"), "context"),
        P(),
    )
    return jax.shard_map(
        shards,
        mesh=mesh,
        in_specs=placed,
        out_specs=(rows, rows),
        check_vma=False,
    )
```

time: 124 us -> 127 us (1.024)
  waiting for transfers between devices: 39.9 us -> 49.4 us
  Pallas kernels: 44.1 us -> 36.8 us
  local copies, waits for them, and re-layouts: 6.09 us -> 8.17 us
    ppermute x6, waiting for transfers between devices: 16.7 us -> 26.8 us  [along(): lax.ppermute(x, 'expert', [(2 * z + y, 2 * ((z + step) % line) + y) for z...]
    pallas_call x3 -> x4, Pallas kernels: 12 us -> 6.84 us  [the longest x2 3.17 us: attend(): pl.pallas_call(attend_kernel, grid=(1,), out_shape=jax.ShapeDtypeStruct(q...]
    ppermute x3, waiting for transfers between devices: 7.76 us -> 12.8 us  [flipped(): lax.ppermute(x, 'expert', [(2 * z + y, 2 * (z ^ span) + y) for z, y in sp...]
    ppermute x3, starting transfers between devices: 10.7 us -> 5.88 us  [flipped(): lax.ppermute(x, 'expert', [(2 * z + y, 2 * (z ^ span) + y) for z, y in sp...]
    ppermute x9, waiting for transfers between devices: 10.8 us -> 6.89 us  [swap_side(): return lax.ppermute(x, 'expert', across)]
    ppermute x1, waiting for transfers between devices: 3.28 us -> 0.02 us  [dense_moe(): lax.ppermute(named, axes, diagonal)]
    ppermute x9, starting transfers between devices: 9.2 us -> 12.3 us  [swap_side(): return lax.ppermute(x, 'expert', across)]
    pallas_call x4, Pallas kernels: 32.1 us -> 30 us  [run_piece(): pl.pallas_call(functools.partial(expert_kernel, place), out_shape=(piece,...]
  transfers between devices with their start and end apart: 25 -> 25, of which waited for: 10 -> 8; matrix products, arithmetic and copies ran while one was open for 1% -> 1% of each run, Pallas kernels for 36% -> 29%
where the time goes in v3:
time: 127 us; the launch traced here: 126 us
  waiting for transfers between devices  49.4 us (39%)
  Pallas kernels  36.8 us (29%)
  starting transfers between devices  29.9 us (24%)
  local copies, waits for them, and re-layouts  8.17 us (6%)
    pallas_call x4, Pallas kernels, run_piece(): pl.pallas_call(functools.partial(expert_kernel, place), out_shape=(piece,...  30 us
    ppermute x6, waiting for transfers between devices, along(): lax.ppermute(x, 'expert', [(2 * z + y, 2 * ((z + step) % line) + y) for z...  26.8 us
    ppermute x3, waiting for transfers between devices, flipped(): lax.ppermute(x, 'expert', [(2 * z + y, 2 * (z ^ span) + y) for z, y in sp...  12.8 us
    ppermute x9, starting transfers between devices, swap_side(): return lax.ppermute(x, 'expert', across)  12.3 us
    ppermute x6, starting transfers between devices, along(): lax.ppermute(x, 'expert', [(2 * z + y, 2 * ((z + step) % line) + y) for z...  10 us
    unnamed x43, local copies, waits for them, and re-layouts  8.17 us
    ppermute x9, waiting for transfers between devices, swap_side(): return lax.ppermute(x, 'expert', across)  6.89 us
    ppermute x3, starting transfers between devices, flipped(): lax.ppermute(x, 'expert', [(2 * z + y, 2 * (z ^ span) + y) for z, y in sp...  5.88 us
  transfers between devices with their start and end apart: 25, of which 8 were waited for; matrix products, arithmetic and copies ran while one was open for 1% of the time, Pallas kernels for 29%

profile of v3, /device:TPU:0, one launch (start us, length us, event | category | flops | bytes accessed | tf_op | source)
XLA Modules:
  0.0 126.2 jit_solution(1537308502972310963)
XLA Ops:
  0.6 0.5 collective-permute-start.11
  1.1 0.1 collective-permute-start.12
  1.2 0.7 copy.16
  1.9 0.4 collective-permute-start.3
  2.4 2.6 %collective-permute-start.4 = (s32[6,1,128]{2,1,0:T(1,128)S(1)}, s32[6,1,128]{2,1,0:T(1,128)S(1)}, u32[]{:S(2)}, u32[]{:S(2)}) collective-permute-start(s32[6,1,128]{2,1,0:T(1,128)S(1)} %broadcast_in_dim.9.refs_0_), channel_id=1, source_target_pairs={{0,2},{2,0},{4,6},{6,4},{8,10},{10,8},{12,14},{14,12},{1,3},{3,1},... | collective-permute-start | bytes 9224 | tf_op jit(solution)/shard_map/ppermute | solution.py:248
  4.9 0.1 collective-permute-start.5
  5.0 2.9 %collective-permute-done.3.refs_1_ = s32[6,1,128]{2,1,0:T(1,128)S(1)} collective-permute-done((s32[6,1,128]{2,1,0:T(1,128)S(1)}, s32[6,1,128]{2,1,0:T(1,128)S(1)}, u32[]{:S(2)}, u32[]{:S(2)}) %collective-permute-start.3) | collective-permute-done | bytes 3104 | tf_op jit(solution)/shard_map/ppermute | solution.py:245
  7.9 0.0 collective-permute-done.5.refs_3_
  8.0 0.5 copy-done.18
  8.5 0.0 copy-done.19
  8.5 0.0 copy-done.20
  8.6 1.7 %shard_map.122 = (bf16[128,1024]{1,0:T(8,128)(2,1)}, s32[4,8,128]{2,1,0:T(8,128)}) custom-call(bf16[128,1024]{1,0:T(8,128)(2,1)} %bitcast.40, s32[6,1,128]{2,1,0:T(1,128)} %copy-done.17, s32[6,1,128]{2,1,0:T(1,128)} %copy-done.18, s32[6,1,128]{2,1,0:T(1,128)} %copy-done.19, s32[6,1,128]{2,1,0:T(1,128)} %copy-done.20), custom_call_target="tpu_custom_call" | custom-call | flops 1024 | bytes 1024 | tf_op jit(solution)/shard_map/pallas_call | solution.py:88
  10.3 2.9 %collective-permute-start.17 = (bf16[128,1024]{1,0:T(8,128)(2,1)}, bf16[128,1024]{1,0:T(8,128)(2,1)S(1)}, u32[]{:S(2)}, u32[]{:S(2)}) collective-permute-start(bf16[128,1024]{1,0:T(8,128)(2,1)} %get-tuple-element.13.xz_ref), channel_id=1, source_target_pairs={{0,2},{2,0},{4,6},{6,4},{8,10},{10,8},{12,14},{14,12},{1,3},{3,1},... | collective-permute-start | bytes 786440 | tf_op jit(solution)/shard_map/ppermute | solution.py:248
  13.1 1.6 %collective-permute-start.15 = (bf16[128,1024]{1,0:T(8,128)(2,1)}, bf16[128,1024]{1,0:T(8,128)(2,1)S(1)}, u32[]{:S(2)}, u32[]{:S(2)}) collective-permute-start(bf16[128,1024]{1,0:T(8,128)(2,1)} %get-tuple-element.13.xz_ref), channel_id=1, source_target_pairs={{0,4},{2,6},{4,8},{6,10},{8,12},{10,14},{12,0},{14,2},{1,5},{3,7},... | collective-permute-start | bytes 786440 | tf_op jit(solution)/shard_map/ppermute | solution.py:251
  14.7 1.6 %collective-permute-start.6 = (s32[4,8,128]{2,1,0:T(8,128)}, s32[4,8,128]{2,1,0:T(8,128)S(1)}, u32[]{:S(2)}, u32[]{:S(2)}) collective-permute-start(s32[4,8,128]{2,1,0:T(8,128)} %get-tuple-element.12.refs_0_), channel_id=1, source_target_pairs={{0,4},{2,6},{4,0},{6,2},{8,12},{10,14},{12,8},{14,10},{1,5},{3,7},... | collective-permute-start | bytes 49160 | tf_op jit(solution)/shard_map/ppermute | solution.py:254
  16.3 6.3 %collective-permute-done.6.refs_1_ = s32[4,8,128]{2,1,0:T(8,128)S(1)} collective-permute-done((s32[4,8,128]{2,1,0:T(8,128)}, s32[4,8,128]{2,1,0:T(8,128)S(1)}, u32[]{:S(2)}, u32[]{:S(2)}) %collective-permute-start.6) | collective-permute-done | bytes 16416 | tf_op jit(solution)/shard_map/ppermute | solution.py:254
  22.6 1.6 %collective-permute-start.7 = (s32[4,8,128]{2,1,0:T(8,128)}, s32[4,8,128]{2,1,0:T(8,128)S(1)}, u32[]{:S(2)}, u32[]{:S(2)}) collective-permute-start(s32[4,8,128]{2,1,0:T(8,128)} %get-tuple-element.12.refs_0_), channel_id=1, source_target_pairs={{0,8},{2,10},{4,12},{6,14},{8,0},{10,2},{12,4},{14,6},{1,9},{3,11}... | collective-permute-start | bytes 49160 | tf_op jit(solution)/shard_map/ppermute | solution.py:254
  24.2 3.3 %collective-permute-done.7.refs_2_ = s32[4,8,128]{2,1,0:T(8,128)S(1)} collective-permute-done((s32[4,8,128]{2,1,0:T(8,128)}, s32[4,8,128]{2,1,0:T(8,128)S(1)}, u32[]{:S(2)}, u32[]{:S(2)}) %collective-permute-start.7) | collective-permute-done | bytes 16416 | tf_op jit(solution)/shard_map/ppermute | solution.py:254
  27.5 2.7 %collective-permute-start.8 = (s32[4,8,128]{2,1,0:T(8,128)}, s32[4,8,128]{2,1,0:T(8,128)S(1)}, u32[]{:S(2)}, u32[]{:S(2)}) collective-permute-start(s32[4,8,128]{2,1,0:T(8,128)} %get-tuple-element.12.refs_0_), channel_id=1, source_target_pairs={{0,12},{2,14},{4,8},{6,10},{8,4},{10,6},{12,0},{14,2},{1,13},{3,15... | collective-permute-start | bytes 49160 | tf_op jit(solution)/shard_map/ppermute | solution.py:254
  30.2 3.1 %collective-permute-done.8.refs_3_ = s32[4,8,128]{2,1,0:T(8,128)S(1)} collective-permute-done((s32[4,8,128]{2,1,0:T(8,128)}, s32[4,8,128]{2,1,0:T(8,128)S(1)}, u32[]{:S(2)}, u32[]{:S(2)}) %collective-permute-start.8) | collective-permute-done | bytes 16416 | tf_op jit(solution)/shard_map/ppermute | solution.py:254
  33.4 0.0 collective-permute-start.13
  33.4 2.9 %collective-permute-start.9 = (bf16[128,1024]{1,0:T(8,128)(2,1)}, bf16[128,1024]{1,0:T(8,128)(2,1)S(1)}, u32[]{:S(2)}, u32[]{:S(2)}) collective-permute-start(bf16[128,1024]{1,0:T(8,128)(2,1)} %get-tuple-element.13.xz_ref), channel_id=1, source_target_pairs={{0,12},{2,14},{4,0},{6,2},{8,4},{10,6},{12,8},{14,10},{1,13},{3,15... | collective-permute-start | bytes 786440 | tf_op jit(solution)/shard_map/ppermute | solution.py:251
  36.3 0.5 collective-permute-start.16
  36.7 9.8 %collective-permute-done.13.xz_ref = bf16[128,1024]{1,0:T(8,128)(2,1)S(1)} collective-permute-done((bf16[128,1024]{1,0:T(8,128)(2,1)}, bf16[128,1024]{1,0:T(8,128)(2,1)S(1)}, u32[]{:S(2)}, u32[]{:S(2)}) %collective-permute-start.13) | collective-permute-done | bytes 262176 | tf_op jit(solution)/shard_map/ppermute | solution.py:251
  46.5 0.6 collective-permute-start.14
  47.2 2.0 %shard_map.123.kept_ref.rest_0_ = s32[8,8,128]{2,1,0:T(8,128)} custom-call(s32[1]{0:T(128)} %bitcast.4.own_ref, s32[16]{0:T(128)} %capacity_ref.1, s32[4,8,128]{2,1,0:T(8,128)} %get-tuple-element.12.refs_0_, s32[4,8,128]{2,1,0:T(8,128)} %copy-done.14, s32[4,8,128]{2,1,0:T(8,128)} %copy-done.15, s32[4,8,128]{2,1,0:T(8,128)} %copy-done.16), custom_call_target="tpu_custom_call" | custom-call | flops 1024 | bytes 1024 | tf_op jit(solution)/shard_map/pallas_call | solution.py:143
  49.1 0.0 collective-permute-done.9.xz_ref
  49.1 1.4 %collective-permute-start.10 = (bf16[128,1024]{1,0:T(8,128)(2,1)S(1)}, bf16[128,1024]{1,0:T(8,128)(2,1)S(1)}, u32[]{:S(2)}, u32[]{:S(2)}) collective-permute-start(bf16[128,1024]{1,0:T(8,128)(2,1)S(1)} %collective-permute-done.9.xz_ref), channel_id=1, source_target_pairs={{0,2},{2,0},{4,6},{6,4},{8,10},{10,8},{12,14},{14,12},{1,3},{3,1},... | collective-permute-start | bytes 786440 | tf_op jit(solution)/shard_map/ppermute | solution.py:248
  50.5 2.2 %copy-done = bf16[1,1024,2048]{2,1,0:T(8,128)(2,1)S(1)} copy-done((bf16[1,1024,2048]{2,1,0:T(8,128)(2,1)S(1)}, bf16[1,1024,2048]{2,1,0:T(8,128)(2,1)}, u32[]{:S(2)}) %copy-start) | copy-done | bytes 4194328
  52.7 2.2 %copy-done.2 = bf16[1,2048,1024]{2,1,0:T(8,128)(2,1)S(1)} copy-done((bf16[1,2048,1024]{2,1,0:T(8,128)(2,1)S(1)}, bf16[1,2048,1024]{2,1,0:T(8,128)(2,1)}, u32[]{:S(2)}) %copy-start.2) | copy-done | bytes 4194328
  54.9 0.8 copy-done.7
  55.7 0.8 copy-done.9
  56.4 0.9 copy-done.11
  57.4 7.9 %shard_map.124 = (bf16[128,1024]{1,0:T(8,128)(2,1)S(1)}, bf16[128,1024]{1,0:T(8,128)(2,1)S(1)}) custom-call(s32[1]{0:T(128)} %bitcast.4.own_ref, s32[8,8,128]{2,1,0:T(8,128)S(1)} %copy-done.7, bf16[16,1024]{1,0:T(8,128)(2,1)S(1)} %bitcast.35, bf16[128,1024]{1,0:T(8,128)(2,1)S(1)} %copy-done.11, bf16[128,1024]{1,0:T(8,128)(2,1)S(1)} %collective-permute-done.17.xy_ref, ...), custom_call_target="tpu_custom_call" | custom-call | flops 1024 | bytes 1024 | tf_op jit(solution)/shard_map/pallas_call | solution.py:219
  65.3 0.0 collective-permute-done.16.xy_ref
  65.3 7.3 %shard_map.125 = (bf16[128,1024]{1,0:T(8,128)(2,1)S(1)}, bf16[128,1024]{1,0:T(8,128)(2,1)S(1)}) custom-call(s32[1]{0:T(128)} %bitcast.4.own_ref, s32[8,8,128]{2,1,0:T(8,128)S(1)} %copy-done.7, bf16[16,1024]{1,0:T(8,128)(2,1)S(1)} %bitcast.36, bf16[128,1024]{1,0:T(8,128)(2,1)S(1)} %collective-permute-done.15.xz_ref, ...), custom_call_target="tpu_custom_call" | custom-call | flops 1024 | bytes 1024 | tf_op jit(solution)/shard_map/pallas_call | solution.py:219
  72.6 0.7 collective-permute-start.19
  73.3 0.0 copy-start.8
  73.4 0.0 copy-start.10
  73.4 7.5 %shard_map.126 = (bf16[128,1024]{1,0:T(8,128)(2,1)S(1)}, bf16[128,1024]{1,0:T(8,128)(2,1)S(1)}) custom-call(s32[1]{0:T(128)} %bitcast.4.own_ref, s32[8,8,128]{2,1,0:T(8,128)S(1)} %copy-done.7, bf16[16,1024]{1,0:T(8,128)(2,1)S(1)} %bitcast.37, bf16[128,1024]{1,0:T(8,128)(2,1)S(1)} %collective-permute-done.13.xz_ref, ...), custom_call_target="tpu_custom_call" | custom-call | flops 1024 | bytes 1024 | tf_op jit(solution)/shard_map/pallas_call | solution.py:219
  80.8 1.5 %collective-permute-start.21 = (bf16[128,1024]{1,0:T(8,128)(2,1)S(1)}, bf16[128,1024]{1,0:T(8,128)(2,1)S(1)}, u32[]{:S(2)}, u32[]{:S(2)}) collective-permute-start(bf16[128,1024]{1,0:T(8,128)(2,1)S(1)} %get-tuple-element.20), channel_id=1, source_target_pairs={{0,2},{2,0},{4,6},{6,4},{8,10},{10,8},{12,14},{14,12},{1,3},{3,1},... | collective-permute-start | bytes 786440 | tf_op jit(solution)/shard_map/ppermute | solution.py:248
  82.3 0.5 collective-permute-start.1
  82.8 0.1 collective-permute-start.2
  82.9 7.3 %shard_map.127 = (bf16[128,1024]{1,0:T(8,128)(2,1)S(1)}, bf16[128,1024]{1,0:T(8,128)(2,1)S(1)}) custom-call(s32[1]{0:T(128)} %bitcast.4.own_ref, s32[8,8,128]{2,1,0:T(8,128)S(1)} %copy-done.8, bf16[16,1024]{1,0:T(8,128)(2,1)S(1)} %bitcast.38, bf16[128,1024]{1,0:T(8,128)(2,1)S(1)} %collective-permute-done.9.xz_ref, ...), custom_call_target="tpu_custom_call" | custom-call | flops 1024 | bytes 1024 | tf_op jit(solution)/shard_map/pallas_call | solution.py:219
  90.2 0.0 collective-permute-done.19
  90.2 0.7 collective-permute-start.23
  90.9 0.1 add_convert_fusion.3
  91.0 0.0 collective-permute-done.21
  91.0 1.5 %collective-permute-start.18 = (bf16[128,1024]{1,0:T(8,128)(2,1)S(1)}, bf16[128,1024]{1,0:T(8,128)(2,1)S(1)}, u32[]{:S(2)}, u32[]{:S(2)}) collective-permute-start(bf16[128,1024]{1,0:T(8,128)(2,1)S(1)} %get-tuple-element.18), channel_id=1, source_target_pairs={{0,2},{2,0},{4,6},{6,4},{8,10},{10,8},{12,14},{14,12},{1,3},{3,1},... | collective-permute-start | bytes 786440 | tf_op jit(solution)/shard_map/ppermute | solution.py:248
  92.5 0.1 add_convert_fusion.2
  92.5 6.9 %collective-permute-done.23 = bf16[128,1024]{1,0:T(8,128)(2,1)S(1)} collective-permute-done((bf16[128,1024]{1,0:T(8,128)(2,1)S(1)}, bf16[128,1024]{1,0:T(8,128)(2,1)S(1)}, u32[]{:S(2)}, u32[]{:S(2)}) %collective-permute-start.23) | collective-permute-done | bytes 262176 | tf_op jit(solution)/shard_map/ppermute | solution.py:248
  99.4 4.9 %collective-permute-start.20 = (bf16[128,1024]{1,0:T(8,128)(2,1)S(1)}, bf16[128,1024]{1,0:T(8,128)(2,1)S(1)}, u32[]{:S(2)}, u32[]{:S(2)}) collective-permute-start(bf16[128,1024]{1,0:T(8,128)(2,1)S(1)} %add_convert_fusion.3), channel_id=1, source_target_pairs={{0,12},{2,14},{4,0},{6,2},{8,4},{10,6},{12,8},{14,10},{1,13},{3,15... | collective-permute-start | bytes 786440 | tf_op jit(solution)/shard_map/ppermute | solution.py:251
  104.4 0.1 add_convert_fusion.1
  104.4 0.0 collective-permute-done.2.doc_far
  104.4 0.1 collective-permute-start.22
  104.5 0.0 collective-permute-done.k_far
  104.5 0.5 collective-permute-start.24
  105.1 0.0 collective-permute-done.1.v_far
  105.1 1.6 %shard_map.128.rest_1_ = bf16[128,2048]{1,0:T(8,128)(2,1)} custom-call(s32[1]{0:T(128)} %bitcast.place_ref, bf16[128,2048]{1,0:T(8,128)(2,1)S(1)} %bitcast.27, bf16[128,2048]{1,0:T(8,128)(2,1)S(1)} %bitcast.30, bf16[128,2048]{1,0:T(8,128)(2,1)S(1)} %collective-permute-done.k_far, bf16[128,2048]{1,0:T(8,128)(2,1)S(1)} %bitcast.33, ...), custom_call_target="tpu_custom_call" | custom-call | flops 1024 | bytes 1024 | tf_op jit(solution)/shard_map/pallas_call | solution.py:65
  106.7 1.6 %shard_map.129 = bf16[128,2048]{1,0:T(8,128)(2,1)} custom-call(s32[1]{0:T(128)} %bitcast.place_ref, bf16[128,2048]{1,0:T(8,128)(2,1)S(1)} %bitcast.28, bf16[128,2048]{1,0:T(8,128)(2,1)S(1)} %bitcast.31, bf16[128,2048]{1,0:T(8,128)(2,1)S(1)} %collective-permute-done.k_far, bf16[128,2048]{1,0:T(8,128)(2,1)S(1)} %bitcast.34, ...), custom_call_target="tpu_custom_call", output_to_operand_aliasing={{}: (10, {})} | custom-call | flops 1024 | bytes 1024 | tf_op jit(solution)/shard_map/pallas_call | solution.py:65
  108.3 0.0 collective-permute-done.18
  108.3 2.9 %collective-permute-done.20 = bf16[128,1024]{1,0:T(8,128)(2,1)S(1)} collective-permute-done((bf16[128,1024]{1,0:T(8,128)(2,1)S(1)}, bf16[128,1024]{1,0:T(8,128)(2,1)S(1)}, u32[]{:S(2)}, u32[]{:S(2)}) %collective-permute-start.20) | collective-permute-done | bytes 262176 | tf_op jit(solution)/shard_map/ppermute | solution.py:251
  111.2 14.1 %collective-permute-done.22 = bf16[128,1024]{1,0:T(8,128)(2,1)S(1)} collective-permute-done((bf16[128,1024]{1,0:T(8,128)(2,1)S(1)}, bf16[128,1024]{1,0:T(8,128)(2,1)S(1)}, u32[]{:S(2)}, u32[]{:S(2)}) %collective-permute-start.22) | collective-permute-done | bytes 262176 | tf_op jit(solution)/shard_map/ppermute | solution.py:251
  125.3 0.9 fusion
  (42 shorter events, 0.1 us)
Async XLA Ops:
  0.6 49.9 %collective-permute-start.11 = (bf16[1024,2048]{1,0:T(8,128)(2,1)}, bf16[1024,2048]{1,0:T(8,128)(2,1)}, u32[]{:S(2)}, u32[]{:S(2)}) collective-permute-start(bf16[1024,2048]{1,0:T(8,128)(2,1)} %bitcast.17), channel_id=1, source_target_pairs={{0,1},{1,0},{2,3},{3,2},{4,5},{5,4},{6,7},{7,6},{8,9},{9,8},{10,11... | collective-permute-start | bytes 12582920 | tf_op jit(solution)/shard_map/ppermute | solution.py:245
  1.1 49.4 %collective-permute-start.12 = (bf16[2048,1024]{1,0:T(8,128)(2,1)}, bf16[2048,1024]{1,0:T(8,128)(2,1)}, u32[]{:S(2)}, u32[]{:S(2)}) collective-permute-start(bf16[2048,1024]{1,0:T(8,128)(2,1)} %bitcast.22), channel_id=1, source_target_pairs={{0,1},{1,0},{2,3},{3,2},{4,5},{5,4},{6,7},{7,6},{8,9},{9,8},{10,11... | collective-permute-start | bytes 12582920 | tf_op jit(solution)/shard_map/ppermute | solution.py:245
  1.9 6.1 %copy-start.17 = (s32[6,1,128]{2,1,0:T(1,128)}, s32[6,1,128]{2,1,0:T(1,128)S(1)}, u32[]{:S(2)}) copy-start(s32[6,1,128]{2,1,0:T(1,128)S(1)} %broadcast_in_dim.9.refs_0_) | copy-start | bytes 9220
  1.9 6.0 %collective-permute-start.3 = (s32[6,1,128]{2,1,0:T(1,128)S(1)}, s32[6,1,128]{2,1,0:T(1,128)S(1)}, u32[]{:S(2)}, u32[]{:S(2)}) collective-permute-start(s32[6,1,128]{2,1,0:T(1,128)S(1)} %broadcast_in_dim.9.refs_0_), channel_id=1, source_target_pairs={{0,1},{1,0},{2,3},{3,2},{4,5},{5,4},{6,7},{7,6},{8,9},{9,8},{10,11... | collective-permute-start | bytes 9224 | tf_op jit(solution)/shard_map/ppermute | solution.py:245
  2.4 5.6 %collective-permute-start.4 = (s32[6,1,128]{2,1,0:T(1,128)S(1)}, s32[6,1,128]{2,1,0:T(1,128)S(1)}, u32[]{:S(2)}, u32[]{:S(2)}) collective-permute-start(s32[6,1,128]{2,1,0:T(1,128)S(1)} %broadcast_in_dim.9.refs_0_), channel_id=1, source_target_pairs={{0,2},{2,0},{4,6},{6,4},{8,10},{10,8},{12,14},{14,12},{1,3},{3,1},... | collective-permute-start | bytes 9224 | tf_op jit(solution)/shard_map/ppermute | solution.py:248
  4.9 3.0 %collective-permute-start.5 = (s32[6,1,128]{2,1,0:T(1,128)S(1)}, s32[6,1,128]{2,1,0:T(1,128)S(1)}, u32[]{:S(2)}, u32[]{:S(2)}) collective-permute-start(s32[6,1,128]{2,1,0:T(1,128)S(1)} %broadcast_in_dim.9.refs_0_), channel_id=1, source_target_pairs={{0,3},{1,2},{2,1},{3,0},{4,7},{5,6},{6,5},{7,4},{8,11},{9,10},{10,... | collective-permute-start | bytes 9224 | tf_op jit(solution)/shard_map/ppermute | solution.py:258
  7.9 0.6 copy-start.18
  7.9 0.6 copy-start.19
  8.0 0.6 copy-start.20
  10.3 23.1 %collective-permute-start.17 = (bf16[128,1024]{1,0:T(8,128)(2,1)}, bf16[128,1024]{1,0:T(8,128)(2,1)S(1)}, u32[]{:S(2)}, u32[]{:S(2)}) collective-permute-start(bf16[128,1024]{1,0:T(8,128)(2,1)} %get-tuple-element.13.xz_ref), channel_id=1, source_target_pairs={{0,2},{2,0},{4,6},{6,4},{8,10},{10,8},{12,14},{14,12},{1,3},{3,1},... | collective-permute-start | bytes 786440 | tf_op jit(solution)/shard_map/ppermute | solution.py:248
  13.1 23.1 %collective-permute-start.15 = (bf16[128,1024]{1,0:T(8,128)(2,1)}, bf16[128,1024]{1,0:T(8,128)(2,1)S(1)}, u32[]{:S(2)}, u32[]{:S(2)}) collective-permute-start(bf16[128,1024]{1,0:T(8,128)(2,1)} %get-tuple-element.13.xz_ref), channel_id=1, source_target_pairs={{0,4},{2,6},{4,8},{6,10},{8,12},{10,14},{12,0},{14,2},{1,5},{3,7},... | collective-permute-start | bytes 786440 | tf_op jit(solution)/shard_map/ppermute | solution.py:251
  14.7 7.9 %collective-permute-start.6 = (s32[4,8,128]{2,1,0:T(8,128)}, s32[4,8,128]{2,1,0:T(8,128)S(1)}, u32[]{:S(2)}, u32[]{:S(2)}) collective-permute-start(s32[4,8,128]{2,1,0:T(8,128)} %get-tuple-element.12.refs_0_), channel_id=1, source_target_pairs={{0,4},{2,6},{4,0},{6,2},{8,12},{10,14},{12,8},{14,10},{1,5},{3,7},... | collective-permute-start | bytes 49160 | tf_op jit(solution)/shard_map/ppermute | solution.py:254
  22.6 24.5 %copy-start.14 = (s32[4,8,128]{2,1,0:T(8,128)}, s32[4,8,128]{2,1,0:T(8,128)S(1)}, u32[]{:S(2)}) copy-start(s32[4,8,128]{2,1,0:T(8,128)S(1)} %collective-permute-done.6.refs_1_) | copy-start | bytes 49156
  22.6 4.9 %collective-permute-start.7 = (s32[4,8,128]{2,1,0:T(8,128)}, s32[4,8,128]{2,1,0:T(8,128)S(1)}, u32[]{:S(2)}, u32[]{:S(2)}) collective-permute-start(s32[4,8,128]{2,1,0:T(8,128)} %get-tuple-element.12.refs_0_), channel_id=1, source_target_pairs={{0,8},{2,10},{4,12},{6,14},{8,0},{10,2},{12,4},{14,6},{1,9},{3,11}... | collective-permute-start | bytes 49160 | tf_op jit(solution)/shard_map/ppermute | solution.py:254
  27.5 19.7 %copy-start.15 = (s32[4,8,128]{2,1,0:T(8,128)}, s32[4,8,128]{2,1,0:T(8,128)S(1)}, u32[]{:S(2)}) copy-start(s32[4,8,128]{2,1,0:T(8,128)S(1)} %collective-permute-done.7.refs_2_) | copy-start | bytes 49156
  27.5 5.8 %collective-permute-start.8 = (s32[4,8,128]{2,1,0:T(8,128)}, s32[4,8,128]{2,1,0:T(8,128)S(1)}, u32[]{:S(2)}, u32[]{:S(2)}) collective-permute-start(s32[4,8,128]{2,1,0:T(8,128)} %get-tuple-element.12.refs_0_), channel_id=1, source_target_pairs={{0,12},{2,14},{4,8},{6,10},{8,4},{10,6},{12,0},{14,2},{1,13},{3,15... | collective-permute-start | bytes 49160 | tf_op jit(solution)/shard_map/ppermute | solution.py:254
  33.3 13.8 %copy-start.16 = (s32[4,8,128]{2,1,0:T(8,128)}, s32[4,8,128]{2,1,0:T(8,128)S(1)}, u32[]{:S(2)}) copy-start(s32[4,8,128]{2,1,0:T(8,128)S(1)} %collective-permute-done.8.refs_3_) | copy-start | bytes 49156
  33.4 13.2 %collective-permute-start.13 = (bf16[128,1024]{1,0:T(8,128)(2,1)}, bf16[128,1024]{1,0:T(8,128)(2,1)S(1)}, u32[]{:S(2)}, u32[]{:S(2)}) collective-permute-start(bf16[128,1024]{1,0:T(8,128)(2,1)} %get-tuple-element.13.xz_ref), channel_id=1, source_target_pairs={{0,8},{2,10},{4,12},{6,14},{8,0},{10,2},{12,4},{14,6},{1,9},{3,11}... | collective-permute-start | bytes 786440 | tf_op jit(solution)/shard_map/ppermute | solution.py:251
  33.4 15.8 %collective-permute-start.9 = (bf16[128,1024]{1,0:T(8,128)(2,1)}, bf16[128,1024]{1,0:T(8,128)(2,1)S(1)}, u32[]{:S(2)}, u32[]{:S(2)}) collective-permute-start(bf16[128,1024]{1,0:T(8,128)(2,1)} %get-tuple-element.13.xz_ref), channel_id=1, source_target_pairs={{0,12},{2,14},{4,0},{6,2},{8,4},{10,6},{12,8},{14,10},{1,13},{3,15... | collective-permute-start | bytes 786440 | tf_op jit(solution)/shard_map/ppermute | solution.py:251
  36.3 29.0 %collective-permute-start.16 = (bf16[128,1024]{1,0:T(8,128)(2,1)S(1)}, bf16[128,1024]{1,0:T(8,128)(2,1)S(1)}, u32[]{:S(2)}, u32[]{:S(2)}) collective-permute-start(bf16[128,1024]{1,0:T(8,128)(2,1)S(1)} %collective-permute-done.15.xz_ref), channel_id=1, source_target_pairs={{0,2},{2,0},{4,6},{6,4},{8,10},{10,8},{12,14},{14,12},{1,3},{3,1},... | collective-permute-start | bytes 786440 | tf_op jit(solution)/shard_map/ppermute | solution.py:248
  46.5 26.8 %collective-permute-start.14 = (bf16[128,1024]{1,0:T(8,128)(2,1)S(1)}, bf16[128,1024]{1,0:T(8,128)(2,1)S(1)}, u32[]{:S(2)}, u32[]{:S(2)}) collective-permute-start(bf16[128,1024]{1,0:T(8,128)(2,1)S(1)} %collective-permute-done.13.xz_ref), channel_id=1, source_target_pairs={{0,2},{2,0},{4,6},{6,4},{8,10},{10,8},{12,14},{14,12},{1,3},{3,1},... | collective-permute-start | bytes 786440 | tf_op jit(solution)/shard_map/ppermute | solution.py:248
  49.1 33.7 %collective-permute-start.10 = (bf16[128,1024]{1,0:T(8,128)(2,1)S(1)}, bf16[128,1024]{1,0:T(8,128)(2,1)S(1)}, u32[]{:S(2)}, u32[]{:S(2)}) collective-permute-start(bf16[128,1024]{1,0:T(8,128)(2,1)S(1)} %collective-permute-done.9.xz_ref), channel_id=1, source_target_pairs={{0,2},{2,0},{4,6},{6,4},{8,10},{10,8},{12,14},{14,12},{1,3},{3,1},... | collective-permute-start | bytes 786440 | tf_op jit(solution)/shard_map/ppermute | solution.py:248
  50.5 2.2 %copy-start = (bf16[1,1024,2048]{2,1,0:T(8,128)(2,1)S(1)}, bf16[1,1024,2048]{2,1,0:T(8,128)(2,1)}, u32[]{:S(2)}) copy-start(bf16[1,1024,2048]{2,1,0:T(8,128)(2,1)} %param.16) | copy-start | bytes 12582916
  52.7 2.2 %copy-start.2 = (bf16[1,2048,1024]{2,1,0:T(8,128)(2,1)S(1)}, bf16[1,2048,1024]{2,1,0:T(8,128)(2,1)}, u32[]{:S(2)}) copy-start(bf16[1,2048,1024]{2,1,0:T(8,128)(2,1)} %param.17) | copy-start | bytes 12582916
  54.9 0.8 copy-start.7
  55.7 0.8 copy-start.9
  56.4 0.9 copy-start.11
  57.4 7.9 %copy-start.1 = (bf16[1,1024,2048]{2,1,0:T(8,128)(2,1)S(1)}, bf16[1,1024,2048]{2,1,0:T(8,128)(2,1)}, u32[]{:S(2)}) copy-start(bf16[1,1024,2048]{2,1,0:T(8,128)(2,1)} %param.16) | copy-start | bytes 12582916
  57.4 7.9 %copy-start.3 = (bf16[1,2048,1024]{2,1,0:T(8,128)(2,1)S(1)}, bf16[1,2048,1024]{2,1,0:T(8,128)(2,1)}, u32[]{:S(2)}) copy-start(bf16[1,2048,1024]{2,1,0:T(8,128)(2,1)} %param.17) | copy-start | bytes 12582916
  72.6 17.6 %collective-permute-start.19 = (bf16[128,1024]{1,0:T(8,128)(2,1)S(1)}, bf16[128,1024]{1,0:T(8,128)(2,1)S(1)}, u32[]{:S(2)}, u32[]{:S(2)}) collective-permute-start(bf16[128,1024]{1,0:T(8,128)(2,1)S(1)} %get-tuple-element.19), channel_id=1, source_target_pairs={{0,2},{2,0},{4,6},{6,4},{8,10},{10,8},{12,14},{14,12},{1,3},{3,1},... | collective-permute-start | bytes 786440 | tf_op jit(solution)/shard_map/ppermute | solution.py:248
  73.3 9.0 %copy-start.5 = (bf16[1,128,2048]{2,1,0:T(8,128)(2,1)S(1)}, bf16[1,128,2048]{2,1,0:T(8,128)(2,1)}, u32[]{:S(2)}) copy-start(bf16[1,128,2048]{2,1,0:T(8,128)(2,1)} %param.12) | copy-start | bytes 1572868
  73.3 9.0 %copy-start.6 = (bf16[1,128,2048]{2,1,0:T(8,128)(2,1)S(1)}, bf16[1,128,2048]{2,1,0:T(8,128)(2,1)}, u32[]{:S(2)}) copy-start(bf16[1,128,2048]{2,1,0:T(8,128)(2,1)} %param.13) | copy-start | bytes 1572868
  73.3 9.5 %copy-start.12 = (s32[1,128]{1,0:T(1,128)S(1)}, s32[1,128]{1,0:T(1,128)}, u32[]{:S(2)}) copy-start(s32[1,128]{1,0:T(1,128)} %doc_own.3) | copy-start | bytes 1540
  73.3 9.6 %copy-start.8 = (s32[8,8,128]{2,1,0:T(8,128)S(1)}, s32[8,8,128]{2,1,0:T(8,128)}, u32[]{:S(2)}) copy-start(s32[8,8,128]{2,1,0:T(8,128)} %shard_map.123.kept_ref.rest_0_) | copy-start | bytes 98308
  73.4 9.6 %copy-start.10 = (bf16[1024,16]{0,1:T(8,128)(2,1)S(1)}, bf16[1024,16]{0,1:T(8,128)(2,1)}, u32[]{:S(2)}) copy-start(bf16[1024,16]{0,1:T(8,128)(2,1)} %param.15) | copy-start | bytes 98308
  80.8 10.2 %collective-permute-start.21 = (bf16[128,1024]{1,0:T(8,128)(2,1)S(1)}, bf16[128,1024]{1,0:T(8,128)(2,1)S(1)}, u32[]{:S(2)}, u32[]{:S(2)}) collective-permute-start(bf16[128,1024]{1,0:T(8,128)(2,1)S(1)} %get-tuple-element.20), channel_id=1, source_target_pairs={{0,2},{2,0},{4,6},{6,4},{8,10},{10,8},{12,14},{14,12},{1,3},{3,1},... | collective-permute-start | bytes 786440 | tf_op jit(solution)/shard_map/ppermute | solution.py:248
  82.3 22.2 %collective-permute-start = (bf16[128,2048]{1,0:T(8,128)(2,1)S(1)}, bf16[128,2048]{1,0:T(8,128)(2,1)S(1)}, u32[]{:S(2)}, u32[]{:S(2)}) collective-permute-start(bf16[128,2048]{1,0:T(8,128)(2,1)S(1)} %bitcast.29), channel_id=1, source_target_pairs={{0,1},{1,0},{2,3},{3,2},{4,5},{5,4},{6,7},{7,6},{8,9},{9,8},{10,11... | collective-permute-start | bytes 1572872 | tf_op jit(solution)/shard_map/ppermute | solution.py:348
  82.3 22.8 %collective-permute-start.1 = (bf16[128,2048]{1,0:T(8,128)(2,1)S(1)}, bf16[128,2048]{1,0:T(8,128)(2,1)S(1)}, u32[]{:S(2)}, u32[]{:S(2)}) collective-permute-start(bf16[128,2048]{1,0:T(8,128)(2,1)S(1)} %bitcast.32), channel_id=1, source_target_pairs={{0,1},{1,0},{2,3},{3,2},{4,5},{5,4},{6,7},{7,6},{8,9},{9,8},{10,11... | collective-permute-start | bytes 1572872 | tf_op jit(solution)/shard_map/ppermute | solution.py:349
  82.8 21.6 %collective-permute-start.2 = (s32[1,128]{1,0:T(1,128)S(1)}, s32[1,128]{1,0:T(1,128)S(1)}, u32[]{:S(2)}, u32[]{:S(2)}) collective-permute-start(s32[1,128]{1,0:T(1,128)S(1)} %copy-done.12), channel_id=1, source_target_pairs={{0,1},{1,0},{2,3},{3,2},{4,5},{5,4},{6,7},{7,6},{8,9},{9,8},{10,11... | collective-permute-start | bytes 1544 | tf_op jit(solution)/shard_map/ppermute | solution.py:350
  82.9 22.2 %copy-start.4 = (bf16[1,128,2048]{2,1,0:T(8,128)(2,1)S(1)}, bf16[1,128,2048]{2,1,0:T(8,128)(2,1)}, u32[]{:S(2)}) copy-start(bf16[1,128,2048]{2,1,0:T(8,128)(2,1)} %param.11) | copy-start | bytes 1572868
  82.9 22.2 %copy-start.13 = (s32[1,128]{1,0:T(1,128)S(1)}, s32[1,128]{1,0:T(1,128)}, u32[]{:S(2)}) copy-start(s32[1,128]{1,0:T(1,128)} %ahead_ref.3) | copy-start | bytes 1540
  90.2 9.2 %collective-permute-start.23 = (bf16[128,1024]{1,0:T(8,128)(2,1)S(1)}, bf16[128,1024]{1,0:T(8,128)(2,1)S(1)}, u32[]{:S(2)}, u32[]{:S(2)}) collective-permute-start(bf16[128,1024]{1,0:T(8,128)(2,1)S(1)} %get-tuple-element.21), channel_id=1, source_target_pairs={{0,2},{2,0},{4,6},{6,4},{8,10},{10,8},{12,14},{14,12},{1,3},{3,1},... | collective-permute-start | bytes 786440 | tf_op jit(solution)/shard_map/ppermute | solution.py:248
  91.0 17.2 %collective-permute-start.18 = (bf16[128,1024]{1,0:T(8,128)(2,1)S(1)}, bf16[128,1024]{1,0:T(8,128)(2,1)S(1)}, u32[]{:S(2)}, u32[]{:S(2)}) collective-permute-start(bf16[128,1024]{1,0:T(8,128)(2,1)S(1)} %get-tuple-element.18), channel_id=1, source_target_pairs={{0,2},{2,0},{4,6},{6,4},{8,10},{10,8},{12,14},{14,12},{1,3},{3,1},... | collective-permute-start | bytes 786440 | tf_op jit(solution)/shard_map/ppermute | solution.py:248
  99.4 11.7 %collective-permute-start.20 = (bf16[128,1024]{1,0:T(8,128)(2,1)S(1)}, bf16[128,1024]{1,0:T(8,128)(2,1)S(1)}, u32[]{:S(2)}, u32[]{:S(2)}) collective-permute-start(bf16[128,1024]{1,0:T(8,128)(2,1)S(1)} %add_convert_fusion.3), channel_id=1, source_target_pairs={{0,12},{2,14},{4,0},{6,2},{8,4},{10,6},{12,8},{14,10},{1,13},{3,15... | collective-permute-start | bytes 786440 | tf_op jit(solution)/shard_map/ppermute | solution.py:251
  104.4 20.9 %collective-permute-start.22 = (bf16[128,1024]{1,0:T(8,128)(2,1)S(1)}, bf16[128,1024]{1,0:T(8,128)(2,1)S(1)}, u32[]{:S(2)}, u32[]{:S(2)}) collective-permute-start(bf16[128,1024]{1,0:T(8,128)(2,1)S(1)} %add_convert_fusion.2), channel_id=1, source_target_pairs={{0,8},{2,10},{4,12},{6,14},{8,0},{10,2},{12,4},{14,6},{1,9},{3,11}... | collective-permute-start | bytes 786440 | tf_op jit(solution)/shard_map/ppermute | solution.py:251
  104.5 20.8 %collective-permute-start.24 = (bf16[128,1024]{1,0:T(8,128)(2,1)S(1)}, bf16[128,1024]{1,0:T(8,128)(2,1)S(1)}, u32[]{:S(2)}, u32[]{:S(2)}) collective-permute-start(bf16[128,1024]{1,0:T(8,128)(2,1)S(1)} %add_convert_fusion.1), channel_id=1, source_target_pairs={{0,4},{2,6},{4,8},{6,10},{8,12},{10,14},{12,0},{14,2},{1,5},{3,7},... | collective-permute-start | bytes 786440 | tf_op jit(solution)/shard_map/ppermute | solution.py:251

commit v4 on v3

--- a/solution.py
+++ b/solution.py
@@ -12,10 +12,10 @@
 LATENT = 1024
 TOPK = 6
 DENSE_EXPERTS = 16
-EXPERT_VMEM = 28 * 1024 * 1024
-ATTEND_VMEM = 16 * 1024 * 1024
-EXPERT_COST = 1024
-ATTEND_COST = 1024
+EXPERT_VMEM = 16 * 1024 * 1024
+ATTEND_VMEM = 10 * 1024 * 1024
+SMALL_VMEM = 4 * 1024 * 1024
+LOAD_VMEM = 44 * 1024 * 1024
 
 
 def run_expert(rows_in, w_first, w_second):
@@ -70,39 +70,92 @@
         out_specs=heads,
         input_output_aliases={} if before is None else {8 + len(extra): 0},
         compiler_params=pltpu.CompilerParams(vmem_limit_bytes=ATTEND_VMEM),
-        cost_estimate=pl.CostEstimate(flops=ATTEND_COST, bytes_accessed=ATTEND_COST, transcendentals=0),
+        cost_estimate=pl.CostEstimate(
+            flops=4 * rows * rows * width, bytes_accessed=6 * rows * width, transcendentals=0
+        ),
     )(place, q, k_own, k_far, v_own, v_far, doc_own, doc_far, ahead, *extra)
 
 
-def prep_kernel(latent_ref, *refs):
-    parts, rows_ref, table_ref = refs[:-2], refs[-2], refs[-1]
+def pack_kernel(latent_ref, named_ref, doc_ref, rows_ref, table_ref):
     rows_ref[...] = latent_ref[...]
-    for index, part in enumerate(parts):
-        for k in range(TOPK):
-            table_ref[index, k : k + 1, :] = part[k]
-        table_ref[index, TOPK:, :] = jnp.full((8 - TOPK, part.shape[2]), -1, jnp.int32)
-
-
-def prepare(latent, parts):
+    for k in range(TOPK):
+        table_ref[0, k : k + 1, :] = named_ref[k]
+    table_ref[0, TOPK : TOPK + 1, :] = doc_ref[...]
+    table_ref[0, TOPK + 1 :, :] = doc_ref[...]
+
+
+def pack(latent, named, doc):
     vmem = pl.BlockSpec(memory_space=pltpu.VMEM)
     return pl.pallas_call(
-        prep_kernel,
+        pack_kernel,
         out_shape=(
             jax.ShapeDtypeStruct(latent.shape, latent.dtype),
-            jax.ShapeDtypeStruct((len(parts), 8, latent.shape[0]), jnp.int32),
+            jax.ShapeDtypeStruct((1, 8, latent.shape[0]), jnp.int32),
         ),
-        in_specs=[vmem] * (1 + len(parts)),
+        in_specs=[vmem] * 3,
         out_specs=(vmem, vmem),
-        cost_estimate=pl.CostEstimate(flops=1024, bytes_accessed=1024, transcendentals=0),
-    )(latent, *parts)
-
-
-def kept_kernel(line, own_ref, capacity_ref, *refs):
-    tables, out_ref = refs[:-1], refs[-1]
+        compiler_params=pltpu.CompilerParams(vmem_limit_bytes=SMALL_VMEM),
+    )(latent, named, doc)
+
+
+def join_kernel(first_ref, second_ref, *refs):
+    count = first_ref.shape[0]
+    refs[-1][:count] = first_ref[...]
+    refs[-1][count:] = second_ref[...]
+
+
+def join(first, second, passed=None, after=()):
+    vmem = pl.BlockSpec(memory_space=pltpu.VMEM)
+    anywhere = pl.BlockSpec(memory_space=pl.ANY)
+    table = jax.ShapeDtypeStruct((2 * first.shape[0],) + first.shape[1:], first.dtype)
+    through = [] if passed is None else [passed]
+    out = pl.pallas_call(
+        join_kernel,
+        out_shape=[jax.ShapeDtypeStruct(x.shape, x.dtype) for x in through] + [table],
+        in_specs=[vmem] * 2 + [anywhere] * (len(through) + len(after)),
+        out_specs=[anywhere] * len(through) + [vmem],
+        input_output_aliases={2: 0} if through else {},
+        compiler_params=pltpu.CompilerParams(vmem_limit_bytes=SMALL_VMEM),
+    )(first, second, *through, *after)
+    return out if through else out[0]
+
+
+def load_kernel(w1_any, w2_any, *refs):
+    w1_ref, w2_ref, sems = refs[-3:]
+    loads = [
+        pltpu.make_async_copy(w1_any, w1_ref, sems.at[0]),
+        pltpu.make_async_copy(w2_any, w2_ref, sems.at[1]),
+    ]
+    for load in loads:
+        load.start()
+    for load in loads:
+        load.wait()
+
+
+def load_weights(w_first, w_second, after):
+    anywhere = pl.BlockSpec(memory_space=pl.ANY)
+    vmem = pl.BlockSpec(memory_space=pltpu.VMEM)
+    return pl.pallas_call(
+        load_kernel,
+        out_shape=(
+            pltpu.VMEM(w_first.shape, w_first.dtype),
+            pltpu.VMEM(w_second.shape, w_second.dtype),
+        ),
+        in_specs=[anywhere] * (2 + len(after)),
+        out_specs=(vmem, vmem),
+        scratch_shapes=[pltpu.SemaphoreType.DMA((2,))],
+        compiler_params=pltpu.CompilerParams(vmem_limit_bytes=LOAD_VMEM),
+    )(w_first, w_second, *after)
+
+
+def kept_kernel(own_ref, capacity_ref, low_ref, high_ref, *refs):
+    out_ref = refs[-1]
+    tables = (low_ref, high_ref)
     own = own_ref[0]
     z = own // 4
-    rows = tables[0].shape[2]
-    sources = 4 * line
+    rows = low_ref.shape[2]
+    sources = 2 * low_ref.shape[0]
+    line = sources // 4
     upto = lax.broadcasted_iota(jnp.int32, (rows, rows), 0) <= lax.broadcasted_iota(
         jnp.int32, (rows, rows), 1
     )
@@ -136,17 +189,17 @@
                 out_ref[2 * step + side, k : k + 1, :] = picked
 
 
-def kept_rows(own, capacity, tables):
+def kept_rows(own, capacity, low, high, after):
     smem = pl.BlockSpec(memory_space=pltpu.SMEM)
     vmem = pl.BlockSpec(memory_space=pltpu.VMEM)
-    line, rows = len(tables), tables[0].shape[2]
+    anywhere = pl.BlockSpec(memory_space=pl.ANY)
     return pl.pallas_call(
-        functools.partial(kept_kernel, line),
-        out_shape=jax.ShapeDtypeStruct((2 * line, 8, rows), jnp.int32),
-        in_specs=[smem, smem] + [vmem] * line,
+        kept_kernel,
+        out_shape=jax.ShapeDtypeStruct(low.shape, jnp.int32),
+        in_specs=[smem, smem, vmem, vmem] + [anywhere] * len(after),
         out_specs=vmem,
-        cost_estimate=pl.CostEstimate(flops=1024, bytes_accessed=1024, transcendentals=0),
-    )(own, capacity, *tables)
+        compiler_params=pltpu.CompilerParams(vmem_limit_bytes=SMALL_VMEM),
+    )(own, capacity, low, high, *after)
 
 
 def gate_columns(own, router_ref, x, kept):
@@ -167,36 +220,22 @@
     return square.T
 
 
-def expert_kernel(
-    place, own_ref, kept_ref, router_ref, xz_ref, xy_ref, w1a, w2a, w1b_any, w2b_any, *rest
-):
-    z_ref, y_ref, hidden_ref, w1b, w2b, sems = rest[-6:]
-    loads = [
-        pltpu.make_async_copy(w1b_any, w1b, sems.at[0]),
-        pltpu.make_async_copy(w2b_any, w2b, sems.at[1]),
-    ]
-    for load in loads:
-        load.start()
+def expert_kernel(place, own_ref, kept_ref, router_ref, xz_ref, xy_ref, w1a, w2a, w1b, w2b, *rest):
+    z_ref, y_ref, hidden_ref = rest[-3:]
     own = own_ref[0]
     rows = xz_ref.shape[0]
     x = jnp.concatenate([xz_ref[...], xy_ref[...]], axis=0)
     step = 512
-
-    def enter(which, w1_ref):
+    for which, w1_ref in enumerate((w1a, w1b)):
         for first in range(0, w1_ref.shape[1], step):
             cols = slice(first, first + step)
             hidden = jnp.dot(x, w1_ref[:, cols], preferred_element_type=jnp.float32)
             hidden = jnp.maximum(hidden, 0.0)
             hidden_ref[which, :, cols] = (hidden * hidden).astype(jnp.bfloat16)
-
-    enter(0, w1a)
     gates = [
         gate_columns(own, router_ref, x_ref[...], kept_ref[2 * place + side])
         for side, x_ref in enumerate((xz_ref, xy_ref))
     ]
-    loads[0].wait()
-    enter(1, w1b)
-    loads[1].wait()
     for first in range(0, w2a.shape[1], step):
         cols = slice(first, first + step)
         results = [
@@ -216,30 +255,51 @@
     vmem = pl.BlockSpec(memory_space=pltpu.VMEM)
     anywhere = pl.BlockSpec(memory_space=pl.ANY)
     piece = jax.ShapeDtypeStruct((rows, width), jnp.bfloat16)
+    weights = [pltpu.with_memory_space_constraint(w, pltpu.VMEM) for w in weights]
     return pl.pallas_call(
         functools.partial(expert_kernel, place),
         out_shape=(piece, piece),
-        in_specs=[smem] + [vmem] * 6 + [anywhere] * (2 + len(after)),
+        in_specs=[smem] + [vmem] * 8 + [anywhere] * len(after),
         out_specs=(vmem, vmem),
-        scratch_shapes=[
-            pltpu.VMEM((2, 2 * rows, hidden), jnp.bfloat16),
-            pltpu.VMEM(weights[2].shape, jnp.bfloat16),
-            pltpu.VMEM(weights[3].shape, jnp.bfloat16),
-            pltpu.SemaphoreType.DMA((2,)),
-        ],
+        scratch_shapes=[pltpu.VMEM((2, 2 * rows, hidden), jnp.bfloat16)],
         compiler_params=pltpu.CompilerParams(vmem_limit_bytes=EXPERT_VMEM),
-        cost_estimate=pl.CostEstimate(flops=EXPERT_COST, bytes_accessed=EXPERT_COST, transcendentals=0),
+        cost_estimate=pl.CostEstimate(
+            flops=16 * rows * width * hidden,
+            bytes_accessed=8 * rows * width,
+            transcendentals=0,
+        ),
     )(own, kept, router, from_line, from_side, *weights, *after)
 
 
-def dense_moe(latent, router, expert_in, expert_out, routes, capacity, attention):
+def add_kernel(count, first_ref, second_ref, *refs):
+    total = first_ref[...].astype(jnp.float32) + second_ref[...].astype(jnp.float32)
+    outs = refs[len(refs) - count - 1 :]
+    outs[-1][...] = total.astype(jnp.bfloat16)
+    for index in range(count):
+        outs[index][...] = refs[index][...]
+
+
+def add(first, second, after=(), staged=()):
+    vmem = pl.BlockSpec(memory_space=pltpu.VMEM)
+    anywhere = pl.BlockSpec(memory_space=pl.ANY)
+    out = pl.pallas_call(
+        functools.partial(add_kernel, len(staged)),
+        out_shape=[jax.ShapeDtypeStruct(x.shape, x.dtype) for x in staged]
+        + [jax.ShapeDtypeStruct(first.shape, first.dtype)],
+        in_specs=[vmem] * (2 + len(staged)) + [anywhere] * len(after),
+        out_specs=[vmem] * (1 + len(staged)),
+        compiler_params=pltpu.CompilerParams(vmem_limit_bytes=SMALL_VMEM),
+        cost_estimate=pl.CostEstimate(flops=first.size, bytes_accessed=first.size, transcendentals=0),
+    )(first, second, *staged, *after)
+    return out if staged else out[0]
+
+
+def dense_moe(latent, router, expert_in, expert_out, routes, segments, capacity, k_near, v_near, attention):
     f32 = jnp.float32
-    axes = ("expert", "context")
     line = router.shape[1] // 4
     spots = [(z, y) for z in range(line) for y in range(2)]
     sibling = [(0, 1), (1, 0)]
     across = [(2 * z + y, 2 * z + 1 - y) for z, y in spots]
-    diagonal = [(4 * z + k, 4 * z + 3 - k) for z in range(line) for k in range(4)]
 
     def swap_core(x):
         return lax.ppermute(x, "context", sibling)
@@ -253,31 +313,52 @@
     def flipped(x, span):
         return lax.ppermute(x, "expert", [(2 * z + y, 2 * (z ^ span) + y) for z, y in spots])
 
-    own = lax.axis_index(axes).astype(jnp.int32).reshape(1)
-    named = routes[0].T[:, None, :]
-    parts = [named, swap_core(named), swap_side(named), lax.ppermute(named, axes, diagonal)]
-    rows, table = prepare(latent[0], parts)
-    tables = [table] + [flipped(table, span) for span in range(1, line)]
-    kept = kept_rows(own, capacity, tables)
-
+    own = lax.axis_index(("expert", "context")).astype(jnp.int32).reshape(1)
     w_first, w_second = expert_in[0], expert_out[0]
-    weights = (w_first, w_second, swap_core(w_first), swap_core(w_second))
-    from_line = [rows] + [along(rows, step) for step in range(1, line)]
-    from_side = [swap_side(x) for x in from_line]
-
-    half = attention(0, after=(kept,))
-    total = None
-    after = ()
-    for step in range(line):
-        mine, theirs = run_piece(
-            step, own, kept, router.T, from_line[step], from_side[step], weights, after
-        )
-        after = (mine,)
-        column = mine.astype(f32) + swap_side(theirs).astype(f32)
-        if step:
-            column = along(column.astype(jnp.bfloat16), line - step).astype(f32)
-        total = column if total is None else total + column
-    return attention(1, before=half, after=after), total.astype(jnp.bfloat16)[None]
+    far_weights = (swap_core(w_first), swap_core(w_second))
+
+    rows, tile = pack(latent[0], routes.transpose(2, 0, 1), segments)
+    arriving = along(latent[0], 1)
+    beside = swap_core(tile)
+    doc_far = beside[0, TOPK : TOPK + 1, :]
+    rows, table = join(tile, beside, passed=rows)
+    from_line = [rows, arriving]
+    from_side = [swap_side(rows)]
+    weights = tuple(load_weights(w_first, w_second, (table,))) + far_weights
+    from_line[1], table = join(table, swap_side(table), passed=arriving, after=weights[:2])
+    for step in range(2, line):
+        from_line.append(along(from_line[-1], 1))
+    from_side += [swap_side(x) for x in from_line[1:]]
+    span = 1
+    while 2 * span < line:
+        table = join(table, flipped(table, span), after=(from_line[1],))
+        span *= 2
+    kept = kept_rows(own, capacity, table, flipped(table, span), (from_line[2], from_side[0]))
+
+    def piece(step, *after):
+        return run_piece(step, own, kept, router.T, from_line[step], from_side[step], weights, after)
+
+    one, theirs = piece(1)
+    one_far = swap_side(theirs)
+    two, theirs = piece(2, one, from_line[3])
+    two_far = swap_side(theirs)
+    k_near, v_near, first = add(one, one_far, after=(two,), staged=(k_near, v_near))
+    home = [along(first, line - 1)]
+    three, theirs = piece(3, two, first)
+    three_far = swap_side(theirs)
+    second = add(two, two_far, after=(three,))
+    home.append(along(second, line - 2))
+    near, theirs = piece(0, three, second)
+    near_far = swap_side(theirs)
+    third = add(three, three_far, after=(near,))
+    home.append(along(third, line - 3))
+    swapped = (k_near, swap_core(k_near), v_near, swap_core(v_near))
+    half = attention(0, doc_far, *swapped, after=(third,))
+    attn_out = attention(1, doc_far, *swapped, before=half)
+    total = near.astype(f32) + near_far.astype(f32)
+    for part in home:
+        total += part.astype(f32)
+    return attn_out, total.astype(jnp.bfloat16)[None]
 
 
 def routed_moe(latent, router, expert_in, expert_out, routes, capacity):
@@ -345,32 +426,32 @@
     capacity,
 ):
     swap = [(0, 1), (1, 0)]
-    k_far = lax.ppermute(key_heads[0], "context", swap)
-    v_far = lax.ppermute(value_heads[0], "context", swap)
-    doc_far = lax.ppermute(segments, "context", swap)
     place = lax.axis_index("context").astype(jnp.int32).reshape(1)
 
-    def attention(half, **order):
+    def attention(half, doc_far, *keys_and_values, **order):
         return attend(
-            half,
-            place,
-            query_heads[0],
-            key_heads[0],
-            k_far,
-            value_heads[0],
-            v_far,
-            segments,
-            doc_far,
-            offsets,
-            **order,
+            half, place, query_heads[0], *keys_and_values, segments, doc_far, offsets, **order
         )
 
     if router.shape[1] <= DENSE_EXPERTS:
         attn_out, moe_out = dense_moe(
-            latent, router, expert_in, expert_out, routes, capacity, attention
+            latent,
+            router,
+            expert_in,
+            expert_out,
+            routes,
+            segments,
+            capacity,
+            key_heads[0],
+            value_heads[0],
+            attention,
         )
     else:
-        attn_out = attention(1, before=attention(0))
+        doc_far = lax.ppermute(segments, "context", swap)
+        k_far = lax.ppermute(key_heads[0], "context", swap)
+        v_far = lax.ppermute(value_heads[0], "context", swap)
+        swapped = (key_heads[0], k_far, value_heads[0], v_far)
+        attn_out = attention(1, doc_far, *swapped, before=attention(0, doc_far, *swapped))
         moe_out = routed_moe(latent, router, expert_in, expert_out, routes, capacity)
     return (attn_out[None], moe_out)
 

time: 127 us -> 96.4 us (0.76)
  waiting for transfers between devices: 49.4 us -> 21.5 us
  starting transfers between devices: 29.9 us -> 21.9 us
  Pallas kernels: 36.8 us -> 41 us
  local copies, waits for them, and re-layouts: 8.17 us -> 9.91 us
    ppermute x6, waiting for transfers between devices: 26.8 us -> 9.36 us  [along(): lax.ppermute(x, 'expert', [(2 * z + y, 2 * ((z + step) % line) + y) for z...]
    ppermute x3 -> x2, waiting for transfers between devices: 12.8 us -> 7.47 us  [flipped(): lax.ppermute(x, 'expert', [(2 * z + y, 2 * (z ^ span) + y) for z, y in sp...]
    ppermute x9, waiting for transfers between devices: 6.89 us -> 3.36 us  [swap_side(): return lax.ppermute(x, 'expert', across)]
    pallas_call x4, Pallas kernels: 30 us -> 33 us  [run_piece(): pl.pallas_call(functools.partial(expert_kernel, place), out_shape=(piece,...]
    ppermute x6, starting transfers between devices: 10 us -> 7 us  [along(): lax.ppermute(x, 'expert', [(2 * z + y, 2 * ((z + step) % line) + y) for z...]
    ppermute x3 -> x2, starting transfers between devices: 5.88 us -> 3.71 us  [flipped(): lax.ppermute(x, 'expert', [(2 * z + y, 2 * (z ^ span) + y) for z, y in sp...]
    ppermute x9, starting transfers between devices: 12.3 us -> 10.5 us  [swap_side(): return lax.ppermute(x, 'expert', across)]
    unnamed x43 -> x30, local copies, waits for them, and re-layouts: 8.17 us -> 9.9 us
  transfers between devices with their start and end apart: 25 -> 22, of which waited for: 8 -> 5; matrix products, arithmetic and copies ran while one was open for 1% -> 0% of each run, Pallas kernels for 29% -> 43%
where the time goes in v4:
time: 96.4 us; the launch traced here: 96.2 us
  Pallas kernels  41 us (43%)
  starting transfers between devices  21.9 us (23%)
  waiting for transfers between devices  21.5 us (22%)
  local copies, waits for them, and re-layouts  9.91 us (10%)
    pallas_call x4, Pallas kernels, run_piece(): pl.pallas_call(functools.partial(expert_kernel, place), out_shape=(piece,...  33 us
    ppermute x9, starting transfers between devices, swap_side(): return lax.ppermute(x, 'expert', across)  10.5 us
    unnamed x30, local copies, waits for them, and re-layouts  9.9 us
    ppermute x6, waiting for transfers between devices, along(): lax.ppermute(x, 'expert', [(2 * z + y, 2 * ((z + step) % line) + y) for z...  9.36 us
    ppermute x2, waiting for transfers between devices, flipped(): lax.ppermute(x, 'expert', [(2 * z + y, 2 * (z ^ span) + y) for z, y in sp...  7.47 us
    ppermute x6, starting transfers between devices, along(): lax.ppermute(x, 'expert', [(2 * z + y, 2 * ((z + step) % line) + y) for z...  7 us
    ppermute x2, starting transfers between devices, flipped(): lax.ppermute(x, 'expert', [(2 * z + y, 2 * (z ^ span) + y) for z, y in sp...  3.71 us
    pallas_call x1, Pallas kernels, load_weights(): pl.pallas_call(load_kernel, out_shape=(pltpu.VMEM(w_first.shape, w_first....  3.48 us
  transfers between devices with their start and end apart: 22, of which 5 were waited for; matrix products, arithmetic and copies ran while one was open for 0% of the time, Pallas kernels for 43%

profile of v4, /device:TPU:0, one launch (start us, length us, event | category | flops | bytes accessed | tf_op | source)
XLA Modules:
  0.0 96.2 jit_solution(11400547190095544704)
XLA Ops:
  0.6 0.5 collective-permute-start.8
  1.1 0.1 collective-permute-start.9
  1.2 3.0 %collective-permute-start.2 = (bf16[128,1024]{1,0:T(8,128)(2,1)}, bf16[128,1024]{1,0:T(8,128)(2,1)S(1)}, u32[]{:S(2)}, u32[]{:S(2)}) collective-permute-start(bf16[128,1024]{1,0:T(8,128)(2,1)} %bitcast.23), channel_id=1, source_target_pairs={{0,4},{2,6},{4,8},{6,10},{8,12},{10,14},{12,0},{14,2},{1,5},{3,7},... | collective-permute-start | bytes 786440 | tf_op jit(solution)/shard_map/ppermute | solution.py:311
  4.2 1.0 %copy-done.9 = bf16[1,128,1024]{2,1,0:T(8,128)(2,1)S(1)} copy-done((bf16[1,128,1024]{2,1,0:T(8,128)(2,1)S(1)}, bf16[1,128,1024]{2,1,0:T(8,128)(2,1)}, u32[]{:S(2)}) %copy-start.9) | copy-done | bytes 262168
  5.2 0.7 copy-done.10
  5.9 0.7 copy-done.12
  6.6 0.1 collective-permute-start
  6.7 1.3 %collective-permute-done.second_ref = s32[1,8,128]{2,1,0:T(8,128)S(1)} collective-permute-done((s32[1,8,128]{2,1,0:T(8,128)S(1)}, s32[1,8,128]{2,1,0:T(8,128)S(1)}, u32[]{:S(2)}, u32[]{:S(2)}) %collective-permute-start) | collective-permute-done | bytes 4128 | tf_op jit(solution)/shard_map/ppermute | solution.py:305
  7.9 2.9 %collective-permute-start.1 = (s32[2,8,128]{2,1,0:T(8,128)S(1)}, s32[2,8,128]{2,1,0:T(8,128)S(1)}, u32[]{:S(2)}, u32[]{:S(2)}) collective-permute-start(s32[2,8,128]{2,1,0:T(8,128)S(1)} %get-tuple-element.23.refs_0_.first_ref), channel_id=1, source_target_pairs={{0,2},{2,0},{4,6},{6,4},{8,10},{10,8},{12,14},{14,12},{1,3},{3,1},... | collective-permute-start | bytes 24584 | tf_op jit(solution)/shard_map/ppermute | solution.py:308
  10.8 3.5 %shard_map.124 = (bf16[1024,2048]{1,0:T(8,128)(2,1)S(1)}, bf16[2048,1024]{1,0:T(8,128)(2,1)S(1)}) custom-call(bf16[1024,2048]{1,0:T(8,128)(2,1)} %bitcast.27, bf16[2048,1024]{1,0:T(8,128)(2,1)} %bitcast.29, s32[2,8,128]{2,1,0:T(8,128)S(1)} %get-tuple-element.23.refs_0_.first_ref), custom_call_target="tpu_custom_call" | custom-call | tf_op jit(solution)/shard_map/pallas_call | solution.py:138
  14.3 0.0 collective-permute-done.1.second_ref
  14.4 0.0 collective-permute-done.2.refs_0_
  14.4 0.0 copy-start.14
  14.4 0.0 copy-start.8
  14.4 2.0 %copy-done = bf16[1024,2048]{1,0:T(8,128)(2,1)} copy-done((bf16[1024,2048]{1,0:T(8,128)(2,1)}, bf16[1024,2048]{1,0:T(8,128)(2,1)S(1)}, u32[]{:S(2)}) %copy-start) | copy-done | bytes 4194328
  16.4 1.2 %copy-done.3 = bf16[2048,1024]{1,0:T(8,128)(2,1)} copy-done((bf16[2048,1024]{1,0:T(8,128)(2,1)}, bf16[2048,1024]{1,0:T(8,128)(2,1)S(1)}, u32[]{:S(2)}) %copy-start.3) | copy-done | bytes 4194328
  17.6 1.6 %collective-permute-start.5 = (bf16[128,1024]{1,0:T(8,128)(2,1)S(1)}, bf16[128,1024]{1,0:T(8,128)(2,1)S(1)}, u32[]{:S(2)}, u32[]{:S(2)}) collective-permute-start(bf16[128,1024]{1,0:T(8,128)(2,1)S(1)} %get-tuple-element.27.refs_0_.xz_ref), channel_id=1, source_target_pairs={{0,4},{2,6},{4,8},{6,10},{8,12},{10,14},{12,0},{14,2},{1,5},{3,7},... | collective-permute-start | bytes 786440 | tf_op jit(solution)/shard_map/ppermute | solution.py:311
  19.2 0.5 collective-permute-start.6
  19.7 1.6 %collective-permute-start.3 = (s32[4,8,128]{2,1,0:T(8,128)S(1)}, s32[4,8,128]{2,1,0:T(8,128)S(1)}, u32[]{:S(2)}, u32[]{:S(2)}) collective-permute-start(s32[4,8,128]{2,1,0:T(8,128)S(1)} %get-tuple-element.26.first_ref), channel_id=1, source_target_pairs={{0,4},{2,6},{4,0},{6,2},{8,12},{10,14},{12,8},{14,10},{1,5},{3,7},... | collective-permute-start | bytes 49160 | tf_op jit(solution)/shard_map/ppermute | solution.py:314
  21.2 6.4 %collective-permute-done.5.refs_0_.xz_ref = bf16[128,1024]{1,0:T(8,128)(2,1)S(1)} collective-permute-done((bf16[128,1024]{1,0:T(8,128)(2,1)S(1)}, bf16[128,1024]{1,0:T(8,128)(2,1)S(1)}, u32[]{:S(2)}, u32[]{:S(2)}) %collective-permute-start.5) | collective-permute-done | bytes 262176 | tf_op jit(solution)/shard_map/ppermute | solution.py:311
  27.7 0.0 collective-permute-start.12
  27.7 0.0 collective-permute-done.3.second_ref
  27.7 0.7 collective-permute-start.7
  28.4 0.0 collective-permute-done.6.refs_1_.xy_ref
  28.4 2.1 %collective-permute-start.4 = (s32[8,8,128]{2,1,0:T(8,128)S(1)}, s32[8,8,128]{2,1,0:T(8,128)S(1)}, u32[]{:S(2)}, u32[]{:S(2)}) collective-permute-start(s32[8,8,128]{2,1,0:T(8,128)S(1)} %shard_map.126.low_ref), channel_id=1, source_target_pairs={{0,8},{2,10},{4,12},{6,14},{8,0},{10,2},{12,4},{14,6},{1,9},{3,11}... | collective-permute-start | bytes 98312 | tf_op jit(solution)/shard_map/ppermute | solution.py:314
  30.5 7.5 %collective-permute-done.4.high_ref = s32[8,8,128]{2,1,0:T(8,128)S(1)} collective-permute-done((s32[8,8,128]{2,1,0:T(8,128)S(1)}, s32[8,8,128]{2,1,0:T(8,128)S(1)}, u32[]{:S(2)}, u32[]{:S(2)}) %collective-permute-start.4) | collective-permute-done | bytes 32800 | tf_op jit(solution)/shard_map/ppermute | solution.py:314
  38.0 0.8 collective-permute-start.11
  38.7 1.1 %shard_map.127.kept_ref = s32[8,8,128]{2,1,0:T(8,128)S(1)} custom-call(s32[1]{0:T(128)} %bitcast.2.own_ref, s32[16]{0:T(128)S(1)} %copy-done.14, s32[8,8,128]{2,1,0:T(8,128)S(1)} %shard_map.126.low_ref, s32[8,8,128]{2,1,0:T(8,128)S(1)} %collective-permute-done.4.high_ref, bf16[128,1024]{1,0:T(8,128)(2,1)S(1)} %collective-permute-done.5.refs_0_.xz_ref, ...), custom_call_target="tpu_custom_call" | custom-call | tf_op jit(solution)/shard_map/pallas_call | solution.py:196
  39.8 0.0 collective-permute-done.12.rest_1_.xz_ref
  39.9 1.3 %collective-permute-start.15 = (bf16[128,1024]{1,0:T(8,128)(2,1)S(1)}, bf16[128,1024]{1,0:T(8,128)(2,1)S(1)}, u32[]{:S(2)}, u32[]{:S(2)}) collective-permute-start(bf16[128,1024]{1,0:T(8,128)(2,1)S(1)} %collective-permute-done.12.rest_1_.xz_ref), channel_id=1, source_target_pairs={{0,2},{2,0},{4,6},{6,4},{8,10},{10,8},{12,14},{14,12},{1,3},{3,1},... | collective-permute-start | bytes 786440 | tf_op jit(solution)/shard_map/ppermute | solution.py:308
  41.2 0.0 collective-permute-done.7.xy_ref
  41.2 0.0 collective-permute-done.8.w1b
  41.2 0.0 collective-permute-done.9.w2b
  41.2 2.2 %copy-done.1 = bf16[1024,2048]{1,0:T(8,128)(2,1)S(1)} copy-done((bf16[1024,2048]{1,0:T(8,128)(2,1)S(1)}, bf16[1024,2048]{1,0:T(8,128)(2,1)}, u32[]{:S(2)}) %copy-start.1) | copy-done | bytes 4194328
  43.4 2.2 %copy-done.4 = bf16[2048,1024]{1,0:T(8,128)(2,1)S(1)} copy-done((bf16[2048,1024]{1,0:T(8,128)(2,1)S(1)}, bf16[2048,1024]{1,0:T(8,128)(2,1)}, u32[]{:S(2)}) %copy-start.4) | copy-done | bytes 4194328
  45.6 8.2 %shard_map.128 = (bf16[128,1024]{1,0:T(8,128)(2,1)S(1)}, bf16[128,1024]{1,0:T(8,128)(2,1)S(1)}) custom-call(s32[1]{0:T(128)} %bitcast.2.own_ref, s32[8,8,128]{2,1,0:T(8,128)S(1)} %shard_map.127.kept_ref, bf16[16,1024]{1,0:T(8,128)(2,1)S(1)} %bitcast.19, bf16[128,1024]{1,0:T(8,128)(2,1)S(1)} %get-tuple-element.27.refs_0_.xz_ref, ...), custom_call_target="tpu_custom_call" | custom-call | flops 4294967296 | bytes 1048576 | tf_op jit(solution)/shard_map/pallas_call | solution.py:259
  53.8 0.8 collective-permute-start.10
  54.6 0.0 collective-permute-done.11.xy_ref
  54.6 8.3 %shard_map.129 = (bf16[128,1024]{1,0:T(8,128)(2,1)S(1)}, bf16[128,1024]{1,0:T(8,128)(2,1)S(1)}) custom-call(s32[1]{0:T(128)} %bitcast.2.own_ref, s32[8,8,128]{2,1,0:T(8,128)S(1)} %shard_map.127.kept_ref, bf16[16,1024]{1,0:T(8,128)(2,1)S(1)} %bitcast.20, bf16[128,1024]{1,0:T(8,128)(2,1)S(1)} %collective-permute-done.5.refs_0_.xz_ref, ...), custom_call_target="tpu_custom_call" | custom-call | flops 4294967296 | bytes 1048576 | tf_op jit(solution)/shard_map/pallas_call | solution.py:259
  62.9 1.3 %collective-permute-start.17 = (bf16[128,1024]{1,0:T(8,128)(2,1)S(1)}, bf16[128,1024]{1,0:T(8,128)(2,1)S(1)}, u32[]{:S(2)}, u32[]{:S(2)}) collective-permute-start(bf16[128,1024]{1,0:T(8,128)(2,1)S(1)} %get-tuple-element.37), channel_id=1, source_target_pairs={{0,2},{2,0},{4,6},{6,4},{8,10},{10,8},{12,14},{14,12},{1,3},{3,1},... | collective-permute-start | bytes 786440 | tf_op jit(solution)/shard_map/ppermute | solution.py:308
  64.2 0.0 collective-permute-done.10.second_ref
  64.2 0.1 shard_map.130
  64.3 0.2 collective-permute-start.19
  64.6 0.1 collective-permute-start.13
  64.7 0.0 collective-permute-done.15.xy_ref
  64.7 8.3 %shard_map.131 = (bf16[128,1024]{1,0:T(8,128)(2,1)S(1)}, bf16[128,1024]{1,0:T(8,128)(2,1)S(1)}) custom-call(s32[1]{0:T(128)} %bitcast.2.own_ref, s32[8,8,128]{2,1,0:T(8,128)S(1)} %shard_map.127.kept_ref, bf16[16,1024]{1,0:T(8,128)(2,1)S(1)} %bitcast.21, bf16[128,1024]{1,0:T(8,128)(2,1)S(1)} %collective-permute-done.12.rest_1_.xz_ref, ...), custom_call_target="tpu_custom_call" | custom-call | flops 4294967296 | bytes 1048576 | tf_op jit(solution)/shard_map/pallas_call | solution.py:259
  73.0 0.8 collective-permute-start.16
  73.8 0.0 collective-permute-done.17.second_ref
  73.8 0.1 shard_map.132.rest_1_
  73.9 1.4 %collective-permute-start.20 = (bf16[128,1024]{1,0:T(8,128)(2,1)S(1)}, bf16[128,1024]{1,0:T(8,128)(2,1)S(1)}, u32[]{:S(2)}, u32[]{:S(2)}) collective-permute-start(bf16[128,1024]{1,0:T(8,128)(2,1)S(1)} %shard_map.132.rest_1_), channel_id=1, source_target_pairs={{0,8},{2,10},{4,12},{6,14},{8,0},{10,2},{12,4},{14,6},{1,9},{3,11}... | collective-permute-start | bytes 786440 | tf_op jit(solution)/shard_map/ppermute | solution.py:311
  75.3 0.0 collective-permute-start.14
  75.3 8.3 %shard_map.133 = (bf16[128,1024]{1,0:T(8,128)(2,1)S(1)}, bf16[128,1024]{1,0:T(8,128)(2,1)S(1)}) custom-call(s32[1]{0:T(128)} %bitcast.2.own_ref, s32[8,8,128]{2,1,0:T(8,128)S(1)} %shard_map.127.kept_ref, bf16[16,1024]{1,0:T(8,128)(2,1)S(1)} %bitcast.22, bf16[128,1024]{1,0:T(8,128)(2,1)S(1)} %get-tuple-element.28.xz_ref, ...), custom_call_target="tpu_custom_call" | custom-call | flops 4294967296 | bytes 1048576 | tf_op jit(solution)/shard_map/pallas_call | solution.py:259
  83.6 0.0 collective-permute-done.16.second_ref
  83.6 1.3 %collective-permute-start.18 = (bf16[128,1024]{1,0:T(8,128)(2,1)S(1)}, bf16[128,1024]{1,0:T(8,128)(2,1)S(1)}, u32[]{:S(2)}, u32[]{:S(2)}) collective-permute-start(bf16[128,1024]{1,0:T(8,128)(2,1)S(1)} %get-tuple-element.39), channel_id=1, source_target_pairs={{0,2},{2,0},{4,6},{6,4},{8,10},{10,8},{12,14},{14,12},{1,3},{3,1},... | collective-permute-start | bytes 786440 | tf_op jit(solution)/shard_map/ppermute | solution.py:308
  84.9 0.1 shard_map.134.rest_0_
  85.0 0.0 collective-permute-done.13.k_far
  85.0 0.8 collective-permute-start.21
  85.8 0.0 collective-permute-done.14.v_far
  85.8 1.6 %shard_map.135.rest_0_ = bf16[128,2048]{1,0:T(8,128)(2,1)} custom-call(s32[1]{0:T(128)} %bitcast.place_ref, bf16[128,2048]{1,0:T(8,128)(2,1)S(1)} %bitcast.15, bf16[128,2048]{1,0:T(8,128)(2,1)S(1)} %get-tuple-element.32.k_own, bf16[128,2048]{1,0:T(8,128)(2,1)S(1)} %collective-permute-done.13.k_far, bf16[128,2048]{1,0:T(8,128)(2,1)S(1)} %get-tuple-element.33.v_own, ...), custom_call_target="tpu_custom_call" | custom-call | flops 134217728 | bytes 1572864 | tf_op jit(solution)/shard_map/pallas_call | solution.py:65
  87.4 1.6 %shard_map.136 = bf16[128,2048]{1,0:T(8,128)(2,1)} custom-call(s32[1]{0:T(128)} %bitcast.place_ref, bf16[128,2048]{1,0:T(8,128)(2,1)S(1)} %bitcast.16, bf16[128,2048]{1,0:T(8,128)(2,1)S(1)} %get-tuple-element.32.k_own, bf16[128,2048]{1,0:T(8,128)(2,1)S(1)} %collective-permute-done.13.k_far, ...), custom_call_target="tpu_custom_call", output_to_operand_aliasing={{}: (9, {})} | custom-call | flops 134217728 | bytes 1572864 | tf_op jit(solution)/shard_map/pallas_call | solution.py:65
  89.0 3.3 %collective-permute-done.18 = bf16[128,1024]{1,0:T(8,128)(2,1)S(1)} collective-permute-done((bf16[128,1024]{1,0:T(8,128)(2,1)S(1)}, bf16[128,1024]{1,0:T(8,128)(2,1)S(1)}, u32[]{:S(2)}, u32[]{:S(2)}) %collective-permute-start.18) | collective-permute-done | bytes 262176 | tf_op jit(solution)/shard_map/ppermute | solution.py:308
  92.3 0.0 collective-permute-done.20
  92.3 2.9 %collective-permute-done.21 = bf16[128,1024]{1,0:T(8,128)(2,1)S(1)} collective-permute-done((bf16[128,1024]{1,0:T(8,128)(2,1)S(1)}, bf16[128,1024]{1,0:T(8,128)(2,1)S(1)}, u32[]{:S(2)}, u32[]{:S(2)}) %collective-permute-start.21) | collective-permute-done | bytes 262176 | tf_op jit(solution)/shard_map/ppermute | solution.py:311
  95.3 0.9 fusion
  (27 shorter events, 0.1 us)
Async XLA Ops:
  0.6 40.6 %collective-permute-start.8 = (bf16[1024,2048]{1,0:T(8,128)(2,1)}, bf16[1024,2048]{1,0:T(8,128)(2,1)}, u32[]{:S(2)}, u32[]{:S(2)}) collective-permute-start(bf16[1024,2048]{1,0:T(8,128)(2,1)} %bitcast.26), channel_id=1, source_target_pairs={{0,1},{1,0},{2,3},{3,2},{4,5},{5,4},{6,7},{7,6},{8,9},{9,8},{10,11... | collective-permute-start | bytes 12582920 | tf_op jit(solution)/shard_map/ppermute | solution.py:305
  1.1 40.1 %collective-permute-start.9 = (bf16[2048,1024]{1,0:T(8,128)(2,1)}, bf16[2048,1024]{1,0:T(8,128)(2,1)}, u32[]{:S(2)}, u32[]{:S(2)}) collective-permute-start(bf16[2048,1024]{1,0:T(8,128)(2,1)} %bitcast.28), channel_id=1, source_target_pairs={{0,1},{1,0},{2,3},{3,2},{4,5},{5,4},{6,7},{7,6},{8,9},{9,8},{10,11... | collective-permute-start | bytes 12582920 | tf_op jit(solution)/shard_map/ppermute | solution.py:305
  1.2 13.1 %collective-permute-start.2 = (bf16[128,1024]{1,0:T(8,128)(2,1)}, bf16[128,1024]{1,0:T(8,128)(2,1)S(1)}, u32[]{:S(2)}, u32[]{:S(2)}) collective-permute-start(bf16[128,1024]{1,0:T(8,128)(2,1)} %bitcast.23), channel_id=1, source_target_pairs={{0,4},{2,6},{4,8},{6,10},{8,12},{10,14},{12,0},{14,2},{1,5},{3,7},... | collective-permute-start | bytes 786440 | tf_op jit(solution)/shard_map/ppermute | solution.py:311
  4.2 1.0 %copy-start.9 = (bf16[1,128,1024]{2,1,0:T(8,128)(2,1)S(1)}, bf16[1,128,1024]{2,1,0:T(8,128)(2,1)}, u32[]{:S(2)}) copy-start(bf16[1,128,1024]{2,1,0:T(8,128)(2,1)} %param.14) | copy-start | bytes 786436
  5.2 0.7 copy-start.10
  5.9 0.7 copy-start.12
  6.6 1.4 %collective-permute-start = (s32[1,8,128]{2,1,0:T(8,128)S(1)}, s32[1,8,128]{2,1,0:T(8,128)S(1)}, u32[]{:S(2)}, u32[]{:S(2)}) collective-permute-start(s32[1,8,128]{2,1,0:T(8,128)S(1)} %get-tuple-element.21.first_ref), channel_id=1, source_target_pairs={{0,1},{1,0},{2,3},{3,2},{4,5},{5,4},{6,7},{7,6},{8,9},{9,8},{10,11... | collective-permute-start | bytes 12296 | tf_op jit(solution)/shard_map/ppermute | solution.py:305
  7.9 6.4 %collective-permute-start.1 = (s32[2,8,128]{2,1,0:T(8,128)S(1)}, s32[2,8,128]{2,1,0:T(8,128)S(1)}, u32[]{:S(2)}, u32[]{:S(2)}) collective-permute-start(s32[2,8,128]{2,1,0:T(8,128)S(1)} %get-tuple-element.23.refs_0_.first_ref), channel_id=1, source_target_pairs={{0,2},{2,0},{4,6},{6,4},{8,10},{10,8},{12,14},{14,12},{1,3},{3,1},... | collective-permute-start | bytes 24584 | tf_op jit(solution)/shard_map/ppermute | solution.py:308
  14.3 2.0 %copy-start = (bf16[1024,2048]{1,0:T(8,128)(2,1)}, bf16[1024,2048]{1,0:T(8,128)(2,1)S(1)}, u32[]{:S(2)}) copy-start(bf16[1024,2048]{1,0:T(8,128)(2,1)S(1)} %get-tuple-element.24.refs_1_.w1a) | copy-start | bytes 12582916
  14.3 3.2 %copy-start.3 = (bf16[2048,1024]{1,0:T(8,128)(2,1)}, bf16[2048,1024]{1,0:T(8,128)(2,1)S(1)}, u32[]{:S(2)}) copy-start(bf16[2048,1024]{1,0:T(8,128)(2,1)S(1)} %get-tuple-element.25.refs_2_.w2a) | copy-start | bytes 12582916
  14.4 24.4 %copy-start.14 = (s32[16]{0:T(128)S(1)}, s32[16]{0:T(128)}, u32[]{:S(2)}) copy-start(s32[16]{0:T(128)} %capacity_ref.1) | copy-start | bytes 196
  14.4 26.8 %copy-start.8 = (bf16[1024,16]{0,1:T(8,128)(2,1)S(1)}, bf16[1024,16]{0,1:T(8,128)(2,1)}, u32[]{:S(2)}) copy-start(bf16[1024,16]{0,1:T(8,128)(2,1)} %param.15) | copy-start | bytes 98308
  17.6 10.1 %collective-permute-start.5 = (bf16[128,1024]{1,0:T(8,128)(2,1)S(1)}, bf16[128,1024]{1,0:T(8,128)(2,1)S(1)}, u32[]{:S(2)}, u32[]{:S(2)}) collective-permute-start(bf16[128,1024]{1,0:T(8,128)(2,1)S(1)} %get-tuple-element.27.refs_0_.xz_ref), channel_id=1, source_target_pairs={{0,4},{2,6},{4,8},{6,10},{8,12},{10,14},{12,0},{14,2},{1,5},{3,7},... | collective-permute-start | bytes 786440 | tf_op jit(solution)/shard_map/ppermute | solution.py:311
  19.2 9.2 %collective-permute-start.6 = (bf16[128,1024]{1,0:T(8,128)(2,1)S(1)}, bf16[128,1024]{1,0:T(8,128)(2,1)S(1)}, u32[]{:S(2)}, u32[]{:S(2)}) collective-permute-start(bf16[128,1024]{1,0:T(8,128)(2,1)S(1)} %get-tuple-element.28.xz_ref), channel_id=1, source_target_pairs={{0,2},{2,0},{4,6},{6,4},{8,10},{10,8},{12,14},{14,12},{1,3},{3,1},... | collective-permute-start | bytes 786440 | tf_op jit(solution)/shard_map/ppermute | solution.py:308
  19.7 8.0 %collective-permute-start.3 = (s32[4,8,128]{2,1,0:T(8,128)S(1)}, s32[4,8,128]{2,1,0:T(8,128)S(1)}, u32[]{:S(2)}, u32[]{:S(2)}) collective-permute-start(s32[4,8,128]{2,1,0:T(8,128)S(1)} %get-tuple-element.26.first_ref), channel_id=1, source_target_pairs={{0,4},{2,6},{4,0},{6,2},{8,12},{10,14},{12,8},{14,10},{1,5},{3,7},... | collective-permute-start | bytes 49160 | tf_op jit(solution)/shard_map/ppermute | solution.py:314
  27.7 12.2 %collective-permute-start.12 = (bf16[128,1024]{1,0:T(8,128)(2,1)S(1)}, bf16[128,1024]{1,0:T(8,128)(2,1)S(1)}, u32[]{:S(2)}, u32[]{:S(2)}) collective-permute-start(bf16[128,1024]{1,0:T(8,128)(2,1)S(1)} %collective-permute-done.5.refs_0_.xz_ref), channel_id=1, source_target_pairs={{0,4},{2,6},{4,8},{6,10},{8,12},{10,14},{12,0},{14,2},{1,5},{3,7},... | collective-permute-start | bytes 786440 | tf_op jit(solution)/shard_map/ppermute | solution.py:311
  27.7 13.5 %collective-permute-start.7 = (bf16[128,1024]{1,0:T(8,128)(2,1)S(1)}, bf16[128,1024]{1,0:T(8,128)(2,1)S(1)}, u32[]{:S(2)}, u32[]{:S(2)}) collective-permute-start(bf16[128,1024]{1,0:T(8,128)(2,1)S(1)} %get-tuple-element.27.refs_0_.xz_ref), channel_id=1, source_target_pairs={{0,2},{2,0},{4,6},{6,4},{8,10},{10,8},{12,14},{14,12},{1,3},{3,1},... | collective-permute-start | bytes 786440 | tf_op jit(solution)/shard_map/ppermute | solution.py:308
  28.4 9.6 %collective-permute-start.4 = (s32[8,8,128]{2,1,0:T(8,128)S(1)}, s32[8,8,128]{2,1,0:T(8,128)S(1)}, u32[]{:S(2)}, u32[]{:S(2)}) collective-permute-start(s32[8,8,128]{2,1,0:T(8,128)S(1)} %shard_map.126.low_ref), channel_id=1, source_target_pairs={{0,8},{2,10},{4,12},{6,14},{8,0},{10,2},{12,4},{14,6},{1,9},{3,11}... | collective-permute-start | bytes 98312 | tf_op jit(solution)/shard_map/ppermute | solution.py:314
  38.0 16.6 %collective-permute-start.11 = (bf16[128,1024]{1,0:T(8,128)(2,1)S(1)}, bf16[128,1024]{1,0:T(8,128)(2,1)S(1)}, u32[]{:S(2)}, u32[]{:S(2)}) collective-permute-start(bf16[128,1024]{1,0:T(8,128)(2,1)S(1)} %collective-permute-done.5.refs_0_.xz_ref), channel_id=1, source_target_pairs={{0,2},{2,0},{4,6},{6,4},{8,10},{10,8},{12,14},{14,12},{1,3},{3,1},... | collective-permute-start | bytes 786440 | tf_op jit(solution)/shard_map/ppermute | solution.py:308
  39.9 24.8 %collective-permute-start.15 = (bf16[128,1024]{1,0:T(8,128)(2,1)S(1)}, bf16[128,1024]{1,0:T(8,128)(2,1)S(1)}, u32[]{:S(2)}, u32[]{:S(2)}) collective-permute-start(bf16[128,1024]{1,0:T(8,128)(2,1)S(1)} %collective-permute-done.12.rest_1_.xz_ref), channel_id=1, source_target_pairs={{0,2},{2,0},{4,6},{6,4},{8,10},{10,8},{12,14},{14,12},{1,3},{3,1},... | collective-permute-start | bytes 786440 | tf_op jit(solution)/shard_map/ppermute | solution.py:308
  41.2 2.2 %copy-start.1 = (bf16[1024,2048]{1,0:T(8,128)(2,1)S(1)}, bf16[1024,2048]{1,0:T(8,128)(2,1)}, u32[]{:S(2)}) copy-start(bf16[1024,2048]{1,0:T(8,128)(2,1)} %copy-done) | copy-start | bytes 12582916
  43.4 2.2 %copy-start.4 = (bf16[2048,1024]{1,0:T(8,128)(2,1)S(1)}, bf16[2048,1024]{1,0:T(8,128)(2,1)}, u32[]{:S(2)}) copy-start(bf16[2048,1024]{1,0:T(8,128)(2,1)} %copy-done.3) | copy-start | bytes 12582916
  53.8 10.4 %collective-permute-start.10 = (bf16[128,1024]{1,0:T(8,128)(2,1)S(1)}, bf16[128,1024]{1,0:T(8,128)(2,1)S(1)}, u32[]{:S(2)}, u32[]{:S(2)}) collective-permute-start(bf16[128,1024]{1,0:T(8,128)(2,1)S(1)} %get-tuple-element.30), channel_id=1, source_target_pairs={{0,2},{2,0},{4,6},{6,4},{8,10},{10,8},{12,14},{14,12},{1,3},{3,1},... | collective-permute-start | bytes 786440 | tf_op jit(solution)/shard_map/ppermute | solution.py:308
  54.6 9.6 %copy-start.6 = (bf16[1,128,2048]{2,1,0:T(8,128)(2,1)S(1)}, bf16[1,128,2048]{2,1,0:T(8,128)(2,1)}, u32[]{:S(2)}) copy-start(bf16[1,128,2048]{2,1,0:T(8,128)(2,1)} %param.12) | copy-start | bytes 1572868
  54.6 9.6 %copy-start.7 = (bf16[1,128,2048]{2,1,0:T(8,128)(2,1)S(1)}, bf16[1,128,2048]{2,1,0:T(8,128)(2,1)}, u32[]{:S(2)}) copy-start(bf16[1,128,2048]{2,1,0:T(8,128)(2,1)} %param.13) | copy-start | bytes 1572868
  62.9 11.0 %collective-permute-start.17 = (bf16[128,1024]{1,0:T(8,128)(2,1)S(1)}, bf16[128,1024]{1,0:T(8,128)(2,1)S(1)}, u32[]{:S(2)}, u32[]{:S(2)}) collective-permute-start(bf16[128,1024]{1,0:T(8,128)(2,1)S(1)} %get-tuple-element.37), channel_id=1, source_target_pairs={{0,2},{2,0},{4,6},{6,4},{8,10},{10,8},{12,14},{14,12},{1,3},{3,1},... | collective-permute-start | bytes 786440 | tf_op jit(solution)/shard_map/ppermute | solution.py:308
  64.3 28.0 %collective-permute-start.19 = (bf16[128,1024]{1,0:T(8,128)(2,1)S(1)}, bf16[128,1024]{1,0:T(8,128)(2,1)S(1)}, u32[]{:S(2)}, u32[]{:S(2)}) collective-permute-start(bf16[128,1024]{1,0:T(8,128)(2,1)S(1)} %get-tuple-element.34.rest_1_), channel_id=1, source_target_pairs={{0,12},{2,14},{4,0},{6,2},{8,4},{10,6},{12,8},{14,10},{1,13},{3,15... | collective-permute-start | bytes 786440 | tf_op jit(solution)/shard_map/ppermute | solution.py:311
  64.6 10.7 %copy-start.2 = (bf16[1024,2048]{1,0:T(8,128)(2,1)S(1)}, bf16[1024,2048]{1,0:T(8,128)(2,1)}, u32[]{:S(2)}) copy-start(bf16[1024,2048]{1,0:T(8,128)(2,1)} %copy-done) | copy-start | bytes 12582916
  64.6 20.4 %collective-permute-start.13 = (bf16[128,2048]{1,0:T(8,128)(2,1)S(1)}, bf16[128,2048]{1,0:T(8,128)(2,1)S(1)}, u32[]{:S(2)}, u32[]{:S(2)}) collective-permute-start(bf16[128,2048]{1,0:T(8,128)(2,1)S(1)} %get-tuple-element.32.k_own), channel_id=1, source_target_pairs={{0,1},{1,0},{2,3},{3,2},{4,5},{5,4},{6,7},{7,6},{8,9},{9,8},{10,11... | collective-permute-start | bytes 1572872 | tf_op jit(solution)/shard_map/ppermute | solution.py:305
  73.0 10.6 %collective-permute-start.16 = (bf16[128,1024]{1,0:T(8,128)(2,1)S(1)}, bf16[128,1024]{1,0:T(8,128)(2,1)S(1)}, u32[]{:S(2)}, u32[]{:S(2)}) collective-permute-start(bf16[128,1024]{1,0:T(8,128)(2,1)S(1)} %get-tuple-element.36), channel_id=1, source_target_pairs={{0,2},{2,0},{4,6},{6,4},{8,10},{10,8},{12,14},{14,12},{1,3},{3,1},... | collective-permute-start | bytes 786440 | tf_op jit(solution)/shard_map/ppermute | solution.py:308
  73.9 18.4 %collective-permute-start.20 = (bf16[128,1024]{1,0:T(8,128)(2,1)S(1)}, bf16[128,1024]{1,0:T(8,128)(2,1)S(1)}, u32[]{:S(2)}, u32[]{:S(2)}) collective-permute-start(bf16[128,1024]{1,0:T(8,128)(2,1)S(1)} %shard_map.132.rest_1_), channel_id=1, source_target_pairs={{0,8},{2,10},{4,12},{6,14},{8,0},{10,2},{12,4},{14,6},{1,9},{3,11}... | collective-permute-start | bytes 786440 | tf_op jit(solution)/shard_map/ppermute | solution.py:311
  75.3 10.5 %copy-start.5 = (bf16[1,128,2048]{2,1,0:T(8,128)(2,1)S(1)}, bf16[1,128,2048]{2,1,0:T(8,128)(2,1)}, u32[]{:S(2)}) copy-start(bf16[1,128,2048]{2,1,0:T(8,128)(2,1)} %param.11) | copy-start | bytes 1572868
  75.3 10.5 %copy-start.11 = (s32[1,128]{1,0:T(1,128)S(1)}, s32[1,128]{1,0:T(1,128)}, u32[]{:S(2)}) copy-start(s32[1,128]{1,0:T(1,128)} %doc_own.3) | copy-start | bytes 1540
  75.3 10.5 %copy-start.13 = (s32[1,128]{1,0:T(1,128)S(1)}, s32[1,128]{1,0:T(1,128)}, u32[]{:S(2)}) copy-start(s32[1,128]{1,0:T(1,128)} %ahead_ref.3) | copy-start | bytes 1540
  75.3 10.5 %collective-permute-start.14 = (bf16[128,2048]{1,0:T(8,128)(2,1)S(1)}, bf16[128,2048]{1,0:T(8,128)(2,1)S(1)}, u32[]{:S(2)}, u32[]{:S(2)}) collective-permute-start(bf16[128,2048]{1,0:T(8,128)(2,1)S(1)} %get-tuple-element.33.v_own), channel_id=1, source_target_pairs={{0,1},{1,0},{2,3},{3,2},{4,5},{5,4},{6,7},{7,6},{8,9},{9,8},{10,11... | collective-permute-start | bytes 1572872 | tf_op jit(solution)/shard_map/ppermute | solution.py:305
  83.6 8.7 %collective-permute-start.18 = (bf16[128,1024]{1,0:T(8,128)(2,1)S(1)}, bf16[128,1024]{1,0:T(8,128)(2,1)S(1)}, u32[]{:S(2)}, u32[]{:S(2)}) collective-permute-start(bf16[128,1024]{1,0:T(8,128)(2,1)S(1)} %get-tuple-element.39), channel_id=1, source_target_pairs={{0,2},{2,0},{4,6},{6,4},{8,10},{10,8},{12,14},{14,12},{1,3},{3,1},... | collective-permute-start | bytes 786440 | tf_op jit(solution)/shard_map/ppermute | solution.py:308
  85.0 10.2 %collective-permute-start.21 = (bf16[128,1024]{1,0:T(8,128)(2,1)S(1)}, bf16[128,1024]{1,0:T(8,128)(2,1)S(1)}, u32[]{:S(2)}, u32[]{:S(2)}) collective-permute-start(bf16[128,1024]{1,0:T(8,128)(2,1)S(1)} %shard_map.134.rest_0_), channel_id=1, source_target_pairs={{0,4},{2,6},{4,8},{6,10},{8,12},{10,14},{12,0},{14,2},{1,5},{3,7},... | collective-permute-start | bytes 786440 | tf_op jit(solution)/shard_map/ppermute | solution.py:311

commit v5 on v4

--- a/solution.py
+++ b/solution.py
@@ -12,10 +12,9 @@
 LATENT = 1024
 TOPK = 6
 DENSE_EXPERTS = 16
-EXPERT_VMEM = 16 * 1024 * 1024
-ATTEND_VMEM = 10 * 1024 * 1024
+EXPERT_VMEM = 20 * 1024 * 1024
+ATTEND_VMEM = 8 * 1024 * 1024
 SMALL_VMEM = 4 * 1024 * 1024
-LOAD_VMEM = 44 * 1024 * 1024
 
 
 def run_expert(rows_in, w_first, w_second):
@@ -76,26 +75,35 @@
     )(place, q, k_own, k_far, v_own, v_far, doc_own, doc_far, ahead, *extra)
 
 
-def pack_kernel(latent_ref, named_ref, doc_ref, rows_ref, table_ref):
-    rows_ref[...] = latent_ref[...]
+def pack_kernel(named_any, doc_any, table_ref, named_ref, doc_ref, sems):
+    loads = [
+        pltpu.make_async_copy(named_any, named_ref, sems.at[0]),
+        pltpu.make_async_copy(doc_any, doc_ref, sems.at[1]),
+    ]
+    for load in loads:
+        load.start()
+    for load in loads:
+        load.wait()
     for k in range(TOPK):
         table_ref[0, k : k + 1, :] = named_ref[k]
     table_ref[0, TOPK : TOPK + 1, :] = doc_ref[...]
     table_ref[0, TOPK + 1 :, :] = doc_ref[...]
 
 
-def pack(latent, named, doc):
-    vmem = pl.BlockSpec(memory_space=pltpu.VMEM)
+def pack(named, doc):
+    anywhere = pl.BlockSpec(memory_space=pl.ANY)
     return pl.pallas_call(
         pack_kernel,
-        out_shape=(
-            jax.ShapeDtypeStruct(latent.shape, latent.dtype),
-            jax.ShapeDtypeStruct((1, 8, latent.shape[0]), jnp.int32),
-        ),
-        in_specs=[vmem] * 3,
-        out_specs=(vmem, vmem),
+        out_shape=jax.ShapeDtypeStruct((1, 8, doc.shape[1]), jnp.int32),
+        in_specs=[anywhere] * 2,
+        out_specs=pl.BlockSpec(memory_space=pltpu.VMEM),
+        scratch_shapes=[
+            pltpu.VMEM(named.shape, jnp.int32),
+            pltpu.VMEM(doc.shape, jnp.int32),
+            pltpu.SemaphoreType.DMA((2,)),
+        ],
         compiler_params=pltpu.CompilerParams(vmem_limit_bytes=SMALL_VMEM),
-    )(latent, named, doc)
+    )(named, doc)
 
 
 def join_kernel(first_ref, second_ref, *refs):
@@ -120,32 +128,36 @@
     return out if through else out[0]
 
 
-def load_kernel(w1_any, w2_any, *refs):
-    w1_ref, w2_ref, sems = refs[-3:]
-    loads = [
-        pltpu.make_async_copy(w1_any, w1_ref, sems.at[0]),
-        pltpu.make_async_copy(w2_any, w2_ref, sems.at[1]),
-    ]
-    for load in loads:
-        load.start()
-    for load in loads:
-        load.wait()
-
-
-def load_weights(w_first, w_second, after):
-    anywhere = pl.BlockSpec(memory_space=pl.ANY)
+def hold_kernel(*refs):
+    refs[-1][...] = jnp.zeros_like(refs[-1])
+
+
+def hold(resident, after):
     vmem = pl.BlockSpec(memory_space=pltpu.VMEM)
+    anywhere = pl.BlockSpec(memory_space=pl.ANY)
     return pl.pallas_call(
-        load_kernel,
-        out_shape=(
-            pltpu.VMEM(w_first.shape, w_first.dtype),
-            pltpu.VMEM(w_second.shape, w_second.dtype),
-        ),
-        in_specs=[anywhere] * (2 + len(after)),
-        out_specs=(vmem, vmem),
-        scratch_shapes=[pltpu.SemaphoreType.DMA((2,))],
-        compiler_params=pltpu.CompilerParams(vmem_limit_bytes=LOAD_VMEM),
-    )(w_first, w_second, *after)
+        hold_kernel,
+        out_shape=jax.ShapeDtypeStruct((8, 128), jnp.int32),
+        in_specs=[vmem] * len(resident) + [anywhere] * len(after),
+        out_specs=vmem,
+        compiler_params=pltpu.CompilerParams(vmem_limit_bytes=EXPERT_VMEM),
+    )(*resident, *after)
+
+
+def behind_kernel(*refs):
+    pass
+
+
+def behind(x, after):
+    anywhere = pl.BlockSpec(memory_space=pl.ANY)
+    return pl.pallas_call(
+        behind_kernel,
+        out_shape=jax.ShapeDtypeStruct(x.shape, x.dtype),
+        in_specs=[anywhere] * (1 + len(after)),
+        out_specs=anywhere,
+        input_output_aliases={0: 0},
+        compiler_params=pltpu.CompilerParams(vmem_limit_bytes=SMALL_VMEM),
+    )(x, *after)
 
 
 def kept_kernel(own_ref, capacity_ref, low_ref, high_ref, *refs):
@@ -220,32 +232,47 @@
     return square.T
 
 
-def expert_kernel(place, own_ref, kept_ref, router_ref, xz_ref, xy_ref, w1a, w2a, w1b, w2b, *rest):
-    z_ref, y_ref, hidden_ref = rest[-3:]
+def expert_kernel(
+    place, own_ref, kept_ref, router_ref, xz_ref, xy_ref, w1a, w2a, w1b_any, w2b_any, *rest
+):
+    z_ref, y_ref, hidden_ref, mixed_ref, w1b, w2b, sems = rest[-7:]
+    loads = [
+        pltpu.make_async_copy(w1b_any, w1b, sems.at[0]),
+        pltpu.make_async_copy(w2b_any, w2b, sems.at[1]),
+    ]
+    for load in loads:
+        load.start()
     own = own_ref[0]
     rows = xz_ref.shape[0]
     x = jnp.concatenate([xz_ref[...], xy_ref[...]], axis=0)
     step = 512
-    for which, w1_ref in enumerate((w1a, w1b)):
+
+    def enter(w1_ref):
         for first in range(0, w1_ref.shape[1], step):
             cols = slice(first, first + step)
             hidden = jnp.dot(x, w1_ref[:, cols], preferred_element_type=jnp.float32)
             hidden = jnp.maximum(hidden, 0.0)
-            hidden_ref[which, :, cols] = (hidden * hidden).astype(jnp.bfloat16)
+            hidden_ref[:, cols] = (hidden * hidden).astype(jnp.bfloat16)
+
+    enter(w1a)
     gates = [
         gate_columns(own, router_ref, x_ref[...], kept_ref[2 * place + side])
         for side, x_ref in enumerate((xz_ref, xy_ref))
     ]
+    gates = [jnp.concatenate([g[:, which : which + 1] for g in gates], axis=0) for which in range(2)]
     for first in range(0, w2a.shape[1], step):
         cols = slice(first, first + step)
-        results = [
-            jnp.dot(hidden_ref[which], w2_ref[:, cols], preferred_element_type=jnp.float32)
-            for which, w2_ref in enumerate((w2a, w2b))
-        ]
-        for side, out_ref in enumerate((z_ref, y_ref)):
-            part = slice(side * rows, (side + 1) * rows)
-            mixed = results[0][part] * gates[side][:, 0:1] + results[1][part] * gates[side][:, 1:2]
-            out_ref[:, cols] = mixed.astype(jnp.bfloat16)
+        result = jnp.dot(hidden_ref[...], w2a[:, cols], preferred_element_type=jnp.float32)
+        mixed_ref[:, cols] = result * gates[0]
+    loads[0].wait()
+    enter(w1b)
+    loads[1].wait()
+    for first in range(0, w2b.shape[1], step):
+        cols = slice(first, first + step)
+        result = jnp.dot(hidden_ref[...], w2b[:, cols], preferred_element_type=jnp.float32)
+        mixed = (mixed_ref[:, cols] + result * gates[1]).astype(jnp.bfloat16)
+        z_ref[:, cols] = mixed[:rows]
+        y_ref[:, cols] = mixed[rows:]
 
 
 def run_piece(place, own, kept, router, from_line, from_side, weights, after):
@@ -255,13 +282,18 @@
     vmem = pl.BlockSpec(memory_space=pltpu.VMEM)
     anywhere = pl.BlockSpec(memory_space=pl.ANY)
     piece = jax.ShapeDtypeStruct((rows, width), jnp.bfloat16)
-    weights = [pltpu.with_memory_space_constraint(w, pltpu.VMEM) for w in weights]
     return pl.pallas_call(
         functools.partial(expert_kernel, place),
         out_shape=(piece, piece),
-        in_specs=[smem] + [vmem] * 8 + [anywhere] * len(after),
+        in_specs=[smem] + [vmem] * 6 + [anywhere] * (2 + len(after)),
         out_specs=(vmem, vmem),
-        scratch_shapes=[pltpu.VMEM((2, 2 * rows, hidden), jnp.bfloat16)],
+        scratch_shapes=[
+            pltpu.VMEM((2 * rows, hidden), jnp.bfloat16),
+            pltpu.VMEM((2 * rows, width), jnp.float32),
+            pltpu.VMEM(weights[2].shape, jnp.bfloat16),
+            pltpu.VMEM(weights[3].shape, jnp.bfloat16),
+            pltpu.SemaphoreType.DMA((2,)),
+        ],
         compiler_params=pltpu.CompilerParams(vmem_limit_bytes=EXPERT_VMEM),
         cost_estimate=pl.CostEstimate(
             flops=16 * rows * width * hidden,
@@ -314,26 +346,25 @@
         return lax.ppermute(x, "expert", [(2 * z + y, 2 * (z ^ span) + y) for z, y in spots])
 
     own = lax.axis_index(("expert", "context")).astype(jnp.int32).reshape(1)
-    w_first, w_second = expert_in[0], expert_out[0]
-    far_weights = (swap_core(w_first), swap_core(w_second))
-
-    rows, tile = pack(latent[0], routes.transpose(2, 0, 1), segments)
-    arriving = along(latent[0], 1)
+    own_weights = (expert_in[0], expert_out[0])
+    weights = own_weights + (swap_core(own_weights[0]), swap_core(own_weights[1]))
+
+    arriving, beside_own = along(latent[0], 1), swap_side(latent[0])
+    tile = pack(routes.transpose(2, 0, 1), segments)
     beside = swap_core(tile)
     doc_far = beside[0, TOPK : TOPK + 1, :]
-    rows, table = join(tile, beside, passed=rows)
-    from_line = [rows, arriving]
-    from_side = [swap_side(rows)]
-    weights = tuple(load_weights(w_first, w_second, (table,))) + far_weights
-    from_line[1], table = join(table, swap_side(table), passed=arriving, after=weights[:2])
-    for step in range(2, line):
+    table = join(tile, beside)
+    arriving, table = join(table, swap_side(table), passed=arriving, after=(beside_own,))
+    flip = flipped(table, 1)
+    from_line = [latent[0], arriving, along(arriving, 1)]
+    from_side = [beside_own, swap_side(arriving)]
+    table = join(table, flip, after=(hold(own_weights, (table,)),))
+    flip = flipped(table, 2)
+    from_line[2] = behind(from_line[2], (table,))
+    for step in range(3, line):
         from_line.append(along(from_line[-1], 1))
-    from_side += [swap_side(x) for x in from_line[1:]]
-    span = 1
-    while 2 * span < line:
-        table = join(table, flipped(table, span), after=(from_line[1],))
-        span *= 2
-    kept = kept_rows(own, capacity, table, flipped(table, span), (from_line[2], from_side[0]))
+    from_side += [swap_side(x) for x in from_line[2:]]
+    kept = kept_rows(own, capacity, table, flip, (from_line[2], from_side[1]))
 
     def piece(step, *after):
         return run_piece(step, own, kept, router.T, from_line[step], from_side[step], weights, after)

time: 96.4 us -> 90.9 us (0.943)
  waiting for transfers between devices: 21.5 us -> 30.5 us
  Pallas kernels: 41 us -> 32.9 us
  starting transfers between devices: 21.9 us -> 15.3 us
    ppermute x5, waiting for transfers between devices: 1.3 us -> 6.75 us  [swap_core(): return lax.ppermute(x, 'context', sibling)]
    pallas_call x4, Pallas kernels: 33 us -> 28.4 us  [run_piece(): pl.pallas_call(functools.partial(expert_kernel, place), out_shape=(piece,...]
    ppermute x6, waiting for transfers between devices: 9.36 us -> 5.19 us  [along(): lax.ppermute(x, 'expert', [(2 * z + y, 2 * ((z + step) % line) + y) for z...]
    ppermute x2, waiting for transfers between devices: 7.47 us -> 11.5 us  [flipped(): lax.ppermute(x, 'expert', [(2 * z + y, 2 * (z ^ span) + y) for z, y in sp...]
    ppermute x9, waiting for transfers between devices: 3.36 us -> 7.03 us  [swap_side(): return lax.ppermute(x, 'expert', across)]
    pallas_call x2 -> x3, Pallas kernels: 3.5 us -> 0.03 us  [the longest x1 0.03 us: pack(): pl.pallas_call(pack_kernel, out_shape=jax.ShapeDtypeStruct((1, 8, doc.sha...]
    ppermute x6, starting transfers between devices: 7 us -> 3.9 us  [along(): lax.ppermute(x, 'expert', [(2 * z + y, 2 * ((z + step) % line) + y) for z...]
    ppermute x2, starting transfers between devices: 3.71 us -> 0.95 us  [flipped(): lax.ppermute(x, 'expert', [(2 * z + y, 2 * (z ^ span) + y) for z, y in sp...]
  transfers between devices with their start and end apart: 22 -> 22, of which waited for: 5 -> 7; matrix products, arithmetic and copies ran while one was open for 0% -> 0% of each run, Pallas kernels for 43% -> 36%
where the time goes in v5:
time: 90.9 us; the launch traced here: 90.6 us
  Pallas kernels  32.9 us (36%)
  waiting for transfers between devices  30.5 us (34%)
  starting transfers between devices  15.3 us (17%)
  local copies, waits for them, and re-layouts  10.1 us (11%)
  other arithmetic  0.92 us (1%)
    pallas_call x4, Pallas kernels, run_piece(): pl.pallas_call(functools.partial(expert_kernel, place), out_shape=(piece,...  28.4 us
    ppermute x2, waiting for transfers between devices, flipped(): lax.ppermute(x, 'expert', [(2 * z + y, 2 * (z ^ span) + y) for z, y in sp...  11.5 us
    unnamed x32, local copies, waits for them, and re-layouts  10.1 us
    ppermute x9, starting transfers between devices, swap_side(): return lax.ppermute(x, 'expert', across)  9.77 us
    ppermute x9, waiting for transfers between devices, swap_side(): return lax.ppermute(x, 'expert', across)  7.03 us
    ppermute x5, waiting for transfers between devices, swap_core(): return lax.ppermute(x, 'context', sibling)  6.75 us
    ppermute x6, waiting for transfers between devices, along(): lax.ppermute(x, 'expert', [(2 * z + y, 2 * ((z + step) % line) + y) for z...  5.19 us
    ppermute x6, starting transfers between devices, along(): lax.ppermute(x, 'expert', [(2 * z + y, 2 * ((z + step) % line) + y) for z...  3.9 us
  transfers between devices with their start and end apart: 22, of which 7 were waited for; matrix products, arithmetic and copies ran while one was open for 0% of the time, Pallas kernels for 36%

profile of v5, /device:TPU:0, one launch (start us, length us, event | category | flops | bytes accessed | tf_op | source)
XLA Modules:
  0.0 90.6 jit_solution(5563398173759378571)
XLA Ops:
  0.6 0.5 collective-permute-start.8
  1.1 0.1 collective-permute-start.9
  1.2 2.9 %collective-permute-start.3 = (bf16[128,1024]{1,0:T(8,128)(2,1)}, bf16[128,1024]{1,0:T(8,128)(2,1)S(1)}, u32[]{:S(2)}, u32[]{:S(2)}) collective-permute-start(bf16[128,1024]{1,0:T(8,128)(2,1)} %bitcast.35), channel_id=1, source_target_pairs={{0,2},{2,0},{4,6},{6,4},{8,10},{10,8},{12,14},{14,12},{1,3},{3,1},... | collective-permute-start | bytes 786440 | tf_op jit(solution)/shard_map/ppermute | solution.py:340
  4.2 1.6 %collective-permute-start.2 = (bf16[128,1024]{1,0:T(8,128)(2,1)}, bf16[128,1024]{1,0:T(8,128)(2,1)S(1)}, u32[]{:S(2)}, u32[]{:S(2)}) collective-permute-start(bf16[128,1024]{1,0:T(8,128)(2,1)} %bitcast.36), channel_id=1, source_target_pairs={{0,4},{2,6},{4,8},{6,10},{8,12},{10,14},{12,0},{14,2},{1,5},{3,7},... | collective-permute-start | bytes 786440 | tf_op jit(solution)/shard_map/ppermute | solution.py:343
  5.8 0.7 copy-done.11
  6.4 0.7 copy-done.13
  7.1 0.1 collective-permute-start
  7.2 6.7 %collective-permute-done.second_ref = s32[1,8,128]{2,1,0:T(8,128)S(1)} collective-permute-done((s32[1,8,128]{2,1,0:T(8,128)S(1)}, s32[1,8,128]{2,1,0:T(8,128)S(1)}, u32[]{:S(2)}, u32[]{:S(2)}) %collective-permute-start) | collective-permute-done | bytes 4128 | tf_op jit(solution)/shard_map/ppermute | solution.py:337
  13.9 0.0 collective-permute-start.1
  13.9 3.7 %collective-permute-done.1.second_ref = s32[2,8,128]{2,1,0:T(8,128)S(1)} collective-permute-done((s32[2,8,128]{2,1,0:T(8,128)S(1)}, s32[2,8,128]{2,1,0:T(8,128)S(1)}, u32[]{:S(2)}, u32[]{:S(2)}) %collective-permute-start.1) | collective-permute-done | bytes 8224 | tf_op jit(solution)/shard_map/ppermute | solution.py:340
  17.6 0.0 collective-permute-done.3.refs_1_.xy_ref
  17.6 0.0 collective-permute-done.2.refs_0_
  17.6 0.1 collective-permute-start.6
  17.7 0.1 collective-permute-start.4
  17.8 0.0 copy-start
  17.8 2.2 %copy-done = bf16[1,1024,2048]{2,1,0:T(8,128)(2,1)S(1)} copy-done((bf16[1,1024,2048]{2,1,0:T(8,128)(2,1)S(1)}, bf16[1,1024,2048]{2,1,0:T(8,128)(2,1)}, u32[]{:S(2)}) %copy-start) | copy-done | bytes 4194328
  20.0 2.2 %copy-done.3 = bf16[1,2048,1024]{2,1,0:T(8,128)(2,1)S(1)} copy-done((bf16[1,2048,1024]{2,1,0:T(8,128)(2,1)S(1)}, bf16[1,2048,1024]{2,1,0:T(8,128)(2,1)}, u32[]{:S(2)}) %copy-start.3) | copy-done | bytes 4194328
  22.2 0.0 collective-permute-start.7
  22.2 3.2 %collective-permute-done.4.second_ref = s32[4,8,128]{2,1,0:T(8,128)S(1)} collective-permute-done((s32[4,8,128]{2,1,0:T(8,128)S(1)}, s32[4,8,128]{2,1,0:T(8,128)S(1)}, u32[]{:S(2)}, u32[]{:S(2)}) %collective-permute-start.4) | collective-permute-done | bytes 16416 | tf_op jit(solution)/shard_map/ppermute | solution.py:346
  25.4 1.7 %collective-permute-done.6.refs_0_ = bf16[128,1024]{1,0:T(8,128)(2,1)S(1)} collective-permute-done((bf16[128,1024]{1,0:T(8,128)(2,1)S(1)}, bf16[128,1024]{1,0:T(8,128)(2,1)S(1)}, u32[]{:S(2)}, u32[]{:S(2)}) %collective-permute-start.6) | collective-permute-done | bytes 262176 | tf_op jit(solution)/shard_map/ppermute | solution.py:343
  27.1 0.0 collective-permute-start.12
  27.1 0.9 collective-permute-start.5
  27.9 8.3 %collective-permute-done.5.high_ref = s32[8,8,128]{2,1,0:T(8,128)S(1)} collective-permute-done((s32[8,8,128]{2,1,0:T(8,128)S(1)}, s32[8,8,128]{2,1,0:T(8,128)S(1)}, u32[]{:S(2)}, u32[]{:S(2)}) %collective-permute-start.5) | collective-permute-done | bytes 32800 | tf_op jit(solution)/shard_map/ppermute | solution.py:346
  36.2 0.6 collective-permute-start.11
  36.8 0.0 collective-permute-done.7.refs_1_.xy_ref
  36.8 1.1 %shard_map.128.kept_ref = s32[8,8,128]{2,1,0:T(8,128)S(1)} custom-call(s32[1]{0:T(128)} %bitcast.2.own_ref, s32[16]{0:T(128)S(1)} %copy-done.15, s32[8,8,128]{2,1,0:T(8,128)S(1)} %shard_map.126.refs_1_.low_ref, s32[8,8,128]{2,1,0:T(8,128)S(1)} %collective-permute-done.5.high_ref, bf16[128,1024]{1,0:T(8,128)(2,1)S(1)} %shard_map.127.refs_0_.xz_ref, ...), custom_call_target="tpu_custom_call" | custom-call | tf_op jit(solution)/shard_map/pallas_call | solution.py:208
  37.9 0.0 collective-permute-done.12.rest_1_.xz_ref
  37.9 1.5 %collective-permute-start.15 = (bf16[128,1024]{1,0:T(8,128)(2,1)S(1)}, bf16[128,1024]{1,0:T(8,128)(2,1)S(1)}, u32[]{:S(2)}, u32[]{:S(2)}) collective-permute-start(bf16[128,1024]{1,0:T(8,128)(2,1)S(1)} %collective-permute-done.12.rest_1_.xz_ref), channel_id=1, source_target_pairs={{0,2},{2,0},{4,6},{6,4},{8,10},{10,8},{12,14},{14,12},{1,3},{3,1},... | collective-permute-start | bytes 786440 | tf_op jit(solution)/shard_map/ppermute | solution.py:340
  39.5 0.0 collective-permute-done.8.w1b_any
  39.5 0.0 collective-permute-done.9.w2b_any
  39.5 0.0 copy-start.1
  39.5 2.2 %copy-done.1 = bf16[1,1024,2048]{2,1,0:T(8,128)(2,1)S(1)} copy-done((bf16[1,1024,2048]{2,1,0:T(8,128)(2,1)S(1)}, bf16[1,1024,2048]{2,1,0:T(8,128)(2,1)}, u32[]{:S(2)}) %copy-start.1) | copy-done | bytes 4194328
  41.7 2.2 %copy-done.4 = bf16[1,2048,1024]{2,1,0:T(8,128)(2,1)S(1)} copy-done((bf16[1,2048,1024]{2,1,0:T(8,128)(2,1)S(1)}, bf16[1,2048,1024]{2,1,0:T(8,128)(2,1)}, u32[]{:S(2)}) %copy-start.4) | copy-done | bytes 4194328
  43.9 7.2 %shard_map.129 = (bf16[128,1024]{1,0:T(8,128)(2,1)S(1)}, bf16[128,1024]{1,0:T(8,128)(2,1)S(1)}) custom-call(s32[1]{0:T(128)} %bitcast.2.own_ref, s32[8,8,128]{2,1,0:T(8,128)S(1)} %shard_map.128.kept_ref, bf16[16,1024]{1,0:T(8,128)(2,1)S(1)} %bitcast.31, bf16[128,1024]{1,0:T(8,128)(2,1)S(1)} %get-tuple-element.16.xz_ref, ...), custom_call_target="tpu_custom_call" | custom-call | flops 4294967296 | bytes 1048576 | tf_op jit(solution)/shard_map/pallas_call | solution.py:285
  51.0 0.7 collective-permute-start.10
  51.7 0.0 collective-permute-done.11.xy_ref
  51.7 0.0 copy-start.7
  51.7 0.0 copy-start.8
  51.7 7.1 %shard_map.130 = (bf16[128,1024]{1,0:T(8,128)(2,1)S(1)}, bf16[128,1024]{1,0:T(8,128)(2,1)S(1)}) custom-call(s32[1]{0:T(128)} %bitcast.2.own_ref, s32[8,8,128]{2,1,0:T(8,128)S(1)} %shard_map.128.kept_ref, bf16[16,1024]{1,0:T(8,128)(2,1)S(1)} %bitcast.32, bf16[128,1024]{1,0:T(8,128)(2,1)S(1)} %shard_map.127.refs_0_.xz_ref, ...), custom_call_target="tpu_custom_call" | custom-call | flops 4294967296 | bytes 1048576 | tf_op jit(solution)/shard_map/pallas_call | solution.py:285
  58.8 1.5 %collective-permute-start.17 = (bf16[128,1024]{1,0:T(8,128)(2,1)S(1)}, bf16[128,1024]{1,0:T(8,128)(2,1)S(1)}, u32[]{:S(2)}, u32[]{:S(2)}) collective-permute-start(bf16[128,1024]{1,0:T(8,128)(2,1)S(1)} %get-tuple-element.25), channel_id=1, source_target_pairs={{0,2},{2,0},{4,6},{6,4},{8,10},{10,8},{12,14},{14,12},{1,3},{3,1},... | collective-permute-start | bytes 786440 | tf_op jit(solution)/shard_map/ppermute | solution.py:340
  60.3 0.0 collective-permute-done.10.second_ref
  60.3 0.1 shard_map.131
  60.4 0.4 collective-permute-start.19
  60.8 0.0 collective-permute-start.13
  60.9 0.0 collective-permute-done.15.xy_ref
  60.9 7.1 %shard_map.132 = (bf16[128,1024]{1,0:T(8,128)(2,1)S(1)}, bf16[128,1024]{1,0:T(8,128)(2,1)S(1)}) custom-call(s32[1]{0:T(128)} %bitcast.2.own_ref, s32[8,8,128]{2,1,0:T(8,128)S(1)} %shard_map.128.kept_ref, bf16[16,1024]{1,0:T(8,128)(2,1)S(1)} %bitcast.33, bf16[128,1024]{1,0:T(8,128)(2,1)S(1)} %collective-permute-done.12.rest_1_.xz_ref, ...), custom_call_target="tpu_custom_call" | custom-call | flops 4294967296 | bytes 1048576 | tf_op jit(solution)/shard_map/pallas_call | solution.py:285
  67.9 1.1 %collective-permute-start.16 = (bf16[128,1024]{1,0:T(8,128)(2,1)S(1)}, bf16[128,1024]{1,0:T(8,128)(2,1)S(1)}, u32[]{:S(2)}, u32[]{:S(2)}) collective-permute-start(bf16[128,1024]{1,0:T(8,128)(2,1)S(1)} %get-tuple-element.24), channel_id=1, source_target_pairs={{0,2},{2,0},{4,6},{6,4},{8,10},{10,8},{12,14},{14,12},{1,3},{3,1},... | collective-permute-start | bytes 786440 | tf_op jit(solution)/shard_map/ppermute | solution.py:340
  69.0 0.0 collective-permute-done.17.second_ref
  69.0 0.1 shard_map.133.rest_1_
  69.1 1.2 %collective-permute-start.20 = (bf16[128,1024]{1,0:T(8,128)(2,1)S(1)}, bf16[128,1024]{1,0:T(8,128)(2,1)S(1)}, u32[]{:S(2)}, u32[]{:S(2)}) collective-permute-start(bf16[128,1024]{1,0:T(8,128)(2,1)S(1)} %shard_map.133.rest_1_), channel_id=1, source_target_pairs={{0,8},{2,10},{4,12},{6,14},{8,0},{10,2},{12,4},{14,6},{1,9},{3,11}... | collective-permute-start | bytes 786440 | tf_op jit(solution)/shard_map/ppermute | solution.py:343
  70.3 0.0 collective-permute-start.14
  70.3 7.1 %shard_map.134 = (bf16[128,1024]{1,0:T(8,128)(2,1)S(1)}, bf16[128,1024]{1,0:T(8,128)(2,1)S(1)}) custom-call(s32[1]{0:T(128)} %bitcast.2.own_ref, s32[8,8,128]{2,1,0:T(8,128)S(1)} %shard_map.128.kept_ref, bf16[16,1024]{1,0:T(8,128)(2,1)S(1)} %bitcast.34, bf16[128,1024]{1,0:T(8,128)(2,1)S(1)} %bitcast.37, ...), custom_call_target="tpu_custom_call" | custom-call | flops 4294967296 | bytes 1048576 | tf_op jit(solution)/shard_map/pallas_call | solution.py:285
  77.4 0.0 collective-permute-done.16.second_ref
  77.4 1.5 %collective-permute-start.18 = (bf16[128,1024]{1,0:T(8,128)(2,1)S(1)}, bf16[128,1024]{1,0:T(8,128)(2,1)S(1)}, u32[]{:S(2)}, u32[]{:S(2)}) collective-permute-start(bf16[128,1024]{1,0:T(8,128)(2,1)S(1)} %get-tuple-element.27), channel_id=1, source_target_pairs={{0,2},{2,0},{4,6},{6,4},{8,10},{10,8},{12,14},{14,12},{1,3},{3,1},... | collective-permute-start | bytes 786440 | tf_op jit(solution)/shard_map/ppermute | solution.py:340
  78.9 0.1 shard_map.135.rest_0_
  79.0 0.0 collective-permute-done.13.k_far
  79.0 0.6 collective-permute-start.21
  79.6 0.0 collective-permute-done.14.v_far
  79.6 1.6 %shard_map.136.rest_0_ = bf16[128,2048]{1,0:T(8,128)(2,1)} custom-call(s32[1]{0:T(128)} %bitcast.place_ref, bf16[128,2048]{1,0:T(8,128)(2,1)S(1)} %bitcast.27, bf16[128,2048]{1,0:T(8,128)(2,1)S(1)} %get-tuple-element.20.k_own, bf16[128,2048]{1,0:T(8,128)(2,1)S(1)} %collective-permute-done.13.k_far, bf16[128,2048]{1,0:T(8,128)(2,1)S(1)} %get-tuple-element.21.v_own, ...), custom_call_target="tpu_custom_call" | custom-call | flops 134217728 | bytes 1572864 | tf_op jit(solution)/shard_map/pallas_call | solution.py:64
  81.2 1.6 %shard_map.137 = bf16[128,2048]{1,0:T(8,128)(2,1)} custom-call(s32[1]{0:T(128)} %bitcast.place_ref, bf16[128,2048]{1,0:T(8,128)(2,1)S(1)} %bitcast.28, bf16[128,2048]{1,0:T(8,128)(2,1)S(1)} %get-tuple-element.20.k_own, bf16[128,2048]{1,0:T(8,128)(2,1)S(1)} %collective-permute-done.13.k_far, ...), custom_call_target="tpu_custom_call", output_to_operand_aliasing={{}: (9, {})} | custom-call | flops 134217728 | bytes 1572864 | tf_op jit(solution)/shard_map/pallas_call | solution.py:64
  82.8 3.3 %collective-permute-done.18 = bf16[128,1024]{1,0:T(8,128)(2,1)S(1)} collective-permute-done((bf16[128,1024]{1,0:T(8,128)(2,1)S(1)}, bf16[128,1024]{1,0:T(8,128)(2,1)S(1)}, u32[]{:S(2)}, u32[]{:S(2)}) %collective-permute-start.18) | collective-permute-done | bytes 262176 | tf_op jit(solution)/shard_map/ppermute | solution.py:340
  86.2 3.5 %collective-permute-done.20 = bf16[128,1024]{1,0:T(8,128)(2,1)S(1)} collective-permute-done((bf16[128,1024]{1,0:T(8,128)(2,1)S(1)}, bf16[128,1024]{1,0:T(8,128)(2,1)S(1)}, u32[]{:S(2)}, u32[]{:S(2)}) %collective-permute-start.20) | collective-permute-done | bytes 262176 | tf_op jit(solution)/shard_map/ppermute | solution.py:343
  89.7 0.0 collective-permute-done.21
  89.7 0.9 %fusion = bf16[1,128,1024]{2,1,0:T(8,128)(2,1)} fusion(bf16[128,1024]{1,0:T(8,128)(2,1)S(1)} %collective-permute-done.21, bf16[128,1024]{1,0:T(8,128)(2,1)S(1)} %collective-permute-done.20, bf16[128,1024]{1,0:T(8,128)(2,1)S(1)} %collective-permute-done.19, bf16[128,1024]{1,0:T(8,128)(2,1)S(1)} %collective-permute-done.18, ...), kind=kLoop, calls=%fused_computation.1 | loop fusion | flops 1310720 | bytes 1572864 | tf_op jit(solution)/shard_map/broadcast_in_dim | solution.py:392
  (30 shorter events, 0.1 us)
Async XLA Ops:
  0.6 38.8 %collective-permute-start.8 = (bf16[1024,2048]{1,0:T(8,128)(2,1)}, bf16[1024,2048]{1,0:T(8,128)(2,1)}, u32[]{:S(2)}, u32[]{:S(2)}) collective-permute-start(bf16[1024,2048]{1,0:T(8,128)(2,1)} %bitcast.15), channel_id=1, source_target_pairs={{0,1},{1,0},{2,3},{3,2},{4,5},{5,4},{6,7},{7,6},{8,9},{9,8},{10,11... | collective-permute-start | bytes 12582920 | tf_op jit(solution)/shard_map/ppermute | solution.py:337
  1.1 38.3 %collective-permute-start.9 = (bf16[2048,1024]{1,0:T(8,128)(2,1)}, bf16[2048,1024]{1,0:T(8,128)(2,1)}, u32[]{:S(2)}, u32[]{:S(2)}) collective-permute-start(bf16[2048,1024]{1,0:T(8,128)(2,1)} %bitcast.21), channel_id=1, source_target_pairs={{0,1},{1,0},{2,3},{3,2},{4,5},{5,4},{6,7},{7,6},{8,9},{9,8},{10,11... | collective-permute-start | bytes 12582920 | tf_op jit(solution)/shard_map/ppermute | solution.py:337
  1.2 16.4 %collective-permute-start.3 = (bf16[128,1024]{1,0:T(8,128)(2,1)}, bf16[128,1024]{1,0:T(8,128)(2,1)S(1)}, u32[]{:S(2)}, u32[]{:S(2)}) collective-permute-start(bf16[128,1024]{1,0:T(8,128)(2,1)} %bitcast.35), channel_id=1, source_target_pairs={{0,2},{2,0},{4,6},{6,4},{8,10},{10,8},{12,14},{14,12},{1,3},{3,1},... | collective-permute-start | bytes 786440 | tf_op jit(solution)/shard_map/ppermute | solution.py:340
  4.2 13.4 %collective-permute-start.2 = (bf16[128,1024]{1,0:T(8,128)(2,1)}, bf16[128,1024]{1,0:T(8,128)(2,1)S(1)}, u32[]{:S(2)}, u32[]{:S(2)}) collective-permute-start(bf16[128,1024]{1,0:T(8,128)(2,1)} %bitcast.36), channel_id=1, source_target_pairs={{0,4},{2,6},{4,8},{6,10},{8,12},{10,14},{12,0},{14,2},{1,5},{3,7},... | collective-permute-start | bytes 786440 | tf_op jit(solution)/shard_map/ppermute | solution.py:343
  5.7 0.7 copy-start.11
  6.4 0.7 copy-start.13
  7.1 6.8 %collective-permute-start = (s32[1,8,128]{2,1,0:T(8,128)S(1)}, s32[1,8,128]{2,1,0:T(8,128)S(1)}, u32[]{:S(2)}, u32[]{:S(2)}) collective-permute-start(s32[1,8,128]{2,1,0:T(8,128)S(1)} %shard_map.122.first_ref), channel_id=1, source_target_pairs={{0,1},{1,0},{2,3},{3,2},{4,5},{5,4},{6,7},{7,6},{8,9},{9,8},{10,11... | collective-permute-start | bytes 12296 | tf_op jit(solution)/shard_map/ppermute | solution.py:337
  13.9 3.7 %collective-permute-start.1 = (s32[2,8,128]{2,1,0:T(8,128)S(1)}, s32[2,8,128]{2,1,0:T(8,128)S(1)}, u32[]{:S(2)}, u32[]{:S(2)}) collective-permute-start(s32[2,8,128]{2,1,0:T(8,128)S(1)} %shard_map.123.first_ref), channel_id=1, source_target_pairs={{0,2},{2,0},{4,6},{6,4},{8,10},{10,8},{12,14},{14,12},{1,3},{3,1},... | collective-permute-start | bytes 24584 | tf_op jit(solution)/shard_map/ppermute | solution.py:340
  17.6 9.4 %collective-permute-start.6 = (bf16[128,1024]{1,0:T(8,128)(2,1)S(1)}, bf16[128,1024]{1,0:T(8,128)(2,1)S(1)}, u32[]{:S(2)}, u32[]{:S(2)}) collective-permute-start(bf16[128,1024]{1,0:T(8,128)(2,1)S(1)} %get-tuple-element.16.xz_ref), channel_id=1, source_target_pairs={{0,4},{2,6},{4,8},{6,10},{8,12},{10,14},{12,0},{14,2},{1,5},{3,7},... | collective-permute-start | bytes 786440 | tf_op jit(solution)/shard_map/ppermute | solution.py:343
  17.7 7.7 %collective-permute-start.4 = (s32[4,8,128]{2,1,0:T(8,128)S(1)}, s32[4,8,128]{2,1,0:T(8,128)S(1)}, u32[]{:S(2)}, u32[]{:S(2)}) collective-permute-start(s32[4,8,128]{2,1,0:T(8,128)S(1)} %get-tuple-element.15.refs_2_.first_ref), channel_id=1, source_target_pairs={{0,4},{2,6},{4,0},{6,2},{8,12},{10,14},{12,8},{14,10},{1,5},{3,7},... | collective-permute-start | bytes 49160 | tf_op jit(solution)/shard_map/ppermute | solution.py:346
  17.8 2.2 %copy-start = (bf16[1,1024,2048]{2,1,0:T(8,128)(2,1)S(1)}, bf16[1,1024,2048]{2,1,0:T(8,128)(2,1)}, u32[]{:S(2)}) copy-start(bf16[1,1024,2048]{2,1,0:T(8,128)(2,1)} %param.16) | copy-start | bytes 12582916
  20.0 2.2 %copy-start.3 = (bf16[1,2048,1024]{2,1,0:T(8,128)(2,1)S(1)}, bf16[1,2048,1024]{2,1,0:T(8,128)(2,1)}, u32[]{:S(2)}) copy-start(bf16[1,2048,1024]{2,1,0:T(8,128)(2,1)} %param.17) | copy-start | bytes 12582916
  22.1 14.7 %copy-start.15 = (s32[16]{0:T(128)S(1)}, s32[16]{0:T(128)}, u32[]{:S(2)}) copy-start(s32[16]{0:T(128)} %capacity_ref.1) | copy-start | bytes 196
  22.1 17.3 %copy-start.9 = (bf16[1024,16]{0,1:T(8,128)(2,1)S(1)}, bf16[1024,16]{0,1:T(8,128)(2,1)}, u32[]{:S(2)}) copy-start(bf16[1024,16]{0,1:T(8,128)(2,1)} %param.15) | copy-start | bytes 98308
  22.2 14.7 %collective-permute-start.7 = (bf16[128,1024]{1,0:T(8,128)(2,1)S(1)}, bf16[128,1024]{1,0:T(8,128)(2,1)S(1)}, u32[]{:S(2)}, u32[]{:S(2)}) collective-permute-start(bf16[128,1024]{1,0:T(8,128)(2,1)S(1)} %get-tuple-element.16.xz_ref), channel_id=1, source_target_pairs={{0,2},{2,0},{4,6},{6,4},{8,10},{10,8},{12,14},{14,12},{1,3},{3,1},... | collective-permute-start | bytes 786440 | tf_op jit(solution)/shard_map/ppermute | solution.py:340
  27.1 10.9 %collective-permute-start.12 = (bf16[128,1024]{1,0:T(8,128)(2,1)S(1)}, bf16[128,1024]{1,0:T(8,128)(2,1)S(1)}, u32[]{:S(2)}, u32[]{:S(2)}) collective-permute-start(bf16[128,1024]{1,0:T(8,128)(2,1)S(1)} %shard_map.127.refs_0_.xz_ref), channel_id=1, source_target_pairs={{0,4},{2,6},{4,8},{6,10},{8,12},{10,14},{12,0},{14,2},{1,5},{3,7},... | collective-permute-start | bytes 786440 | tf_op jit(solution)/shard_map/ppermute | solution.py:343
  27.1 9.2 %collective-permute-start.5 = (s32[8,8,128]{2,1,0:T(8,128)S(1)}, s32[8,8,128]{2,1,0:T(8,128)S(1)}, u32[]{:S(2)}, u32[]{:S(2)}) collective-permute-start(s32[8,8,128]{2,1,0:T(8,128)S(1)} %shard_map.126.refs_1_.low_ref), channel_id=1, source_target_pairs={{0,8},{2,10},{4,12},{6,14},{8,0},{10,2},{12,4},{14,6},{1,9},{3,11}... | collective-permute-start | bytes 98312 | tf_op jit(solution)/shard_map/ppermute | solution.py:346
  36.2 15.4 %collective-permute-start.11 = (bf16[128,1024]{1,0:T(8,128)(2,1)S(1)}, bf16[128,1024]{1,0:T(8,128)(2,1)S(1)}, u32[]{:S(2)}, u32[]{:S(2)}) collective-permute-start(bf16[128,1024]{1,0:T(8,128)(2,1)S(1)} %shard_map.127.refs_0_.xz_ref), channel_id=1, source_target_pairs={{0,2},{2,0},{4,6},{6,4},{8,10},{10,8},{12,14},{14,12},{1,3},{3,1},... | collective-permute-start | bytes 786440 | tf_op jit(solution)/shard_map/ppermute | solution.py:340
  37.9 22.9 %collective-permute-start.15 = (bf16[128,1024]{1,0:T(8,128)(2,1)S(1)}, bf16[128,1024]{1,0:T(8,128)(2,1)S(1)}, u32[]{:S(2)}, u32[]{:S(2)}) collective-permute-start(bf16[128,1024]{1,0:T(8,128)(2,1)S(1)} %collective-permute-done.12.rest_1_.xz_ref), channel_id=1, source_target_pairs={{0,2},{2,0},{4,6},{6,4},{8,10},{10,8},{12,14},{14,12},{1,3},{3,1},... | collective-permute-start | bytes 786440 | tf_op jit(solution)/shard_map/ppermute | solution.py:340
  39.5 2.2 %copy-start.1 = (bf16[1,1024,2048]{2,1,0:T(8,128)(2,1)S(1)}, bf16[1,1024,2048]{2,1,0:T(8,128)(2,1)}, u32[]{:S(2)}) copy-start(bf16[1,1024,2048]{2,1,0:T(8,128)(2,1)} %param.16) | copy-start | bytes 12582916
  41.7 2.2 %copy-start.4 = (bf16[1,2048,1024]{2,1,0:T(8,128)(2,1)S(1)}, bf16[1,2048,1024]{2,1,0:T(8,128)(2,1)}, u32[]{:S(2)}) copy-start(bf16[1,2048,1024]{2,1,0:T(8,128)(2,1)} %param.17) | copy-start | bytes 12582916
  43.8 7.8 %copy-start.2 = (bf16[1,1024,2048]{2,1,0:T(8,128)(2,1)S(1)}, bf16[1,1024,2048]{2,1,0:T(8,128)(2,1)}, u32[]{:S(2)}) copy-start(bf16[1,1024,2048]{2,1,0:T(8,128)(2,1)} %param.16) | copy-start | bytes 12582916
  43.8 7.8 %copy-start.5 = (bf16[1,2048,1024]{2,1,0:T(8,128)(2,1)S(1)}, bf16[1,2048,1024]{2,1,0:T(8,128)(2,1)}, u32[]{:S(2)}) copy-start(bf16[1,2048,1024]{2,1,0:T(8,128)(2,1)} %param.17) | copy-start | bytes 12582916
  51.0 9.3 %collective-permute-start.10 = (bf16[128,1024]{1,0:T(8,128)(2,1)S(1)}, bf16[128,1024]{1,0:T(8,128)(2,1)S(1)}, u32[]{:S(2)}, u32[]{:S(2)}) collective-permute-start(bf16[128,1024]{1,0:T(8,128)(2,1)S(1)} %get-tuple-element.18), channel_id=1, source_target_pairs={{0,2},{2,0},{4,6},{6,4},{8,10},{10,8},{12,14},{14,12},{1,3},{3,1},... | collective-permute-start | bytes 786440 | tf_op jit(solution)/shard_map/ppermute | solution.py:340
  51.7 8.6 %copy-start.7 = (bf16[1,128,2048]{2,1,0:T(8,128)(2,1)S(1)}, bf16[1,128,2048]{2,1,0:T(8,128)(2,1)}, u32[]{:S(2)}) copy-start(bf16[1,128,2048]{2,1,0:T(8,128)(2,1)} %param.12) | copy-start | bytes 1572868
  51.7 8.6 %copy-start.8 = (bf16[1,128,2048]{2,1,0:T(8,128)(2,1)S(1)}, bf16[1,128,2048]{2,1,0:T(8,128)(2,1)}, u32[]{:S(2)}) copy-start(bf16[1,128,2048]{2,1,0:T(8,128)(2,1)} %param.13) | copy-start | bytes 1572868
  58.8 10.2 %collective-permute-start.17 = (bf16[128,1024]{1,0:T(8,128)(2,1)S(1)}, bf16[128,1024]{1,0:T(8,128)(2,1)S(1)}, u32[]{:S(2)}, u32[]{:S(2)}) collective-permute-start(bf16[128,1024]{1,0:T(8,128)(2,1)S(1)} %get-tuple-element.25), channel_id=1, source_target_pairs={{0,2},{2,0},{4,6},{6,4},{8,10},{10,8},{12,14},{14,12},{1,3},{3,1},... | collective-permute-start | bytes 786440 | tf_op jit(solution)/shard_map/ppermute | solution.py:340
  60.4 29.3 %collective-permute-start.19 = (bf16[128,1024]{1,0:T(8,128)(2,1)S(1)}, bf16[128,1024]{1,0:T(8,128)(2,1)S(1)}, u32[]{:S(2)}, u32[]{:S(2)}) collective-permute-start(bf16[128,1024]{1,0:T(8,128)(2,1)S(1)} %get-tuple-element.22.rest_1_), channel_id=1, source_target_pairs={{0,12},{2,14},{4,0},{6,2},{8,4},{10,6},{12,8},{14,10},{1,13},{3,15... | collective-permute-start | bytes 786440 | tf_op jit(solution)/shard_map/ppermute | solution.py:343
  60.8 9.5 %copy-start.10 = (bf16[1,128,1024]{2,1,0:T(8,128)(2,1)S(1)}, bf16[1,128,1024]{2,1,0:T(8,128)(2,1)}, u32[]{:S(2)}) copy-start(bf16[1,128,1024]{2,1,0:T(8,128)(2,1)} %param.14) | copy-start | bytes 786436
  60.8 18.1 %collective-permute-start.13 = (bf16[128,2048]{1,0:T(8,128)(2,1)S(1)}, bf16[128,2048]{1,0:T(8,128)(2,1)S(1)}, u32[]{:S(2)}, u32[]{:S(2)}) collective-permute-start(bf16[128,2048]{1,0:T(8,128)(2,1)S(1)} %get-tuple-element.20.k_own), channel_id=1, source_target_pairs={{0,1},{1,0},{2,3},{3,2},{4,5},{5,4},{6,7},{7,6},{8,9},{9,8},{10,11... | collective-permute-start | bytes 1572872 | tf_op jit(solution)/shard_map/ppermute | solution.py:337
  67.9 9.5 %collective-permute-start.16 = (bf16[128,1024]{1,0:T(8,128)(2,1)S(1)}, bf16[128,1024]{1,0:T(8,128)(2,1)S(1)}, u32[]{:S(2)}, u32[]{:S(2)}) collective-permute-start(bf16[128,1024]{1,0:T(8,128)(2,1)S(1)} %get-tuple-element.24), channel_id=1, source_target_pairs={{0,2},{2,0},{4,6},{6,4},{8,10},{10,8},{12,14},{14,12},{1,3},{3,1},... | collective-permute-start | bytes 786440 | tf_op jit(solution)/shard_map/ppermute | solution.py:340
  69.1 20.6 %collective-permute-start.20 = (bf16[128,1024]{1,0:T(8,128)(2,1)S(1)}, bf16[128,1024]{1,0:T(8,128)(2,1)S(1)}, u32[]{:S(2)}, u32[]{:S(2)}) collective-permute-start(bf16[128,1024]{1,0:T(8,128)(2,1)S(1)} %shard_map.133.rest_1_), channel_id=1, source_target_pairs={{0,8},{2,10},{4,12},{6,14},{8,0},{10,2},{12,4},{14,6},{1,9},{3,11}... | collective-permute-start | bytes 786440 | tf_op jit(solution)/shard_map/ppermute | solution.py:343
  70.3 9.3 %copy-start.6 = (bf16[1,128,2048]{2,1,0:T(8,128)(2,1)S(1)}, bf16[1,128,2048]{2,1,0:T(8,128)(2,1)}, u32[]{:S(2)}) copy-start(bf16[1,128,2048]{2,1,0:T(8,128)(2,1)} %param.11) | copy-start | bytes 1572868
  70.3 9.3 %copy-start.12 = (s32[1,128]{1,0:T(1,128)S(1)}, s32[1,128]{1,0:T(1,128)}, u32[]{:S(2)}) copy-start(s32[1,128]{1,0:T(1,128)} %doc_own.3) | copy-start | bytes 1540
  70.3 9.3 %copy-start.14 = (s32[1,128]{1,0:T(1,128)S(1)}, s32[1,128]{1,0:T(1,128)}, u32[]{:S(2)}) copy-start(s32[1,128]{1,0:T(1,128)} %ahead_ref.3) | copy-start | bytes 1540
  70.3 9.3 %collective-permute-start.14 = (bf16[128,2048]{1,0:T(8,128)(2,1)S(1)}, bf16[128,2048]{1,0:T(8,128)(2,1)S(1)}, u32[]{:S(2)}, u32[]{:S(2)}) collective-permute-start(bf16[128,2048]{1,0:T(8,128)(2,1)S(1)} %get-tuple-element.21.v_own), channel_id=1, source_target_pairs={{0,1},{1,0},{2,3},{3,2},{4,5},{5,4},{6,7},{7,6},{8,9},{9,8},{10,11... | collective-permute-start | bytes 1572872 | tf_op jit(solution)/shard_map/ppermute | solution.py:337
  77.4 8.8 %collective-permute-start.18 = (bf16[128,1024]{1,0:T(8,128)(2,1)S(1)}, bf16[128,1024]{1,0:T(8,128)(2,1)S(1)}, u32[]{:S(2)}, u32[]{:S(2)}) collective-permute-start(bf16[128,1024]{1,0:T(8,128)(2,1)S(1)} %get-tuple-element.27), channel_id=1, source_target_pairs={{0,2},{2,0},{4,6},{6,4},{8,10},{10,8},{12,14},{14,12},{1,3},{3,1},... | collective-permute-start | bytes 786440 | tf_op jit(solution)/shard_map/ppermute | solution.py:340
  79.0 10.7 %collective-permute-start.21 = (bf16[128,1024]{1,0:T(8,128)(2,1)S(1)}, bf16[128,1024]{1,0:T(8,128)(2,1)S(1)}, u32[]{:S(2)}, u32[]{:S(2)}) collective-permute-start(bf16[128,1024]{1,0:T(8,128)(2,1)S(1)} %shard_map.135.rest_0_), channel_id=1, source_target_pairs={{0,4},{2,6},{4,8},{6,10},{8,12},{10,14},{12,0},{14,2},{1,5},{3,7},... | collective-permute-start | bytes 786440 | tf_op jit(solution)/shard_map/ppermute | solution.py:343

commit v6 on v5

--- a/solution.py
+++ b/solution.py
@@ -12,9 +12,11 @@
 LATENT = 1024
 TOPK = 6
 DENSE_EXPERTS = 16
-EXPERT_VMEM = 20 * 1024 * 1024
+EXPERT_VMEM = 26 * 1024 * 1024
+FIRST_VMEM = 40 * 1024 * 1024
 ATTEND_VMEM = 8 * 1024 * 1024
 SMALL_VMEM = 4 * 1024 * 1024
+WINDOW = 4
 
 
 def run_expert(rows_in, w_first, w_second):
@@ -112,36 +114,26 @@
     refs[-1][count:] = second_ref[...]
 
 
-def join(first, second, passed=None, after=()):
+def copy_join_kernel(first_ref, second_ref, rows_ref, copy_ref, out_ref):
+    join_kernel(first_ref, second_ref, out_ref)
+    copy_ref[...] = rows_ref[...]
+
+
+def join(first, second, passed=None, after=(), copy=False):
     vmem = pl.BlockSpec(memory_space=pltpu.VMEM)
     anywhere = pl.BlockSpec(memory_space=pl.ANY)
     table = jax.ShapeDtypeStruct((2 * first.shape[0],) + first.shape[1:], first.dtype)
     through = [] if passed is None else [passed]
+    place = vmem if copy else anywhere
     out = pl.pallas_call(
-        join_kernel,
+        copy_join_kernel if copy else join_kernel,
         out_shape=[jax.ShapeDtypeStruct(x.shape, x.dtype) for x in through] + [table],
-        in_specs=[vmem] * 2 + [anywhere] * (len(through) + len(after)),
-        out_specs=[anywhere] * len(through) + [vmem],
-        input_output_aliases={2: 0} if through else {},
+        in_specs=[vmem] * 2 + [place] * len(through) + [anywhere] * len(after),
+        out_specs=[place] * len(through) + [vmem],
+        input_output_aliases={2: 0} if through and not copy else {},
         compiler_params=pltpu.CompilerParams(vmem_limit_bytes=SMALL_VMEM),
     )(first, second, *through, *after)
     return out if through else out[0]
-
-
-def hold_kernel(*refs):
-    refs[-1][...] = jnp.zeros_like(refs[-1])
-
-
-def hold(resident, after):
-    vmem = pl.BlockSpec(memory_space=pltpu.VMEM)
-    anywhere = pl.BlockSpec(memory_space=pl.ANY)
-    return pl.pallas_call(
-        hold_kernel,
-        out_shape=jax.ShapeDtypeStruct((8, 128), jnp.int32),
-        in_specs=[vmem] * len(resident) + [anywhere] * len(after),
-        out_specs=vmem,
-        compiler_params=pltpu.CompilerParams(vmem_limit_bytes=EXPERT_VMEM),
-    )(*resident, *after)
 
 
 def behind_kernel(*refs):
@@ -161,7 +153,7 @@
 
 
 def kept_kernel(own_ref, capacity_ref, low_ref, high_ref, *refs):
-    out_ref = refs[-1]
+    out_ref = refs[-2]
     tables = (low_ref, high_ref)
     own = own_ref[0]
     z = own // 4
@@ -201,17 +193,21 @@
                 out_ref[2 * step + side, k : k + 1, :] = picked
 
 
-def kept_rows(own, capacity, low, high, after):
+def kept_rows(own, capacity, low, high, passed, after):
     smem = pl.BlockSpec(memory_space=pltpu.SMEM)
     vmem = pl.BlockSpec(memory_space=pltpu.VMEM)
     anywhere = pl.BlockSpec(memory_space=pl.ANY)
     return pl.pallas_call(
         kept_kernel,
-        out_shape=jax.ShapeDtypeStruct(low.shape, jnp.int32),
-        in_specs=[smem, smem, vmem, vmem] + [anywhere] * len(after),
-        out_specs=vmem,
+        out_shape=(
+            jax.ShapeDtypeStruct(low.shape, jnp.int32),
+            jax.ShapeDtypeStruct(passed.shape, passed.dtype),
+        ),
+        in_specs=[smem, smem, vmem, vmem] + [anywhere] * (1 + len(after)),
+        out_specs=(vmem, anywhere),
+        input_output_aliases={4: 1},
         compiler_params=pltpu.CompilerParams(vmem_limit_bytes=SMALL_VMEM),
-    )(own, capacity, low, high, *after)
+    )(own, capacity, low, high, passed, *after)
 
 
 def gate_columns(own, router_ref, x, kept):
@@ -232,69 +228,83 @@
     return square.T
 
 
-def expert_kernel(
-    place, own_ref, kept_ref, router_ref, xz_ref, xy_ref, w1a, w2a, w1b_any, w2b_any, *rest
-):
-    z_ref, y_ref, hidden_ref, mixed_ref, w1b, w2b, sems = rest[-7:]
-    loads = [
-        pltpu.make_async_copy(w1b_any, w1b, sems.at[0]),
-        pltpu.make_async_copy(w2b_any, w2b, sems.at[1]),
-    ]
-    for load in loads:
-        load.start()
+def expert_kernel(place, first, own_ref, kept_ref, router_ref, xz_ref, xy_ref, *refs):
+    step = 512
+    if first:
+        sources = refs[:4]
+        z_ref, y_ref, *weights, hidden_ref, mixed_ref, sems = refs[-9:]
+    else:
+        weights = refs[:4]
+        z_ref, y_ref, hidden_ref, mixed_ref = refs[-4:]
+    chunks = [(w, c) for w in range(4) for c in range(0, weights[w].shape[1], step)]
+
+    def load(index):
+        which, column = chunks[index]
+        cols = pl.ds(column, step)
+        return pltpu.make_async_copy(
+            sources[which].at[:, cols], weights[which].at[:, cols], sems.at[index]
+        )
+
+    def ready(which, column):
+        if first:
+            index = chunks.index((which, column))
+            load(index).wait()
+            if index + WINDOW < len(chunks):
+                load(index + WINDOW).start()
+
+    if first:
+        for index in range(WINDOW):
+            load(index).start()
     own = own_ref[0]
     rows = xz_ref.shape[0]
     x = jnp.concatenate([xz_ref[...], xy_ref[...]], axis=0)
-    step = 512
-
-    def enter(w1_ref):
-        for first in range(0, w1_ref.shape[1], step):
-            cols = slice(first, first + step)
-            hidden = jnp.dot(x, w1_ref[:, cols], preferred_element_type=jnp.float32)
-            hidden = jnp.maximum(hidden, 0.0)
-            hidden_ref[:, cols] = (hidden * hidden).astype(jnp.bfloat16)
-
-    enter(w1a)
     gates = [
         gate_columns(own, router_ref, x_ref[...], kept_ref[2 * place + side])
         for side, x_ref in enumerate((xz_ref, xy_ref))
     ]
-    gates = [jnp.concatenate([g[:, which : which + 1] for g in gates], axis=0) for which in range(2)]
-    for first in range(0, w2a.shape[1], step):
-        cols = slice(first, first + step)
-        result = jnp.dot(hidden_ref[...], w2a[:, cols], preferred_element_type=jnp.float32)
-        mixed_ref[:, cols] = result * gates[0]
-    loads[0].wait()
-    enter(w1b)
-    loads[1].wait()
-    for first in range(0, w2b.shape[1], step):
-        cols = slice(first, first + step)
-        result = jnp.dot(hidden_ref[...], w2b[:, cols], preferred_element_type=jnp.float32)
-        mixed = (mixed_ref[:, cols] + result * gates[1]).astype(jnp.bfloat16)
-        z_ref[:, cols] = mixed[:rows]
-        y_ref[:, cols] = mixed[rows:]
-
-
-def run_piece(place, own, kept, router, from_line, from_side, weights, after):
+    for which in range(2):
+        gate = jnp.concatenate([g[:, which : which + 1] for g in gates], axis=0)
+        w1_ref, w2_ref = weights[2 * which], weights[2 * which + 1]
+        for column in range(0, w1_ref.shape[1], step):
+            cols = slice(column, column + step)
+            ready(2 * which, column)
+            hidden = jnp.dot(x, w1_ref[:, cols], preferred_element_type=jnp.float32)
+            hidden = jnp.maximum(hidden, 0.0)
+            hidden_ref[which, :, cols] = (hidden * hidden).astype(jnp.bfloat16)
+        for column in range(0, w2_ref.shape[1], step):
+            cols = slice(column, column + step)
+            ready(2 * which + 1, column)
+            result = jnp.dot(hidden_ref[which], w2_ref[:, cols], preferred_element_type=jnp.float32)
+            if which == 0:
+                mixed_ref[:, cols] = result * gate
+            else:
+                mixed = (mixed_ref[:, cols] + result * gate).astype(jnp.bfloat16)
+                z_ref[:, cols] = mixed[:rows]
+                y_ref[:, cols] = mixed[rows:]
+
+
+def run_piece(place, first, own, kept, router, from_line, from_side, weights, after):
     rows, width = from_line.shape
     hidden = weights[0].shape[1]
     smem = pl.BlockSpec(memory_space=pltpu.SMEM)
     vmem = pl.BlockSpec(memory_space=pltpu.VMEM)
+    hbm = pl.BlockSpec(memory_space=pltpu.HBM)
     anywhere = pl.BlockSpec(memory_space=pl.ANY)
     piece = jax.ShapeDtypeStruct((rows, width), jnp.bfloat16)
+    staged = [pltpu.VMEM(w.shape, w.dtype) for w in weights] if first else []
+    scratch = [
+        pltpu.VMEM((2, 2 * rows, hidden), jnp.bfloat16),
+        pltpu.VMEM((2 * rows, width), jnp.float32),
+    ]
+    if first:
+        scratch.append(pltpu.SemaphoreType.DMA((4 * (hidden + width) // 1024,)))
     return pl.pallas_call(
-        functools.partial(expert_kernel, place),
-        out_shape=(piece, piece),
-        in_specs=[smem] + [vmem] * 6 + [anywhere] * (2 + len(after)),
-        out_specs=(vmem, vmem),
-        scratch_shapes=[
-            pltpu.VMEM((2 * rows, hidden), jnp.bfloat16),
-            pltpu.VMEM((2 * rows, width), jnp.float32),
-            pltpu.VMEM(weights[2].shape, jnp.bfloat16),
-            pltpu.VMEM(weights[3].shape, jnp.bfloat16),
-            pltpu.SemaphoreType.DMA((2,)),
-        ],
-        compiler_params=pltpu.CompilerParams(vmem_limit_bytes=EXPERT_VMEM),
+        functools.partial(expert_kernel, place, first),
+        out_shape=[piece, piece] + staged,
+        in_specs=[smem] + [vmem] * 4 + [hbm if first else vmem] * 4 + [anywhere] * len(after),
+        out_specs=[vmem] * (2 + len(staged)),
+        scratch_shapes=scratch,
+        compiler_params=pltpu.CompilerParams(vmem_limit_bytes=FIRST_VMEM if first else EXPERT_VMEM),
         cost_estimate=pl.CostEstimate(
             flops=16 * rows * width * hidden,
             bytes_accessed=8 * rows * width,
@@ -355,31 +365,33 @@
     doc_far = beside[0, TOPK : TOPK + 1, :]
     table = join(tile, beside)
     arriving, table = join(table, swap_side(table), passed=arriving, after=(beside_own,))
-    flip = flipped(table, 1)
-    from_line = [latent[0], arriving, along(arriving, 1)]
     from_side = [beside_own, swap_side(arriving)]
-    table = join(table, flip, after=(hold(own_weights, (table,)),))
+    passed, table = join(table, flipped(table, 1), passed=arriving, copy=True)
     flip = flipped(table, 2)
-    from_line[2] = behind(from_line[2], (table,))
-    for step in range(3, line):
-        from_line.append(along(from_line[-1], 1))
-    from_side += [swap_side(x) for x in from_line[2:]]
-    kept = kept_rows(own, capacity, table, flip, (from_line[2], from_side[1]))
-
-    def piece(step, *after):
-        return run_piece(step, own, kept, router.T, from_line[step], from_side[step], weights, after)
-
-    one, theirs = piece(1)
+    kept, passed = kept_rows(own, capacity, table, flip, along(passed, 1), (from_side[1],))
+    from_line = [latent[0], arriving, passed]
+    from_side.append(swap_side(passed))
+    last = along(passed, 1)
+
+    def piece(step, weights, *after):
+        return run_piece(
+            step, step == 1, own, kept, router.T, from_line[step], from_side[step], weights, after
+        )
+
+    one, theirs, *weights = piece(1, weights)
     one_far = swap_side(theirs)
-    two, theirs = piece(2, one, from_line[3])
+    last = behind(last, (one,))
+    from_line.append(last)
+    from_side.append(swap_side(last))
+    two, theirs = piece(2, weights, one, from_line[3])
     two_far = swap_side(theirs)
     k_near, v_near, first = add(one, one_far, after=(two,), staged=(k_near, v_near))
     home = [along(first, line - 1)]
-    three, theirs = piece(3, two, first)
+    three, theirs = piece(3, weights, two, first)
     three_far = swap_side(theirs)
     second = add(two, two_far, after=(three,))
     home.append(along(second, line - 2))
-    near, theirs = piece(0, three, second)
+    near, theirs = piece(0, weights, three, second)
     near_far = swap_side(theirs)
     third = add(three, three_far, after=(near,))
     home.append(along(third, line - 3))

time: 90.9 us -> 82.9 us (0.912)
  local copies, waits for them, and re-layouts: 10.1 us -> 4.55 us
  Pallas kernels: 32.9 us -> 28.6 us
  waiting for transfers between devices: 30.5 us -> 32.6 us
    unnamed x32, local copies, waits for them, and re-layouts: 10.1 us -> 4.55 us
    pallas_call x9 -> x8, Pallas kernels: 29.5 us -> 25.1 us  [the longest x4 24 us: run_piece(): pl.pallas_call(functools.partial(expert_kernel, place, first), out_shape=...]
    ppermute x9, waiting for transfers between devices: 7.03 us -> 10.9 us  [swap_side(): return lax.ppermute(x, 'expert', across)]
    ppermute x6, waiting for transfers between devices: 5.19 us -> 2.33 us  [along(): lax.ppermute(x, 'expert', [(2 * z + y, 2 * ((z + step) % line) + y) for z...]
    ppermute x6, starting transfers between devices: 3.9 us -> 6.22 us  [along(): lax.ppermute(x, 'expert', [(2 * z + y, 2 * ((z + step) % line) + y) for z...]
    ppermute x9, starting transfers between devices: 9.77 us -> 8.02 us  [swap_side(): return lax.ppermute(x, 'expert', across)]
    ppermute x2, waiting for transfers between devices: 11.5 us -> 12.7 us  [flipped(): lax.ppermute(x, 'expert', [(2 * z + y, 2 * (z ^ span) + y) for z, y in sp...]
  transfers between devices with their start and end apart: 22 -> 22, of which waited for: 7 -> 7; matrix products, arithmetic and copies ran while one was open for 0% -> 0% of each run, Pallas kernels for 36% -> 35%
where the time goes in v6:
time: 82.9 us; the launch traced here: 82.6 us
  waiting for transfers between devices  32.6 us (39%)
  Pallas kernels  28.6 us (34%)
  starting transfers between devices  15.1 us (18%)
  local copies, waits for them, and re-layouts  4.55 us (5%)
  other arithmetic  0.92 us (1%)
  between operations  0.87 us (1%)
    pallas_call x4, Pallas kernels, run_piece(): pl.pallas_call(functools.partial(expert_kernel, place, first), out_shape=...  24 us
    ppermute x2, waiting for transfers between devices, flipped(): lax.ppermute(x, 'expert', [(2 * z + y, 2 * (z ^ span) + y) for z, y in sp...  12.7 us
    ppermute x9, waiting for transfers between devices, swap_side(): return lax.ppermute(x, 'expert', across)  10.9 us
    ppermute x9, starting transfers between devices, swap_side(): return lax.ppermute(x, 'expert', across)  8.02 us
    ppermute x5, waiting for transfers between devices, swap_core(): return lax.ppermute(x, 'context', sibling)  6.75 us
    ppermute x6, starting transfers between devices, along(): lax.ppermute(x, 'expert', [(2 * z + y, 2 * ((z + step) % line) + y) for z...  6.22 us
    unnamed x32, local copies, waits for them, and re-layouts  4.55 us
    pallas_call x2, Pallas kernels, attend(): pl.pallas_call(attend_kernel, grid=(1,), out_shape=jax.ShapeDtypeStruct(q...  3.17 us
  transfers between devices with their start and end apart: 22, of which 7 were waited for; matrix products, arithmetic and copies ran while one was open for 0% of the time, Pallas kernels for 35%

profile of v6, /device:TPU:0, one launch (start us, length us, event | category | flops | bytes accessed | tf_op | source)
XLA Modules:
  0.0 82.6 jit_solution(7168649630921888850)
XLA Ops:
  0.6 0.5 collective-permute-start.8
  1.1 0.1 collective-permute-start.9
  1.2 2.9 %collective-permute-start.3 = (bf16[128,1024]{1,0:T(8,128)(2,1)}, bf16[128,1024]{1,0:T(8,128)(2,1)S(1)}, u32[]{:S(2)}, u32[]{:S(2)}) collective-permute-start(bf16[128,1024]{1,0:T(8,128)(2,1)} %bitcast.23), channel_id=1, source_target_pairs={{0,2},{2,0},{4,6},{6,4},{8,10},{10,8},{12,14},{14,12},{1,3},{3,1},... | collective-permute-start | bytes 786440 | tf_op jit(solution)/shard_map/ppermute | solution.py:350
  4.2 1.6 %collective-permute-start.2 = (bf16[128,1024]{1,0:T(8,128)(2,1)}, bf16[128,1024]{1,0:T(8,128)(2,1)S(1)}, u32[]{:S(2)}, u32[]{:S(2)}) collective-permute-start(bf16[128,1024]{1,0:T(8,128)(2,1)} %bitcast.24), channel_id=1, source_target_pairs={{0,4},{2,6},{4,8},{6,10},{8,12},{10,14},{12,0},{14,2},{1,5},{3,7},... | collective-permute-start | bytes 786440 | tf_op jit(solution)/shard_map/ppermute | solution.py:353
  5.8 0.7 copy-done.11
  6.4 0.7 copy-done.13
  7.1 0.1 collective-permute-start
  7.2 6.7 %collective-permute-done.second_ref = s32[1,8,128]{2,1,0:T(8,128)S(1)} collective-permute-done((s32[1,8,128]{2,1,0:T(8,128)S(1)}, s32[1,8,128]{2,1,0:T(8,128)S(1)}, u32[]{:S(2)}, u32[]{:S(2)}) %collective-permute-start) | collective-permute-done | bytes 4128 | tf_op jit(solution)/shard_map/ppermute | solution.py:347
  13.9 0.0 collective-permute-start.1
  13.9 3.7 %collective-permute-done.1.second_ref = s32[2,8,128]{2,1,0:T(8,128)S(1)} collective-permute-done((s32[2,8,128]{2,1,0:T(8,128)S(1)}, s32[2,8,128]{2,1,0:T(8,128)S(1)}, u32[]{:S(2)}, u32[]{:S(2)}) %collective-permute-start.1) | collective-permute-done | bytes 8224 | tf_op jit(solution)/shard_map/ppermute | solution.py:350
  17.6 0.0 collective-permute-done.3.refs_1_.xy_ref
  17.6 0.0 collective-permute-done.2.refs_0_
  17.6 0.0 copy-start
  17.6 0.1 collective-permute-start.4
  17.7 0.1 collective-permute-start.7
  17.8 3.6 %collective-permute-done.4.second_ref = s32[4,8,128]{2,1,0:T(8,128)S(1)} collective-permute-done((s32[4,8,128]{2,1,0:T(8,128)S(1)}, s32[4,8,128]{2,1,0:T(8,128)S(1)}, u32[]{:S(2)}, u32[]{:S(2)}) %collective-permute-start.4) | collective-permute-done | bytes 16416 | tf_op jit(solution)/shard_map/ppermute | solution.py:356
  21.5 0.1 collective-permute-start.6
  21.5 0.1 collective-permute-start.5
  21.6 9.0 %collective-permute-done.5.high_ref = s32[8,8,128]{2,1,0:T(8,128)S(1)} collective-permute-done((s32[8,8,128]{2,1,0:T(8,128)S(1)}, s32[8,8,128]{2,1,0:T(8,128)S(1)}, u32[]{:S(2)}, u32[]{:S(2)}) %collective-permute-start.5) | collective-permute-done | bytes 32800 | tf_op jit(solution)/shard_map/ppermute | solution.py:356
  30.6 0.0 collective-permute-done.7.refs_1_.xy_ref
  30.6 0.0 collective-permute-done.6.refs_0_
  30.6 0.0 copy-start.15
  30.7 0.7 copy-done.15
  31.3 1.1 %shard_map.126 = (s32[8,8,128]{2,1,0:T(8,128)S(1)}, bf16[128,1024]{1,0:T(8,128)(2,1)S(1)}) custom-call(s32[1]{0:T(128)} %bitcast.2.own_ref, s32[16]{0:T(128)S(1)} %copy-done.15, s32[8,8,128]{2,1,0:T(8,128)S(1)} %get-tuple-element.25.low_ref, s32[8,8,128]{2,1,0:T(8,128)S(1)} %collective-permute-done.5.high_ref, ...), custom_call_target="tpu_custom_call", output_to_operand_aliasing={{1}: (4, {})} | custom-call | tf_op jit(solution)/shard_map/pallas_call | solution.py:200
  32.4 0.6 copy-done.8
  33.0 0.3 collective-permute-start.12
  33.4 0.3 collective-permute-start.11
  33.6 0.0 collective-permute-done.8.refs_2_
  33.6 0.0 collective-permute-done.9.refs_3_
  33.7 0.0 copy-start.7
  33.7 9.8 %shard_map.127 = (bf16[128,1024]{1,0:T(8,128)(2,1)}, bf16[128,1024]{1,0:T(8,128)(2,1)}, bf16[1024,2048]{1,0:T(8,128)(2,1)S(1)}, bf16[2048,1024]{1,0:T(8,128)(2,1...) custom-call(s32[1]{0:T(128)} %bitcast.2.own_ref, s32[8,8,128]{2,1,0:T(8,128)} %copy-done.8, ...), custom_call_target="tpu_custom_call" | custom-call | flops 4294967296 | bytes 1048576 | tf_op jit(solution)/shard_map/pallas_call | solution.py:301
  43.5 1.8 %collective-permute-start.10 = (bf16[128,1024]{1,0:T(8,128)(2,1)}, bf16[128,1024]{1,0:T(8,128)(2,1)S(1)}, u32[]{:S(2)}, u32[]{:S(2)}) collective-permute-start(bf16[128,1024]{1,0:T(8,128)(2,1)} %get-tuple-element.29), channel_id=1, source_target_pairs={{0,2},{2,0},{4,6},{6,4},{8,10},{10,8},{12,14},{14,12},{1,3},{3,1},... | collective-permute-start | bytes 786440 | tf_op jit(solution)/shard_map/ppermute | solution.py:350
  45.3 0.0 collective-permute-done.12.refs_0_
  45.3 0.9 %copy-done.1 = bf16[128,1024]{1,0:T(8,128)(2,1)S(1)} copy-done((bf16[128,1024]{1,0:T(8,128)(2,1)S(1)}, bf16[128,1024]{1,0:T(8,128)(2,1)}, u32[]{:S(2)}) %copy-start.1) | copy-done | bytes 262168
  46.3 0.3 collective-permute-start.15
  46.6 0.0 collective-permute-done.11.xy_ref
  46.6 0.9 %copy-done.2 = bf16[128,1024]{1,0:T(8,128)(2,1)S(1)} copy-done((bf16[128,1024]{1,0:T(8,128)(2,1)S(1)}, bf16[128,1024]{1,0:T(8,128)(2,1)}, u32[]{:S(2)}) %copy-start.2) | copy-done | bytes 262168
  47.5 4.7 %shard_map.129 = (bf16[128,1024]{1,0:T(8,128)(2,1)S(1)}, bf16[128,1024]{1,0:T(8,128)(2,1)S(1)}) custom-call(s32[1]{0:T(128)} %bitcast.2.own_ref, s32[8,8,128]{2,1,0:T(8,128)S(1)} %copy-done.9, bf16[16,1024]{1,0:T(8,128)(2,1)S(1)} %bitcast.20, bf16[128,1024]{1,0:T(8,128)(2,1)S(1)} %get-tuple-element.30.xz_ref, ...), custom_call_target="tpu_custom_call" | custom-call | flops 4294967296 | bytes 1048576 | tf_op jit(solution)/shard_map/pallas_call | solution.py:301
  52.3 1.8 %collective-permute-start.17 = (bf16[128,1024]{1,0:T(8,128)(2,1)S(1)}, bf16[128,1024]{1,0:T(8,128)(2,1)S(1)}, u32[]{:S(2)}, u32[]{:S(2)}) collective-permute-start(bf16[128,1024]{1,0:T(8,128)(2,1)S(1)} %get-tuple-element.41), channel_id=1, source_target_pairs={{0,2},{2,0},{4,6},{6,4},{8,10},{10,8},{12,14},{14,12},{1,3},{3,1},... | collective-permute-start | bytes 786440 | tf_op jit(solution)/shard_map/ppermute | solution.py:350
  54.1 0.0 collective-permute-done.10.second_ref
  54.1 0.1 shard_map.130
  54.2 3.7 %collective-permute-start.19 = (bf16[128,1024]{1,0:T(8,128)(2,1)S(1)}, bf16[128,1024]{1,0:T(8,128)(2,1)S(1)}, u32[]{:S(2)}, u32[]{:S(2)}) collective-permute-start(bf16[128,1024]{1,0:T(8,128)(2,1)S(1)} %get-tuple-element.38.refs_5_), channel_id=1, source_target_pairs={{0,12},{2,14},{4,0},{6,2},{8,4},{10,6},{12,8},{14,10},{1,13},{3,15... | collective-permute-start | bytes 786440 | tf_op jit(solution)/shard_map/ppermute | solution.py:353
  57.9 0.0 collective-permute-start.13
  57.9 0.0 collective-permute-done.15.xy_ref
  58.0 4.7 %shard_map.131 = (bf16[128,1024]{1,0:T(8,128)(2,1)S(1)}, bf16[128,1024]{1,0:T(8,128)(2,1)S(1)}) custom-call(s32[1]{0:T(128)} %bitcast.2.own_ref, s32[8,8,128]{2,1,0:T(8,128)S(1)} %copy-done.9, bf16[16,1024]{1,0:T(8,128)(2,1)S(1)} %bitcast.21, bf16[128,1024]{1,0:T(8,128)(2,1)S(1)} %shard_map.128.refs_5_.xz_ref, ...), custom_call_target="tpu_custom_call" | custom-call | flops 4294967296 | bytes 1048576 | tf_op jit(solution)/shard_map/pallas_call | solution.py:301
  62.7 0.5 collective-permute-start.16
  63.2 0.0 collective-permute-done.17.second_ref
  63.2 0.1 shard_map.132.refs_5_
  63.3 0.2 collective-permute-start.20
  63.5 0.1 collective-permute-start.14
  63.5 4.7 %shard_map.133 = (bf16[128,1024]{1,0:T(8,128)(2,1)S(1)}, bf16[128,1024]{1,0:T(8,128)(2,1)S(1)}) custom-call(s32[1]{0:T(128)} %bitcast.2.own_ref, s32[8,8,128]{2,1,0:T(8,128)S(1)} %copy-done.9, bf16[16,1024]{1,0:T(8,128)(2,1)S(1)} %bitcast.22, bf16[128,1024]{1,0:T(8,128)(2,1)S(1)} %bitcast.25, bf16[128,1024]{1,0:T(8,128)(2,1)S(1)} %collective-permute-done.3.refs_1_.xy_ref, ...), custom_call_target="tpu_custom_call" | custom-call | flops 4294967296 | bytes 1048576 | tf_op jit(solution)/shard_map/pallas_call | solution.py:301
  68.3 3.2 %collective-permute-done.16.second_ref = bf16[128,1024]{1,0:T(8,128)(2,1)S(1)} collective-permute-done((bf16[128,1024]{1,0:T(8,128)(2,1)S(1)}, bf16[128,1024]{1,0:T(8,128)(2,1)S(1)}, u32[]{:S(2)}, u32[]{:S(2)}) %collective-permute-start.16) | collective-permute-done | bytes 262176 | tf_op jit(solution)/shard_map/ppermute | solution.py:350
  71.5 0.3 collective-permute-start.18
  71.8 0.1 shard_map.134.rest_0_
  71.8 0.0 collective-permute-done.13.k_far
  71.8 0.4 collective-permute-start.21
  72.2 0.0 collective-permute-done.14.v_far
  72.2 1.6 %shard_map.135.rest_0_ = bf16[128,2048]{1,0:T(8,128)(2,1)} custom-call(s32[1]{0:T(128)} %bitcast.place_ref, bf16[128,2048]{1,0:T(8,128)(2,1)S(1)} %bitcast.15, bf16[128,2048]{1,0:T(8,128)(2,1)S(1)} %get-tuple-element.36.k_own, bf16[128,2048]{1,0:T(8,128)(2,1)S(1)} %collective-permute-done.13.k_far, bf16[128,2048]{1,0:T(8,128)(2,1)S(1)} %get-tuple-element.37.v_own, ...), custom_call_target="tpu_custom_call" | custom-call | flops 134217728 | bytes 1572864 | tf_op jit(solution)/shard_map/pallas_call | solution.py:66
  73.8 1.6 %shard_map.136 = bf16[128,2048]{1,0:T(8,128)(2,1)} custom-call(s32[1]{0:T(128)} %bitcast.place_ref, bf16[128,2048]{1,0:T(8,128)(2,1)S(1)} %bitcast.16, bf16[128,2048]{1,0:T(8,128)(2,1)S(1)} %get-tuple-element.36.k_own, bf16[128,2048]{1,0:T(8,128)(2,1)S(1)} %collective-permute-done.13.k_far, ...), custom_call_target="tpu_custom_call", output_to_operand_aliasing={{}: (9, {})} | custom-call | flops 134217728 | bytes 1572864 | tf_op jit(solution)/shard_map/pallas_call | solution.py:66
  75.4 4.0 %collective-permute-done.18 = bf16[128,1024]{1,0:T(8,128)(2,1)S(1)} collective-permute-done((bf16[128,1024]{1,0:T(8,128)(2,1)S(1)}, bf16[128,1024]{1,0:T(8,128)(2,1)S(1)}, u32[]{:S(2)}, u32[]{:S(2)}) %collective-permute-start.18) | collective-permute-done | bytes 262176 | tf_op jit(solution)/shard_map/ppermute | solution.py:350
  79.4 2.3 %collective-permute-done.20 = bf16[128,1024]{1,0:T(8,128)(2,1)S(1)} collective-permute-done((bf16[128,1024]{1,0:T(8,128)(2,1)S(1)}, bf16[128,1024]{1,0:T(8,128)(2,1)S(1)}, u32[]{:S(2)}, u32[]{:S(2)}) %collective-permute-start.20) | collective-permute-done | bytes 262176 | tf_op jit(solution)/shard_map/ppermute | solution.py:353
  81.7 0.0 collective-permute-done.19
  81.7 0.0 collective-permute-done.21
  81.7 0.9 %fusion = bf16[1,128,1024]{2,1,0:T(8,128)(2,1)} fusion(bf16[128,1024]{1,0:T(8,128)(2,1)S(1)} %collective-permute-done.21, bf16[128,1024]{1,0:T(8,128)(2,1)S(1)} %collective-permute-done.20, bf16[128,1024]{1,0:T(8,128)(2,1)S(1)} %collective-permute-done.19, bf16[128,1024]{1,0:T(8,128)(2,1)S(1)} %collective-permute-done.18, ...), kind=kLoop, calls=%fused_computation.1 | loop fusion | flops 1310720 | bytes 1572864 | tf_op jit(solution)/shard_map/broadcast_in_dim | solution.py:404
  (29 shorter events, 0.1 us)
Async XLA Ops:
  0.6 33.0 %collective-permute-start.8 = (bf16[1024,2048]{1,0:T(8,128)(2,1)}, bf16[1024,2048]{1,0:T(8,128)(2,1)}, u32[]{:S(2)}, u32[]{:S(2)}) collective-permute-start(bf16[1024,2048]{1,0:T(8,128)(2,1)} %bitcast.27), channel_id=1, source_target_pairs={{0,1},{1,0},{2,3},{3,2},{4,5},{5,4},{6,7},{7,6},{8,9},{9,8},{10,11... | collective-permute-start | bytes 12582920 | tf_op jit(solution)/shard_map/ppermute | solution.py:347
  1.1 32.5 %collective-permute-start.9 = (bf16[2048,1024]{1,0:T(8,128)(2,1)}, bf16[2048,1024]{1,0:T(8,128)(2,1)}, u32[]{:S(2)}, u32[]{:S(2)}) collective-permute-start(bf16[2048,1024]{1,0:T(8,128)(2,1)} %bitcast.29), channel_id=1, source_target_pairs={{0,1},{1,0},{2,3},{3,2},{4,5},{5,4},{6,7},{7,6},{8,9},{9,8},{10,11... | collective-permute-start | bytes 12582920 | tf_op jit(solution)/shard_map/ppermute | solution.py:347
  1.2 16.4 %collective-permute-start.3 = (bf16[128,1024]{1,0:T(8,128)(2,1)}, bf16[128,1024]{1,0:T(8,128)(2,1)S(1)}, u32[]{:S(2)}, u32[]{:S(2)}) collective-permute-start(bf16[128,1024]{1,0:T(8,128)(2,1)} %bitcast.23), channel_id=1, source_target_pairs={{0,2},{2,0},{4,6},{6,4},{8,10},{10,8},{12,14},{14,12},{1,3},{3,1},... | collective-permute-start | bytes 786440 | tf_op jit(solution)/shard_map/ppermute | solution.py:350
  4.2 13.4 %collective-permute-start.2 = (bf16[128,1024]{1,0:T(8,128)(2,1)}, bf16[128,1024]{1,0:T(8,128)(2,1)S(1)}, u32[]{:S(2)}, u32[]{:S(2)}) collective-permute-start(bf16[128,1024]{1,0:T(8,128)(2,1)} %bitcast.24), channel_id=1, source_target_pairs={{0,4},{2,6},{4,8},{6,10},{8,12},{10,14},{12,0},{14,2},{1,5},{3,7},... | collective-permute-start | bytes 786440 | tf_op jit(solution)/shard_map/ppermute | solution.py:353
  5.7 0.7 copy-start.11
  6.4 0.7 copy-start.13
  7.1 6.8 %collective-permute-start = (s32[1,8,128]{2,1,0:T(8,128)S(1)}, s32[1,8,128]{2,1,0:T(8,128)S(1)}, u32[]{:S(2)}, u32[]{:S(2)}) collective-permute-start(s32[1,8,128]{2,1,0:T(8,128)S(1)} %shard_map.122.first_ref), channel_id=1, source_target_pairs={{0,1},{1,0},{2,3},{3,2},{4,5},{5,4},{6,7},{7,6},{8,9},{9,8},{10,11... | collective-permute-start | bytes 12296 | tf_op jit(solution)/shard_map/ppermute | solution.py:347
  13.9 3.7 %collective-permute-start.1 = (s32[2,8,128]{2,1,0:T(8,128)S(1)}, s32[2,8,128]{2,1,0:T(8,128)S(1)}, u32[]{:S(2)}, u32[]{:S(2)}) collective-permute-start(s32[2,8,128]{2,1,0:T(8,128)S(1)} %shard_map.123.first_ref), channel_id=1, source_target_pairs={{0,2},{2,0},{4,6},{6,4},{8,10},{10,8},{12,14},{14,12},{1,3},{3,1},... | collective-permute-start | bytes 24584 | tf_op jit(solution)/shard_map/ppermute | solution.py:350
  17.6 16.0 %copy-start = (bf16[128,1024]{1,0:T(8,128)(2,1)}, bf16[128,1024]{1,0:T(8,128)(2,1)S(1)}, u32[]{:S(2)}) copy-start(bf16[128,1024]{1,0:T(8,128)(2,1)S(1)} %get-tuple-element.24.rows_ref.xz_ref) | copy-start | bytes 786436
  17.6 3.8 %collective-permute-start.4 = (s32[4,8,128]{2,1,0:T(8,128)S(1)}, s32[4,8,128]{2,1,0:T(8,128)S(1)}, u32[]{:S(2)}, u32[]{:S(2)}) collective-permute-start(s32[4,8,128]{2,1,0:T(8,128)S(1)} %get-tuple-element.23.first_ref), channel_id=1, source_target_pairs={{0,4},{2,6},{4,0},{6,2},{8,12},{10,14},{12,8},{14,10},{1,5},{3,7},... | collective-permute-start | bytes 49160 | tf_op jit(solution)/shard_map/ppermute | solution.py:356
  17.7 12.9 %collective-permute-start.7 = (bf16[128,1024]{1,0:T(8,128)(2,1)S(1)}, bf16[128,1024]{1,0:T(8,128)(2,1)S(1)}, u32[]{:S(2)}, u32[]{:S(2)}) collective-permute-start(bf16[128,1024]{1,0:T(8,128)(2,1)S(1)} %get-tuple-element.24.rows_ref.xz_ref), channel_id=1, source_target_pairs={{0,2},{2,0},{4,6},{6,4},{8,10},{10,8},{12,14},{14,12},{1,3},{3,1},... | collective-permute-start | bytes 786440 | tf_op jit(solution)/shard_map/ppermute | solution.py:350
  21.5 9.2 %collective-permute-start.6 = (bf16[128,1024]{1,0:T(8,128)(2,1)S(1)}, bf16[128,1024]{1,0:T(8,128)(2,1)S(1)}, u32[]{:S(2)}, u32[]{:S(2)}) collective-permute-start(bf16[128,1024]{1,0:T(8,128)(2,1)S(1)} %get-tuple-element.26), channel_id=1, source_target_pairs={{0,4},{2,6},{4,8},{6,10},{8,12},{10,14},{12,0},{14,2},{1,5},{3,7},... | collective-permute-start | bytes 786440 | tf_op jit(solution)/shard_map/ppermute | solution.py:353
  21.5 9.1 %collective-permute-start.5 = (s32[8,8,128]{2,1,0:T(8,128)S(1)}, s32[8,8,128]{2,1,0:T(8,128)S(1)}, u32[]{:S(2)}, u32[]{:S(2)}) collective-permute-start(s32[8,8,128]{2,1,0:T(8,128)S(1)} %get-tuple-element.25.low_ref), channel_id=1, source_target_pairs={{0,8},{2,10},{4,12},{6,14},{8,0},{10,2},{12,4},{14,6},{1,9},{3,11}... | collective-permute-start | bytes 98312 | tf_op jit(solution)/shard_map/ppermute | solution.py:356
  30.6 3.0 %copy-start.4 = (bf16[128,1024]{1,0:T(8,128)(2,1)}, bf16[128,1024]{1,0:T(8,128)(2,1)S(1)}, u32[]{:S(2)}) copy-start(bf16[128,1024]{1,0:T(8,128)(2,1)S(1)} %collective-permute-done.7.refs_1_.xy_ref) | copy-start | bytes 786436
  30.6 0.7 copy-start.15
  32.4 0.6 copy-start.8
  33.0 12.3 %collective-permute-start.12 = (bf16[128,1024]{1,0:T(8,128)(2,1)S(1)}, bf16[128,1024]{1,0:T(8,128)(2,1)S(1)}, u32[]{:S(2)}, u32[]{:S(2)}) collective-permute-start(bf16[128,1024]{1,0:T(8,128)(2,1)S(1)} %get-tuple-element.30.xz_ref), channel_id=1, source_target_pairs={{0,4},{2,6},{4,8},{6,10},{8,12},{10,14},{12,0},{14,2},{1,5},{3,7},... | collective-permute-start | bytes 786440 | tf_op jit(solution)/shard_map/ppermute | solution.py:353
  33.4 13.2 %collective-permute-start.11 = (bf16[128,1024]{1,0:T(8,128)(2,1)S(1)}, bf16[128,1024]{1,0:T(8,128)(2,1)S(1)}, u32[]{:S(2)}, u32[]{:S(2)}) collective-permute-start(bf16[128,1024]{1,0:T(8,128)(2,1)S(1)} %get-tuple-element.30.xz_ref), channel_id=1, source_target_pairs={{0,2},{2,0},{4,6},{6,4},{8,10},{10,8},{12,14},{14,12},{1,3},{3,1},... | collective-permute-start | bytes 786440 | tf_op jit(solution)/shard_map/ppermute | solution.py:350
  33.7 12.9 %copy-start.7 = (bf16[1024,16]{0,1:T(8,128)(2,1)S(1)}, bf16[1024,16]{0,1:T(8,128)(2,1)}, u32[]{:S(2)}) copy-start(bf16[1024,16]{0,1:T(8,128)(2,1)} %param.15) | copy-start | bytes 98308
  33.7 12.9 %copy-start.9 = (s32[8,8,128]{2,1,0:T(8,128)S(1)}, s32[8,8,128]{2,1,0:T(8,128)}, u32[]{:S(2)}) copy-start(s32[8,8,128]{2,1,0:T(8,128)} %copy-done.8) | copy-start | bytes 98308
  43.5 10.5 %collective-permute-start.10 = (bf16[128,1024]{1,0:T(8,128)(2,1)}, bf16[128,1024]{1,0:T(8,128)(2,1)S(1)}, u32[]{:S(2)}, u32[]{:S(2)}) collective-permute-start(bf16[128,1024]{1,0:T(8,128)(2,1)} %get-tuple-element.29), channel_id=1, source_target_pairs={{0,2},{2,0},{4,6},{6,4},{8,10},{10,8},{12,14},{14,12},{1,3},{3,1},... | collective-permute-start | bytes 786440 | tf_op jit(solution)/shard_map/ppermute | solution.py:350
  45.3 1.0 %copy-start.1 = (bf16[128,1024]{1,0:T(8,128)(2,1)S(1)}, bf16[128,1024]{1,0:T(8,128)(2,1)}, u32[]{:S(2)}) copy-start(bf16[128,1024]{1,0:T(8,128)(2,1)} %get-tuple-element.28.refs_1_.refs_4_.first_ref) | copy-start | bytes 786436
  46.3 11.7 %collective-permute-start.15 = (bf16[128,1024]{1,0:T(8,128)(2,1)S(1)}, bf16[128,1024]{1,0:T(8,128)(2,1)S(1)}, u32[]{:S(2)}, u32[]{:S(2)}) collective-permute-start(bf16[128,1024]{1,0:T(8,128)(2,1)S(1)} %shard_map.128.refs_5_.xz_ref), channel_id=1, source_target_pairs={{0,2},{2,0},{4,6},{6,4},{8,10},{10,8},{12,14},{14,12},{1,3},{3,1},... | collective-permute-start | bytes 786440 | tf_op jit(solution)/shard_map/ppermute | solution.py:350
  46.6 1.0 %copy-start.2 = (bf16[128,1024]{1,0:T(8,128)(2,1)S(1)}, bf16[128,1024]{1,0:T(8,128)(2,1)}, u32[]{:S(2)}) copy-start(bf16[128,1024]{1,0:T(8,128)(2,1)} %get-tuple-element.28.refs_1_.refs_4_.first_ref) | copy-start | bytes 786436
  47.5 6.5 %copy-start.5 = (bf16[1,128,2048]{2,1,0:T(8,128)(2,1)S(1)}, bf16[1,128,2048]{2,1,0:T(8,128)(2,1)}, u32[]{:S(2)}) copy-start(bf16[1,128,2048]{2,1,0:T(8,128)(2,1)} %param.12) | copy-start | bytes 1572868
  47.5 6.5 %copy-start.6 = (bf16[1,128,2048]{2,1,0:T(8,128)(2,1)S(1)}, bf16[1,128,2048]{2,1,0:T(8,128)(2,1)}, u32[]{:S(2)}) copy-start(bf16[1,128,2048]{2,1,0:T(8,128)(2,1)} %param.13) | copy-start | bytes 1572868
  52.3 11.0 %collective-permute-start.17 = (bf16[128,1024]{1,0:T(8,128)(2,1)S(1)}, bf16[128,1024]{1,0:T(8,128)(2,1)S(1)}, u32[]{:S(2)}, u32[]{:S(2)}) collective-permute-start(bf16[128,1024]{1,0:T(8,128)(2,1)S(1)} %get-tuple-element.41), channel_id=1, source_target_pairs={{0,2},{2,0},{4,6},{6,4},{8,10},{10,8},{12,14},{14,12},{1,3},{3,1},... | collective-permute-start | bytes 786440 | tf_op jit(solution)/shard_map/ppermute | solution.py:350
  54.2 27.5 %collective-permute-start.19 = (bf16[128,1024]{1,0:T(8,128)(2,1)S(1)}, bf16[128,1024]{1,0:T(8,128)(2,1)S(1)}, u32[]{:S(2)}, u32[]{:S(2)}) collective-permute-start(bf16[128,1024]{1,0:T(8,128)(2,1)S(1)} %get-tuple-element.38.refs_5_), channel_id=1, source_target_pairs={{0,12},{2,14},{4,0},{6,2},{8,4},{10,6},{12,8},{14,10},{1,13},{3,15... | collective-permute-start | bytes 786440 | tf_op jit(solution)/shard_map/ppermute | solution.py:353
  57.9 5.6 %copy-start.10 = (bf16[1,128,1024]{2,1,0:T(8,128)(2,1)S(1)}, bf16[1,128,1024]{2,1,0:T(8,128)(2,1)}, u32[]{:S(2)}) copy-start(bf16[1,128,1024]{2,1,0:T(8,128)(2,1)} %param.14) | copy-start | bytes 786436
  57.9 13.9 %collective-permute-start.13 = (bf16[128,2048]{1,0:T(8,128)(2,1)S(1)}, bf16[128,2048]{1,0:T(8,128)(2,1)S(1)}, u32[]{:S(2)}, u32[]{:S(2)}) collective-permute-start(bf16[128,2048]{1,0:T(8,128)(2,1)S(1)} %get-tuple-element.36.k_own), channel_id=1, source_target_pairs={{0,1},{1,0},{2,3},{3,2},{4,5},{5,4},{6,7},{7,6},{8,9},{9,8},{10,11... | collective-permute-start | bytes 1572872 | tf_op jit(solution)/shard_map/ppermute | solution.py:347
  62.7 8.8 %collective-permute-start.16 = (bf16[128,1024]{1,0:T(8,128)(2,1)S(1)}, bf16[128,1024]{1,0:T(8,128)(2,1)S(1)}, u32[]{:S(2)}, u32[]{:S(2)}) collective-permute-start(bf16[128,1024]{1,0:T(8,128)(2,1)S(1)} %get-tuple-element.40), channel_id=1, source_target_pairs={{0,2},{2,0},{4,6},{6,4},{8,10},{10,8},{12,14},{14,12},{1,3},{3,1},... | collective-permute-start | bytes 786440 | tf_op jit(solution)/shard_map/ppermute | solution.py:350
  63.3 18.4 %collective-permute-start.20 = (bf16[128,1024]{1,0:T(8,128)(2,1)S(1)}, bf16[128,1024]{1,0:T(8,128)(2,1)S(1)}, u32[]{:S(2)}, u32[]{:S(2)}) collective-permute-start(bf16[128,1024]{1,0:T(8,128)(2,1)S(1)} %shard_map.132.refs_5_), channel_id=1, source_target_pairs={{0,8},{2,10},{4,12},{6,14},{8,0},{10,2},{12,4},{14,6},{1,9},{3,11}... | collective-permute-start | bytes 786440 | tf_op jit(solution)/shard_map/ppermute | solution.py:353
  63.5 8.7 %copy-start.3 = (bf16[1,128,2048]{2,1,0:T(8,128)(2,1)S(1)}, bf16[1,128,2048]{2,1,0:T(8,128)(2,1)}, u32[]{:S(2)}) copy-start(bf16[1,128,2048]{2,1,0:T(8,128)(2,1)} %param.11) | copy-start | bytes 1572868
  63.5 8.7 %copy-start.12 = (s32[1,128]{1,0:T(1,128)S(1)}, s32[1,128]{1,0:T(1,128)}, u32[]{:S(2)}) copy-start(s32[1,128]{1,0:T(1,128)} %doc_own.3) | copy-start | bytes 1540
  63.5 8.8 %copy-start.14 = (s32[1,128]{1,0:T(1,128)S(1)}, s32[1,128]{1,0:T(1,128)}, u32[]{:S(2)}) copy-start(s32[1,128]{1,0:T(1,128)} %ahead_ref.3) | copy-start | bytes 1540
  63.5 8.7 %collective-permute-start.14 = (bf16[128,2048]{1,0:T(8,128)(2,1)S(1)}, bf16[128,2048]{1,0:T(8,128)(2,1)S(1)}, u32[]{:S(2)}, u32[]{:S(2)}) collective-permute-start(bf16[128,2048]{1,0:T(8,128)(2,1)S(1)} %get-tuple-element.37.v_own), channel_id=1, source_target_pairs={{0,1},{1,0},{2,3},{3,2},{4,5},{5,4},{6,7},{7,6},{8,9},{9,8},{10,11... | collective-permute-start | bytes 1572872 | tf_op jit(solution)/shard_map/ppermute | solution.py:347
  71.5 7.9 %collective-permute-start.18 = (bf16[128,1024]{1,0:T(8,128)(2,1)S(1)}, bf16[128,1024]{1,0:T(8,128)(2,1)S(1)}, u32[]{:S(2)}, u32[]{:S(2)}) collective-permute-start(bf16[128,1024]{1,0:T(8,128)(2,1)S(1)} %get-tuple-element.43), channel_id=1, source_target_pairs={{0,2},{2,0},{4,6},{6,4},{8,10},{10,8},{12,14},{14,12},{1,3},{3,1},... | collective-permute-start | bytes 786440 | tf_op jit(solution)/shard_map/ppermute | solution.py:350
  71.8 9.9 %collective-permute-start.21 = (bf16[128,1024]{1,0:T(8,128)(2,1)S(1)}, bf16[128,1024]{1,0:T(8,128)(2,1)S(1)}, u32[]{:S(2)}, u32[]{:S(2)}) collective-permute-start(bf16[128,1024]{1,0:T(8,128)(2,1)S(1)} %shard_map.134.rest_0_), channel_id=1, source_target_pairs={{0,4},{2,6},{4,8},{6,10},{8,12},{10,14},{12,0},{14,2},{1,5},{3,7},... | collective-permute-start | bytes 786440 | tf_op jit(solution)/shard_map/ppermute | solution.py:353

commit v7 on v6

--- a/solution.py
+++ b/solution.py
@@ -13,7 +13,8 @@
 TOPK = 6
 DENSE_EXPERTS = 16
 EXPERT_VMEM = 26 * 1024 * 1024
-FIRST_VMEM = 40 * 1024 * 1024
+FIRST_VMEM = 26 * 1024 * 1024
+LOAD_VMEM = 44 * 1024 * 1024
 ATTEND_VMEM = 8 * 1024 * 1024
 SMALL_VMEM = 4 * 1024 * 1024
 WINDOW = 4
@@ -136,6 +137,36 @@
     return out if through else out[0]
 
 
+def load_kernel(w1_any, w2_any, *refs):
+    w1_ref, w2_ref, sems = refs[-3:]
+    loads = []
+    for index, (source, target) in enumerate(((w1_any, w1_ref), (w2_any, w2_ref))):
+        rows = source.shape[0] // 2
+        for half in range(2):
+            part = pl.ds(half * rows, rows)
+            loads.append(
+                pltpu.make_async_copy(source.at[part], target.at[part], sems.at[2 * index + half])
+            )
+    for load in loads:
+        load.start()
+    for load in loads:
+        load.wait()
+
+
+def load_weights(w_first, w_second, after):
+    hbm = pl.BlockSpec(memory_space=pltpu.HBM)
+    anywhere = pl.BlockSpec(memory_space=pl.ANY)
+    vmem = pl.BlockSpec(memory_space=pltpu.VMEM)
+    return pl.pallas_call(
+        load_kernel,
+        out_shape=[pltpu.VMEM(w.shape, w.dtype) for w in (w_first, w_second)],
+        in_specs=[hbm] * 2 + [anywhere] * len(after),
+        out_specs=[vmem] * 2,
+        scratch_shapes=[pltpu.SemaphoreType.DMA((4,))],
+        compiler_params=pltpu.CompilerParams(vmem_limit_bytes=LOAD_VMEM),
+    )(w_first, w_second, *after)
+
+
 def behind_kernel(*refs):
     pass
 
@@ -164,8 +195,13 @@
         jnp.int32, (rows, rows), 1
     )
     upto = jnp.where(upto, 1.0, 0.0).astype(jnp.bfloat16)
-    device = lax.broadcasted_iota(jnp.int32, (sources, sources), 0) ^ own
-    other = lax.broadcasted_iota(jnp.int32, (sources, sources), 1) ^ own
+
+    def device_of(entry):
+        flips = 4 * lax.rem(entry, line) + 2 * lax.rem(lax.div(entry, line), 2)
+        return own ^ (flips + lax.div(entry, 2 * line))
+
+    device = device_of(lax.broadcasted_iota(jnp.int32, (sources, sources), 0))
+    other = device_of(lax.broadcasted_iota(jnp.int32, (sources, sources), 1))
     lower = jnp.where(other < device, 1.0, 0.0).astype(jnp.bfloat16)
     entry = lax.broadcasted_iota(jnp.int32, (sources, rows), 0)
     named = []
@@ -185,9 +221,9 @@
         limit = capacity_ref[expert].astype(jnp.float32)
         kept.append(jnp.where(mine & (slots < limit), 1, 0))
     for step in range(line):
-        home = 4 * (z ^ lax.rem(z + line - step, line))
+        home = z ^ lax.rem(z + line - step, line)
         for side in range(2):
-            here = entry == home + 2 * side
+            here = entry == home + line * side
             for k, part in enumerate(named + kept):
                 picked = jnp.sum(jnp.where(here, part, 0), axis=0, keepdims=True)
                 out_ref[2 * step + side, k : k + 1, :] = picked
@@ -232,11 +268,12 @@
     step = 512
     if first:
         sources = refs[:4]
-        z_ref, y_ref, *weights, hidden_ref, mixed_ref, sems = refs[-9:]
+        z_ref, y_ref, *staged, hidden_ref, mixed_ref, sems = refs[-7:]
+        weights = list(refs[:2]) + staged
     else:
         weights = refs[:4]
         z_ref, y_ref, hidden_ref, mixed_ref = refs[-4:]
-    chunks = [(w, c) for w in range(4) for c in range(0, weights[w].shape[1], step)]
+    chunks = [(w, c) for w in (2, 3) for c in range(0, weights[w].shape[1], step)]
 
     def load(index):
         which, column = chunks[index]
@@ -246,7 +283,7 @@
         )
 
     def ready(which, column):
-        if first:
+        if first and which > 1:
             index = chunks.index((which, column))
             load(index).wait()
             if index + WINDOW < len(chunks):
@@ -291,17 +328,17 @@
     hbm = pl.BlockSpec(memory_space=pltpu.HBM)
     anywhere = pl.BlockSpec(memory_space=pl.ANY)
     piece = jax.ShapeDtypeStruct((rows, width), jnp.bfloat16)
-    staged = [pltpu.VMEM(w.shape, w.dtype) for w in weights] if first else []
+    staged = [pltpu.VMEM(w.shape, w.dtype) for w in weights[2:]] if first else []
     scratch = [
         pltpu.VMEM((2, 2 * rows, hidden), jnp.bfloat16),
         pltpu.VMEM((2 * rows, width), jnp.float32),
     ]
     if first:
-        scratch.append(pltpu.SemaphoreType.DMA((4 * (hidden + width) // 1024,)))
+        scratch.append(pltpu.SemaphoreType.DMA(((hidden + width) // 512,)))
     return pl.pallas_call(
         functools.partial(expert_kernel, place, first),
         out_shape=[piece, piece] + staged,
-        in_specs=[smem] + [vmem] * 4 + [hbm if first else vmem] * 4 + [anywhere] * len(after),
+        in_specs=[smem] + [vmem] * 6 + [hbm if first else vmem] * 2 + [anywhere] * len(after),
         out_specs=[vmem] * (2 + len(staged)),
         scratch_shapes=scratch,
         compiler_params=pltpu.CompilerParams(vmem_limit_bytes=FIRST_VMEM if first else EXPERT_VMEM),
@@ -356,29 +393,33 @@
         return lax.ppermute(x, "expert", [(2 * z + y, 2 * (z ^ span) + y) for z, y in spots])
 
     own = lax.axis_index(("expert", "context")).astype(jnp.int32).reshape(1)
-    own_weights = (expert_in[0], expert_out[0])
-    weights = own_weights + (swap_core(own_weights[0]), swap_core(own_weights[1]))
+    far_weights = [swap_core(expert_in[0]), swap_core(expert_out[0])]
 
     arriving, beside_own = along(latent[0], 1), swap_side(latent[0])
-    tile = pack(routes.transpose(2, 0, 1), segments)
-    beside = swap_core(tile)
-    doc_far = beside[0, TOPK : TOPK + 1, :]
-    table = join(tile, beside)
-    arriving, table = join(table, swap_side(table), passed=arriving, after=(beside_own,))
-    from_side = [beside_own, swap_side(arriving)]
-    passed, table = join(table, flipped(table, 1), passed=arriving, copy=True)
-    flip = flipped(table, 2)
-    kept, passed = kept_rows(own, capacity, table, flip, along(passed, 1), (from_side[1],))
+    table = pack(routes.transpose(2, 0, 1), segments)
+    span = 1
+    while 2 * span < line:
+        table = join(table, flipped(table, span))
+        span *= 2
+    arriving, table = join(table, flipped(table, span), passed=arriving, after=(beside_own,))
+    across_table = swap_side(table)
+    chained = along(arriving, 1)
+    passed, table = join(table, across_table, passed=arriving, copy=True)
+    far_table = swap_core(table)
+    from_side = [beside_own, swap_side(passed)]
+    kept, passed = kept_rows(own, capacity, table, far_table, chained, ())
+    doc_far = far_table[0, TOPK : TOPK + 1, :]
     from_line = [latent[0], arriving, passed]
+    last = along(passed, 1)
     from_side.append(swap_side(passed))
-    last = along(passed, 1)
+    weights = list(load_weights(expert_in[0], expert_out[0], (kept,))) + far_weights
 
     def piece(step, weights, *after):
         return run_piece(
             step, step == 1, own, kept, router.T, from_line[step], from_side[step], weights, after
         )
 
-    one, theirs, *weights = piece(1, weights)
+    one, theirs, *weights[2:] = piece(1, weights)
     one_far = swap_side(theirs)
     last = behind(last, (one,))
     from_line.append(last)

time: 82.9 us -> 79 us (0.953)
  waiting for transfers between devices: 32.6 us -> 20.3 us
  starting transfers between devices: 15.1 us -> 26.7 us
  local copies, waits for them, and re-layouts: 4.55 us -> 2.02 us
    ppermute x2, waiting for transfers between devices: 12.7 us -> 4.5 us  [flipped(): lax.ppermute(x, 'expert', [(2 * z + y, 2 * (z ^ span) + y) for z, y in sp...]
    ppermute x5, waiting for transfers between devices: 6.75 us -> 1.22 us  [swap_core(): return lax.ppermute(x, 'context', sibling)]
    ppermute x2, starting transfers between devices: 0.14 us -> 4.94 us  [flipped(): lax.ppermute(x, 'expert', [(2 * z + y, 2 * (z ^ span) + y) for z, y in sp...]
    ppermute x6, starting transfers between devices: 6.22 us -> 10.8 us  [along(): lax.ppermute(x, 'expert', [(2 * z + y, 2 * ((z + step) % line) + y) for z...]
    ppermute x6, waiting for transfers between devices: 2.33 us -> 6.45 us  [along(): lax.ppermute(x, 'expert', [(2 * z + y, 2 * ((z + step) % line) + y) for z...]
    pallas_call x4, Pallas kernels: 24 us -> 19.9 us  [run_piece(): pl.pallas_call(functools.partial(expert_kernel, place, first), out_shape=...]
    pallas_call x0 -> x1, Pallas kernels: none -> 3.51 us  [load_weights(): pl.pallas_call(load_kernel, out_shape=[pltpu.VMEM(w.shape, w.dtype) for w...]
    ppermute x9, waiting for transfers between devices: 10.9 us -> 8.16 us  [swap_side(): return lax.ppermute(x, 'expert', across)]
  transfers between devices with their start and end apart: 22 -> 22, of which waited for: 7 -> 9; matrix products, arithmetic and copies ran while one was open for 0% -> 0% of each run, Pallas kernels for 35% -> 35%
where the time goes in v7:
time: 79 us; the launch traced here: 78.8 us
  Pallas kernels  28 us (35%)
  starting transfers between devices  26.7 us (34%)
  waiting for transfers between devices  20.3 us (26%)
  local copies, waits for them, and re-layouts  2.02 us (3%)
  other arithmetic  0.92 us (1%)
  between operations  0.82 us (1%)
    pallas_call x4, Pallas kernels, run_piece(): pl.pallas_call(functools.partial(expert_kernel, place, first), out_shape=...  19.9 us
    ppermute x6, starting transfers between devices, along(): lax.ppermute(x, 'expert', [(2 * z + y, 2 * ((z + step) % line) + y) for z...  10.8 us
    ppermute x9, starting transfers between devices, swap_side(): return lax.ppermute(x, 'expert', across)  10.4 us
    ppermute x9, waiting for transfers between devices, swap_side(): return lax.ppermute(x, 'expert', across)  8.16 us
    ppermute x6, waiting for transfers between devices, along(): lax.ppermute(x, 'expert', [(2 * z + y, 2 * ((z + step) % line) + y) for z...  6.45 us
    ppermute x2, starting transfers between devices, flipped(): lax.ppermute(x, 'expert', [(2 * z + y, 2 * (z ^ span) + y) for z, y in sp...  4.94 us
    ppermute x2, waiting for transfers between devices, flipped(): lax.ppermute(x, 'expert', [(2 * z + y, 2 * (z ^ span) + y) for z, y in sp...  4.5 us
    pallas_call x1, Pallas kernels, load_weights(): pl.pallas_call(load_kernel, out_shape=[pltpu.VMEM(w.shape, w.dtype) for w...  3.51 us
  transfers between devices with their start and end apart: 22, of which 9 were waited for; matrix products, arithmetic and copies ran while one was open for 0% of the time, Pallas kernels for 35%

profile of v7, /device:TPU:0, one launch (start us, length us, event | category | flops | bytes accessed | tf_op | source)
XLA Modules:
  0.0 78.8 jit_solution(12340044217844029524)
XLA Ops:
  0.6 0.5 collective-permute-start.8
  1.1 0.1 collective-permute-start.9
  1.2 2.9 %collective-permute-start.3 = (bf16[128,1024]{1,0:T(8,128)(2,1)}, bf16[128,1024]{1,0:T(8,128)(2,1)S(1)}, u32[]{:S(2)}, u32[]{:S(2)}) collective-permute-start(bf16[128,1024]{1,0:T(8,128)(2,1)} %bitcast.23), channel_id=1, source_target_pairs={{0,2},{2,0},{4,6},{6,4},{8,10},{10,8},{12,14},{14,12},{1,3},{3,1},... | collective-permute-start | bytes 786440 | tf_op jit(solution)/shard_map/ppermute | solution.py:387
  4.2 1.6 %collective-permute-start.2 = (bf16[128,1024]{1,0:T(8,128)(2,1)}, bf16[128,1024]{1,0:T(8,128)(2,1)S(1)}, u32[]{:S(2)}, u32[]{:S(2)}) collective-permute-start(bf16[128,1024]{1,0:T(8,128)(2,1)} %bitcast.24), channel_id=1, source_target_pairs={{0,4},{2,6},{4,8},{6,10},{8,12},{10,14},{12,0},{14,2},{1,5},{3,7},... | collective-permute-start | bytes 786440 | tf_op jit(solution)/shard_map/ppermute | solution.py:390
  5.8 0.7 copy-done.5
  6.4 0.7 copy-done.7
  7.1 1.6 %collective-permute-start = (s32[1,8,128]{2,1,0:T(8,128)S(1)}, s32[1,8,128]{2,1,0:T(8,128)S(1)}, u32[]{:S(2)}, u32[]{:S(2)}) collective-permute-start(s32[1,8,128]{2,1,0:T(8,128)S(1)} %shard_map.122.first_ref), channel_id=1, source_target_pairs={{0,4},{2,6},{4,0},{6,2},{8,12},{10,14},{12,8},{14,10},{1,5},{3,7},... | collective-permute-start | bytes 12296 | tf_op jit(solution)/shard_map/ppermute | solution.py:393
  8.8 2.9 %collective-permute-done.second_ref = s32[1,8,128]{2,1,0:T(8,128)S(1)} collective-permute-done((s32[1,8,128]{2,1,0:T(8,128)S(1)}, s32[1,8,128]{2,1,0:T(8,128)S(1)}, u32[]{:S(2)}, u32[]{:S(2)}) %collective-permute-start) | collective-permute-done | bytes 4128 | tf_op jit(solution)/shard_map/ppermute | solution.py:393
  11.6 3.3 %collective-permute-start.1 = (s32[2,8,128]{2,1,0:T(8,128)S(1)}, s32[2,8,128]{2,1,0:T(8,128)S(1)}, u32[]{:S(2)}, u32[]{:S(2)}) collective-permute-start(s32[2,8,128]{2,1,0:T(8,128)S(1)} %shard_map.123.first_ref), channel_id=1, source_target_pairs={{0,8},{2,10},{4,12},{6,14},{8,0},{10,2},{12,4},{14,6},{1,9},{3,11}... | collective-permute-start | bytes 24584 | tf_op jit(solution)/shard_map/ppermute | solution.py:393
  14.9 1.6 %collective-permute-done.1.second_ref = s32[2,8,128]{2,1,0:T(8,128)S(1)} collective-permute-done((s32[2,8,128]{2,1,0:T(8,128)S(1)}, s32[2,8,128]{2,1,0:T(8,128)S(1)}, u32[]{:S(2)}, u32[]{:S(2)}) %collective-permute-start.1) | collective-permute-done | bytes 8224 | tf_op jit(solution)/shard_map/ppermute | solution.py:393
  16.6 0.0 collective-permute-done.3.refs_1_.xy_ref
  16.6 0.0 collective-permute-done.2.refs_0_
  16.6 0.6 collective-permute-start.4
  17.2 2.0 %collective-permute-start.6 = (bf16[128,1024]{1,0:T(8,128)(2,1)S(1)}, bf16[128,1024]{1,0:T(8,128)(2,1)S(1)}, u32[]{:S(2)}, u32[]{:S(2)}) collective-permute-start(bf16[128,1024]{1,0:T(8,128)(2,1)S(1)} %get-tuple-element.24.rows_ref.xz_ref), channel_id=1, source_target_pairs={{0,4},{2,6},{4,8},{6,10},{8,12},{10,14},{12,0},{14,2},{1,5},{3,7},... | collective-permute-start | bytes 786440 | tf_op jit(solution)/shard_map/ppermute | solution.py:390
  19.2 1.4 %collective-permute-done.4.second_ref = s32[4,8,128]{2,1,0:T(8,128)S(1)} collective-permute-done((s32[4,8,128]{2,1,0:T(8,128)S(1)}, s32[4,8,128]{2,1,0:T(8,128)S(1)}, u32[]{:S(2)}, u32[]{:S(2)}) %collective-permute-start.4) | collective-permute-done | bytes 16416 | tf_op jit(solution)/shard_map/ppermute | solution.py:387
  20.6 0.5 collective-permute-start.7
  21.1 0.0 collective-permute-start.5
  21.1 1.2 %collective-permute-done.5.high_ref = s32[8,8,128]{2,1,0:T(8,128)S(1)} collective-permute-done((s32[8,8,128]{2,1,0:T(8,128)S(1)}, s32[8,8,128]{2,1,0:T(8,128)S(1)}, u32[]{:S(2)}, u32[]{:S(2)}) %collective-permute-start.5) | collective-permute-done | bytes 32800 | tf_op jit(solution)/shard_map/ppermute | solution.py:384
  22.3 3.3 %collective-permute-done.6.refs_0_ = bf16[128,1024]{1,0:T(8,128)(2,1)S(1)} collective-permute-done((bf16[128,1024]{1,0:T(8,128)(2,1)S(1)}, bf16[128,1024]{1,0:T(8,128)(2,1)S(1)}, u32[]{:S(2)}, u32[]{:S(2)}) %collective-permute-start.6) | collective-permute-done | bytes 262176 | tf_op jit(solution)/shard_map/ppermute | solution.py:390
  25.6 0.7 copy-done.9
  26.2 1.1 %shard_map.126 = (s32[8,8,128]{2,1,0:T(8,128)S(1)}, bf16[128,1024]{1,0:T(8,128)(2,1)S(1)}) custom-call(s32[1]{0:T(128)} %bitcast.2.own_ref, s32[16]{0:T(128)S(1)} %copy-done.9, s32[8,8,128]{2,1,0:T(8,128)S(1)} %get-tuple-element.25.low_ref, s32[8,8,128]{2,1,0:T(8,128)S(1)} %collective-permute-done.5.high_ref, ...), custom_call_target="tpu_custom_call", output_to_operand_aliasing={{1}: (4, {})} | custom-call | tf_op jit(solution)/shard_map/pallas_call | solution.py:236
  27.3 0.1 collective-permute-start.12
  27.4 1.6 %collective-permute-start.11 = (bf16[128,1024]{1,0:T(8,128)(2,1)S(1)}, bf16[128,1024]{1,0:T(8,128)(2,1)S(1)}, u32[]{:S(2)}, u32[]{:S(2)}) collective-permute-start(bf16[128,1024]{1,0:T(8,128)(2,1)S(1)} %get-tuple-element.32.xz_ref), channel_id=1, source_target_pairs={{0,2},{2,0},{4,6},{6,4},{8,10},{10,8},{12,14},{14,12},{1,3},{3,1},... | collective-permute-start | bytes 786440 | tf_op jit(solution)/shard_map/ppermute | solution.py:387
  29.0 3.5 %shard_map.127 = (bf16[1024,2048]{1,0:T(8,128)(2,1)S(1)}, bf16[2048,1024]{1,0:T(8,128)(2,1)S(1)}) custom-call(bf16[1024,2048]{1,0:T(8,128)(2,1)} %bitcast.28, bf16[2048,1024]{1,0:T(8,128)(2,1)} %bitcast.30, s32[8,8,128]{2,1,0:T(8,128)S(1)} %get-tuple-element.26.refs_0_.kept_ref), custom_call_target="tpu_custom_call" | custom-call | tf_op jit(solution)/shard_map/pallas_call | solution.py:160
  32.5 0.0 collective-permute-done.7.xy_ref
  32.5 0.0 collective-permute-done.8.refs_2_
  32.5 0.0 collective-permute-done.9.refs_3_
  32.5 0.0 copy-done.3
  32.5 5.8 %shard_map.128 = (bf16[128,1024]{1,0:T(8,128)(2,1)S(1)}, bf16[128,1024]{1,0:T(8,128)(2,1)S(1)}, bf16[1024,2048]{1,0:T(8,128)(2,1)S(1)}, bf16[2048,1024]{1,0:T(8,128)(2,1)S(1)}) custom-call(s32[1]{0:T(128)} %bitcast.2.own_ref, s32[8,8,128]{2,1,0:T(8,128)S(1)} %get-tuple-element.26.refs_0_.kept_ref, bf16[16,1024]{1,0:T(8,128)(2,1)S(1)} %bitcast.19, ...), custom_call_target="tpu_custom_call" | custom-call | flops 4294967296 | bytes 1048576 | tf_op jit(solution)/shard_map/pallas_call | solution.py:338
  38.3 0.6 collective-permute-start.10
  38.9 0.0 collective-permute-done.12.refs_0_
  38.9 1.5 %collective-permute-start.15 = (bf16[128,1024]{1,0:T(8,128)(2,1)S(1)}, bf16[128,1024]{1,0:T(8,128)(2,1)S(1)}, u32[]{:S(2)}, u32[]{:S(2)}) collective-permute-start(bf16[128,1024]{1,0:T(8,128)(2,1)S(1)} %shard_map.129.refs_5_.xz_ref), channel_id=1, source_target_pairs={{0,2},{2,0},{4,6},{6,4},{8,10},{10,8},{12,14},{14,12},{1,3},{3,1},... | collective-permute-start | bytes 786440 | tf_op jit(solution)/shard_map/ppermute | solution.py:387
  40.4 0.0 collective-permute-done.11.xy_ref
  40.4 4.7 %shard_map.130 = (bf16[128,1024]{1,0:T(8,128)(2,1)S(1)}, bf16[128,1024]{1,0:T(8,128)(2,1)S(1)}) custom-call(s32[1]{0:T(128)} %bitcast.2.own_ref, s32[8,8,128]{2,1,0:T(8,128)S(1)} %get-tuple-element.26.refs_0_.kept_ref, bf16[16,1024]{1,0:T(8,128)(2,1)S(1)} %bitcast.20, bf16[128,1024]{1,0:T(8,128)(2,1)S(1)} %get-tuple-element.32.xz_ref, ...), custom_call_target="tpu_custom_call" | custom-call | flops 4294967296 | bytes 1048576 | tf_op jit(solution)/shard_map/pallas_call | solution.py:338
  45.2 0.6 collective-permute-start.17
  45.7 1.9 %collective-permute-done.10.second_ref = bf16[128,1024]{1,0:T(8,128)(2,1)S(1)} collective-permute-done((bf16[128,1024]{1,0:T(8,128)(2,1)S(1)}, bf16[128,1024]{1,0:T(8,128)(2,1)S(1)}, u32[]{:S(2)}, u32[]{:S(2)}) %collective-permute-start.10) | collective-permute-done | bytes 262176 | tf_op jit(solution)/shard_map/ppermute | solution.py:387
  47.7 0.0 copy-done.1
  47.7 0.0 copy-done.2
  47.7 0.1 shard_map.131
  47.8 4.0 %collective-permute-start.19 = (bf16[128,1024]{1,0:T(8,128)(2,1)S(1)}, bf16[128,1024]{1,0:T(8,128)(2,1)S(1)}, u32[]{:S(2)}, u32[]{:S(2)}) collective-permute-start(bf16[128,1024]{1,0:T(8,128)(2,1)S(1)} %get-tuple-element.38.refs_5_), channel_id=1, source_target_pairs={{0,12},{2,14},{4,0},{6,2},{8,4},{10,6},{12,8},{14,10},{1,13},{3,15... | collective-permute-start | bytes 786440 | tf_op jit(solution)/shard_map/ppermute | solution.py:390
  51.7 0.0 collective-permute-start.13
  51.7 1.5 %collective-permute-done.15.xy_ref = bf16[128,1024]{1,0:T(8,128)(2,1)S(1)} collective-permute-done((bf16[128,1024]{1,0:T(8,128)(2,1)S(1)}, bf16[128,1024]{1,0:T(8,128)(2,1)S(1)}, u32[]{:S(2)}, u32[]{:S(2)}) %collective-permute-start.15) | collective-permute-done | bytes 262176 | tf_op jit(solution)/shard_map/ppermute | solution.py:387
  53.3 4.7 %shard_map.132 = (bf16[128,1024]{1,0:T(8,128)(2,1)S(1)}, bf16[128,1024]{1,0:T(8,128)(2,1)S(1)}) custom-call(s32[1]{0:T(128)} %bitcast.2.own_ref, s32[8,8,128]{2,1,0:T(8,128)S(1)} %get-tuple-element.26.refs_0_.kept_ref, bf16[16,1024]{1,0:T(8,128)(2,1)S(1)} %bitcast.21, bf16[128,1024]{1,0:T(8,128)(2,1)S(1)} %shard_map.129.refs_5_.xz_ref, ...), custom_call_target="tpu_custom_call" | custom-call | flops 4294967296 | bytes 1048576 | tf_op jit(solution)/shard_map/pallas_call | solution.py:338
  58.0 0.6 collective-permute-start.16
  58.6 0.0 collective-permute-done.17.second_ref
  58.6 0.1 shard_map.133.refs_5_
  58.6 2.6 %collective-permute-start.20 = (bf16[128,1024]{1,0:T(8,128)(2,1)S(1)}, bf16[128,1024]{1,0:T(8,128)(2,1)S(1)}, u32[]{:S(2)}, u32[]{:S(2)}) collective-permute-start(bf16[128,1024]{1,0:T(8,128)(2,1)S(1)} %shard_map.133.refs_5_), channel_id=1, source_target_pairs={{0,8},{2,10},{4,12},{6,14},{8,0},{10,2},{12,4},{14,6},{1,9},{3,11}... | collective-permute-start | bytes 786440 | tf_op jit(solution)/shard_map/ppermute | solution.py:390
  61.2 0.0 collective-permute-start.14
  61.2 0.0 copy-done.4
  61.2 4.7 %shard_map.134 = (bf16[128,1024]{1,0:T(8,128)(2,1)S(1)}, bf16[128,1024]{1,0:T(8,128)(2,1)S(1)}) custom-call(s32[1]{0:T(128)} %bitcast.2.own_ref, s32[8,8,128]{2,1,0:T(8,128)S(1)} %get-tuple-element.26.refs_0_.kept_ref, bf16[16,1024]{1,0:T(8,128)(2,1)S(1)} %bitcast.22, bf16[128,1024]{1,0:T(8,128)(2,1)S(1)} %bitcast.25, ...), custom_call_target="tpu_custom_call" | custom-call | flops 4294967296 | bytes 1048576 | tf_op jit(solution)/shard_map/pallas_call | solution.py:338
  65.9 0.0 collective-permute-done.16.second_ref
  65.9 1.6 %collective-permute-start.18 = (bf16[128,1024]{1,0:T(8,128)(2,1)S(1)}, bf16[128,1024]{1,0:T(8,128)(2,1)S(1)}, u32[]{:S(2)}, u32[]{:S(2)}) collective-permute-start(bf16[128,1024]{1,0:T(8,128)(2,1)S(1)} %get-tuple-element.43), channel_id=1, source_target_pairs={{0,2},{2,0},{4,6},{6,4},{8,10},{10,8},{12,14},{14,12},{1,3},{3,1},... | collective-permute-start | bytes 786440 | tf_op jit(solution)/shard_map/ppermute | solution.py:387
  67.5 0.1 shard_map.135.rest_0_
  67.6 0.0 collective-permute-done.13.k_far
  67.6 0.6 collective-permute-start.21
  68.2 0.0 collective-permute-done.14.v_far
  68.2 0.0 copy-done
  68.2 1.6 %shard_map.136.rest_0_ = bf16[128,2048]{1,0:T(8,128)(2,1)} custom-call(s32[1]{0:T(128)} %bitcast.place_ref, bf16[128,2048]{1,0:T(8,128)(2,1)S(1)} %bitcast.15, bf16[128,2048]{1,0:T(8,128)(2,1)S(1)} %get-tuple-element.36.k_own, bf16[128,2048]{1,0:T(8,128)(2,1)S(1)} %collective-permute-done.13.k_far, bf16[128,2048]{1,0:T(8,128)(2,1)S(1)} %get-tuple-element.37.v_own, ...), custom_call_target="tpu_custom_call" | custom-call | flops 134217728 | bytes 1572864 | tf_op jit(solution)/shard_map/pallas_call | solution.py:67
  69.8 1.6 %shard_map.137 = bf16[128,2048]{1,0:T(8,128)(2,1)} custom-call(s32[1]{0:T(128)} %bitcast.place_ref, bf16[128,2048]{1,0:T(8,128)(2,1)S(1)} %bitcast.16, bf16[128,2048]{1,0:T(8,128)(2,1)S(1)} %get-tuple-element.36.k_own, bf16[128,2048]{1,0:T(8,128)(2,1)S(1)} %collective-permute-done.13.k_far, ...), custom_call_target="tpu_custom_call", output_to_operand_aliasing={{}: (9, {})} | custom-call | flops 134217728 | bytes 1572864 | tf_op jit(solution)/shard_map/pallas_call | solution.py:67
  71.4 3.3 %collective-permute-done.18 = bf16[128,1024]{1,0:T(8,128)(2,1)S(1)} collective-permute-done((bf16[128,1024]{1,0:T(8,128)(2,1)S(1)}, bf16[128,1024]{1,0:T(8,128)(2,1)S(1)}, u32[]{:S(2)}, u32[]{:S(2)}) %collective-permute-start.18) | collective-permute-done | bytes 262176 | tf_op jit(solution)/shard_map/ppermute | solution.py:387
  74.7 0.0 collective-permute-done.20
  74.7 0.0 collective-permute-done.19
  74.7 3.1 %collective-permute-done.21 = bf16[128,1024]{1,0:T(8,128)(2,1)S(1)} collective-permute-done((bf16[128,1024]{1,0:T(8,128)(2,1)S(1)}, bf16[128,1024]{1,0:T(8,128)(2,1)S(1)}, u32[]{:S(2)}, u32[]{:S(2)}) %collective-permute-start.21) | collective-permute-done | bytes 262176 | tf_op jit(solution)/shard_map/ppermute | solution.py:390
  77.9 0.9 %fusion = bf16[1,128,1024]{2,1,0:T(8,128)(2,1)} fusion(bf16[128,1024]{1,0:T(8,128)(2,1)S(1)} %collective-permute-done.21, bf16[128,1024]{1,0:T(8,128)(2,1)S(1)} %collective-permute-done.20, bf16[128,1024]{1,0:T(8,128)(2,1)S(1)} %collective-permute-done.19, bf16[128,1024]{1,0:T(8,128)(2,1)S(1)} %collective-permute-done.18, ...), kind=kLoop, calls=%fused_computation.1 | loop fusion | flops 1310720 | bytes 1572864 | tf_op jit(solution)/shard_map/broadcast_in_dim | solution.py:445
  (18 shorter events, 0.1 us)
Async XLA Ops:
  0.6 31.9 %collective-permute-start.8 = (bf16[1024,2048]{1,0:T(8,128)(2,1)}, bf16[1024,2048]{1,0:T(8,128)(2,1)}, u32[]{:S(2)}, u32[]{:S(2)}) collective-permute-start(bf16[1024,2048]{1,0:T(8,128)(2,1)} %bitcast.27), channel_id=1, source_target_pairs={{0,1},{1,0},{2,3},{3,2},{4,5},{5,4},{6,7},{7,6},{8,9},{9,8},{10,11... | collective-permute-start | bytes 12582920 | tf_op jit(solution)/shard_map/ppermute | solution.py:384
  1.1 31.4 %collective-permute-start.9 = (bf16[2048,1024]{1,0:T(8,128)(2,1)}, bf16[2048,1024]{1,0:T(8,128)(2,1)}, u32[]{:S(2)}, u32[]{:S(2)}) collective-permute-start(bf16[2048,1024]{1,0:T(8,128)(2,1)} %bitcast.29), channel_id=1, source_target_pairs={{0,1},{1,0},{2,3},{3,2},{4,5},{5,4},{6,7},{7,6},{8,9},{9,8},{10,11... | collective-permute-start | bytes 12582920 | tf_op jit(solution)/shard_map/ppermute | solution.py:384
  1.2 15.3 %collective-permute-start.3 = (bf16[128,1024]{1,0:T(8,128)(2,1)}, bf16[128,1024]{1,0:T(8,128)(2,1)S(1)}, u32[]{:S(2)}, u32[]{:S(2)}) collective-permute-start(bf16[128,1024]{1,0:T(8,128)(2,1)} %bitcast.23), channel_id=1, source_target_pairs={{0,2},{2,0},{4,6},{6,4},{8,10},{10,8},{12,14},{14,12},{1,3},{3,1},... | collective-permute-start | bytes 786440 | tf_op jit(solution)/shard_map/ppermute | solution.py:387
  4.2 12.4 %collective-permute-start.2 = (bf16[128,1024]{1,0:T(8,128)(2,1)}, bf16[128,1024]{1,0:T(8,128)(2,1)S(1)}, u32[]{:S(2)}, u32[]{:S(2)}) collective-permute-start(bf16[128,1024]{1,0:T(8,128)(2,1)} %bitcast.24), channel_id=1, source_target_pairs={{0,4},{2,6},{4,8},{6,10},{8,12},{10,14},{12,0},{14,2},{1,5},{3,7},... | collective-permute-start | bytes 786440 | tf_op jit(solution)/shard_map/ppermute | solution.py:390
  5.7 0.7 copy-start.5
  6.4 0.7 copy-start.7
  7.1 4.5 %collective-permute-start = (s32[1,8,128]{2,1,0:T(8,128)S(1)}, s32[1,8,128]{2,1,0:T(8,128)S(1)}, u32[]{:S(2)}, u32[]{:S(2)}) collective-permute-start(s32[1,8,128]{2,1,0:T(8,128)S(1)} %shard_map.122.first_ref), channel_id=1, source_target_pairs={{0,4},{2,6},{4,0},{6,2},{8,12},{10,14},{12,8},{14,10},{1,5},{3,7},... | collective-permute-start | bytes 12296 | tf_op jit(solution)/shard_map/ppermute | solution.py:393
  11.6 4.9 %collective-permute-start.1 = (s32[2,8,128]{2,1,0:T(8,128)S(1)}, s32[2,8,128]{2,1,0:T(8,128)S(1)}, u32[]{:S(2)}, u32[]{:S(2)}) collective-permute-start(s32[2,8,128]{2,1,0:T(8,128)S(1)} %shard_map.123.first_ref), channel_id=1, source_target_pairs={{0,8},{2,10},{4,12},{6,14},{8,0},{10,2},{12,4},{14,6},{1,9},{3,11}... | collective-permute-start | bytes 24584 | tf_op jit(solution)/shard_map/ppermute | solution.py:393
  16.6 4.0 %collective-permute-start.4 = (s32[4,8,128]{2,1,0:T(8,128)S(1)}, s32[4,8,128]{2,1,0:T(8,128)S(1)}, u32[]{:S(2)}, u32[]{:S(2)}) collective-permute-start(s32[4,8,128]{2,1,0:T(8,128)S(1)} %get-tuple-element.23.first_ref), channel_id=1, source_target_pairs={{0,2},{2,0},{4,6},{6,4},{8,10},{10,8},{12,14},{14,12},{1,3},{3,1},... | collective-permute-start | bytes 49160 | tf_op jit(solution)/shard_map/ppermute | solution.py:387
  17.2 8.4 %collective-permute-start.6 = (bf16[128,1024]{1,0:T(8,128)(2,1)S(1)}, bf16[128,1024]{1,0:T(8,128)(2,1)S(1)}, u32[]{:S(2)}, u32[]{:S(2)}) collective-permute-start(bf16[128,1024]{1,0:T(8,128)(2,1)S(1)} %get-tuple-element.24.rows_ref.xz_ref), channel_id=1, source_target_pairs={{0,4},{2,6},{4,8},{6,10},{8,12},{10,14},{12,0},{14,2},{1,5},{3,7},... | collective-permute-start | bytes 786440 | tf_op jit(solution)/shard_map/ppermute | solution.py:390
  20.6 11.9 %collective-permute-start.7 = (bf16[128,1024]{1,0:T(8,128)(2,1)S(1)}, bf16[128,1024]{1,0:T(8,128)(2,1)S(1)}, u32[]{:S(2)}, u32[]{:S(2)}) collective-permute-start(bf16[128,1024]{1,0:T(8,128)(2,1)S(1)} %get-tuple-element.27), channel_id=1, source_target_pairs={{0,2},{2,0},{4,6},{6,4},{8,10},{10,8},{12,14},{14,12},{1,3},{3,1},... | collective-permute-start | bytes 786440 | tf_op jit(solution)/shard_map/ppermute | solution.py:387
  21.1 1.2 %collective-permute-start.5 = (s32[8,8,128]{2,1,0:T(8,128)S(1)}, s32[8,8,128]{2,1,0:T(8,128)S(1)}, u32[]{:S(2)}, u32[]{:S(2)}) collective-permute-start(s32[8,8,128]{2,1,0:T(8,128)S(1)} %get-tuple-element.25.low_ref), channel_id=1, source_target_pairs={{0,1},{1,0},{2,3},{3,2},{4,5},{5,4},{6,7},{7,6},{8,9},{9,8},{10,11... | collective-permute-start | bytes 98312 | tf_op jit(solution)/shard_map/ppermute | solution.py:384
  25.6 0.7 copy-start.9
  27.3 11.6 %collective-permute-start.12 = (bf16[128,1024]{1,0:T(8,128)(2,1)S(1)}, bf16[128,1024]{1,0:T(8,128)(2,1)S(1)}, u32[]{:S(2)}, u32[]{:S(2)}) collective-permute-start(bf16[128,1024]{1,0:T(8,128)(2,1)S(1)} %get-tuple-element.32.xz_ref), channel_id=1, source_target_pairs={{0,4},{2,6},{4,8},{6,10},{8,12},{10,14},{12,0},{14,2},{1,5},{3,7},... | collective-permute-start | bytes 786440 | tf_op jit(solution)/shard_map/ppermute | solution.py:390
  27.4 13.0 %collective-permute-start.11 = (bf16[128,1024]{1,0:T(8,128)(2,1)S(1)}, bf16[128,1024]{1,0:T(8,128)(2,1)S(1)}, u32[]{:S(2)}, u32[]{:S(2)}) collective-permute-start(bf16[128,1024]{1,0:T(8,128)(2,1)S(1)} %get-tuple-element.32.xz_ref), channel_id=1, source_target_pairs={{0,2},{2,0},{4,6},{6,4},{8,10},{10,8},{12,14},{14,12},{1,3},{3,1},... | collective-permute-start | bytes 786440 | tf_op jit(solution)/shard_map/ppermute | solution.py:387
  29.0 3.5 %copy-start.3 = (bf16[1024,16]{0,1:T(8,128)(2,1)S(1)}, bf16[1024,16]{0,1:T(8,128)(2,1)}, u32[]{:S(2)}) copy-start(bf16[1024,16]{0,1:T(8,128)(2,1)} %param.15) | copy-start | bytes 98308
  38.3 9.3 %collective-permute-start.10 = (bf16[128,1024]{1,0:T(8,128)(2,1)S(1)}, bf16[128,1024]{1,0:T(8,128)(2,1)S(1)}, u32[]{:S(2)}, u32[]{:S(2)}) collective-permute-start(bf16[128,1024]{1,0:T(8,128)(2,1)S(1)} %get-tuple-element.31), channel_id=1, source_target_pairs={{0,2},{2,0},{4,6},{6,4},{8,10},{10,8},{12,14},{14,12},{1,3},{3,1},... | collective-permute-start | bytes 786440 | tf_op jit(solution)/shard_map/ppermute | solution.py:387
  38.9 14.4 %collective-permute-start.15 = (bf16[128,1024]{1,0:T(8,128)(2,1)S(1)}, bf16[128,1024]{1,0:T(8,128)(2,1)S(1)}, u32[]{:S(2)}, u32[]{:S(2)}) collective-permute-start(bf16[128,1024]{1,0:T(8,128)(2,1)S(1)} %shard_map.129.refs_5_.xz_ref), channel_id=1, source_target_pairs={{0,2},{2,0},{4,6},{6,4},{8,10},{10,8},{12,14},{14,12},{1,3},{3,1},... | collective-permute-start | bytes 786440 | tf_op jit(solution)/shard_map/ppermute | solution.py:387
  40.4 7.2 %copy-start.1 = (bf16[1,128,2048]{2,1,0:T(8,128)(2,1)S(1)}, bf16[1,128,2048]{2,1,0:T(8,128)(2,1)}, u32[]{:S(2)}) copy-start(bf16[1,128,2048]{2,1,0:T(8,128)(2,1)} %param.12) | copy-start | bytes 1572868
  40.4 7.2 %copy-start.2 = (bf16[1,128,2048]{2,1,0:T(8,128)(2,1)S(1)}, bf16[1,128,2048]{2,1,0:T(8,128)(2,1)}, u32[]{:S(2)}) copy-start(bf16[1,128,2048]{2,1,0:T(8,128)(2,1)} %param.13) | copy-start | bytes 1572868
  45.2 13.4 %collective-permute-start.17 = (bf16[128,1024]{1,0:T(8,128)(2,1)S(1)}, bf16[128,1024]{1,0:T(8,128)(2,1)S(1)}, u32[]{:S(2)}, u32[]{:S(2)}) collective-permute-start(bf16[128,1024]{1,0:T(8,128)(2,1)S(1)} %get-tuple-element.41), channel_id=1, source_target_pairs={{0,2},{2,0},{4,6},{6,4},{8,10},{10,8},{12,14},{14,12},{1,3},{3,1},... | collective-permute-start | bytes 786440 | tf_op jit(solution)/shard_map/ppermute | solution.py:387
  47.8 27.0 %collective-permute-start.19 = (bf16[128,1024]{1,0:T(8,128)(2,1)S(1)}, bf16[128,1024]{1,0:T(8,128)(2,1)S(1)}, u32[]{:S(2)}, u32[]{:S(2)}) collective-permute-start(bf16[128,1024]{1,0:T(8,128)(2,1)S(1)} %get-tuple-element.38.refs_5_), channel_id=1, source_target_pairs={{0,12},{2,14},{4,0},{6,2},{8,4},{10,6},{12,8},{14,10},{1,13},{3,15... | collective-permute-start | bytes 786440 | tf_op jit(solution)/shard_map/ppermute | solution.py:390
  51.7 9.5 %copy-start.4 = (bf16[1,128,1024]{2,1,0:T(8,128)(2,1)S(1)}, bf16[1,128,1024]{2,1,0:T(8,128)(2,1)}, u32[]{:S(2)}) copy-start(bf16[1,128,1024]{2,1,0:T(8,128)(2,1)} %param.14) | copy-start | bytes 786436
  51.7 15.8 %collective-permute-start.13 = (bf16[128,2048]{1,0:T(8,128)(2,1)S(1)}, bf16[128,2048]{1,0:T(8,128)(2,1)S(1)}, u32[]{:S(2)}, u32[]{:S(2)}) collective-permute-start(bf16[128,2048]{1,0:T(8,128)(2,1)S(1)} %get-tuple-element.36.k_own), channel_id=1, source_target_pairs={{0,1},{1,0},{2,3},{3,2},{4,5},{5,4},{6,7},{7,6},{8,9},{9,8},{10,11... | collective-permute-start | bytes 1572872 | tf_op jit(solution)/shard_map/ppermute | solution.py:384
  58.0 8.0 %collective-permute-start.16 = (bf16[128,1024]{1,0:T(8,128)(2,1)S(1)}, bf16[128,1024]{1,0:T(8,128)(2,1)S(1)}, u32[]{:S(2)}, u32[]{:S(2)}) collective-permute-start(bf16[128,1024]{1,0:T(8,128)(2,1)S(1)} %get-tuple-element.40), channel_id=1, source_target_pairs={{0,2},{2,0},{4,6},{6,4},{8,10},{10,8},{12,14},{14,12},{1,3},{3,1},... | collective-permute-start | bytes 786440 | tf_op jit(solution)/shard_map/ppermute | solution.py:387
  58.6 16.1 %collective-permute-start.20 = (bf16[128,1024]{1,0:T(8,128)(2,1)S(1)}, bf16[128,1024]{1,0:T(8,128)(2,1)S(1)}, u32[]{:S(2)}, u32[]{:S(2)}) collective-permute-start(bf16[128,1024]{1,0:T(8,128)(2,1)S(1)} %shard_map.133.refs_5_), channel_id=1, source_target_pairs={{0,8},{2,10},{4,12},{6,14},{8,0},{10,2},{12,4},{14,6},{1,9},{3,11}... | collective-permute-start | bytes 786440 | tf_op jit(solution)/shard_map/ppermute | solution.py:390
  61.2 7.0 %copy-start = (bf16[1,128,2048]{2,1,0:T(8,128)(2,1)S(1)}, bf16[1,128,2048]{2,1,0:T(8,128)(2,1)}, u32[]{:S(2)}) copy-start(bf16[1,128,2048]{2,1,0:T(8,128)(2,1)} %param.11) | copy-start | bytes 1572868
  61.2 7.0 %copy-start.6 = (s32[1,128]{1,0:T(1,128)S(1)}, s32[1,128]{1,0:T(1,128)}, u32[]{:S(2)}) copy-start(s32[1,128]{1,0:T(1,128)} %doc_own.3) | copy-start | bytes 1540
  61.2 7.0 %copy-start.8 = (s32[1,128]{1,0:T(1,128)S(1)}, s32[1,128]{1,0:T(1,128)}, u32[]{:S(2)}) copy-start(s32[1,128]{1,0:T(1,128)} %ahead_ref.3) | copy-start | bytes 1540
  61.2 7.0 %collective-permute-start.14 = (bf16[128,2048]{1,0:T(8,128)(2,1)S(1)}, bf16[128,2048]{1,0:T(8,128)(2,1)S(1)}, u32[]{:S(2)}, u32[]{:S(2)}) collective-permute-start(bf16[128,2048]{1,0:T(8,128)(2,1)S(1)} %get-tuple-element.37.v_own), channel_id=1, source_target_pairs={{0,1},{1,0},{2,3},{3,2},{4,5},{5,4},{6,7},{7,6},{8,9},{9,8},{10,11... | collective-permute-start | bytes 1572872 | tf_op jit(solution)/shard_map/ppermute | solution.py:384
  65.9 8.8 %collective-permute-start.18 = (bf16[128,1024]{1,0:T(8,128)(2,1)S(1)}, bf16[128,1024]{1,0:T(8,128)(2,1)S(1)}, u32[]{:S(2)}, u32[]{:S(2)}) collective-permute-start(bf16[128,1024]{1,0:T(8,128)(2,1)S(1)} %get-tuple-element.43), channel_id=1, source_target_pairs={{0,2},{2,0},{4,6},{6,4},{8,10},{10,8},{12,14},{14,12},{1,3},{3,1},... | collective-permute-start | bytes 786440 | tf_op jit(solution)/shard_map/ppermute | solution.py:387
  67.6 10.3 %collective-permute-start.21 = (bf16[128,1024]{1,0:T(8,128)(2,1)S(1)}, bf16[128,1024]{1,0:T(8,128)(2,1)S(1)}, u32[]{:S(2)}, u32[]{:S(2)}) collective-permute-start(bf16[128,1024]{1,0:T(8,128)(2,1)S(1)} %shard_map.135.rest_0_), channel_id=1, source_target_pairs={{0,4},{2,6},{4,8},{6,10},{8,12},{10,14},{12,0},{14,2},{1,5},{3,7},... | collective-permute-start | bytes 786440 | tf_op jit(solution)/shard_map/ppermute | solution.py:390

commit v8 on v7

--- a/solution.py
+++ b/solution.py
@@ -115,23 +115,17 @@
     refs[-1][count:] = second_ref[...]
 
 
-def copy_join_kernel(first_ref, second_ref, rows_ref, copy_ref, out_ref):
-    join_kernel(first_ref, second_ref, out_ref)
-    copy_ref[...] = rows_ref[...]
-
-
-def join(first, second, passed=None, after=(), copy=False):
+def join(first, second, passed=None, after=()):
     vmem = pl.BlockSpec(memory_space=pltpu.VMEM)
     anywhere = pl.BlockSpec(memory_space=pl.ANY)
     table = jax.ShapeDtypeStruct((2 * first.shape[0],) + first.shape[1:], first.dtype)
     through = [] if passed is None else [passed]
-    place = vmem if copy else anywhere
     out = pl.pallas_call(
-        copy_join_kernel if copy else join_kernel,
+        join_kernel,
         out_shape=[jax.ShapeDtypeStruct(x.shape, x.dtype) for x in through] + [table],
-        in_specs=[vmem] * 2 + [place] * len(through) + [anywhere] * len(after),
-        out_specs=[place] * len(through) + [vmem],
-        input_output_aliases={2: 0} if through and not copy else {},
+        in_specs=[vmem] * 2 + [anywhere] * (len(through) + len(after)),
+        out_specs=[anywhere] * len(through) + [vmem],
+        input_output_aliases={2: 0} if through else {},
         compiler_params=pltpu.CompilerParams(vmem_limit_bytes=SMALL_VMEM),
     )(first, second, *through, *after)
     return out if through else out[0]
@@ -165,22 +159,6 @@
         scratch_shapes=[pltpu.SemaphoreType.DMA((4,))],
         compiler_params=pltpu.CompilerParams(vmem_limit_bytes=LOAD_VMEM),
     )(w_first, w_second, *after)
-
-
-def behind_kernel(*refs):
-    pass
-
-
-def behind(x, after):
-    anywhere = pl.BlockSpec(memory_space=pl.ANY)
-    return pl.pallas_call(
-        behind_kernel,
-        out_shape=jax.ShapeDtypeStruct(x.shape, x.dtype),
-        in_specs=[anywhere] * (1 + len(after)),
-        out_specs=anywhere,
-        input_output_aliases={0: 0},
-        compiler_params=pltpu.CompilerParams(vmem_limit_bytes=SMALL_VMEM),
-    )(x, *after)
 
 
 def kept_kernel(own_ref, capacity_ref, low_ref, high_ref, *refs):
@@ -395,24 +373,24 @@
     own = lax.axis_index(("expert", "context")).astype(jnp.int32).reshape(1)
     far_weights = [swap_core(expert_in[0]), swap_core(expert_out[0])]
 
-    arriving, beside_own = along(latent[0], 1), swap_side(latent[0])
+    from_line = [latent[0], along(latent[0], 1)]
+    from_side = [swap_side(latent[0])]
     table = pack(routes.transpose(2, 0, 1), segments)
     span = 1
-    while 2 * span < line:
-        table = join(table, flipped(table, span))
+    while span < line:
+        here = len(from_line) - 1
+        flip = flipped(table, span)
+        from_line[here], table = join(table, flip, passed=from_line[here], after=(from_side[-1],))
         span *= 2
-    arriving, table = join(table, flipped(table, span), passed=arriving, after=(beside_own,))
-    across_table = swap_side(table)
-    chained = along(arriving, 1)
-    passed, table = join(table, across_table, passed=arriving, copy=True)
+        from_line.append(along(from_line[here], 1))
+        from_side.append(swap_side(from_line[here]))
+    table = join(table, swap_side(table))
     far_table = swap_core(table)
-    from_side = [beside_own, swap_side(passed)]
-    kept, passed = kept_rows(own, capacity, table, far_table, chained, ())
     doc_far = far_table[0, TOPK : TOPK + 1, :]
-    from_line = [latent[0], arriving, passed]
-    last = along(passed, 1)
-    from_side.append(swap_side(passed))
-    weights = list(load_weights(expert_in[0], expert_out[0], (kept,))) + far_weights
+    own_weights = load_weights(expert_in[0], expert_out[0], (table,))
+    kept, from_line[-1] = kept_rows(own, capacity, table, far_table, from_line[-1], own_weights)
+    from_side.append(swap_side(from_line[-1]))
+    weights = list(own_weights) + far_weights
 
     def piece(step, weights, *after):
         return run_piece(
@@ -421,10 +399,7 @@
 
     one, theirs, *weights[2:] = piece(1, weights)
     one_far = swap_side(theirs)
-    last = behind(last, (one,))
-    from_line.append(last)
-    from_side.append(swap_side(last))
-    two, theirs = piece(2, weights, one, from_line[3])
+    two, theirs = piece(2, weights, one)
     two_far = swap_side(theirs)
     k_near, v_near, first = add(one, one_far, after=(two,), staged=(k_near, v_near))
     home = [along(first, line - 1)]

time: 79 us -> 79.2 us (level)
  waiting for transfers between devices: 20.3 us -> 24.9 us
  starting transfers between devices: 26.7 us -> 23 us
    ppermute x6, starting transfers between devices: 10.8 us -> 5.77 us  [along(): lax.ppermute(x, 'expert', [(2 * z + y, 2 * ((z + step) % line) + y) for z...]
    ppermute x6, waiting for transfers between devices: 6.45 us -> 9.21 us  [along(): lax.ppermute(x, 'expert', [(2 * z + y, 2 * ((z + step) % line) + y) for z...]
    ppermute x9, starting transfers between devices: 10.4 us -> 12.4 us  [swap_side(): return lax.ppermute(x, 'expert', across)]
    ppermute x9, waiting for transfers between devices: 8.16 us -> 9.85 us  [swap_side(): return lax.ppermute(x, 'expert', across)]
    ppermute x2, waiting for transfers between devices: 4.5 us -> 5.88 us  [flipped(): lax.ppermute(x, 'expert', [(2 * z + y, 2 * (z ^ span) + y) for z, y in sp...]
    ppermute x5, waiting for transfers between devices: 1.22 us -> 0.01 us  [swap_core(): return lax.ppermute(x, 'context', sibling)]
    ppermute x2, starting transfers between devices: 4.94 us -> 3.99 us  [flipped(): lax.ppermute(x, 'expert', [(2 * z + y, 2 * (z ^ span) + y) for z, y in sp...]
  transfers between devices with their start and end apart: 22 -> 22, of which waited for: 9 -> 10; matrix products, arithmetic and copies ran while one was open for 0% -> 0% of each run, Pallas kernels for 35% -> 35%
where the time goes in v8:
time: 79.2 us; the launch traced here: 79 us
  Pallas kernels  27.9 us (35%)
  waiting for transfers between devices  24.9 us (31%)
  starting transfers between devices  23 us (29%)
  local copies, waits for them, and re-layouts  1.38 us (2%)
  other arithmetic  0.92 us (1%)
  between operations  0.85 us (1%)
    pallas_call x4, Pallas kernels, run_piece(): pl.pallas_call(functools.partial(expert_kernel, place, first), out_shape=...  19.8 us
    ppermute x9, starting transfers between devices, swap_side(): return lax.ppermute(x, 'expert', across)  12.4 us
    ppermute x9, waiting for transfers between devices, swap_side(): return lax.ppermute(x, 'expert', across)  9.85 us
    ppermute x6, waiting for transfers between devices, along(): lax.ppermute(x, 'expert', [(2 * z + y, 2 * ((z + step) % line) + y) for z...  9.21 us
    ppermute x2, waiting for transfers between devices, flipped(): lax.ppermute(x, 'expert', [(2 * z + y, 2 * (z ^ span) + y) for z, y in sp...  5.88 us
    ppermute x6, starting transfers between devices, along(): lax.ppermute(x, 'expert', [(2 * z + y, 2 * ((z + step) % line) + y) for z...  5.77 us
    ppermute x2, starting transfers between devices, flipped(): lax.ppermute(x, 'expert', [(2 * z + y, 2 * (z ^ span) + y) for z, y in sp...  3.99 us
    pallas_call x1, Pallas kernels, load_weights(): pl.pallas_call(load_kernel, out_shape=[pltpu.VMEM(w.shape, w.dtype) for w...  3.5 us
  transfers between devices with their start and end apart: 22, of which 10 were waited for; matrix products, arithmetic and copies ran while one was open for 0% of the time, Pallas kernels for 35%

profile of v8, /device:TPU:0, one launch (start us, length us, event | category | flops | bytes accessed | tf_op | source)
XLA Modules:
  0.0 79.0 jit_solution(17918886773768836721)
XLA Ops:
  0.6 0.5 collective-permute-start.10
  1.1 0.1 collective-permute-start.9
  1.2 2.9 %collective-permute-start.2 = (bf16[128,1024]{1,0:T(8,128)(2,1)}, bf16[128,1024]{1,0:T(8,128)(2,1)S(1)}, u32[]{:S(2)}, u32[]{:S(2)}) collective-permute-start(bf16[128,1024]{1,0:T(8,128)(2,1)} %bitcast.23), channel_id=1, source_target_pairs={{0,2},{2,0},{4,6},{6,4},{8,10},{10,8},{12,14},{14,12},{1,3},{3,1},... | collective-permute-start | bytes 786440 | tf_op jit(solution)/shard_map/ppermute | solution.py:365
  4.2 1.6 %collective-permute-start.1 = (bf16[128,1024]{1,0:T(8,128)(2,1)}, bf16[128,1024]{1,0:T(8,128)(2,1)S(1)}, u32[]{:S(2)}, u32[]{:S(2)}) collective-permute-start(bf16[128,1024]{1,0:T(8,128)(2,1)} %bitcast.24), channel_id=1, source_target_pairs={{0,4},{2,6},{4,8},{6,10},{8,12},{10,14},{12,0},{14,2},{1,5},{3,7},... | collective-permute-start | bytes 786440 | tf_op jit(solution)/shard_map/ppermute | solution.py:368
  5.8 0.7 copy-done.5
  6.4 0.7 copy-done.7
  7.1 1.6 %collective-permute-start = (s32[1,8,128]{2,1,0:T(8,128)S(1)}, s32[1,8,128]{2,1,0:T(8,128)S(1)}, u32[]{:S(2)}, u32[]{:S(2)}) collective-permute-start(s32[1,8,128]{2,1,0:T(8,128)S(1)} %shard_map.122.first_ref), channel_id=1, source_target_pairs={{0,4},{2,6},{4,0},{6,2},{8,12},{10,14},{12,8},{14,10},{1,5},{3,7},... | collective-permute-start | bytes 12296 | tf_op jit(solution)/shard_map/ppermute | solution.py:371
  8.8 2.9 %collective-permute-done.second_ref = s32[1,8,128]{2,1,0:T(8,128)S(1)} collective-permute-done((s32[1,8,128]{2,1,0:T(8,128)S(1)}, s32[1,8,128]{2,1,0:T(8,128)S(1)}, u32[]{:S(2)}, u32[]{:S(2)}) %collective-permute-start) | collective-permute-done | bytes 4128 | tf_op jit(solution)/shard_map/ppermute | solution.py:371
  11.6 0.0 collective-permute-done.2.refs_1_.xy_ref
  11.6 2.7 %collective-permute-done.1.refs_0_ = bf16[128,1024]{1,0:T(8,128)(2,1)S(1)} collective-permute-done((bf16[128,1024]{1,0:T(8,128)(2,1)}, bf16[128,1024]{1,0:T(8,128)(2,1)S(1)}, u32[]{:S(2)}, u32[]{:S(2)}) %collective-permute-start.1) | collective-permute-done | bytes 262176 | tf_op jit(solution)/shard_map/ppermute | solution.py:368
  14.4 0.5 collective-permute-start.5
  14.9 0.0 collective-permute-start.4
  14.9 2.3 %collective-permute-start.3 = (s32[2,8,128]{2,1,0:T(8,128)S(1)}, s32[2,8,128]{2,1,0:T(8,128)S(1)}, u32[]{:S(2)}, u32[]{:S(2)}) collective-permute-start(s32[2,8,128]{2,1,0:T(8,128)S(1)} %get-tuple-element.23.first_ref), channel_id=1, source_target_pairs={{0,8},{2,10},{4,12},{6,14},{8,0},{10,2},{12,4},{14,6},{1,9},{3,11}... | collective-permute-start | bytes 24584 | tf_op jit(solution)/shard_map/ppermute | solution.py:371
  17.2 3.0 %collective-permute-done.3.second_ref = s32[2,8,128]{2,1,0:T(8,128)S(1)} collective-permute-done((s32[2,8,128]{2,1,0:T(8,128)S(1)}, s32[2,8,128]{2,1,0:T(8,128)S(1)}, u32[]{:S(2)}, u32[]{:S(2)}) %collective-permute-start.3) | collective-permute-done | bytes 8224 | tf_op jit(solution)/shard_map/ppermute | solution.py:371
  20.2 1.3 %collective-permute-done.5.refs_1_.xy_ref = bf16[128,1024]{1,0:T(8,128)(2,1)S(1)} collective-permute-done((bf16[128,1024]{1,0:T(8,128)(2,1)S(1)}, bf16[128,1024]{1,0:T(8,128)(2,1)S(1)}, u32[]{:S(2)}, u32[]{:S(2)}) %collective-permute-start.5) | collective-permute-done | bytes 262176 | tf_op jit(solution)/shard_map/ppermute | solution.py:365
  21.5 2.4 %collective-permute-done.4.refs_0_ = bf16[128,1024]{1,0:T(8,128)(2,1)S(1)} collective-permute-done((bf16[128,1024]{1,0:T(8,128)(2,1)S(1)}, bf16[128,1024]{1,0:T(8,128)(2,1)S(1)}, u32[]{:S(2)}, u32[]{:S(2)}) %collective-permute-start.4) | collective-permute-done | bytes 262176 | tf_op jit(solution)/shard_map/ppermute | solution.py:368
  23.9 0.7 collective-permute-start.8
  24.7 1.3 %collective-permute-start.6 = (s32[4,8,128]{2,1,0:T(8,128)S(1)}, s32[4,8,128]{2,1,0:T(8,128)S(1)}, u32[]{:S(2)}, u32[]{:S(2)}) collective-permute-start(s32[4,8,128]{2,1,0:T(8,128)S(1)} %get-tuple-element.25.first_ref), channel_id=1, source_target_pairs={{0,2},{2,0},{4,6},{6,4},{8,10},{10,8},{12,14},{14,12},{1,3},{3,1},... | collective-permute-start | bytes 49160 | tf_op jit(solution)/shard_map/ppermute | solution.py:365
  26.0 2.4 %collective-permute-done.6.second_ref = s32[4,8,128]{2,1,0:T(8,128)S(1)} collective-permute-done((s32[4,8,128]{2,1,0:T(8,128)S(1)}, s32[4,8,128]{2,1,0:T(8,128)S(1)}, u32[]{:S(2)}, u32[]{:S(2)}) %collective-permute-start.6) | collective-permute-done | bytes 16416 | tf_op jit(solution)/shard_map/ppermute | solution.py:365
  28.4 0.0 collective-permute-start.7
  28.4 1.4 %collective-permute-start.12 = (bf16[128,1024]{1,0:T(8,128)(2,1)S(1)}, bf16[128,1024]{1,0:T(8,128)(2,1)S(1)}, u32[]{:S(2)}, u32[]{:S(2)}) collective-permute-start(bf16[128,1024]{1,0:T(8,128)(2,1)S(1)} %get-tuple-element.26.xz_ref), channel_id=1, source_target_pairs={{0,2},{2,0},{4,6},{6,4},{8,10},{10,8},{12,14},{14,12},{1,3},{3,1},... | collective-permute-start | bytes 786440 | tf_op jit(solution)/shard_map/ppermute | solution.py:365
  29.8 3.5 %shard_map.126 = (bf16[1024,2048]{1,0:T(8,128)(2,1)S(1)}, bf16[2048,1024]{1,0:T(8,128)(2,1)S(1)}) custom-call(bf16[1024,2048]{1,0:T(8,128)(2,1)} %bitcast.30, bf16[2048,1024]{1,0:T(8,128)(2,1)} %bitcast.28, s32[8,8,128]{2,1,0:T(8,128)S(1)} %shard_map.125.refs_0_.low_ref), custom_call_target="tpu_custom_call" | custom-call | tf_op jit(solution)/shard_map/pallas_call | solution.py:154
  33.3 0.0 collective-permute-done.7.high_ref
  33.3 0.0 collective-permute-done.8.refs_0_
  33.3 0.0 copy-done.9
  33.3 0.0 copy-start.3
  33.3 1.1 %shard_map.127 = (s32[8,8,128]{2,1,0:T(8,128)S(1)}, bf16[128,1024]{1,0:T(8,128)(2,1)S(1)}) custom-call(s32[1]{0:T(128)} %bitcast.2.own_ref, s32[16]{0:T(128)S(1)} %copy-done.9, s32[8,8,128]{2,1,0:T(8,128)S(1)} %shard_map.125.refs_0_.low_ref, s32[8,8,128]{2,1,0:T(8,128)S(1)} %collective-permute-done.7.high_ref, ...), custom_call_target="tpu_custom_call", output_to_operand_aliasing={{1}: (4, {})} | custom-call | tf_op jit(solution)/shard_map/pallas_call | solution.py:214
  34.4 0.8 %collective-permute-start.15 = (bf16[128,1024]{1,0:T(8,128)(2,1)S(1)}, bf16[128,1024]{1,0:T(8,128)(2,1)S(1)}, u32[]{:S(2)}, u32[]{:S(2)}) collective-permute-start(bf16[128,1024]{1,0:T(8,128)(2,1)S(1)} %get-tuple-element.37.xz_ref), channel_id=1, source_target_pairs={{0,2},{2,0},{4,6},{6,4},{8,10},{10,8},{12,14},{14,12},{1,3},{3,1},... | collective-permute-start | bytes 786440 | tf_op jit(solution)/shard_map/ppermute | solution.py:365
  35.2 0.0 collective-permute-done.10.refs_3_
  35.2 0.0 collective-permute-done.9.refs_2_
  35.2 5.8 %shard_map.128 = (bf16[128,1024]{1,0:T(8,128)(2,1)S(1)}, bf16[128,1024]{1,0:T(8,128)(2,1)S(1)}, bf16[1024,2048]{1,0:T(8,128)(2,1)S(1)}, bf16[2048,1024]{1,0:T(8,128)(2,1)S(1)}) custom-call(s32[1]{0:T(128)} %bitcast.2.own_ref, s32[8,8,128]{2,1,0:T(8,128)S(1)} %get-tuple-element.29.kept_ref, bf16[16,1024]{1,0:T(8,128)(2,1)S(1)} %bitcast.19, ...), custom_call_target="tpu_custom_call" | custom-call | flops 4294967296 | bytes 1048576 | tf_op jit(solution)/shard_map/pallas_call | solution.py:316
  41.0 1.4 %collective-permute-start.11 = (bf16[128,1024]{1,0:T(8,128)(2,1)S(1)}, bf16[128,1024]{1,0:T(8,128)(2,1)S(1)}, u32[]{:S(2)}, u32[]{:S(2)}) collective-permute-start(bf16[128,1024]{1,0:T(8,128)(2,1)S(1)} %get-tuple-element.31), channel_id=1, source_target_pairs={{0,2},{2,0},{4,6},{6,4},{8,10},{10,8},{12,14},{14,12},{1,3},{3,1},... | collective-permute-start | bytes 786440 | tf_op jit(solution)/shard_map/ppermute | solution.py:365
  42.4 0.0 collective-permute-done.12.xy_ref
  42.4 4.7 %shard_map.129 = (bf16[128,1024]{1,0:T(8,128)(2,1)S(1)}, bf16[128,1024]{1,0:T(8,128)(2,1)S(1)}) custom-call(s32[1]{0:T(128)} %bitcast.2.own_ref, s32[8,8,128]{2,1,0:T(8,128)S(1)} %get-tuple-element.29.kept_ref, bf16[16,1024]{1,0:T(8,128)(2,1)S(1)} %bitcast.20, bf16[128,1024]{1,0:T(8,128)(2,1)S(1)} %get-tuple-element.26.xz_ref, ...), custom_call_target="tpu_custom_call" | custom-call | flops 4294967296 | bytes 1048576 | tf_op jit(solution)/shard_map/pallas_call | solution.py:316
  47.1 0.8 %collective-permute-start.17 = (bf16[128,1024]{1,0:T(8,128)(2,1)S(1)}, bf16[128,1024]{1,0:T(8,128)(2,1)S(1)}, u32[]{:S(2)}, u32[]{:S(2)}) collective-permute-start(bf16[128,1024]{1,0:T(8,128)(2,1)S(1)} %get-tuple-element.41), channel_id=1, source_target_pairs={{0,2},{2,0},{4,6},{6,4},{8,10},{10,8},{12,14},{14,12},{1,3},{3,1},... | collective-permute-start | bytes 786440 | tf_op jit(solution)/shard_map/ppermute | solution.py:365
  47.9 1.3 %collective-permute-done.11.second_ref = bf16[128,1024]{1,0:T(8,128)(2,1)S(1)} collective-permute-done((bf16[128,1024]{1,0:T(8,128)(2,1)S(1)}, bf16[128,1024]{1,0:T(8,128)(2,1)S(1)}, u32[]{:S(2)}, u32[]{:S(2)}) %collective-permute-start.11) | collective-permute-done | bytes 262176 | tf_op jit(solution)/shard_map/ppermute | solution.py:365
  49.2 0.0 copy-done.1
  49.2 0.1 shard_map.130
  49.3 3.3 %collective-permute-start.19 = (bf16[128,1024]{1,0:T(8,128)(2,1)S(1)}, bf16[128,1024]{1,0:T(8,128)(2,1)S(1)}, u32[]{:S(2)}, u32[]{:S(2)}) collective-permute-start(bf16[128,1024]{1,0:T(8,128)(2,1)S(1)} %get-tuple-element.38.refs_5_), channel_id=1, source_target_pairs={{0,12},{2,14},{4,0},{6,2},{8,4},{10,6},{12,8},{14,10},{1,13},{3,15... | collective-permute-start | bytes 786440 | tf_op jit(solution)/shard_map/ppermute | solution.py:368
  52.6 0.0 collective-permute-start.13
  52.6 0.0 collective-permute-done.15.xy_ref
  52.6 4.7 %shard_map.131 = (bf16[128,1024]{1,0:T(8,128)(2,1)S(1)}, bf16[128,1024]{1,0:T(8,128)(2,1)S(1)}) custom-call(s32[1]{0:T(128)} %bitcast.2.own_ref, s32[8,8,128]{2,1,0:T(8,128)S(1)} %get-tuple-element.29.kept_ref, bf16[16,1024]{1,0:T(8,128)(2,1)S(1)} %bitcast.21, bf16[128,1024]{1,0:T(8,128)(2,1)S(1)} %get-tuple-element.37.xz_ref, ...), custom_call_target="tpu_custom_call" | custom-call | flops 4294967296 | bytes 1048576 | tf_op jit(solution)/shard_map/pallas_call | solution.py:316
  57.4 1.7 %collective-permute-start.16 = (bf16[128,1024]{1,0:T(8,128)(2,1)S(1)}, bf16[128,1024]{1,0:T(8,128)(2,1)S(1)}, u32[]{:S(2)}, u32[]{:S(2)}) collective-permute-start(bf16[128,1024]{1,0:T(8,128)(2,1)S(1)} %get-tuple-element.40), channel_id=1, source_target_pairs={{0,2},{2,0},{4,6},{6,4},{8,10},{10,8},{12,14},{14,12},{1,3},{3,1},... | collective-permute-start | bytes 786440 | tf_op jit(solution)/shard_map/ppermute | solution.py:365
  59.0 0.0 collective-permute-done.17.second_ref
  59.0 0.1 shard_map.132.refs_5_
  59.1 0.1 collective-permute-start.20
  59.2 0.0 copy-start
  59.2 0.0 copy-start.6
  59.2 0.0 copy-start.8
  59.2 0.3 collective-permute-start.14
  59.5 4.7 %shard_map.133 = (bf16[128,1024]{1,0:T(8,128)(2,1)S(1)}, bf16[128,1024]{1,0:T(8,128)(2,1)S(1)}) custom-call(s32[1]{0:T(128)} %bitcast.2.own_ref, s32[8,8,128]{2,1,0:T(8,128)S(1)} %get-tuple-element.29.kept_ref, bf16[16,1024]{1,0:T(8,128)(2,1)S(1)} %bitcast.22, bf16[128,1024]{1,0:T(8,128)(2,1)S(1)} %bitcast.25, ...), custom_call_target="tpu_custom_call" | custom-call | flops 4294967296 | bytes 1048576 | tf_op jit(solution)/shard_map/pallas_call | solution.py:316
  64.2 1.9 %collective-permute-done.16.second_ref = bf16[128,1024]{1,0:T(8,128)(2,1)S(1)} collective-permute-done((bf16[128,1024]{1,0:T(8,128)(2,1)S(1)}, bf16[128,1024]{1,0:T(8,128)(2,1)S(1)}, u32[]{:S(2)}, u32[]{:S(2)}) %collective-permute-start.16) | collective-permute-done | bytes 262176 | tf_op jit(solution)/shard_map/ppermute | solution.py:365
  66.1 1.6 %collective-permute-start.18 = (bf16[128,1024]{1,0:T(8,128)(2,1)S(1)}, bf16[128,1024]{1,0:T(8,128)(2,1)S(1)}, u32[]{:S(2)}, u32[]{:S(2)}) collective-permute-start(bf16[128,1024]{1,0:T(8,128)(2,1)S(1)} %get-tuple-element.43), channel_id=1, source_target_pairs={{0,2},{2,0},{4,6},{6,4},{8,10},{10,8},{12,14},{14,12},{1,3},{3,1},... | collective-permute-start | bytes 786440 | tf_op jit(solution)/shard_map/ppermute | solution.py:365
  67.8 0.1 shard_map.134.rest_0_
  67.8 0.0 collective-permute-done.13.k_far
  67.8 0.1 collective-permute-start.21
  67.9 0.0 collective-permute-done.14.v_far
  68.0 1.6 %shard_map.135.rest_0_ = bf16[128,2048]{1,0:T(8,128)(2,1)} custom-call(s32[1]{0:T(128)} %bitcast.place_ref, bf16[128,2048]{1,0:T(8,128)(2,1)S(1)} %bitcast.15, bf16[128,2048]{1,0:T(8,128)(2,1)S(1)} %get-tuple-element.35.k_own, bf16[128,2048]{1,0:T(8,128)(2,1)S(1)} %collective-permute-done.13.k_far, bf16[128,2048]{1,0:T(8,128)(2,1)S(1)} %get-tuple-element.36.v_own, ...), custom_call_target="tpu_custom_call" | custom-call | flops 134217728 | bytes 1572864 | tf_op jit(solution)/shard_map/pallas_call | solution.py:67
  69.6 1.6 %shard_map.136 = bf16[128,2048]{1,0:T(8,128)(2,1)} custom-call(s32[1]{0:T(128)} %bitcast.place_ref, bf16[128,2048]{1,0:T(8,128)(2,1)S(1)} %bitcast.16, bf16[128,2048]{1,0:T(8,128)(2,1)S(1)} %get-tuple-element.35.k_own, bf16[128,2048]{1,0:T(8,128)(2,1)S(1)} %collective-permute-done.13.k_far, ...), custom_call_target="tpu_custom_call", output_to_operand_aliasing={{}: (9, {})} | custom-call | flops 134217728 | bytes 1572864 | tf_op jit(solution)/shard_map/pallas_call | solution.py:67
  71.1 2.9 %collective-permute-done.18 = bf16[128,1024]{1,0:T(8,128)(2,1)S(1)} collective-permute-done((bf16[128,1024]{1,0:T(8,128)(2,1)S(1)}, bf16[128,1024]{1,0:T(8,128)(2,1)S(1)}, u32[]{:S(2)}, u32[]{:S(2)}) %collective-permute-start.18) | collective-permute-done | bytes 262176 | tf_op jit(solution)/shard_map/ppermute | solution.py:365
  74.1 4.0 %collective-permute-done.20 = bf16[128,1024]{1,0:T(8,128)(2,1)S(1)} collective-permute-done((bf16[128,1024]{1,0:T(8,128)(2,1)S(1)}, bf16[128,1024]{1,0:T(8,128)(2,1)S(1)}, u32[]{:S(2)}, u32[]{:S(2)}) %collective-permute-start.20) | collective-permute-done | bytes 262176 | tf_op jit(solution)/shard_map/ppermute | solution.py:368
  78.1 0.0 collective-permute-done.19
  78.1 0.0 collective-permute-done.21
  78.1 0.9 %fusion = bf16[1,128,1024]{2,1,0:T(8,128)(2,1)} fusion(bf16[128,1024]{1,0:T(8,128)(2,1)S(1)} %collective-permute-done.21, bf16[128,1024]{1,0:T(8,128)(2,1)S(1)} %collective-permute-done.20, bf16[128,1024]{1,0:T(8,128)(2,1)S(1)} %collective-permute-done.19, bf16[128,1024]{1,0:T(8,128)(2,1)S(1)} %collective-permute-done.18, ...), kind=kLoop, calls=%fused_computation.1 | loop fusion | flops 1310720 | bytes 1572864 | tf_op jit(solution)/shard_map/broadcast_in_dim | solution.py:420
  (17 shorter events, 0.1 us)
Async XLA Ops:
  0.6 34.6 %collective-permute-start.10 = (bf16[2048,1024]{1,0:T(8,128)(2,1)}, bf16[2048,1024]{1,0:T(8,128)(2,1)}, u32[]{:S(2)}, u32[]{:S(2)}) collective-permute-start(bf16[2048,1024]{1,0:T(8,128)(2,1)} %bitcast.27), channel_id=1, source_target_pairs={{0,1},{1,0},{2,3},{3,2},{4,5},{5,4},{6,7},{7,6},{8,9},{9,8},{10,11... | collective-permute-start | bytes 12582920 | tf_op jit(solution)/shard_map/ppermute | solution.py:362
  1.1 34.1 %collective-permute-start.9 = (bf16[1024,2048]{1,0:T(8,128)(2,1)}, bf16[1024,2048]{1,0:T(8,128)(2,1)}, u32[]{:S(2)}, u32[]{:S(2)}) collective-permute-start(bf16[1024,2048]{1,0:T(8,128)(2,1)} %bitcast.29), channel_id=1, source_target_pairs={{0,1},{1,0},{2,3},{3,2},{4,5},{5,4},{6,7},{7,6},{8,9},{9,8},{10,11... | collective-permute-start | bytes 12582920 | tf_op jit(solution)/shard_map/ppermute | solution.py:362
  1.2 10.4 %collective-permute-start.2 = (bf16[128,1024]{1,0:T(8,128)(2,1)}, bf16[128,1024]{1,0:T(8,128)(2,1)S(1)}, u32[]{:S(2)}, u32[]{:S(2)}) collective-permute-start(bf16[128,1024]{1,0:T(8,128)(2,1)} %bitcast.23), channel_id=1, source_target_pairs={{0,2},{2,0},{4,6},{6,4},{8,10},{10,8},{12,14},{14,12},{1,3},{3,1},... | collective-permute-start | bytes 786440 | tf_op jit(solution)/shard_map/ppermute | solution.py:365
  4.2 10.2 %collective-permute-start.1 = (bf16[128,1024]{1,0:T(8,128)(2,1)}, bf16[128,1024]{1,0:T(8,128)(2,1)S(1)}, u32[]{:S(2)}, u32[]{:S(2)}) collective-permute-start(bf16[128,1024]{1,0:T(8,128)(2,1)} %bitcast.24), channel_id=1, source_target_pairs={{0,4},{2,6},{4,8},{6,10},{8,12},{10,14},{12,0},{14,2},{1,5},{3,7},... | collective-permute-start | bytes 786440 | tf_op jit(solution)/shard_map/ppermute | solution.py:368
  5.7 0.7 copy-start.5
  6.4 0.7 copy-start.7
  7.1 4.5 %collective-permute-start = (s32[1,8,128]{2,1,0:T(8,128)S(1)}, s32[1,8,128]{2,1,0:T(8,128)S(1)}, u32[]{:S(2)}, u32[]{:S(2)}) collective-permute-start(s32[1,8,128]{2,1,0:T(8,128)S(1)} %shard_map.122.first_ref), channel_id=1, source_target_pairs={{0,4},{2,6},{4,0},{6,2},{8,12},{10,14},{12,8},{14,10},{1,5},{3,7},... | collective-permute-start | bytes 12296 | tf_op jit(solution)/shard_map/ppermute | solution.py:371
  14.4 7.1 %collective-permute-start.5 = (bf16[128,1024]{1,0:T(8,128)(2,1)S(1)}, bf16[128,1024]{1,0:T(8,128)(2,1)S(1)}, u32[]{:S(2)}, u32[]{:S(2)}) collective-permute-start(bf16[128,1024]{1,0:T(8,128)(2,1)S(1)} %get-tuple-element.24.xz_ref), channel_id=1, source_target_pairs={{0,2},{2,0},{4,6},{6,4},{8,10},{10,8},{12,14},{14,12},{1,3},{3,1},... | collective-permute-start | bytes 786440 | tf_op jit(solution)/shard_map/ppermute | solution.py:365
  14.9 9.1 %collective-permute-start.4 = (bf16[128,1024]{1,0:T(8,128)(2,1)S(1)}, bf16[128,1024]{1,0:T(8,128)(2,1)S(1)}, u32[]{:S(2)}, u32[]{:S(2)}) collective-permute-start(bf16[128,1024]{1,0:T(8,128)(2,1)S(1)} %get-tuple-element.24.xz_ref), channel_id=1, source_target_pairs={{0,4},{2,6},{4,8},{6,10},{8,12},{10,14},{12,0},{14,2},{1,5},{3,7},... | collective-permute-start | bytes 786440 | tf_op jit(solution)/shard_map/ppermute | solution.py:368
  14.9 5.3 %collective-permute-start.3 = (s32[2,8,128]{2,1,0:T(8,128)S(1)}, s32[2,8,128]{2,1,0:T(8,128)S(1)}, u32[]{:S(2)}, u32[]{:S(2)}) collective-permute-start(s32[2,8,128]{2,1,0:T(8,128)S(1)} %get-tuple-element.23.first_ref), channel_id=1, source_target_pairs={{0,8},{2,10},{4,12},{6,14},{8,0},{10,2},{12,4},{14,6},{1,9},{3,11}... | collective-permute-start | bytes 24584 | tf_op jit(solution)/shard_map/ppermute | solution.py:371
  23.9 9.4 %collective-permute-start.8 = (bf16[128,1024]{1,0:T(8,128)(2,1)S(1)}, bf16[128,1024]{1,0:T(8,128)(2,1)S(1)}, u32[]{:S(2)}, u32[]{:S(2)}) collective-permute-start(bf16[128,1024]{1,0:T(8,128)(2,1)S(1)} %get-tuple-element.26.xz_ref), channel_id=1, source_target_pairs={{0,4},{2,6},{4,8},{6,10},{8,12},{10,14},{12,0},{14,2},{1,5},{3,7},... | collective-permute-start | bytes 786440 | tf_op jit(solution)/shard_map/ppermute | solution.py:368
  24.7 3.7 %collective-permute-start.6 = (s32[4,8,128]{2,1,0:T(8,128)S(1)}, s32[4,8,128]{2,1,0:T(8,128)S(1)}, u32[]{:S(2)}, u32[]{:S(2)}) collective-permute-start(s32[4,8,128]{2,1,0:T(8,128)S(1)} %get-tuple-element.25.first_ref), channel_id=1, source_target_pairs={{0,2},{2,0},{4,6},{6,4},{8,10},{10,8},{12,14},{14,12},{1,3},{3,1},... | collective-permute-start | bytes 49160 | tf_op jit(solution)/shard_map/ppermute | solution.py:365
  28.4 4.9 %collective-permute-start.7 = (s32[8,8,128]{2,1,0:T(8,128)S(1)}, s32[8,8,128]{2,1,0:T(8,128)S(1)}, u32[]{:S(2)}, u32[]{:S(2)}) collective-permute-start(s32[8,8,128]{2,1,0:T(8,128)S(1)} %shard_map.125.refs_0_.low_ref), channel_id=1, source_target_pairs={{0,1},{1,0},{2,3},{3,2},{4,5},{5,4},{6,7},{7,6},{8,9},{9,8},{10,11... | collective-permute-start | bytes 98312 | tf_op jit(solution)/shard_map/ppermute | solution.py:362
  28.4 4.9 %copy-start.9 = (s32[16]{0:T(128)S(1)}, s32[16]{0:T(128)}, u32[]{:S(2)}) copy-start(s32[16]{0:T(128)} %capacity_ref.1) | copy-start | bytes 196
  28.4 14.0 %collective-permute-start.12 = (bf16[128,1024]{1,0:T(8,128)(2,1)S(1)}, bf16[128,1024]{1,0:T(8,128)(2,1)S(1)}, u32[]{:S(2)}, u32[]{:S(2)}) collective-permute-start(bf16[128,1024]{1,0:T(8,128)(2,1)S(1)} %get-tuple-element.26.xz_ref), channel_id=1, source_target_pairs={{0,2},{2,0},{4,6},{6,4},{8,10},{10,8},{12,14},{14,12},{1,3},{3,1},... | collective-permute-start | bytes 786440 | tf_op jit(solution)/shard_map/ppermute | solution.py:365
  33.3 1.9 %copy-start.3 = (bf16[1024,16]{0,1:T(8,128)(2,1)S(1)}, bf16[1024,16]{0,1:T(8,128)(2,1)}, u32[]{:S(2)}) copy-start(bf16[1024,16]{0,1:T(8,128)(2,1)} %param.15) | copy-start | bytes 98308
  34.4 18.2 %collective-permute-start.15 = (bf16[128,1024]{1,0:T(8,128)(2,1)S(1)}, bf16[128,1024]{1,0:T(8,128)(2,1)S(1)}, u32[]{:S(2)}, u32[]{:S(2)}) collective-permute-start(bf16[128,1024]{1,0:T(8,128)(2,1)S(1)} %get-tuple-element.37.xz_ref), channel_id=1, source_target_pairs={{0,2},{2,0},{4,6},{6,4},{8,10},{10,8},{12,14},{14,12},{1,3},{3,1},... | collective-permute-start | bytes 786440 | tf_op jit(solution)/shard_map/ppermute | solution.py:365
  41.0 8.2 %collective-permute-start.11 = (bf16[128,1024]{1,0:T(8,128)(2,1)S(1)}, bf16[128,1024]{1,0:T(8,128)(2,1)S(1)}, u32[]{:S(2)}, u32[]{:S(2)}) collective-permute-start(bf16[128,1024]{1,0:T(8,128)(2,1)S(1)} %get-tuple-element.31), channel_id=1, source_target_pairs={{0,2},{2,0},{4,6},{6,4},{8,10},{10,8},{12,14},{14,12},{1,3},{3,1},... | collective-permute-start | bytes 786440 | tf_op jit(solution)/shard_map/ppermute | solution.py:365
  42.4 6.8 %copy-start.1 = (bf16[1,128,2048]{2,1,0:T(8,128)(2,1)S(1)}, bf16[1,128,2048]{2,1,0:T(8,128)(2,1)}, u32[]{:S(2)}) copy-start(bf16[1,128,2048]{2,1,0:T(8,128)(2,1)} %param.12) | copy-start | bytes 1572868
  42.4 6.8 %copy-start.2 = (bf16[1,128,2048]{2,1,0:T(8,128)(2,1)S(1)}, bf16[1,128,2048]{2,1,0:T(8,128)(2,1)}, u32[]{:S(2)}) copy-start(bf16[1,128,2048]{2,1,0:T(8,128)(2,1)} %param.13) | copy-start | bytes 1572868
  47.1 12.0 %collective-permute-start.17 = (bf16[128,1024]{1,0:T(8,128)(2,1)S(1)}, bf16[128,1024]{1,0:T(8,128)(2,1)S(1)}, u32[]{:S(2)}, u32[]{:S(2)}) collective-permute-start(bf16[128,1024]{1,0:T(8,128)(2,1)S(1)} %get-tuple-element.41), channel_id=1, source_target_pairs={{0,2},{2,0},{4,6},{6,4},{8,10},{10,8},{12,14},{14,12},{1,3},{3,1},... | collective-permute-start | bytes 786440 | tf_op jit(solution)/shard_map/ppermute | solution.py:365
  49.3 28.8 %collective-permute-start.19 = (bf16[128,1024]{1,0:T(8,128)(2,1)S(1)}, bf16[128,1024]{1,0:T(8,128)(2,1)S(1)}, u32[]{:S(2)}, u32[]{:S(2)}) collective-permute-start(bf16[128,1024]{1,0:T(8,128)(2,1)S(1)} %get-tuple-element.38.refs_5_), channel_id=1, source_target_pairs={{0,12},{2,14},{4,0},{6,2},{8,4},{10,6},{12,8},{14,10},{1,13},{3,15... | collective-permute-start | bytes 786440 | tf_op jit(solution)/shard_map/ppermute | solution.py:368
  52.6 6.9 %copy-start.4 = (bf16[1,128,1024]{2,1,0:T(8,128)(2,1)S(1)}, bf16[1,128,1024]{2,1,0:T(8,128)(2,1)}, u32[]{:S(2)}) copy-start(bf16[1,128,1024]{2,1,0:T(8,128)(2,1)} %param.14) | copy-start | bytes 786436
  52.6 15.2 %collective-permute-start.13 = (bf16[128,2048]{1,0:T(8,128)(2,1)S(1)}, bf16[128,2048]{1,0:T(8,128)(2,1)S(1)}, u32[]{:S(2)}, u32[]{:S(2)}) collective-permute-start(bf16[128,2048]{1,0:T(8,128)(2,1)S(1)} %get-tuple-element.35.k_own), channel_id=1, source_target_pairs={{0,1},{1,0},{2,3},{3,2},{4,5},{5,4},{6,7},{7,6},{8,9},{9,8},{10,11... | collective-permute-start | bytes 1572872 | tf_op jit(solution)/shard_map/ppermute | solution.py:362
  57.4 8.8 %collective-permute-start.16 = (bf16[128,1024]{1,0:T(8,128)(2,1)S(1)}, bf16[128,1024]{1,0:T(8,128)(2,1)S(1)}, u32[]{:S(2)}, u32[]{:S(2)}) collective-permute-start(bf16[128,1024]{1,0:T(8,128)(2,1)S(1)} %get-tuple-element.40), channel_id=1, source_target_pairs={{0,2},{2,0},{4,6},{6,4},{8,10},{10,8},{12,14},{14,12},{1,3},{3,1},... | collective-permute-start | bytes 786440 | tf_op jit(solution)/shard_map/ppermute | solution.py:365
  59.1 19.0 %collective-permute-start.20 = (bf16[128,1024]{1,0:T(8,128)(2,1)S(1)}, bf16[128,1024]{1,0:T(8,128)(2,1)S(1)}, u32[]{:S(2)}, u32[]{:S(2)}) collective-permute-start(bf16[128,1024]{1,0:T(8,128)(2,1)S(1)} %shard_map.132.refs_5_), channel_id=1, source_target_pairs={{0,8},{2,10},{4,12},{6,14},{8,0},{10,2},{12,4},{14,6},{1,9},{3,11}... | collective-permute-start | bytes 786440 | tf_op jit(solution)/shard_map/ppermute | solution.py:368
  59.2 8.7 %copy-start = (bf16[1,128,2048]{2,1,0:T(8,128)(2,1)S(1)}, bf16[1,128,2048]{2,1,0:T(8,128)(2,1)}, u32[]{:S(2)}) copy-start(bf16[1,128,2048]{2,1,0:T(8,128)(2,1)} %param.11) | copy-start | bytes 1572868
  59.2 8.7 %copy-start.6 = (s32[1,128]{1,0:T(1,128)S(1)}, s32[1,128]{1,0:T(1,128)}, u32[]{:S(2)}) copy-start(s32[1,128]{1,0:T(1,128)} %doc_own.3) | copy-start | bytes 1540
  59.2 8.7 %copy-start.8 = (s32[1,128]{1,0:T(1,128)S(1)}, s32[1,128]{1,0:T(1,128)}, u32[]{:S(2)}) copy-start(s32[1,128]{1,0:T(1,128)} %ahead_ref.3) | copy-start | bytes 1540
  59.2 8.7 %collective-permute-start.14 = (bf16[128,2048]{1,0:T(8,128)(2,1)S(1)}, bf16[128,2048]{1,0:T(8,128)(2,1)S(1)}, u32[]{:S(2)}, u32[]{:S(2)}) collective-permute-start(bf16[128,2048]{1,0:T(8,128)(2,1)S(1)} %get-tuple-element.36.v_own), channel_id=1, source_target_pairs={{0,1},{1,0},{2,3},{3,2},{4,5},{5,4},{6,7},{7,6},{8,9},{9,8},{10,11... | collective-permute-start | bytes 1572872 | tf_op jit(solution)/shard_map/ppermute | solution.py:362
  66.1 7.9 %collective-permute-start.18 = (bf16[128,1024]{1,0:T(8,128)(2,1)S(1)}, bf16[128,1024]{1,0:T(8,128)(2,1)S(1)}, u32[]{:S(2)}, u32[]{:S(2)}) collective-permute-start(bf16[128,1024]{1,0:T(8,128)(2,1)S(1)} %get-tuple-element.43), channel_id=1, source_target_pairs={{0,2},{2,0},{4,6},{6,4},{8,10},{10,8},{12,14},{14,12},{1,3},{3,1},... | collective-permute-start | bytes 786440 | tf_op jit(solution)/shard_map/ppermute | solution.py:365
  67.8 10.3 %collective-permute-start.21 = (bf16[128,1024]{1,0:T(8,128)(2,1)S(1)}, bf16[128,1024]{1,0:T(8,128)(2,1)S(1)}, u32[]{:S(2)}, u32[]{:S(2)}) collective-permute-start(bf16[128,1024]{1,0:T(8,128)(2,1)S(1)} %shard_map.134.rest_0_), channel_id=1, source_target_pairs={{0,4},{2,6},{4,8},{6,10},{8,12},{10,14},{12,0},{14,2},{1,5},{3,7},... | collective-permute-start | bytes 786440 | tf_op jit(solution)/shard_map/ppermute | solution.py:368

commit v9 on v8

--- a/solution.py
+++ b/solution.py
@@ -17,6 +17,7 @@
 LOAD_VMEM = 44 * 1024 * 1024
 ATTEND_VMEM = 8 * 1024 * 1024
 SMALL_VMEM = 4 * 1024 * 1024
+STEP = 512
 WINDOW = 4
 
 
@@ -242,88 +243,143 @@
     return square.T
 
 
-def expert_kernel(place, first, own_ref, kept_ref, router_ref, xz_ref, xy_ref, *refs):
-    step = 512
-    if first:
-        sources = refs[:4]
-        z_ref, y_ref, *staged, hidden_ref, mixed_ref, sems = refs[-7:]
-        weights = list(refs[:2]) + staged
-    else:
-        weights = refs[:4]
-        z_ref, y_ref, hidden_ref, mixed_ref = refs[-4:]
-    chunks = [(w, c) for w in (2, 3) for c in range(0, weights[w].shape[1], step)]
-
-    def load(index):
-        which, column = chunks[index]
-        cols = pl.ds(column, step)
-        return pltpu.make_async_copy(
-            sources[which].at[:, cols], weights[which].at[:, cols], sems.at[index]
-        )
-
-    def ready(which, column):
-        if first and which > 1:
-            index = chunks.index((which, column))
-            load(index).wait()
-            if index + WINDOW < len(chunks):
-                load(index + WINDOW).start()
-
-    if first:
-        for index in range(WINDOW):
-            load(index).start()
-    own = own_ref[0]
-    rows = xz_ref.shape[0]
-    x = jnp.concatenate([xz_ref[...], xy_ref[...]], axis=0)
+def gate_pairs(place, own_ref, kept_ref, router_ref, xz_ref, xy_ref):
     gates = [
-        gate_columns(own, router_ref, x_ref[...], kept_ref[2 * place + side])
+        gate_columns(own_ref[0], router_ref, x_ref[...], kept_ref[2 * place + side])
         for side, x_ref in enumerate((xz_ref, xy_ref))
     ]
+    return [jnp.concatenate([g[:, which : which + 1] for g in gates], axis=0) for which in range(2)]
+
+
+def run_expert_pair(xz_ref, xy_ref, weights, hidden_ref, ready, emit):
+    x = jnp.concatenate([xz_ref[...], xy_ref[...]], axis=0)
     for which in range(2):
-        gate = jnp.concatenate([g[:, which : which + 1] for g in gates], axis=0)
         w1_ref, w2_ref = weights[2 * which], weights[2 * which + 1]
-        for column in range(0, w1_ref.shape[1], step):
-            cols = slice(column, column + step)
+        for column in range(0, w1_ref.shape[1], STEP):
+            cols = slice(column, column + STEP)
             ready(2 * which, column)
             hidden = jnp.dot(x, w1_ref[:, cols], preferred_element_type=jnp.float32)
             hidden = jnp.maximum(hidden, 0.0)
             hidden_ref[which, :, cols] = (hidden * hidden).astype(jnp.bfloat16)
-        for column in range(0, w2_ref.shape[1], step):
-            cols = slice(column, column + step)
+        for column in range(0, w2_ref.shape[1], STEP):
+            cols = slice(column, column + STEP)
             ready(2 * which + 1, column)
             result = jnp.dot(hidden_ref[which], w2_ref[:, cols], preferred_element_type=jnp.float32)
-            if which == 0:
-                mixed_ref[:, cols] = result * gate
-            else:
-                mixed = (mixed_ref[:, cols] + result * gate).astype(jnp.bfloat16)
-                z_ref[:, cols] = mixed[:rows]
-                y_ref[:, cols] = mixed[rows:]
-
-
-def run_piece(place, first, own, kept, router, from_line, from_side, weights, after):
+            emit(which, cols, result)
+
+
+def expert_kernel(
+    place, own_ref, kept_ref, router_ref, xz_ref, xy_ref, w1a, w2a, w1b, w2b, *refs
+):
+    z_ref, y_ref, hidden_ref, mixed_ref = refs[-4:]
+    rows = xz_ref.shape[0]
+    gates = gate_pairs(place, own_ref, kept_ref, router_ref, xz_ref, xy_ref)
+
+    def emit(which, cols, result):
+        if which == 0:
+            mixed_ref[:, cols] = result * gates[0]
+        else:
+            mixed = (mixed_ref[:, cols] + result * gates[1]).astype(jnp.bfloat16)
+            z_ref[:, cols] = mixed[:rows]
+            y_ref[:, cols] = mixed[rows:]
+
+    weights = (w1a, w2a, w1b, w2b)
+    run_expert_pair(xz_ref, xy_ref, weights, hidden_ref, lambda which, column: None, emit)
+
+
+def first_kernel(xz_ref, xy_ref, w1a, w2a, *refs):
+    sources = refs[:2]
+    own_ref, far_ref, w1b, w2b, hidden_ref, sems = refs[-6:]
+    targets = (w1b, w2b)
+    chunks = [(w, c) for w in range(2) for c in range(0, targets[w].shape[1], STEP)]
+
+    def load(index):
+        which, column = chunks[index]
+        cols = pl.ds(column, STEP)
+        return pltpu.make_async_copy(
+            sources[which].at[:, cols], targets[which].at[:, cols], sems.at[index]
+        )
+
+    def ready(which, column):
+        if which > 1:
+            index = chunks.index((which - 2, column))
+            load(index).wait()
+            if index + WINDOW < len(chunks):
+                load(index + WINDOW).start()
+
+    def emit(which, cols, result):
+        (own_ref, far_ref)[which][:, cols] = result.astype(jnp.bfloat16)
+
+    for index in range(WINDOW):
+        load(index).start()
+    run_expert_pair(xz_ref, xy_ref, (w1a, w2a, w1b, w2b), hidden_ref, ready, emit)
+
+
+def gate_kernel(place, own_ref, kept_ref, router_ref, xz_ref, xy_ref, mine_ref, far_ref, *refs):
+    z_ref, y_ref = refs[-2:]
+    rows = xz_ref.shape[0]
+    gates = gate_pairs(place, own_ref, kept_ref, router_ref, xz_ref, xy_ref)
+    mixed = mine_ref[...].astype(jnp.float32) * gates[0]
+    mixed = (mixed + far_ref[...].astype(jnp.float32) * gates[1]).astype(jnp.bfloat16)
+    z_ref[...] = mixed[:rows]
+    y_ref[...] = mixed[rows:]
+
+
+def gate_piece(place, own, kept, router, from_line, from_side, raw, after):
+    smem = pl.BlockSpec(memory_space=pltpu.SMEM)
+    vmem = pl.BlockSpec(memory_space=pltpu.VMEM)
+    anywhere = pl.BlockSpec(memory_space=pl.ANY)
+    piece = jax.ShapeDtypeStruct(from_line.shape, jnp.bfloat16)
+    return pl.pallas_call(
+        functools.partial(gate_kernel, place),
+        out_shape=(piece, piece),
+        in_specs=[smem] + [vmem] * 6 + [anywhere] * len(after),
+        out_specs=(vmem, vmem),
+        compiler_params=pltpu.CompilerParams(vmem_limit_bytes=ATTEND_VMEM),
+    )(own, kept, router, from_line, from_side, *raw, *after)
+
+
+def run_first(from_line, from_side, own_weights, far_weights):
+    rows, width = from_line.shape
+    hidden = own_weights[0].shape[1]
+    vmem = pl.BlockSpec(memory_space=pltpu.VMEM)
+    hbm = pl.BlockSpec(memory_space=pltpu.HBM)
+    raw = jax.ShapeDtypeStruct((2 * rows, width), jnp.bfloat16)
+    return pl.pallas_call(
+        first_kernel,
+        out_shape=[raw, raw] + [pltpu.VMEM(w.shape, w.dtype) for w in far_weights],
+        in_specs=[vmem] * 4 + [hbm] * 2,
+        out_specs=[vmem] * 4,
+        scratch_shapes=[
+            pltpu.VMEM((2, 2 * rows, hidden), jnp.bfloat16),
+            pltpu.SemaphoreType.DMA(((hidden + width) // STEP,)),
+        ],
+        compiler_params=pltpu.CompilerParams(vmem_limit_bytes=FIRST_VMEM),
+        cost_estimate=pl.CostEstimate(
+            flops=16 * rows * width * hidden, bytes_accessed=8 * rows * width, transcendentals=0
+        ),
+    )(from_line, from_side, *own_weights, *far_weights)
+
+
+def run_piece(place, own, kept, router, from_line, from_side, weights, after):
     rows, width = from_line.shape
     hidden = weights[0].shape[1]
     smem = pl.BlockSpec(memory_space=pltpu.SMEM)
     vmem = pl.BlockSpec(memory_space=pltpu.VMEM)
-    hbm = pl.BlockSpec(memory_space=pltpu.HBM)
     anywhere = pl.BlockSpec(memory_space=pl.ANY)
     piece = jax.ShapeDtypeStruct((rows, width), jnp.bfloat16)
-    staged = [pltpu.VMEM(w.shape, w.dtype) for w in weights[2:]] if first else []
-    scratch = [
-        pltpu.VMEM((2, 2 * rows, hidden), jnp.bfloat16),
-        pltpu.VMEM((2 * rows, width), jnp.float32),
-    ]
-    if first:
-        scratch.append(pltpu.SemaphoreType.DMA(((hidden + width) // 512,)))
     return pl.pallas_call(
-        functools.partial(expert_kernel, place, first),
-        out_shape=[piece, piece] + staged,
-        in_specs=[smem] + [vmem] * 6 + [hbm if first else vmem] * 2 + [anywhere] * len(after),
-        out_specs=[vmem] * (2 + len(staged)),
-        scratch_shapes=scratch,
-        compiler_params=pltpu.CompilerParams(vmem_limit_bytes=FIRST_VMEM if first else EXPERT_VMEM),
+        functools.partial(expert_kernel, place),
+        out_shape=(piece, piece),
+        in_specs=[smem] + [vmem] * 8 + [anywhere] * len(after),
+        out_specs=(vmem, vmem),
+        scratch_shapes=[
+            pltpu.VMEM((2, 2 * rows, hidden), jnp.bfloat16),
+            pltpu.VMEM((2 * rows, width), jnp.float32),
+        ],
+        compiler_params=pltpu.CompilerParams(vmem_limit_bytes=EXPERT_VMEM),
         cost_estimate=pl.CostEstimate(
-            flops=16 * rows * width * hidden,
-            bytes_accessed=8 * rows * width,
-            transcendentals=0,
+            flops=16 * rows * width * hidden, bytes_accessed=8 * rows * width, transcendentals=0
         ),
     )(own, kept, router, from_line, from_side, *weights, *after)
 
@@ -376,40 +432,51 @@
     from_line = [latent[0], along(latent[0], 1)]
     from_side = [swap_side(latent[0])]
     table = pack(routes.transpose(2, 0, 1), segments)
+    own_weights = load_weights(expert_in[0], expert_out[0], (table,))
+    hold = own_weights
     span = 1
     while span < line:
         here = len(from_line) - 1
         flip = flipped(table, span)
-        from_line[here], table = join(table, flip, passed=from_line[here], after=(from_side[-1],))
-        span *= 2
+        after = (from_side[-1], *hold)
+        from_line[here], table = join(table, flip, passed=from_line[here], after=after)
         from_line.append(along(from_line[here], 1))
         from_side.append(swap_side(from_line[here]))
+        if span == 1:
+            *raw, far_first, far_second = run_first(
+                from_line[0], from_side[0], own_weights, far_weights
+            )
+            weights = (*own_weights, far_first, far_second)
+            hold = raw
+        span *= 2
     table = join(table, swap_side(table))
     far_table = swap_core(table)
     doc_far = far_table[0, TOPK : TOPK + 1, :]
-    own_weights = load_weights(expert_in[0], expert_out[0], (table,))
-    kept, from_line[-1] = kept_rows(own, capacity, table, far_table, from_line[-1], own_weights)
+    kept, from_line[-1] = kept_rows(own, capacity, table, far_table, from_line[-1], ())
     from_side.append(swap_side(from_line[-1]))
-    weights = list(own_weights) + far_weights
-
-    def piece(step, weights, *after):
+
+    def piece(step, *after):
         return run_piece(
-            step, step == 1, own, kept, router.T, from_line[step], from_side[step], weights, after
+            step, own, kept, router.T, from_line[step], from_side[step], weights, after
         )
 
-    one, theirs, *weights[2:] = piece(1, weights)
+    one, theirs = piece(1)
     one_far = swap_side(theirs)
-    two, theirs = piece(2, weights, one)
+    two, theirs = piece(2, one)
     two_far = swap_side(theirs)
-    k_near, v_near, first = add(one, one_far, after=(two,), staged=(k_near, v_near))
+    first = add(one, one_far, after=(two,))
     home = [along(first, line - 1)]
-    three, theirs = piece(3, weights, two, first)
+    near, theirs = gate_piece(
+        0, own, kept, router.T, from_line[0], from_side[0], raw, (first,)
+    )
+    near_far = swap_side(theirs)
+    three, theirs = piece(3, two, near)
     three_far = swap_side(theirs)
-    second = add(two, two_far, after=(three,))
+    k_near, v_near, second = add(
+        two, two_far, after=(three, home[0]), staged=(k_near, v_near)
+    )
     home.append(along(second, line - 2))
-    near, theirs = piece(0, weights, three, second)
-    near_far = swap_side(theirs)
-    third = add(three, three_far, after=(near,))
+    third = add(three, three_far, after=(second, near_far))
     home.append(along(third, line - 3))
     swapped = (k_near, swap_core(k_near), v_near, swap_core(v_near))
     half = attention(0, doc_far, *swapped, after=(third,))

time: 79.2 us -> 113 us (1.43)
  local copies, waits for them, and re-layouts: 1.38 us -> 22.5 us
  waiting for transfers between devices: 24.9 us -> 32.7 us
  starting transfers between devices: 23 us -> 25.7 us
  Pallas kernels: 27.9 us -> 30 us
    unnamed x20 -> x48, local copies, waits for them, and re-layouts: 1.38 us -> 22.5 us
    ppermute x6, waiting for transfers between devices: 9.21 us -> 17.3 us  [along(): lax.ppermute(x, 'expert', [(2 * z + y, 2 * ((z + step) % line) + y) for z...]
    ppermute x2, waiting for transfers between devices: 5.88 us -> 0.01 us  [flipped(): lax.ppermute(x, 'expert', [(2 * z + y, 2 * (z ^ span) + y) for z, y in sp...]
    ppermute x9, waiting for transfers between devices: 9.85 us -> 15.3 us  [swap_side(): return lax.ppermute(x, 'expert', across)]
    ppermute x6, starting transfers between devices: 5.77 us -> 8.32 us  [along(): lax.ppermute(x, 'expert', [(2 * z + y, 2 * ((z + step) % line) + y) for z...]
    pallas_call x4 -> x5, Pallas kernels: 19.8 us -> 21.9 us  [the longest x3 14.1 us: run_piece(): pl.pallas_call(functools.partial(expert_kernel, place), out_shape=(piece,...]
  transfers between devices with their start and end apart: 22 -> 22, of which waited for: 10 -> 9; matrix products, arithmetic and copies ran while one was open for 0% -> 1% of each run, Pallas kernels for 35% -> 24%
where the time goes in v9:
time: 113 us
  waiting for transfers between devices  32.7 us (29%)
  Pallas kernels  30 us (27%)
  starting transfers between devices  25.7 us (23%)
  local copies, waits for them, and re-layouts  22.5 us (20%)
    unnamed x48, local copies, waits for them, and re-layouts  22.5 us
    ppermute x6, waiting for transfers between devices, along(): lax.ppermute(x, 'expert', [(2 * z + y, 2 * ((z + step) % line) + y) for z...  17.3 us
    ppermute x9, waiting for transfers between devices, swap_side(): return lax.ppermute(x, 'expert', across)  15.3 us
    pallas_call x3, Pallas kernels, run_piece(): pl.pallas_call(functools.partial(expert_kernel, place), out_shape=(piece,...  14.1 us
    ppermute x9, starting transfers between devices, swap_side(): return lax.ppermute(x, 'expert', across)  12.3 us
    ppermute x6, starting transfers between devices, along(): lax.ppermute(x, 'expert', [(2 * z + y, 2 * ((z + step) % line) + y) for z...  8.32 us
    pallas_call x1, Pallas kernels, run_first(): pl.pallas_call(first_kernel, out_shape=[raw, raw] + [pltpu.VMEM(w.shape,...  7.21 us
    ppermute x2, starting transfers between devices, flipped(): lax.ppermute(x, 'expert', [(2 * z + y, 2 * (z ^ span) + y) for z, y in sp...  4 us
  transfers between devices with their start and end apart: 22, of which 9 were waited for; matrix products, arithmetic and copies ran while one was open for 1% of the time, Pallas kernels for 24%

profile of v9, /device:TPU:0, one launch (start us, length us, event | category | flops | bytes accessed | tf_op | source)
XLA Modules:
  0.0 112.7 jit_solution(276962870297250760)
XLA Ops:
  0.6 0.5 collective-permute-start.6
  1.1 0.1 collective-permute-start.7
  1.2 2.9 %collective-permute-start.2 = (bf16[128,1024]{1,0:T(8,128)(2,1)}, bf16[128,1024]{1,0:T(8,128)(2,1)S(1)}, u32[]{:S(2)}, u32[]{:S(2)}) collective-permute-start(bf16[128,1024]{1,0:T(8,128)(2,1)} %bitcast.17), channel_id=1, source_target_pairs={{0,2},{2,0},{4,6},{6,4},{8,10},{10,8},{12,14},{14,12},{1,3},{3,1},... | collective-permute-start | bytes 786440 | tf_op jit(solution)/shard_map/ppermute | solution.py:421
  4.2 1.6 %collective-permute-start.1 = (bf16[128,1024]{1,0:T(8,128)(2,1)}, bf16[128,1024]{1,0:T(8,128)(2,1)S(1)}, u32[]{:S(2)}, u32[]{:S(2)}) collective-permute-start(bf16[128,1024]{1,0:T(8,128)(2,1)} %bitcast.18), channel_id=1, source_target_pairs={{0,4},{2,6},{4,8},{6,10},{8,12},{10,14},{12,0},{14,2},{1,5},{3,7},... | collective-permute-start | bytes 786440 | tf_op jit(solution)/shard_map/ppermute | solution.py:424
  5.8 0.7 copy-done.19
  6.4 0.7 copy-done.21
  7.1 1.6 %collective-permute-start = (s32[1,8,128]{2,1,0:T(8,128)S(1)}, s32[1,8,128]{2,1,0:T(8,128)S(1)}, u32[]{:S(2)}, u32[]{:S(2)}) collective-permute-start(s32[1,8,128]{2,1,0:T(8,128)S(1)} %shard_map.122.refs_0_.first_ref), channel_id=1, source_target_pairs={{0,4},{2,6},{4,0},{6,2},{8,12},{10,14},{12,8},{14,10},{1,5},{3,7},... | collective-permute-start | bytes 12296 | tf_op jit(solution)/shard_map/ppermute | solution.py:427
  8.8 3.5 %shard_map.123 = (bf16[1024,2048]{1,0:T(8,128)(2,1)S(1)}, bf16[2048,1024]{1,0:T(8,128)(2,1)S(1)}) custom-call(bf16[1024,2048]{1,0:T(8,128)(2,1)} %bitcast.29, bf16[2048,1024]{1,0:T(8,128)(2,1)} %bitcast.31, s32[1,8,128]{2,1,0:T(8,128)S(1)} %shard_map.122.refs_0_.first_ref), custom_call_target="tpu_custom_call" | custom-call | tf_op jit(solution)/shard_map/pallas_call | solution.py:155
  12.3 0.0 collective-permute-done.2.refs_1_.xy_ref
  12.3 2.1 %collective-permute-done.1.refs_0_ = bf16[128,1024]{1,0:T(8,128)(2,1)S(1)} collective-permute-done((bf16[128,1024]{1,0:T(8,128)(2,1)}, bf16[128,1024]{1,0:T(8,128)(2,1)S(1)}, u32[]{:S(2)}, u32[]{:S(2)}) %collective-permute-start.1) | collective-permute-done | bytes 262176 | tf_op jit(solution)/shard_map/ppermute | solution.py:424
  14.4 0.5 collective-permute-start.5
  14.9 0.0 collective-permute-start.4
  14.9 2.4 %collective-permute-start.3 = (s32[2,8,128]{2,1,0:T(8,128)S(1)}, s32[2,8,128]{2,1,0:T(8,128)S(1)}, u32[]{:S(2)}, u32[]{:S(2)}) collective-permute-start(s32[2,8,128]{2,1,0:T(8,128)S(1)} %get-tuple-element.27.first_ref), channel_id=1, source_target_pairs={{0,8},{2,10},{4,12},{6,14},{8,0},{10,2},{12,4},{14,6},{1,9},{3,11}... | collective-permute-start | bytes 24584 | tf_op jit(solution)/shard_map/ppermute | solution.py:427
  17.3 2.1 %copy-done.10 = bf16[1024,2048]{1,0:T(8,128)(2,1)} copy-done((bf16[1024,2048]{1,0:T(8,128)(2,1)}, bf16[1024,2048]{1,0:T(8,128)(2,1)S(1)}, u32[]{:S(2)}) %copy-start.10) | copy-done | bytes 4194328
  19.3 0.0 collective-permute-done.7.refs_1_
  19.3 1.9 %copy-done.12 = bf16[2048,1024]{1,0:T(8,128)(2,1)} copy-done((bf16[2048,1024]{1,0:T(8,128)(2,1)}, bf16[2048,1024]{1,0:T(8,128)(2,1)S(1)}, u32[]{:S(2)}) %copy-start.12) | copy-done | bytes 4194328
  21.3 2.2 %copy-done.11 = bf16[1024,2048]{1,0:T(8,128)(2,1)S(1)} copy-done((bf16[1024,2048]{1,0:T(8,128)(2,1)S(1)}, bf16[1024,2048]{1,0:T(8,128)(2,1)}, u32[]{:S(2)}) %copy-start.11) | copy-done | bytes 4194328
  23.5 2.2 %copy-done.13 = bf16[2048,1024]{1,0:T(8,128)(2,1)S(1)} copy-done((bf16[2048,1024]{1,0:T(8,128)(2,1)S(1)}, bf16[2048,1024]{1,0:T(8,128)(2,1)}, u32[]{:S(2)}) %copy-start.13) | copy-done | bytes 4194328
  25.7 7.2 %shard_map.125 = (bf16[256,1024]{1,0:T(8,128)(2,1)S(1)}, bf16[256,1024]{1,0:T(8,128)(2,1)S(1)}, bf16[1024,2048]{1,0:T(8,128)(2,1)S(1)}, bf16[2048,1024]{1,0:T(8,128)(2,1)S(1)}) custom-call(bf16[128,1024]{1,0:T(8,128)(2,1)S(1)} %bitcast.19, bf16[128,1024]{1,0:T(8,128)(2,1)S(1)} %collective-permute-done.2.refs_1_.xy_ref, ...), custom_call_target="tpu_custom_call" | custom-call | flops 4294967296 | bytes 1048576 | tf_op jit(solution)/shard_map/pallas_call | solution.py:348
  32.9 2.1 %copy-done.4 = bf16[1024,2048]{1,0:T(8,128)(2,1)} copy-done((bf16[1024,2048]{1,0:T(8,128)(2,1)}, bf16[1024,2048]{1,0:T(8,128)(2,1)S(1)}, u32[]{:S(2)}) %copy-start.4) | copy-done | bytes 4194328
  35.0 1.9 %copy-done.7 = bf16[2048,1024]{1,0:T(8,128)(2,1)} copy-done((bf16[2048,1024]{1,0:T(8,128)(2,1)}, bf16[2048,1024]{1,0:T(8,128)(2,1)S(1)}, u32[]{:S(2)}) %copy-start.7) | copy-done | bytes 4194328
  36.9 2.3 %collective-permute-start.10 = (bf16[128,1024]{1,0:T(8,128)(2,1)S(1)}, bf16[128,1024]{1,0:T(8,128)(2,1)S(1)}, u32[]{:S(2)}, u32[]{:S(2)}) collective-permute-start(bf16[128,1024]{1,0:T(8,128)(2,1)S(1)} %get-tuple-element.32.xz_ref), channel_id=1, source_target_pairs={{0,4},{2,6},{4,8},{6,10},{8,12},{10,14},{12,0},{14,2},{1,5},{3,7},... | collective-permute-start | bytes 786440 | tf_op jit(solution)/shard_map/ppermute | solution.py:424
  39.2 1.5 %collective-permute-start.8 = (s32[4,8,128]{2,1,0:T(8,128)S(1)}, s32[4,8,128]{2,1,0:T(8,128)S(1)}, u32[]{:S(2)}, u32[]{:S(2)}) collective-permute-start(s32[4,8,128]{2,1,0:T(8,128)S(1)} %get-tuple-element.31.first_ref), channel_id=1, source_target_pairs={{0,2},{2,0},{4,6},{6,4},{8,10},{10,8},{12,14},{14,12},{1,3},{3,1},... | collective-permute-start | bytes 49160 | tf_op jit(solution)/shard_map/ppermute | solution.py:421
  40.7 2.2 %collective-permute-done.8.second_ref = s32[4,8,128]{2,1,0:T(8,128)S(1)} collective-permute-done((s32[4,8,128]{2,1,0:T(8,128)S(1)}, s32[4,8,128]{2,1,0:T(8,128)S(1)}, u32[]{:S(2)}, u32[]{:S(2)}) %collective-permute-start.8) | collective-permute-done | bytes 16416 | tf_op jit(solution)/shard_map/ppermute | solution.py:421
  42.9 0.0 collective-permute-start.9
  42.9 1.5 %collective-permute-start.11 = (bf16[128,1024]{1,0:T(8,128)(2,1)S(1)}, bf16[128,1024]{1,0:T(8,128)(2,1)S(1)}, u32[]{:S(2)}, u32[]{:S(2)}) collective-permute-start(bf16[128,1024]{1,0:T(8,128)(2,1)S(1)} %get-tuple-element.32.xz_ref), channel_id=1, source_target_pairs={{0,2},{2,0},{4,6},{6,4},{8,10},{10,8},{12,14},{14,12},{1,3},{3,1},... | collective-permute-start | bytes 786440 | tf_op jit(solution)/shard_map/ppermute | solution.py:421
  44.5 0.9 collective-permute-done.10.refs_0_
  45.3 1.1 shard_map.128
  46.4 2.2 %copy-done.1 = bf16[1024,2048]{1,0:T(8,128)(2,1)S(1)} copy-done((bf16[1024,2048]{1,0:T(8,128)(2,1)S(1)}, bf16[1024,2048]{1,0:T(8,128)(2,1)}, u32[]{:S(2)}) %copy-start.1) | copy-done | bytes 4194328
  48.6 2.2 %copy-done.3 = bf16[2048,1024]{1,0:T(8,128)(2,1)S(1)} copy-done((bf16[2048,1024]{1,0:T(8,128)(2,1)S(1)}, bf16[2048,1024]{1,0:T(8,128)(2,1)}, u32[]{:S(2)}) %copy-start.3) | copy-done | bytes 4194328
  50.8 2.2 %copy-done.5 = bf16[1024,2048]{1,0:T(8,128)(2,1)S(1)} copy-done((bf16[1024,2048]{1,0:T(8,128)(2,1)S(1)}, bf16[1024,2048]{1,0:T(8,128)(2,1)}, u32[]{:S(2)}) %copy-start.5) | copy-done | bytes 4194328
  53.0 2.2 %copy-done.8 = bf16[2048,1024]{1,0:T(8,128)(2,1)S(1)} copy-done((bf16[2048,1024]{1,0:T(8,128)(2,1)S(1)}, bf16[2048,1024]{1,0:T(8,128)(2,1)}, u32[]{:S(2)}) %copy-start.8) | copy-done | bytes 4194328
  55.2 4.7 %shard_map.129 = (bf16[128,1024]{1,0:T(8,128)(2,1)S(1)}, bf16[128,1024]{1,0:T(8,128)(2,1)S(1)}) custom-call(s32[1]{0:T(128)} %bitcast.2.own_ref, s32[8,8,128]{2,1,0:T(8,128)S(1)} %get-tuple-element.33.kept_ref, bf16[16,1024]{1,0:T(8,128)(2,1)S(1)} %bitcast.23, bf16[128,1024]{1,0:T(8,128)(2,1)S(1)} %get-tuple-element.28.xz_ref, ...), custom_call_target="tpu_custom_call" | custom-call | flops 4294967296 | bytes 1048576 | tf_op jit(solution)/shard_map/pallas_call | solution.py:371
  59.9 1.6 %collective-permute-start.14 = (bf16[128,1024]{1,0:T(8,128)(2,1)S(1)}, bf16[128,1024]{1,0:T(8,128)(2,1)S(1)}, u32[]{:S(2)}, u32[]{:S(2)}) collective-permute-start(bf16[128,1024]{1,0:T(8,128)(2,1)S(1)} %get-tuple-element.40), channel_id=1, source_target_pairs={{0,2},{2,0},{4,6},{6,4},{8,10},{10,8},{12,14},{14,12},{1,3},{3,1},... | collective-permute-start | bytes 786440 | tf_op jit(solution)/shard_map/ppermute | solution.py:421
  61.4 0.5 collective-permute-start.13
  61.9 0.0 collective-permute-done.11.xy_ref
  62.0 4.7 %shard_map.130 = (bf16[128,1024]{1,0:T(8,128)(2,1)S(1)}, bf16[128,1024]{1,0:T(8,128)(2,1)S(1)}) custom-call(s32[1]{0:T(128)} %bitcast.2.own_ref, s32[8,8,128]{2,1,0:T(8,128)S(1)} %get-tuple-element.33.kept_ref, bf16[16,1024]{1,0:T(8,128)(2,1)S(1)} %bitcast.24, bf16[128,1024]{1,0:T(8,128)(2,1)S(1)} %get-tuple-element.32.xz_ref, ...), custom_call_target="tpu_custom_call" | custom-call | flops 4294967296 | bytes 1048576 | tf_op jit(solution)/shard_map/pallas_call | solution.py:371
  66.7 1.6 %collective-permute-start.12 = (bf16[128,1024]{1,0:T(8,128)(2,1)S(1)}, bf16[128,1024]{1,0:T(8,128)(2,1)S(1)}, u32[]{:S(2)}, u32[]{:S(2)}) collective-permute-start(bf16[128,1024]{1,0:T(8,128)(2,1)S(1)} %get-tuple-element.38), channel_id=1, source_target_pairs={{0,2},{2,0},{4,6},{6,4},{8,10},{10,8},{12,14},{14,12},{1,3},{3,1},... | collective-permute-start | bytes 786440 | tf_op jit(solution)/shard_map/ppermute | solution.py:421
  68.3 0.9 collective-permute-done.14.second_ref
  69.2 0.1 shard_map.131.refs_0_
  69.2 1.1 collective-permute-start.15
  70.3 0.7 shard_map.132
  71.0 3.8 %collective-permute-done.13.xy_ref = bf16[128,1024]{1,0:T(8,128)(2,1)S(1)} collective-permute-done((bf16[128,1024]{1,0:T(8,128)(2,1)S(1)}, bf16[128,1024]{1,0:T(8,128)(2,1)S(1)}, u32[]{:S(2)}, u32[]{:S(2)}) %collective-permute-start.13) | collective-permute-done | bytes 262176 | tf_op jit(solution)/shard_map/ppermute | solution.py:421
  74.8 4.7 %shard_map.133 = (bf16[128,1024]{1,0:T(8,128)(2,1)S(1)}, bf16[128,1024]{1,0:T(8,128)(2,1)S(1)}) custom-call(s32[1]{0:T(128)} %bitcast.2.own_ref, s32[8,8,128]{2,1,0:T(8,128)S(1)} %get-tuple-element.33.kept_ref, bf16[16,1024]{1,0:T(8,128)(2,1)S(1)} %bitcast.26, bf16[128,1024]{1,0:T(8,128)(2,1)S(1)} %get-tuple-element.39.xz_ref, ...), custom_call_target="tpu_custom_call" | custom-call | flops 4294967296 | bytes 1048576 | tf_op jit(solution)/shard_map/pallas_call | solution.py:371
  79.5 0.0 copy-start.14
  79.5 0.0 copy-start.20
  79.5 0.0 copy-start.22
  79.5 1.6 %collective-permute-start.18 = (bf16[128,1024]{1,0:T(8,128)(2,1)S(1)}, bf16[128,1024]{1,0:T(8,128)(2,1)S(1)}, u32[]{:S(2)}, u32[]{:S(2)}) collective-permute-start(bf16[128,1024]{1,0:T(8,128)(2,1)S(1)} %get-tuple-element.45), channel_id=1, source_target_pairs={{0,2},{2,0},{4,6},{6,4},{8,10},{10,8},{12,14},{14,12},{1,3},{3,1},... | collective-permute-start | bytes 786440 | tf_op jit(solution)/shard_map/ppermute | solution.py:421
  81.1 0.5 collective-permute-start.19
  81.6 0.0 collective-permute-done.12.second_ref
  81.6 0.0 collective-permute-done.15.refs_3_
  81.7 0.1 shard_map.134
  81.8 5.6 %collective-permute-done.18.second_ref = bf16[128,1024]{1,0:T(8,128)(2,1)S(1)} collective-permute-done((bf16[128,1024]{1,0:T(8,128)(2,1)S(1)}, bf16[128,1024]{1,0:T(8,128)(2,1)S(1)}, u32[]{:S(2)}, u32[]{:S(2)}) %collective-permute-start.18) | collective-permute-done | bytes 262176 | tf_op jit(solution)/shard_map/ppermute | solution.py:421
  87.4 2.8 %collective-permute-done.19.refs_1_ = bf16[128,1024]{1,0:T(8,128)(2,1)S(1)} collective-permute-done((bf16[128,1024]{1,0:T(8,128)(2,1)S(1)}, bf16[128,1024]{1,0:T(8,128)(2,1)S(1)}, u32[]{:S(2)}, u32[]{:S(2)}) %collective-permute-start.19) | collective-permute-done | bytes 262176 | tf_op jit(solution)/shard_map/ppermute | solution.py:421
  90.2 0.1 shard_map.135.rest_0_
  90.3 0.1 collective-permute-start.21
  90.3 3.3 %collective-permute-start.20 = (bf16[128,1024]{1,0:T(8,128)(2,1)S(1)}, bf16[128,1024]{1,0:T(8,128)(2,1)S(1)}, u32[]{:S(2)}, u32[]{:S(2)}) collective-permute-start(bf16[128,1024]{1,0:T(8,128)(2,1)S(1)} %get-tuple-element.46.refs_0_), channel_id=1, source_target_pairs={{0,8},{2,10},{4,12},{6,14},{8,0},{10,2},{12,4},{14,6},{1,9},{3,11}... | collective-permute-start | bytes 786440 | tf_op jit(solution)/shard_map/ppermute | solution.py:424
  93.6 0.0 collective-permute-start.16
  93.6 0.5 collective-permute-start.17
  94.2 6.1 %collective-permute-done.21 = bf16[128,1024]{1,0:T(8,128)(2,1)S(1)} collective-permute-done((bf16[128,1024]{1,0:T(8,128)(2,1)S(1)}, bf16[128,1024]{1,0:T(8,128)(2,1)S(1)}, u32[]{:S(2)}, u32[]{:S(2)}) %collective-permute-start.21) | collective-permute-done | bytes 262176 | tf_op jit(solution)/shard_map/ppermute | solution.py:424
  100.2 8.3 %collective-permute-done.20 = bf16[128,1024]{1,0:T(8,128)(2,1)S(1)} collective-permute-done((bf16[128,1024]{1,0:T(8,128)(2,1)S(1)}, bf16[128,1024]{1,0:T(8,128)(2,1)S(1)}, u32[]{:S(2)}, u32[]{:S(2)}) %collective-permute-start.20) | collective-permute-done | bytes 262176 | tf_op jit(solution)/shard_map/ppermute | solution.py:424
  108.6 0.9 fusion
  109.5 1.6 %shard_map.136.rest_0_ = bf16[128,2048]{1,0:T(8,128)(2,1)} custom-call(s32[1]{0:T(128)} %bitcast.place_ref, bf16[128,2048]{1,0:T(8,128)(2,1)S(1)} %bitcast.15, bf16[128,2048]{1,0:T(8,128)(2,1)S(1)} %get-tuple-element.43.k_own, bf16[128,2048]{1,0:T(8,128)(2,1)S(1)} %collective-permute-done.16.k_far, bf16[128,2048]{1,0:T(8,128)(2,1)S(1)} %get-tuple-element.44.v_own, ...), custom_call_target="tpu_custom_call" | custom-call | flops 134217728 | bytes 1572864 | tf_op jit(solution)/shard_map/pallas_call | solution.py:68
  111.1 1.6 %shard_map.137 = bf16[128,2048]{1,0:T(8,128)(2,1)} custom-call(s32[1]{0:T(128)} %bitcast.place_ref, bf16[128,2048]{1,0:T(8,128)(2,1)S(1)} %bitcast.16, bf16[128,2048]{1,0:T(8,128)(2,1)S(1)} %get-tuple-element.43.k_own, bf16[128,2048]{1,0:T(8,128)(2,1)S(1)} %collective-permute-done.16.k_far, ...), custom_call_target="tpu_custom_call", output_to_operand_aliasing={{}: (9, {})} | custom-call | flops 134217728 | bytes 1572864 | tf_op jit(solution)/shard_map/pallas_call | solution.py:68
  (46 shorter events, 0.1 us)
Async XLA Ops:
  0.6 16.6 %collective-permute-start.6 = (bf16[1024,2048]{1,0:T(8,128)(2,1)}, bf16[1024,2048]{1,0:T(8,128)(2,1)S(1)}, u32[]{:S(2)}, u32[]{:S(2)}) collective-permute-start(bf16[1024,2048]{1,0:T(8,128)(2,1)} %bitcast.28), channel_id=1, source_target_pairs={{0,1},{1,0},{2,3},{3,2},{4,5},{5,4},{6,7},{7,6},{8,9},{9,8},{10,11... | collective-permute-start | bytes 12582920 | tf_op jit(solution)/shard_map/ppermute | solution.py:418
  1.1 18.2 %collective-permute-start.7 = (bf16[2048,1024]{1,0:T(8,128)(2,1)}, bf16[2048,1024]{1,0:T(8,128)(2,1)S(1)}, u32[]{:S(2)}, u32[]{:S(2)}) collective-permute-start(bf16[2048,1024]{1,0:T(8,128)(2,1)} %bitcast.30), channel_id=1, source_target_pairs={{0,1},{1,0},{2,3},{3,2},{4,5},{5,4},{6,7},{7,6},{8,9},{9,8},{10,11... | collective-permute-start | bytes 12582920 | tf_op jit(solution)/shard_map/ppermute | solution.py:418
  1.2 11.1 %collective-permute-start.2 = (bf16[128,1024]{1,0:T(8,128)(2,1)}, bf16[128,1024]{1,0:T(8,128)(2,1)S(1)}, u32[]{:S(2)}, u32[]{:S(2)}) collective-permute-start(bf16[128,1024]{1,0:T(8,128)(2,1)} %bitcast.17), channel_id=1, source_target_pairs={{0,2},{2,0},{4,6},{6,4},{8,10},{10,8},{12,14},{14,12},{1,3},{3,1},... | collective-permute-start | bytes 786440 | tf_op jit(solution)/shard_map/ppermute | solution.py:421
  4.2 10.2 %collective-permute-start.1 = (bf16[128,1024]{1,0:T(8,128)(2,1)}, bf16[128,1024]{1,0:T(8,128)(2,1)S(1)}, u32[]{:S(2)}, u32[]{:S(2)}) collective-permute-start(bf16[128,1024]{1,0:T(8,128)(2,1)} %bitcast.18), channel_id=1, source_target_pairs={{0,4},{2,6},{4,8},{6,10},{8,12},{10,14},{12,0},{14,2},{1,5},{3,7},... | collective-permute-start | bytes 786440 | tf_op jit(solution)/shard_map/ppermute | solution.py:424
  5.7 0.7 copy-start.19
  6.4 0.7 copy-start.21
  7.1 5.2 %collective-permute-start = (s32[1,8,128]{2,1,0:T(8,128)S(1)}, s32[1,8,128]{2,1,0:T(8,128)S(1)}, u32[]{:S(2)}, u32[]{:S(2)}) collective-permute-start(s32[1,8,128]{2,1,0:T(8,128)S(1)} %shard_map.122.refs_0_.first_ref), channel_id=1, source_target_pairs={{0,4},{2,6},{4,0},{6,2},{8,12},{10,14},{12,8},{14,10},{1,5},{3,7},... | collective-permute-start | bytes 12296 | tf_op jit(solution)/shard_map/ppermute | solution.py:427
  12.3 7.1 %copy-start = (bf16[1024,2048]{1,0:T(8,128)(2,1)}, bf16[1024,2048]{1,0:T(8,128)(2,1)S(1)}, u32[]{:S(2)}) copy-start(bf16[1024,2048]{1,0:T(8,128)(2,1)S(1)} %get-tuple-element.25.refs_2_.w1a) | copy-start | bytes 12582916
  12.3 7.0 %copy-start.2 = (bf16[2048,1024]{1,0:T(8,128)(2,1)}, bf16[2048,1024]{1,0:T(8,128)(2,1)S(1)}, u32[]{:S(2)}) copy-start(bf16[2048,1024]{1,0:T(8,128)(2,1)S(1)} %get-tuple-element.26.refs_3_.w2a) | copy-start | bytes 12582916
  14.4 6.9 %copy-start.15 = (bf16[1,128,1024]{2,1,0:T(8,128)(2,1)S(1)}, bf16[1,128,1024]{2,1,0:T(8,128)(2,1)}, u32[]{:S(2)}) copy-start(bf16[1,128,1024]{2,1,0:T(8,128)(2,1)} %param.14) | copy-start | bytes 786436
  14.4 22.5 %collective-permute-start.5 = (bf16[128,1024]{1,0:T(8,128)(2,1)S(1)}, bf16[128,1024]{1,0:T(8,128)(2,1)S(1)}, u32[]{:S(2)}, u32[]{:S(2)}) collective-permute-start(bf16[128,1024]{1,0:T(8,128)(2,1)S(1)} %get-tuple-element.28.xz_ref), channel_id=1, source_target_pairs={{0,2},{2,0},{4,6},{6,4},{8,10},{10,8},{12,14},{14,12},{1,3},{3,1},... | collective-permute-start | bytes 786440 | tf_op jit(solution)/shard_map/ppermute | solution.py:421
  14.9 22.0 %collective-permute-start.4 = (bf16[128,1024]{1,0:T(8,128)(2,1)S(1)}, bf16[128,1024]{1,0:T(8,128)(2,1)S(1)}, u32[]{:S(2)}, u32[]{:S(2)}) collective-permute-start(bf16[128,1024]{1,0:T(8,128)(2,1)S(1)} %get-tuple-element.28.xz_ref), channel_id=1, source_target_pairs={{0,4},{2,6},{4,8},{6,10},{8,12},{10,14},{12,0},{14,2},{1,5},{3,7},... | collective-permute-start | bytes 786440 | tf_op jit(solution)/shard_map/ppermute | solution.py:424
  14.9 30.4 %copy-start.23 = (s32[16]{0:T(128)S(1)}, s32[16]{0:T(128)}, u32[]{:S(2)}) copy-start(s32[16]{0:T(128)} %capacity_ref.1) | copy-start | bytes 196
  14.9 22.0 %collective-permute-start.3 = (s32[2,8,128]{2,1,0:T(8,128)S(1)}, s32[2,8,128]{2,1,0:T(8,128)S(1)}, u32[]{:S(2)}, u32[]{:S(2)}) collective-permute-start(s32[2,8,128]{2,1,0:T(8,128)S(1)} %get-tuple-element.27.first_ref), channel_id=1, source_target_pairs={{0,8},{2,10},{4,12},{6,14},{8,0},{10,2},{12,4},{14,6},{1,9},{3,11}... | collective-permute-start | bytes 24584 | tf_op jit(solution)/shard_map/ppermute | solution.py:427
  17.3 2.1 %copy-start.10 = (bf16[1024,2048]{1,0:T(8,128)(2,1)}, bf16[1024,2048]{1,0:T(8,128)(2,1)S(1)}, u32[]{:S(2)}) copy-start(bf16[1024,2048]{1,0:T(8,128)(2,1)S(1)} %collective-permute-done.6.refs_0_) | copy-start | bytes 12582916
  19.3 1.9 %copy-start.12 = (bf16[2048,1024]{1,0:T(8,128)(2,1)}, bf16[2048,1024]{1,0:T(8,128)(2,1)S(1)}, u32[]{:S(2)}) copy-start(bf16[2048,1024]{1,0:T(8,128)(2,1)S(1)} %collective-permute-done.7.refs_1_) | copy-start | bytes 12582916
  21.3 2.2 %copy-start.11 = (bf16[1024,2048]{1,0:T(8,128)(2,1)S(1)}, bf16[1024,2048]{1,0:T(8,128)(2,1)}, u32[]{:S(2)}) copy-start(bf16[1024,2048]{1,0:T(8,128)(2,1)} %copy-done.10) | copy-start | bytes 12582916
  23.5 2.2 %copy-start.13 = (bf16[2048,1024]{1,0:T(8,128)(2,1)S(1)}, bf16[2048,1024]{1,0:T(8,128)(2,1)}, u32[]{:S(2)}) copy-start(bf16[2048,1024]{1,0:T(8,128)(2,1)} %copy-done.12) | copy-start | bytes 12582916
  25.7 20.8 %copy-start.18 = (bf16[1024,16]{0,1:T(8,128)(2,1)S(1)}, bf16[1024,16]{0,1:T(8,128)(2,1)}, u32[]{:S(2)}) copy-start(bf16[1024,16]{0,1:T(8,128)(2,1)} %param.15) | copy-start | bytes 98308
  32.9 2.1 %copy-start.4 = (bf16[1024,2048]{1,0:T(8,128)(2,1)}, bf16[1024,2048]{1,0:T(8,128)(2,1)S(1)}, u32[]{:S(2)}) copy-start(bf16[1024,2048]{1,0:T(8,128)(2,1)S(1)} %get-tuple-element.34.w1b) | copy-start | bytes 12582916
  35.0 1.9 %copy-start.7 = (bf16[2048,1024]{1,0:T(8,128)(2,1)}, bf16[2048,1024]{1,0:T(8,128)(2,1)S(1)}, u32[]{:S(2)}) copy-start(bf16[2048,1024]{1,0:T(8,128)(2,1)S(1)} %get-tuple-element.35.w2b) | copy-start | bytes 12582916
  36.9 8.4 %collective-permute-start.10 = (bf16[128,1024]{1,0:T(8,128)(2,1)S(1)}, bf16[128,1024]{1,0:T(8,128)(2,1)S(1)}, u32[]{:S(2)}, u32[]{:S(2)}) collective-permute-start(bf16[128,1024]{1,0:T(8,128)(2,1)S(1)} %get-tuple-element.32.xz_ref), channel_id=1, source_target_pairs={{0,4},{2,6},{4,8},{6,10},{8,12},{10,14},{12,0},{14,2},{1,5},{3,7},... | collective-permute-start | bytes 786440 | tf_op jit(solution)/shard_map/ppermute | solution.py:424
  39.2 3.7 %collective-permute-start.8 = (s32[4,8,128]{2,1,0:T(8,128)S(1)}, s32[4,8,128]{2,1,0:T(8,128)S(1)}, u32[]{:S(2)}, u32[]{:S(2)}) collective-permute-start(s32[4,8,128]{2,1,0:T(8,128)S(1)} %get-tuple-element.31.first_ref), channel_id=1, source_target_pairs={{0,2},{2,0},{4,6},{6,4},{8,10},{10,8},{12,14},{14,12},{1,3},{3,1},... | collective-permute-start | bytes 49160 | tf_op jit(solution)/shard_map/ppermute | solution.py:421
  42.9 1.5 %collective-permute-start.9 = (s32[8,8,128]{2,1,0:T(8,128)S(1)}, s32[8,8,128]{2,1,0:T(8,128)S(1)}, u32[]{:S(2)}, u32[]{:S(2)}) collective-permute-start(s32[8,8,128]{2,1,0:T(8,128)S(1)} %shard_map.127.low_ref), channel_id=1, source_target_pairs={{0,1},{1,0},{2,3},{3,2},{4,5},{5,4},{6,7},{7,6},{8,9},{9,8},{10,11... | collective-permute-start | bytes 98312 | tf_op jit(solution)/shard_map/ppermute | solution.py:418
  42.9 19.0 %collective-permute-start.11 = (bf16[128,1024]{1,0:T(8,128)(2,1)S(1)}, bf16[128,1024]{1,0:T(8,128)(2,1)S(1)}, u32[]{:S(2)}, u32[]{:S(2)}) collective-permute-start(bf16[128,1024]{1,0:T(8,128)(2,1)S(1)} %get-tuple-element.32.xz_ref), channel_id=1, source_target_pairs={{0,2},{2,0},{4,6},{6,4},{8,10},{10,8},{12,14},{14,12},{1,3},{3,1},... | collective-permute-start | bytes 786440 | tf_op jit(solution)/shard_map/ppermute | solution.py:421
  46.4 2.2 %copy-start.1 = (bf16[1024,2048]{1,0:T(8,128)(2,1)S(1)}, bf16[1024,2048]{1,0:T(8,128)(2,1)}, u32[]{:S(2)}) copy-start(bf16[1024,2048]{1,0:T(8,128)(2,1)} %copy-done) | copy-start | bytes 12582916
  48.6 2.2 %copy-start.3 = (bf16[2048,1024]{1,0:T(8,128)(2,1)S(1)}, bf16[2048,1024]{1,0:T(8,128)(2,1)}, u32[]{:S(2)}) copy-start(bf16[2048,1024]{1,0:T(8,128)(2,1)} %copy-done.2) | copy-start | bytes 12582916
  50.8 2.2 %copy-start.5 = (bf16[1024,2048]{1,0:T(8,128)(2,1)S(1)}, bf16[1024,2048]{1,0:T(8,128)(2,1)}, u32[]{:S(2)}) copy-start(bf16[1024,2048]{1,0:T(8,128)(2,1)} %copy-done.4) | copy-start | bytes 12582916
  53.0 2.2 %copy-start.8 = (bf16[2048,1024]{1,0:T(8,128)(2,1)S(1)}, bf16[2048,1024]{1,0:T(8,128)(2,1)}, u32[]{:S(2)}) copy-start(bf16[2048,1024]{1,0:T(8,128)(2,1)} %copy-done.7) | copy-start | bytes 12582916
  55.2 6.8 %copy-start.6 = (bf16[1024,2048]{1,0:T(8,128)(2,1)S(1)}, bf16[1024,2048]{1,0:T(8,128)(2,1)}, u32[]{:S(2)}) copy-start(bf16[1024,2048]{1,0:T(8,128)(2,1)} %copy-done.4) | copy-start | bytes 12582916
  55.2 6.8 %copy-start.9 = (bf16[2048,1024]{1,0:T(8,128)(2,1)S(1)}, bf16[2048,1024]{1,0:T(8,128)(2,1)}, u32[]{:S(2)}) copy-start(bf16[2048,1024]{1,0:T(8,128)(2,1)} %copy-done.7) | copy-start | bytes 12582916
  59.9 9.3 %collective-permute-start.14 = (bf16[128,1024]{1,0:T(8,128)(2,1)S(1)}, bf16[128,1024]{1,0:T(8,128)(2,1)S(1)}, u32[]{:S(2)}, u32[]{:S(2)}) collective-permute-start(bf16[128,1024]{1,0:T(8,128)(2,1)S(1)} %get-tuple-element.40), channel_id=1, source_target_pairs={{0,2},{2,0},{4,6},{6,4},{8,10},{10,8},{12,14},{14,12},{1,3},{3,1},... | collective-permute-start | bytes 786440 | tf_op jit(solution)/shard_map/ppermute | solution.py:421
  61.4 13.3 %collective-permute-start.13 = (bf16[128,1024]{1,0:T(8,128)(2,1)S(1)}, bf16[128,1024]{1,0:T(8,128)(2,1)S(1)}, u32[]{:S(2)}, u32[]{:S(2)}) collective-permute-start(bf16[128,1024]{1,0:T(8,128)(2,1)S(1)} %get-tuple-element.39.xz_ref), channel_id=1, source_target_pairs={{0,2},{2,0},{4,6},{6,4},{8,10},{10,8},{12,14},{14,12},{1,3},{3,1},... | collective-permute-start | bytes 786440 | tf_op jit(solution)/shard_map/ppermute | solution.py:421
  66.7 14.9 %collective-permute-start.12 = (bf16[128,1024]{1,0:T(8,128)(2,1)S(1)}, bf16[128,1024]{1,0:T(8,128)(2,1)S(1)}, u32[]{:S(2)}, u32[]{:S(2)}) collective-permute-start(bf16[128,1024]{1,0:T(8,128)(2,1)S(1)} %get-tuple-element.38), channel_id=1, source_target_pairs={{0,2},{2,0},{4,6},{6,4},{8,10},{10,8},{12,14},{14,12},{1,3},{3,1},... | collective-permute-start | bytes 786440 | tf_op jit(solution)/shard_map/ppermute | solution.py:421
  69.2 12.4 %collective-permute-start.15 = (bf16[128,1024]{1,0:T(8,128)(2,1)S(1)}, bf16[128,1024]{1,0:T(8,128)(2,1)S(1)}, u32[]{:S(2)}, u32[]{:S(2)}) collective-permute-start(bf16[128,1024]{1,0:T(8,128)(2,1)S(1)} %shard_map.131.refs_0_), channel_id=1, source_target_pairs={{0,12},{2,14},{4,0},{6,2},{8,4},{10,6},{12,8},{14,10},{1,13},{3,15... | collective-permute-start | bytes 786440 | tf_op jit(solution)/shard_map/ppermute | solution.py:424
  74.8 6.9 %copy-start.16 = (bf16[1,128,2048]{2,1,0:T(8,128)(2,1)S(1)}, bf16[1,128,2048]{2,1,0:T(8,128)(2,1)}, u32[]{:S(2)}) copy-start(bf16[1,128,2048]{2,1,0:T(8,128)(2,1)} %param.12) | copy-start | bytes 1572868
  74.8 6.9 %copy-start.17 = (bf16[1,128,2048]{2,1,0:T(8,128)(2,1)S(1)}, bf16[1,128,2048]{2,1,0:T(8,128)(2,1)}, u32[]{:S(2)}) copy-start(bf16[1,128,2048]{2,1,0:T(8,128)(2,1)} %param.13) | copy-start | bytes 1572868
  79.5 30.0 %copy-start.14 = (bf16[1,128,2048]{2,1,0:T(8,128)(2,1)S(1)}, bf16[1,128,2048]{2,1,0:T(8,128)(2,1)}, u32[]{:S(2)}) copy-start(bf16[1,128,2048]{2,1,0:T(8,128)(2,1)} %param.11) | copy-start | bytes 1572868
  79.5 30.0 %copy-start.20 = (s32[1,128]{1,0:T(1,128)S(1)}, s32[1,128]{1,0:T(1,128)}, u32[]{:S(2)}) copy-start(s32[1,128]{1,0:T(1,128)} %doc_own.3) | copy-start | bytes 1540
  79.5 30.0 %copy-start.22 = (s32[1,128]{1,0:T(1,128)S(1)}, s32[1,128]{1,0:T(1,128)}, u32[]{:S(2)}) copy-start(s32[1,128]{1,0:T(1,128)} %ahead_ref.3) | copy-start | bytes 1540
  79.5 7.9 %collective-permute-start.18 = (bf16[128,1024]{1,0:T(8,128)(2,1)S(1)}, bf16[128,1024]{1,0:T(8,128)(2,1)S(1)}, u32[]{:S(2)}, u32[]{:S(2)}) collective-permute-start(bf16[128,1024]{1,0:T(8,128)(2,1)S(1)} %get-tuple-element.45), channel_id=1, source_target_pairs={{0,2},{2,0},{4,6},{6,4},{8,10},{10,8},{12,14},{14,12},{1,3},{3,1},... | collective-permute-start | bytes 786440 | tf_op jit(solution)/shard_map/ppermute | solution.py:421
  81.1 9.1 %collective-permute-start.19 = (bf16[128,1024]{1,0:T(8,128)(2,1)S(1)}, bf16[128,1024]{1,0:T(8,128)(2,1)S(1)}, u32[]{:S(2)}, u32[]{:S(2)}) collective-permute-start(bf16[128,1024]{1,0:T(8,128)(2,1)S(1)} %get-tuple-element.47), channel_id=1, source_target_pairs={{0,2},{2,0},{4,6},{6,4},{8,10},{10,8},{12,14},{14,12},{1,3},{3,1},... | collective-permute-start | bytes 786440 | tf_op jit(solution)/shard_map/ppermute | solution.py:421
  90.3 10.0 %collective-permute-start.21 = (bf16[128,1024]{1,0:T(8,128)(2,1)S(1)}, bf16[128,1024]{1,0:T(8,128)(2,1)S(1)}, u32[]{:S(2)}, u32[]{:S(2)}) collective-permute-start(bf16[128,1024]{1,0:T(8,128)(2,1)S(1)} %shard_map.135.rest_0_), channel_id=1, source_target_pairs={{0,4},{2,6},{4,8},{6,10},{8,12},{10,14},{12,0},{14,2},{1,5},{3,7},... | collective-permute-start | bytes 786440 | tf_op jit(solution)/shard_map/ppermute | solution.py:424
  90.3 18.2 %collective-permute-start.20 = (bf16[128,1024]{1,0:T(8,128)(2,1)S(1)}, bf16[128,1024]{1,0:T(8,128)(2,1)S(1)}, u32[]{:S(2)}, u32[]{:S(2)}) collective-permute-start(bf16[128,1024]{1,0:T(8,128)(2,1)S(1)} %get-tuple-element.46.refs_0_), channel_id=1, source_target_pairs={{0,8},{2,10},{4,12},{6,14},{8,0},{10,2},{12,4},{14,6},{1,9},{3,11}... | collective-permute-start | bytes 786440 | tf_op jit(solution)/shard_map/ppermute | solution.py:424
  93.6 15.8 %collective-permute-start.16 = (bf16[128,2048]{1,0:T(8,128)(2,1)S(1)}, bf16[128,2048]{1,0:T(8,128)(2,1)S(1)}, u32[]{:S(2)}, u32[]{:S(2)}) collective-permute-start(bf16[128,2048]{1,0:T(8,128)(2,1)S(1)} %get-tuple-element.43.k_own), channel_id=1, source_target_pairs={{0,1},{1,0},{2,3},{3,2},{4,5},{5,4},{6,7},{7,6},{8,9},{9,8},{10,11... | collective-permute-start | bytes 1572872 | tf_op jit(solution)/shard_map/ppermute | solution.py:418
  93.6 15.8 %collective-permute-start.17 = (bf16[128,2048]{1,0:T(8,128)(2,1)S(1)}, bf16[128,2048]{1,0:T(8,128)(2,1)S(1)}, u32[]{:S(2)}, u32[]{:S(2)}) collective-permute-start(bf16[128,2048]{1,0:T(8,128)(2,1)S(1)} %get-tuple-element.44.v_own), channel_id=1, source_target_pairs={{0,1},{1,0},{2,3},{3,2},{4,5},{5,4},{6,7},{7,6},{8,9},{9,8},{10,11... | collective-permute-start | bytes 1572872 | tf_op jit(solution)/shard_map/ppermute | solution.py:418

commit v10 on v8

--- a/solution.py
+++ b/solution.py
@@ -328,26 +328,29 @@
     )(own, kept, router, from_line, from_side, *weights, *after)
 
 
-def add_kernel(count, first_ref, second_ref, *refs):
-    total = first_ref[...].astype(jnp.float32) + second_ref[...].astype(jnp.float32)
+def add_kernel(terms, count, *refs):
+    total = refs[0][...].astype(jnp.float32)
+    for term in refs[1:terms]:
+        total += term[...].astype(jnp.float32)
     outs = refs[len(refs) - count - 1 :]
     outs[-1][...] = total.astype(jnp.bfloat16)
     for index in range(count):
-        outs[index][...] = refs[index][...]
-
-
-def add(first, second, after=(), staged=()):
+        outs[index][...] = refs[terms + index][...]
+
+
+def add(*terms, after=(), staged=()):
     vmem = pl.BlockSpec(memory_space=pltpu.VMEM)
     anywhere = pl.BlockSpec(memory_space=pl.ANY)
+    first = terms[0]
     out = pl.pallas_call(
-        functools.partial(add_kernel, len(staged)),
+        functools.partial(add_kernel, len(terms), len(staged)),
         out_shape=[jax.ShapeDtypeStruct(x.shape, x.dtype) for x in staged]
         + [jax.ShapeDtypeStruct(first.shape, first.dtype)],
-        in_specs=[vmem] * (2 + len(staged)) + [anywhere] * len(after),
+        in_specs=[vmem] * (len(terms) + len(staged)) + [anywhere] * len(after),
         out_specs=[vmem] * (1 + len(staged)),
         compiler_params=pltpu.CompilerParams(vmem_limit_bytes=SMALL_VMEM),
         cost_estimate=pl.CostEstimate(flops=first.size, bytes_accessed=first.size, transcendentals=0),
-    )(first, second, *staged, *after)
+    )(*terms, *staged, *after)
     return out if staged else out[0]
 
 
@@ -394,26 +397,26 @@
 
     def piece(step, weights, *after):
         return run_piece(
-            step, step == 1, own, kept, router.T, from_line[step], from_side[step], weights, after
+            step, step == 2, own, kept, router.T, from_line[step], from_side[step], weights, after
         )
 
-    one, theirs, *weights[2:] = piece(1, weights)
+    two, theirs, *weights[2:] = piece(2, weights)
+    two_far = swap_side(theirs)
+    one, theirs = piece(1, weights, two)
     one_far = swap_side(theirs)
-    two, theirs = piece(2, weights, one)
-    two_far = swap_side(theirs)
-    k_near, v_near, first = add(one, one_far, after=(two,), staged=(k_near, v_near))
+    k_near, v_near, second = add(two, two_far, after=(one,), staged=(k_near, v_near))
+    passing = along(second, line - 1)
+    three, theirs = piece(3, weights, one, second)
+    three_far = swap_side(theirs)
+    swapped = (k_near, swap_core(k_near), v_near, swap_core(v_near))
+    half = attention(0, doc_far, *swapped, after=(three,))
+    attn_out = attention(1, doc_far, *swapped, before=half)
+    first = add(one, one_far, passing, after=(attn_out,))
     home = [along(first, line - 1)]
-    three, theirs = piece(3, weights, two, first)
-    three_far = swap_side(theirs)
-    second = add(two, two_far, after=(three,))
-    home.append(along(second, line - 2))
-    near, theirs = piece(0, weights, three, second)
+    near, theirs = piece(0, weights, three, first)
     near_far = swap_side(theirs)
-    third = add(three, three_far, after=(near,))
+    third = add(three, three_far, after=(near, home[0]))
     home.append(along(third, line - 3))
-    swapped = (k_near, swap_core(k_near), v_near, swap_core(v_near))
-    half = attention(0, doc_far, *swapped, after=(third,))
-    attn_out = attention(1, doc_far, *swapped, before=half)
     total = near.astype(f32) + near_far.astype(f32)
     for part in home:
         total += part.astype(f32)

time: 79.2 us -> 83.6 us (1.056)
  waiting for transfers between devices: 24.9 us -> 29 us
  local copies, waits for them, and re-layouts: 1.38 us -> 2.42 us
    ppermute x9, waiting for transfers between devices: 9.85 us -> 13.4 us  [swap_side(): return lax.ppermute(x, 'expert', across)]
    ppermute x9, starting transfers between devices: 12.4 us -> 11.1 us  [swap_side(): return lax.ppermute(x, 'expert', across)]
    unnamed x20 -> x22, local copies, waits for them, and re-layouts: 1.38 us -> 2.41 us
  transfers between devices with their start and end apart: 22 -> 22, of which waited for: 10 -> 10; matrix products, arithmetic and copies ran while one was open for 0% -> 0% of each run, Pallas kernels for 35% -> 34%
where the time goes in v10:
time: 83.6 us; the launch traced here: 83.4 us
  waiting for transfers between devices  29 us (35%)
  Pallas kernels  27.9 us (33%)
  starting transfers between devices  22.3 us (27%)
  local copies, waits for them, and re-layouts  2.42 us (3%)
  other arithmetic  0.87 us (1%)
    pallas_call x4, Pallas kernels, run_piece(): pl.pallas_call(functools.partial(expert_kernel, place, first), out_shape=...  19.8 us
    ppermute x9, waiting for transfers between devices, swap_side(): return lax.ppermute(x, 'expert', across)  13.4 us
    ppermute x9, starting transfers between devices, swap_side(): return lax.ppermute(x, 'expert', across)  11.1 us
    ppermute x6, waiting for transfers between devices, along(): lax.ppermute(x, 'expert', [(2 * z + y, 2 * ((z + step) % line) + y) for z...  9.69 us
    ppermute x6, starting transfers between devices, along(): lax.ppermute(x, 'expert', [(2 * z + y, 2 * ((z + step) % line) + y) for z...  6.09 us
    ppermute x2, waiting for transfers between devices, flipped(): lax.ppermute(x, 'expert', [(2 * z + y, 2 * (z ^ span) + y) for z, y in sp...  5.88 us
    ppermute x2, starting transfers between devices, flipped(): lax.ppermute(x, 'expert', [(2 * z + y, 2 * (z ^ span) + y) for z, y in sp...  3.99 us
    pallas_call x1, Pallas kernels, load_weights(): pl.pallas_call(load_kernel, out_shape=[pltpu.VMEM(w.shape, w.dtype) for w...  3.51 us
  transfers between devices with their start and end apart: 22, of which 10 were waited for; matrix products, arithmetic and copies ran while one was open for 0% of the time, Pallas kernels for 34%

profile of v10, /device:TPU:0, one launch (start us, length us, event | category | flops | bytes accessed | tf_op | source)
XLA Modules:
  0.0 83.4 jit_solution(9890983166299253086)
XLA Ops:
  0.6 0.5 collective-permute-start.10
  1.1 0.1 collective-permute-start.11
  1.2 2.9 %collective-permute-start.2 = (bf16[128,1024]{1,0:T(8,128)(2,1)}, bf16[128,1024]{1,0:T(8,128)(2,1)S(1)}, u32[]{:S(2)}, u32[]{:S(2)}) collective-permute-start(bf16[128,1024]{1,0:T(8,128)(2,1)} %bitcast.24), channel_id=1, source_target_pairs={{0,2},{2,0},{4,6},{6,4},{8,10},{10,8},{12,14},{14,12},{1,3},{3,1},... | collective-permute-start | bytes 786440 | tf_op jit(solution)/shard_map/ppermute | solution.py:368
  4.2 1.6 %collective-permute-start.1 = (bf16[128,1024]{1,0:T(8,128)(2,1)}, bf16[128,1024]{1,0:T(8,128)(2,1)S(1)}, u32[]{:S(2)}, u32[]{:S(2)}) collective-permute-start(bf16[128,1024]{1,0:T(8,128)(2,1)} %bitcast.25), channel_id=1, source_target_pairs={{0,4},{2,6},{4,8},{6,10},{8,12},{10,14},{12,0},{14,2},{1,5},{3,7},... | collective-permute-start | bytes 786440 | tf_op jit(solution)/shard_map/ppermute | solution.py:371
  5.8 0.7 copy-done.6
  6.4 0.7 copy-done.8
  7.1 1.6 %collective-permute-start = (s32[1,8,128]{2,1,0:T(8,128)S(1)}, s32[1,8,128]{2,1,0:T(8,128)S(1)}, u32[]{:S(2)}, u32[]{:S(2)}) collective-permute-start(s32[1,8,128]{2,1,0:T(8,128)S(1)} %shard_map.122.first_ref), channel_id=1, source_target_pairs={{0,4},{2,6},{4,0},{6,2},{8,12},{10,14},{12,8},{14,10},{1,5},{3,7},... | collective-permute-start | bytes 12296 | tf_op jit(solution)/shard_map/ppermute | solution.py:374
  8.8 2.9 %collective-permute-done.second_ref = s32[1,8,128]{2,1,0:T(8,128)S(1)} collective-permute-done((s32[1,8,128]{2,1,0:T(8,128)S(1)}, s32[1,8,128]{2,1,0:T(8,128)S(1)}, u32[]{:S(2)}, u32[]{:S(2)}) %collective-permute-start) | collective-permute-done | bytes 4128 | tf_op jit(solution)/shard_map/ppermute | solution.py:374
  11.6 0.0 collective-permute-done.2.refs_1_.xy_ref
  11.6 2.7 %collective-permute-done.1.refs_0_ = bf16[128,1024]{1,0:T(8,128)(2,1)S(1)} collective-permute-done((bf16[128,1024]{1,0:T(8,128)(2,1)}, bf16[128,1024]{1,0:T(8,128)(2,1)S(1)}, u32[]{:S(2)}, u32[]{:S(2)}) %collective-permute-start.1) | collective-permute-done | bytes 262176 | tf_op jit(solution)/shard_map/ppermute | solution.py:371
  14.4 0.5 collective-permute-start.5
  14.9 0.0 collective-permute-start.4
  14.9 2.3 %collective-permute-start.3 = (s32[2,8,128]{2,1,0:T(8,128)S(1)}, s32[2,8,128]{2,1,0:T(8,128)S(1)}, u32[]{:S(2)}, u32[]{:S(2)}) collective-permute-start(s32[2,8,128]{2,1,0:T(8,128)S(1)} %get-tuple-element.23.first_ref), channel_id=1, source_target_pairs={{0,8},{2,10},{4,12},{6,14},{8,0},{10,2},{12,4},{14,6},{1,9},{3,11}... | collective-permute-start | bytes 24584 | tf_op jit(solution)/shard_map/ppermute | solution.py:374
  17.2 3.0 %collective-permute-done.3.second_ref = s32[2,8,128]{2,1,0:T(8,128)S(1)} collective-permute-done((s32[2,8,128]{2,1,0:T(8,128)S(1)}, s32[2,8,128]{2,1,0:T(8,128)S(1)}, u32[]{:S(2)}, u32[]{:S(2)}) %collective-permute-start.3) | collective-permute-done | bytes 8224 | tf_op jit(solution)/shard_map/ppermute | solution.py:374
  20.2 1.3 %collective-permute-done.5.refs_1_.xy_ref = bf16[128,1024]{1,0:T(8,128)(2,1)S(1)} collective-permute-done((bf16[128,1024]{1,0:T(8,128)(2,1)S(1)}, bf16[128,1024]{1,0:T(8,128)(2,1)S(1)}, u32[]{:S(2)}, u32[]{:S(2)}) %collective-permute-start.5) | collective-permute-done | bytes 262176 | tf_op jit(solution)/shard_map/ppermute | solution.py:368
  21.5 2.4 %collective-permute-done.4.refs_0_ = bf16[128,1024]{1,0:T(8,128)(2,1)S(1)} collective-permute-done((bf16[128,1024]{1,0:T(8,128)(2,1)S(1)}, bf16[128,1024]{1,0:T(8,128)(2,1)S(1)}, u32[]{:S(2)}, u32[]{:S(2)}) %collective-permute-start.4) | collective-permute-done | bytes 262176 | tf_op jit(solution)/shard_map/ppermute | solution.py:371
  23.9 0.7 collective-permute-start.8
  24.7 1.3 %collective-permute-start.9 = (bf16[128,1024]{1,0:T(8,128)(2,1)S(1)}, bf16[128,1024]{1,0:T(8,128)(2,1)S(1)}, u32[]{:S(2)}, u32[]{:S(2)}) collective-permute-start(bf16[128,1024]{1,0:T(8,128)(2,1)S(1)} %get-tuple-element.26.xz_ref), channel_id=1, source_target_pairs={{0,2},{2,0},{4,6},{6,4},{8,10},{10,8},{12,14},{14,12},{1,3},{3,1},... | collective-permute-start | bytes 786440 | tf_op jit(solution)/shard_map/ppermute | solution.py:368
  26.0 0.7 collective-permute-start.6
  26.7 4.5 %collective-permute-done.6.second_ref = s32[4,8,128]{2,1,0:T(8,128)S(1)} collective-permute-done((s32[4,8,128]{2,1,0:T(8,128)S(1)}, s32[4,8,128]{2,1,0:T(8,128)S(1)}, u32[]{:S(2)}, u32[]{:S(2)}) %collective-permute-start.6) | collective-permute-done | bytes 16416 | tf_op jit(solution)/shard_map/ppermute | solution.py:368
  31.2 0.0 collective-permute-start.7
  31.2 3.5 %shard_map.126 = (bf16[1024,2048]{1,0:T(8,128)(2,1)S(1)}, bf16[2048,1024]{1,0:T(8,128)(2,1)S(1)}) custom-call(bf16[1024,2048]{1,0:T(8,128)(2,1)} %bitcast.29, bf16[2048,1024]{1,0:T(8,128)(2,1)} %bitcast.31, s32[8,8,128]{2,1,0:T(8,128)S(1)} %shard_map.125.refs_0_.low_ref), custom_call_target="tpu_custom_call" | custom-call | tf_op jit(solution)/shard_map/pallas_call | solution.py:154
  34.7 0.0 collective-permute-done.7.high_ref
  34.8 0.0 collective-permute-done.8.refs_0_
  34.8 0.0 copy-done.10
  34.8 0.0 copy-start.4
  34.8 1.1 %shard_map.127 = (s32[8,8,128]{2,1,0:T(8,128)S(1)}, bf16[128,1024]{1,0:T(8,128)(2,1)S(1)}) custom-call(s32[1]{0:T(128)} %bitcast.2.own_ref, s32[16]{0:T(128)S(1)} %copy-done.10, s32[8,8,128]{2,1,0:T(8,128)S(1)} %shard_map.125.refs_0_.low_ref, s32[8,8,128]{2,1,0:T(8,128)S(1)} %collective-permute-done.7.high_ref, ...), custom_call_target="tpu_custom_call", output_to_operand_aliasing={{1}: (4, {})} | custom-call | tf_op jit(solution)/shard_map/pallas_call | solution.py:214
  35.9 1.4 %collective-permute-start.15 = (bf16[128,1024]{1,0:T(8,128)(2,1)S(1)}, bf16[128,1024]{1,0:T(8,128)(2,1)S(1)}, u32[]{:S(2)}, u32[]{:S(2)}) collective-permute-start(bf16[128,1024]{1,0:T(8,128)(2,1)S(1)} %get-tuple-element.37.xz_ref), channel_id=1, source_target_pairs={{0,2},{2,0},{4,6},{6,4},{8,10},{10,8},{12,14},{14,12},{1,3},{3,1},... | collective-permute-start | bytes 786440 | tf_op jit(solution)/shard_map/ppermute | solution.py:368
  37.3 0.0 collective-permute-done.9.xy_ref
  37.3 0.0 collective-permute-done.10.refs_2_
  37.3 0.0 collective-permute-done.11.refs_3_
  37.3 0.0 copy-done.4
  37.3 5.8 %shard_map.128 = (bf16[128,1024]{1,0:T(8,128)(2,1)S(1)}, bf16[128,1024]{1,0:T(8,128)(2,1)S(1)}, bf16[1024,2048]{1,0:T(8,128)(2,1)S(1)}, bf16[2048,1024]{1,0:T(8,128)(2,1)S(1)}) custom-call(s32[1]{0:T(128)} %bitcast.2.own_ref, s32[8,8,128]{2,1,0:T(8,128)S(1)} %get-tuple-element.29.kept_ref, bf16[16,1024]{1,0:T(8,128)(2,1)S(1)} %bitcast.20, ...), custom_call_target="tpu_custom_call" | custom-call | flops 4294967296 | bytes 1048576 | tf_op jit(solution)/shard_map/pallas_call | solution.py:316
  43.1 0.8 collective-permute-start.12
  43.8 4.7 %shard_map.129 = (bf16[128,1024]{1,0:T(8,128)(2,1)S(1)}, bf16[128,1024]{1,0:T(8,128)(2,1)S(1)}) custom-call(s32[1]{0:T(128)} %bitcast.2.own_ref, s32[8,8,128]{2,1,0:T(8,128)S(1)} %get-tuple-element.29.kept_ref, bf16[16,1024]{1,0:T(8,128)(2,1)S(1)} %bitcast.21, bf16[128,1024]{1,0:T(8,128)(2,1)S(1)} %get-tuple-element.24.xz_ref, ...), custom_call_target="tpu_custom_call" | custom-call | flops 4294967296 | bytes 1048576 | tf_op jit(solution)/shard_map/pallas_call | solution.py:316
  48.5 3.0 %collective-permute-done.12.refs_1_ = bf16[128,1024]{1,0:T(8,128)(2,1)S(1)} collective-permute-done((bf16[128,1024]{1,0:T(8,128)(2,1)S(1)}, bf16[128,1024]{1,0:T(8,128)(2,1)S(1)}, u32[]{:S(2)}, u32[]{:S(2)}) %collective-permute-start.12) | collective-permute-done | bytes 262176 | tf_op jit(solution)/shard_map/ppermute | solution.py:368
  51.6 0.0 copy-done.2
  51.6 0.1 shard_map.130
  51.7 0.1 collective-permute-start.13
  51.8 0.5 collective-permute-start.14
  52.3 0.7 collective-permute-start.16
  53.0 3.1 %collective-permute-start.17 = (bf16[128,1024]{1,0:T(8,128)(2,1)S(1)}, bf16[128,1024]{1,0:T(8,128)(2,1)S(1)}, u32[]{:S(2)}, u32[]{:S(2)}) collective-permute-start(bf16[128,1024]{1,0:T(8,128)(2,1)S(1)} %get-tuple-element.38.refs_5_), channel_id=1, source_target_pairs={{0,12},{2,14},{4,0},{6,2},{8,4},{10,6},{12,8},{14,10},{1,13},{3,15... | collective-permute-start | bytes 786440 | tf_op jit(solution)/shard_map/ppermute | solution.py:371
  56.1 0.0 collective-permute-done.15.xy_ref
  56.1 4.7 %shard_map.131 = (bf16[128,1024]{1,0:T(8,128)(2,1)S(1)}, bf16[128,1024]{1,0:T(8,128)(2,1)S(1)}) custom-call(s32[1]{0:T(128)} %bitcast.2.own_ref, s32[8,8,128]{2,1,0:T(8,128)S(1)} %get-tuple-element.29.kept_ref, bf16[16,1024]{1,0:T(8,128)(2,1)S(1)} %bitcast.22, bf16[128,1024]{1,0:T(8,128)(2,1)S(1)} %get-tuple-element.37.xz_ref, ...), custom_call_target="tpu_custom_call" | custom-call | flops 4294967296 | bytes 1048576 | tf_op jit(solution)/shard_map/pallas_call | solution.py:316
  60.8 1.4 %collective-permute-start.20 = (bf16[128,1024]{1,0:T(8,128)(2,1)S(1)}, bf16[128,1024]{1,0:T(8,128)(2,1)S(1)}, u32[]{:S(2)}, u32[]{:S(2)}) collective-permute-start(bf16[128,1024]{1,0:T(8,128)(2,1)S(1)} %get-tuple-element.43), channel_id=1, source_target_pairs={{0,2},{2,0},{4,6},{6,4},{8,10},{10,8},{12,14},{14,12},{1,3},{3,1},... | collective-permute-start | bytes 786440 | tf_op jit(solution)/shard_map/ppermute | solution.py:368
  62.2 0.0 collective-permute-done.13.k_far
  62.2 0.0 collective-permute-done.14.v_far
  62.2 0.0 copy-start.5
  62.2 1.6 %shard_map.132.rest_0_ = bf16[128,2048]{1,0:T(8,128)(2,1)} custom-call(s32[1]{0:T(128)} %bitcast.place_ref, bf16[128,2048]{1,0:T(8,128)(2,1)S(1)} %bitcast.16, bf16[128,2048]{1,0:T(8,128)(2,1)S(1)} %get-tuple-element.35.k_own, bf16[128,2048]{1,0:T(8,128)(2,1)S(1)} %collective-permute-done.13.k_far, bf16[128,2048]{1,0:T(8,128)(2,1)S(1)} %get-tuple-element.36.v_own, ...), custom_call_target="tpu_custom_call" | custom-call | flops 134217728 | bytes 1572864 | tf_op jit(solution)/shard_map/pallas_call | solution.py:67
  63.8 1.6 %shard_map.133.refs_3_ = bf16[128,2048]{1,0:T(8,128)(2,1)} custom-call(s32[1]{0:T(128)} %bitcast.place_ref, bf16[128,2048]{1,0:T(8,128)(2,1)S(1)} %bitcast.17, bf16[128,2048]{1,0:T(8,128)(2,1)S(1)} %get-tuple-element.35.k_own, bf16[128,2048]{1,0:T(8,128)(2,1)S(1)} %collective-permute-done.13.k_far, ...), custom_call_target="tpu_custom_call", output_to_operand_aliasing={{}: (9, {})} | custom-call | flops 134217728 | bytes 1572864 | tf_op jit(solution)/shard_map/pallas_call | solution.py:67
  65.4 0.0 collective-permute-done.16.refs_1_
  65.4 0.0 collective-permute-done.17.refs_2_
  65.4 1.0 %copy-done = bf16[128,2048]{1,0:T(8,128)(2,1)S(1)} copy-done((bf16[128,2048]{1,0:T(8,128)(2,1)S(1)}, bf16[128,2048]{1,0:T(8,128)(2,1)}, u32[]{:S(2)}) %copy-start) | copy-done | bytes 524312
  66.5 0.1 shard_map.134.refs_5_
  66.6 0.6 collective-permute-start.19
  67.1 4.7 %shard_map.135 = (bf16[128,1024]{1,0:T(8,128)(2,1)S(1)}, bf16[128,1024]{1,0:T(8,128)(2,1)S(1)}) custom-call(s32[1]{0:T(128)} %bitcast.2.own_ref, s32[8,8,128]{2,1,0:T(8,128)S(1)} %get-tuple-element.29.kept_ref, bf16[16,1024]{1,0:T(8,128)(2,1)S(1)} %bitcast.23, bf16[128,1024]{1,0:T(8,128)(2,1)S(1)} %bitcast.26, ...), custom_call_target="tpu_custom_call" | custom-call | flops 4294967296 | bytes 1048576 | tf_op jit(solution)/shard_map/pallas_call | solution.py:316
  71.8 1.4 %collective-permute-start.18 = (bf16[128,1024]{1,0:T(8,128)(2,1)S(1)}, bf16[128,1024]{1,0:T(8,128)(2,1)S(1)}, u32[]{:S(2)}, u32[]{:S(2)}) collective-permute-start(bf16[128,1024]{1,0:T(8,128)(2,1)S(1)} %get-tuple-element.42), channel_id=1, source_target_pairs={{0,2},{2,0},{4,6},{6,4},{8,10},{10,8},{12,14},{14,12},{1,3},{3,1},... | collective-permute-start | bytes 786440 | tf_op jit(solution)/shard_map/ppermute | solution.py:368
  73.2 0.0 collective-permute-done.20.refs_1_
  73.2 0.9 %collective-permute-done.19.refs_3_ = bf16[128,1024]{1,0:T(8,128)(2,1)S(1)} collective-permute-done((bf16[128,1024]{1,0:T(8,128)(2,1)S(1)}, bf16[128,1024]{1,0:T(8,128)(2,1)S(1)}, u32[]{:S(2)}, u32[]{:S(2)}) %collective-permute-start.19) | collective-permute-done | bytes 262176 | tf_op jit(solution)/shard_map/ppermute | solution.py:371
  74.1 0.1 shard_map.136
  74.1 0.1 collective-permute-start.21
  74.3 4.6 %collective-permute-done.18 = bf16[128,1024]{1,0:T(8,128)(2,1)S(1)} collective-permute-done((bf16[128,1024]{1,0:T(8,128)(2,1)S(1)}, bf16[128,1024]{1,0:T(8,128)(2,1)S(1)}, u32[]{:S(2)}, u32[]{:S(2)}) %collective-permute-start.18) | collective-permute-done | bytes 262176 | tf_op jit(solution)/shard_map/ppermute | solution.py:368
  78.9 3.6 %collective-permute-done.21 = bf16[128,1024]{1,0:T(8,128)(2,1)S(1)} collective-permute-done((bf16[128,1024]{1,0:T(8,128)(2,1)S(1)}, bf16[128,1024]{1,0:T(8,128)(2,1)S(1)}, u32[]{:S(2)}, u32[]{:S(2)}) %collective-permute-start.21) | collective-permute-done | bytes 262176 | tf_op jit(solution)/shard_map/ppermute | solution.py:371
  82.5 0.9 %fusion = bf16[1,128,1024]{2,1,0:T(8,128)(2,1)} fusion(bf16[128,1024]{1,0:T(8,128)(2,1)S(1)} %collective-permute-done.21, bf16[128,1024]{1,0:T(8,128)(2,1)S(1)} %collective-permute-done.19.refs_3_, bf16[128,1024]{1,0:T(8,128)(2,1)S(1)} %collective-permute-done.18, bf16[128,1024]{1,0:T(8,128)(2,1)S(1)} %get-tuple-element.41.refs_2_), kind=kLoop, calls=%fused_computation.1 | loop fusion | flops 1048576 | bytes 1310720 | tf_op jit(solution)/shard_map/broadcast_in_dim | solution.py:423
  (19 shorter events, 0.1 us)
Async XLA Ops:
  0.6 36.6 %collective-permute-start.10 = (bf16[1024,2048]{1,0:T(8,128)(2,1)}, bf16[1024,2048]{1,0:T(8,128)(2,1)}, u32[]{:S(2)}, u32[]{:S(2)}) collective-permute-start(bf16[1024,2048]{1,0:T(8,128)(2,1)} %bitcast.28), channel_id=1, source_target_pairs={{0,1},{1,0},{2,3},{3,2},{4,5},{5,4},{6,7},{7,6},{8,9},{9,8},{10,11... | collective-permute-start | bytes 12582920 | tf_op jit(solution)/shard_map/ppermute | solution.py:365
  1.1 36.1 %collective-permute-start.11 = (bf16[2048,1024]{1,0:T(8,128)(2,1)}, bf16[2048,1024]{1,0:T(8,128)(2,1)}, u32[]{:S(2)}, u32[]{:S(2)}) collective-permute-start(bf16[2048,1024]{1,0:T(8,128)(2,1)} %bitcast.30), channel_id=1, source_target_pairs={{0,1},{1,0},{2,3},{3,2},{4,5},{5,4},{6,7},{7,6},{8,9},{9,8},{10,11... | collective-permute-start | bytes 12582920 | tf_op jit(solution)/shard_map/ppermute | solution.py:365
  1.2 10.4 %collective-permute-start.2 = (bf16[128,1024]{1,0:T(8,128)(2,1)}, bf16[128,1024]{1,0:T(8,128)(2,1)S(1)}, u32[]{:S(2)}, u32[]{:S(2)}) collective-permute-start(bf16[128,1024]{1,0:T(8,128)(2,1)} %bitcast.24), channel_id=1, source_target_pairs={{0,2},{2,0},{4,6},{6,4},{8,10},{10,8},{12,14},{14,12},{1,3},{3,1},... | collective-permute-start | bytes 786440 | tf_op jit(solution)/shard_map/ppermute | solution.py:368
  4.2 10.2 %collective-permute-start.1 = (bf16[128,1024]{1,0:T(8,128)(2,1)}, bf16[128,1024]{1,0:T(8,128)(2,1)S(1)}, u32[]{:S(2)}, u32[]{:S(2)}) collective-permute-start(bf16[128,1024]{1,0:T(8,128)(2,1)} %bitcast.25), channel_id=1, source_target_pairs={{0,4},{2,6},{4,8},{6,10},{8,12},{10,14},{12,0},{14,2},{1,5},{3,7},... | collective-permute-start | bytes 786440 | tf_op jit(solution)/shard_map/ppermute | solution.py:371
  5.7 0.7 copy-start.6
  6.4 0.7 copy-start.8
  7.1 4.5 %collective-permute-start = (s32[1,8,128]{2,1,0:T(8,128)S(1)}, s32[1,8,128]{2,1,0:T(8,128)S(1)}, u32[]{:S(2)}, u32[]{:S(2)}) collective-permute-start(s32[1,8,128]{2,1,0:T(8,128)S(1)} %shard_map.122.first_ref), channel_id=1, source_target_pairs={{0,4},{2,6},{4,0},{6,2},{8,12},{10,14},{12,8},{14,10},{1,5},{3,7},... | collective-permute-start | bytes 12296 | tf_op jit(solution)/shard_map/ppermute | solution.py:374
  14.4 7.1 %collective-permute-start.5 = (bf16[128,1024]{1,0:T(8,128)(2,1)S(1)}, bf16[128,1024]{1,0:T(8,128)(2,1)S(1)}, u32[]{:S(2)}, u32[]{:S(2)}) collective-permute-start(bf16[128,1024]{1,0:T(8,128)(2,1)S(1)} %get-tuple-element.24.xz_ref), channel_id=1, source_target_pairs={{0,2},{2,0},{4,6},{6,4},{8,10},{10,8},{12,14},{14,12},{1,3},{3,1},... | collective-permute-start | bytes 786440 | tf_op jit(solution)/shard_map/ppermute | solution.py:368
  14.9 9.1 %collective-permute-start.4 = (bf16[128,1024]{1,0:T(8,128)(2,1)S(1)}, bf16[128,1024]{1,0:T(8,128)(2,1)S(1)}, u32[]{:S(2)}, u32[]{:S(2)}) collective-permute-start(bf16[128,1024]{1,0:T(8,128)(2,1)S(1)} %get-tuple-element.24.xz_ref), channel_id=1, source_target_pairs={{0,4},{2,6},{4,8},{6,10},{8,12},{10,14},{12,0},{14,2},{1,5},{3,7},... | collective-permute-start | bytes 786440 | tf_op jit(solution)/shard_map/ppermute | solution.py:371
  14.9 5.3 %collective-permute-start.3 = (s32[2,8,128]{2,1,0:T(8,128)S(1)}, s32[2,8,128]{2,1,0:T(8,128)S(1)}, u32[]{:S(2)}, u32[]{:S(2)}) collective-permute-start(s32[2,8,128]{2,1,0:T(8,128)S(1)} %get-tuple-element.23.first_ref), channel_id=1, source_target_pairs={{0,8},{2,10},{4,12},{6,14},{8,0},{10,2},{12,4},{14,6},{1,9},{3,11}... | collective-permute-start | bytes 24584 | tf_op jit(solution)/shard_map/ppermute | solution.py:374
  23.9 10.8 %collective-permute-start.8 = (bf16[128,1024]{1,0:T(8,128)(2,1)S(1)}, bf16[128,1024]{1,0:T(8,128)(2,1)S(1)}, u32[]{:S(2)}, u32[]{:S(2)}) collective-permute-start(bf16[128,1024]{1,0:T(8,128)(2,1)S(1)} %get-tuple-element.26.xz_ref), channel_id=1, source_target_pairs={{0,4},{2,6},{4,8},{6,10},{8,12},{10,14},{12,0},{14,2},{1,5},{3,7},... | collective-permute-start | bytes 786440 | tf_op jit(solution)/shard_map/ppermute | solution.py:371
  24.7 12.6 %collective-permute-start.9 = (bf16[128,1024]{1,0:T(8,128)(2,1)S(1)}, bf16[128,1024]{1,0:T(8,128)(2,1)S(1)}, u32[]{:S(2)}, u32[]{:S(2)}) collective-permute-start(bf16[128,1024]{1,0:T(8,128)(2,1)S(1)} %get-tuple-element.26.xz_ref), channel_id=1, source_target_pairs={{0,2},{2,0},{4,6},{6,4},{8,10},{10,8},{12,14},{14,12},{1,3},{3,1},... | collective-permute-start | bytes 786440 | tf_op jit(solution)/shard_map/ppermute | solution.py:368
  26.0 5.2 %collective-permute-start.6 = (s32[4,8,128]{2,1,0:T(8,128)S(1)}, s32[4,8,128]{2,1,0:T(8,128)S(1)}, u32[]{:S(2)}, u32[]{:S(2)}) collective-permute-start(s32[4,8,128]{2,1,0:T(8,128)S(1)} %get-tuple-element.25.first_ref), channel_id=1, source_target_pairs={{0,2},{2,0},{4,6},{6,4},{8,10},{10,8},{12,14},{14,12},{1,3},{3,1},... | collective-permute-start | bytes 49160 | tf_op jit(solution)/shard_map/ppermute | solution.py:368
  31.2 3.5 %collective-permute-start.7 = (s32[8,8,128]{2,1,0:T(8,128)S(1)}, s32[8,8,128]{2,1,0:T(8,128)S(1)}, u32[]{:S(2)}, u32[]{:S(2)}) collective-permute-start(s32[8,8,128]{2,1,0:T(8,128)S(1)} %shard_map.125.refs_0_.low_ref), channel_id=1, source_target_pairs={{0,1},{1,0},{2,3},{3,2},{4,5},{5,4},{6,7},{7,6},{8,9},{9,8},{10,11... | collective-permute-start | bytes 98312 | tf_op jit(solution)/shard_map/ppermute | solution.py:365
  31.2 3.5 %copy-start.10 = (s32[16]{0:T(128)S(1)}, s32[16]{0:T(128)}, u32[]{:S(2)}) copy-start(s32[16]{0:T(128)} %capacity_ref.1) | copy-start | bytes 196
  34.8 2.5 %copy-start.4 = (bf16[1024,16]{0,1:T(8,128)(2,1)S(1)}, bf16[1024,16]{0,1:T(8,128)(2,1)}, u32[]{:S(2)}) copy-start(bf16[1024,16]{0,1:T(8,128)(2,1)} %param.15) | copy-start | bytes 98308
  35.9 20.2 %collective-permute-start.15 = (bf16[128,1024]{1,0:T(8,128)(2,1)S(1)}, bf16[128,1024]{1,0:T(8,128)(2,1)S(1)}, u32[]{:S(2)}, u32[]{:S(2)}) collective-permute-start(bf16[128,1024]{1,0:T(8,128)(2,1)S(1)} %get-tuple-element.37.xz_ref), channel_id=1, source_target_pairs={{0,2},{2,0},{4,6},{6,4},{8,10},{10,8},{12,14},{14,12},{1,3},{3,1},... | collective-permute-start | bytes 786440 | tf_op jit(solution)/shard_map/ppermute | solution.py:368
  43.1 8.5 %collective-permute-start.12 = (bf16[128,1024]{1,0:T(8,128)(2,1)S(1)}, bf16[128,1024]{1,0:T(8,128)(2,1)S(1)}, u32[]{:S(2)}, u32[]{:S(2)}) collective-permute-start(bf16[128,1024]{1,0:T(8,128)(2,1)S(1)} %get-tuple-element.31), channel_id=1, source_target_pairs={{0,2},{2,0},{4,6},{6,4},{8,10},{10,8},{12,14},{14,12},{1,3},{3,1},... | collective-permute-start | bytes 786440 | tf_op jit(solution)/shard_map/ppermute | solution.py:368
  43.8 7.7 %copy-start.2 = (bf16[1,128,2048]{2,1,0:T(8,128)(2,1)S(1)}, bf16[1,128,2048]{2,1,0:T(8,128)(2,1)}, u32[]{:S(2)}) copy-start(bf16[1,128,2048]{2,1,0:T(8,128)(2,1)} %param.12) | copy-start | bytes 1572868
  43.8 7.7 %copy-start.3 = (bf16[1,128,2048]{2,1,0:T(8,128)(2,1)S(1)}, bf16[1,128,2048]{2,1,0:T(8,128)(2,1)}, u32[]{:S(2)}) copy-start(bf16[1,128,2048]{2,1,0:T(8,128)(2,1)} %param.13) | copy-start | bytes 1572868
  51.7 10.5 %collective-permute-start.13 = (bf16[128,2048]{1,0:T(8,128)(2,1)S(1)}, bf16[128,2048]{1,0:T(8,128)(2,1)S(1)}, u32[]{:S(2)}, u32[]{:S(2)}) collective-permute-start(bf16[128,2048]{1,0:T(8,128)(2,1)S(1)} %get-tuple-element.35.k_own), channel_id=1, source_target_pairs={{0,1},{1,0},{2,3},{3,2},{4,5},{5,4},{6,7},{7,6},{8,9},{9,8},{10,11... | collective-permute-start | bytes 1572872 | tf_op jit(solution)/shard_map/ppermute | solution.py:365
  51.8 10.4 %collective-permute-start.14 = (bf16[128,2048]{1,0:T(8,128)(2,1)S(1)}, bf16[128,2048]{1,0:T(8,128)(2,1)S(1)}, u32[]{:S(2)}, u32[]{:S(2)}) collective-permute-start(bf16[128,2048]{1,0:T(8,128)(2,1)S(1)} %get-tuple-element.36.v_own), channel_id=1, source_target_pairs={{0,1},{1,0},{2,3},{3,2},{4,5},{5,4},{6,7},{7,6},{8,9},{9,8},{10,11... | collective-permute-start | bytes 1572872 | tf_op jit(solution)/shard_map/ppermute | solution.py:365
  52.3 13.1 %collective-permute-start.16 = (bf16[128,1024]{1,0:T(8,128)(2,1)S(1)}, bf16[128,1024]{1,0:T(8,128)(2,1)S(1)}, u32[]{:S(2)}, u32[]{:S(2)}) collective-permute-start(bf16[128,1024]{1,0:T(8,128)(2,1)S(1)} %get-tuple-element.40), channel_id=1, source_target_pairs={{0,2},{2,0},{4,6},{6,4},{8,10},{10,8},{12,14},{14,12},{1,3},{3,1},... | collective-permute-start | bytes 786440 | tf_op jit(solution)/shard_map/ppermute | solution.py:368
  53.0 9.2 %copy-start.1 = (bf16[1,128,2048]{2,1,0:T(8,128)(2,1)S(1)}, bf16[1,128,2048]{2,1,0:T(8,128)(2,1)}, u32[]{:S(2)}) copy-start(bf16[1,128,2048]{2,1,0:T(8,128)(2,1)} %param.11) | copy-start | bytes 1572868
  53.0 9.2 %copy-start.7 = (s32[1,128]{1,0:T(1,128)S(1)}, s32[1,128]{1,0:T(1,128)}, u32[]{:S(2)}) copy-start(s32[1,128]{1,0:T(1,128)} %doc_own.3) | copy-start | bytes 1540
  53.0 9.2 %copy-start.9 = (s32[1,128]{1,0:T(1,128)S(1)}, s32[1,128]{1,0:T(1,128)}, u32[]{:S(2)}) copy-start(s32[1,128]{1,0:T(1,128)} %ahead_ref.3) | copy-start | bytes 1540
  53.0 12.4 %collective-permute-start.17 = (bf16[128,1024]{1,0:T(8,128)(2,1)S(1)}, bf16[128,1024]{1,0:T(8,128)(2,1)S(1)}, u32[]{:S(2)}, u32[]{:S(2)}) collective-permute-start(bf16[128,1024]{1,0:T(8,128)(2,1)S(1)} %get-tuple-element.38.refs_5_), channel_id=1, source_target_pairs={{0,12},{2,14},{4,0},{6,2},{8,4},{10,6},{12,8},{14,10},{1,13},{3,15... | collective-permute-start | bytes 786440 | tf_op jit(solution)/shard_map/ppermute | solution.py:371
  60.8 12.4 %collective-permute-start.20 = (bf16[128,1024]{1,0:T(8,128)(2,1)S(1)}, bf16[128,1024]{1,0:T(8,128)(2,1)S(1)}, u32[]{:S(2)}, u32[]{:S(2)}) collective-permute-start(bf16[128,1024]{1,0:T(8,128)(2,1)S(1)} %get-tuple-element.43), channel_id=1, source_target_pairs={{0,2},{2,0},{4,6},{6,4},{8,10},{10,8},{12,14},{14,12},{1,3},{3,1},... | collective-permute-start | bytes 786440 | tf_op jit(solution)/shard_map/ppermute | solution.py:368
  62.2 4.9 %copy-start.5 = (bf16[1,128,1024]{2,1,0:T(8,128)(2,1)S(1)}, bf16[1,128,1024]{2,1,0:T(8,128)(2,1)}, u32[]{:S(2)}) copy-start(bf16[1,128,1024]{2,1,0:T(8,128)(2,1)} %param.14) | copy-start | bytes 786436
  65.4 1.0 %copy-start = (bf16[128,2048]{1,0:T(8,128)(2,1)S(1)}, bf16[128,2048]{1,0:T(8,128)(2,1)}, u32[]{:S(2)}) copy-start(bf16[128,2048]{1,0:T(8,128)(2,1)} %shard_map.133.refs_3_) | copy-start | bytes 1572868
  66.6 7.5 %collective-permute-start.19 = (bf16[128,1024]{1,0:T(8,128)(2,1)S(1)}, bf16[128,1024]{1,0:T(8,128)(2,1)S(1)}, u32[]{:S(2)}, u32[]{:S(2)}) collective-permute-start(bf16[128,1024]{1,0:T(8,128)(2,1)S(1)} %shard_map.134.refs_5_), channel_id=1, source_target_pairs={{0,12},{2,14},{4,0},{6,2},{8,4},{10,6},{12,8},{14,10},{1,13},{3,15... | collective-permute-start | bytes 786440 | tf_op jit(solution)/shard_map/ppermute | solution.py:371
  71.8 7.0 %collective-permute-start.18 = (bf16[128,1024]{1,0:T(8,128)(2,1)S(1)}, bf16[128,1024]{1,0:T(8,128)(2,1)S(1)}, u32[]{:S(2)}, u32[]{:S(2)}) collective-permute-start(bf16[128,1024]{1,0:T(8,128)(2,1)S(1)} %get-tuple-element.42), channel_id=1, source_target_pairs={{0,2},{2,0},{4,6},{6,4},{8,10},{10,8},{12,14},{14,12},{1,3},{3,1},... | collective-permute-start | bytes 786440 | tf_op jit(solution)/shard_map/ppermute | solution.py:368
  74.1 8.4 %collective-permute-start.21 = (bf16[128,1024]{1,0:T(8,128)(2,1)S(1)}, bf16[128,1024]{1,0:T(8,128)(2,1)S(1)}, u32[]{:S(2)}, u32[]{:S(2)}) collective-permute-start(bf16[128,1024]{1,0:T(8,128)(2,1)S(1)} %shard_map.136), channel_id=1, source_target_pairs={{0,4},{2,6},{4,8},{6,10},{8,12},{10,14},{12,0},{14,2},{1,5},{3,7},... | collective-permute-start | bytes 786440 | tf_op jit(solution)/shard_map/ppermute | solution.py:371

commit v11 on v7

--- a/solution.py
+++ b/solution.py
@@ -115,9 +115,9 @@
     refs[-1][count:] = second_ref[...]
 
 
-def copy_join_kernel(first_ref, second_ref, rows_ref, copy_ref, out_ref):
-    join_kernel(first_ref, second_ref, out_ref)
-    copy_ref[...] = rows_ref[...]
+def copy_join_kernel(first_ref, second_ref, rows_ref, *refs):
+    join_kernel(first_ref, second_ref, refs[-1])
+    refs[-2][...] = rows_ref[...]
 
 
 def join(first, second, passed=None, after=(), copy=False):
@@ -197,7 +197,7 @@
     upto = jnp.where(upto, 1.0, 0.0).astype(jnp.bfloat16)
 
     def device_of(entry):
-        flips = 4 * lax.rem(entry, line) + 2 * lax.rem(lax.div(entry, line), 2)
+        flips = 2 * lax.rem(entry, 2) + 4 * lax.rem(lax.div(entry, 2), line)
         return own ^ (flips + lax.div(entry, 2 * line))
 
     device = device_of(lax.broadcasted_iota(jnp.int32, (sources, sources), 0))
@@ -221,9 +221,9 @@
         limit = capacity_ref[expert].astype(jnp.float32)
         kept.append(jnp.where(mine & (slots < limit), 1, 0))
     for step in range(line):
-        home = z ^ lax.rem(z + line - step, line)
+        home = 2 * (z ^ lax.rem(z + line - step, line))
         for side in range(2):
-            here = entry == home + line * side
+            here = entry == home + side
             for k, part in enumerate(named + kept):
                 picked = jnp.sum(jnp.where(here, part, 0), axis=0, keepdims=True)
                 out_ref[2 * step + side, k : k + 1, :] = picked
@@ -395,24 +395,23 @@
     own = lax.axis_index(("expert", "context")).astype(jnp.int32).reshape(1)
     far_weights = [swap_core(expert_in[0]), swap_core(expert_out[0])]
 
-    arriving, beside_own = along(latent[0], 1), swap_side(latent[0])
+    arriving = along(latent[0], 1)
     table = pack(routes.transpose(2, 0, 1), segments)
-    span = 1
-    while 2 * span < line:
-        table = join(table, flipped(table, span))
-        span *= 2
-    arriving, table = join(table, flipped(table, span), passed=arriving, after=(beside_own,))
-    across_table = swap_side(table)
+    rows, table = join(table, swap_side(table), passed=latent[0], copy=True)
+    beside_own = swap_side(rows)
+    arriving, table = join(table, flipped(table, 1), passed=arriving)
+    flip = flipped(table, 2)
     chained = along(arriving, 1)
-    passed, table = join(table, across_table, passed=arriving, copy=True)
+    passed, table = join(table, flip, passed=arriving, copy=True, after=(beside_own,))
     far_table = swap_core(table)
     from_side = [beside_own, swap_side(passed)]
-    kept, passed = kept_rows(own, capacity, table, far_table, chained, ())
+    own_weights = load_weights(expert_in[0], expert_out[0], (table,))
+    kept, passed = kept_rows(own, capacity, table, far_table, chained, own_weights)
     doc_far = far_table[0, TOPK : TOPK + 1, :]
     from_line = [latent[0], arriving, passed]
     last = along(passed, 1)
     from_side.append(swap_side(passed))
-    weights = list(load_weights(expert_in[0], expert_out[0], (kept,))) + far_weights
+    weights = list(own_weights) + far_weights
 
     def piece(step, weights, *after):
         return run_piece(

time: 79 us -> 76.3 us (0.966)
  starting transfers between devices: 26.7 us -> 24.2 us
    ppermute x9, waiting for transfers between devices: 8.16 us -> 5.34 us  [swap_side(): return lax.ppermute(x, 'expert', across)]
    ppermute x2, waiting for transfers between devices: 4.5 us -> 6.64 us  [flipped(): lax.ppermute(x, 'expert', [(2 * z + y, 2 * (z ^ span) + y) for z, y in sp...]
    ppermute x6, waiting for transfers between devices: 6.45 us -> 7.93 us  [along(): lax.ppermute(x, 'expert', [(2 * z + y, 2 * ((z + step) % line) + y) for z...]
    ppermute x9, starting transfers between devices: 10.4 us -> 9.04 us  [swap_side(): return lax.ppermute(x, 'expert', across)]
    ppermute x5, waiting for transfers between devices: 1.22 us -> 0.01 us  [swap_core(): return lax.ppermute(x, 'context', sibling)]
    unnamed x20 -> x22, local copies, waits for them, and re-layouts: 2.02 us -> 2.33 us
  transfers between devices with their start and end apart: 22 -> 22, of which waited for: 9 -> 7; matrix products, arithmetic and copies ran while one was open for 0% -> 0% of each run, Pallas kernels for 35% -> 37%
where the time goes in v11:
time: 76.3 us; the launch traced here: 76.1 us
  Pallas kernels  27.9 us (37%)
  starting transfers between devices  24.2 us (32%)
  waiting for transfers between devices  19.9 us (26%)
  local copies, waits for them, and re-layouts  2.33 us (3%)
  other arithmetic  0.92 us (1%)
  between operations  0.85 us (1%)
    pallas_call x4, Pallas kernels, run_piece(): pl.pallas_call(functools.partial(expert_kernel, place, first), out_shape=...  19.9 us
    ppermute x6, starting transfers between devices, along(): lax.ppermute(x, 'expert', [(2 * z + y, 2 * ((z + step) % line) + y) for z...  10.3 us
    ppermute x9, starting transfers between devices, swap_side(): return lax.ppermute(x, 'expert', across)  9.04 us
    ppermute x6, waiting for transfers between devices, along(): lax.ppermute(x, 'expert', [(2 * z + y, 2 * ((z + step) % line) + y) for z...  7.93 us
    ppermute x2, waiting for transfers between devices, flipped(): lax.ppermute(x, 'expert', [(2 * z + y, 2 * (z ^ span) + y) for z, y in sp...  6.64 us
    ppermute x9, waiting for transfers between devices, swap_side(): return lax.ppermute(x, 'expert', across)  5.34 us
    ppermute x2, starting transfers between devices, flipped(): lax.ppermute(x, 'expert', [(2 * z + y, 2 * (z ^ span) + y) for z, y in sp...  4.17 us
    pallas_call x1, Pallas kernels, load_weights(): pl.pallas_call(load_kernel, out_shape=[pltpu.VMEM(w.shape, w.dtype) for w...  3.51 us
  transfers between devices with their start and end apart: 22, of which 7 were waited for; matrix products, arithmetic and copies ran while one was open for 0% of the time, Pallas kernels for 37%

profile of v11, /device:TPU:0, one launch (start us, length us, event | category | flops | bytes accessed | tf_op | source)
XLA Modules:
  0.0 76.1 jit_solution(1317921634455438947)
XLA Ops:
  0.6 0.5 collective-permute-start.8
  1.1 0.1 collective-permute-start.9
  1.2 3.0 %collective-permute-start.2 = (bf16[128,1024]{1,0:T(8,128)(2,1)}, bf16[128,1024]{1,0:T(8,128)(2,1)S(1)}, u32[]{:S(2)}, u32[]{:S(2)}) collective-permute-start(bf16[128,1024]{1,0:T(8,128)(2,1)} %bitcast.17), channel_id=1, source_target_pairs={{0,4},{2,6},{4,8},{6,10},{8,12},{10,14},{12,0},{14,2},{1,5},{3,7},... | collective-permute-start | bytes 786440 | tf_op jit(solution)/shard_map/ppermute | solution.py:390
  4.2 0.7 copy-done.6
  4.9 0.7 copy-done.8
  5.6 1.6 %collective-permute-start = (s32[1,8,128]{2,1,0:T(8,128)S(1)}, s32[1,8,128]{2,1,0:T(8,128)S(1)}, u32[]{:S(2)}, u32[]{:S(2)}) collective-permute-start(s32[1,8,128]{2,1,0:T(8,128)S(1)} %shard_map.122.first_ref), channel_id=1, source_target_pairs={{0,2},{2,0},{4,6},{6,4},{8,10},{10,8},{12,14},{14,12},{1,3},{3,1},... | collective-permute-start | bytes 12296 | tf_op jit(solution)/shard_map/ppermute | solution.py:387
  7.2 2.1 %collective-permute-done.second_ref = s32[1,8,128]{2,1,0:T(8,128)S(1)} collective-permute-done((s32[1,8,128]{2,1,0:T(8,128)S(1)}, s32[1,8,128]{2,1,0:T(8,128)S(1)}, u32[]{:S(2)}, u32[]{:S(2)}) %collective-permute-start) | collective-permute-done | bytes 4128 | tf_op jit(solution)/shard_map/ppermute | solution.py:387
  9.3 0.9 %copy-done.1 = bf16[1,128,1024]{2,1,0:T(8,128)(2,1)S(1)} copy-done((bf16[1,128,1024]{2,1,0:T(8,128)(2,1)S(1)}, bf16[1,128,1024]{2,1,0:T(8,128)(2,1)}, u32[]{:S(2)}) %copy-start.1) | copy-done | bytes 262168
  10.2 1.6 %collective-permute-start.4 = (bf16[128,1024]{1,0:T(8,128)(2,1)S(1)}, bf16[128,1024]{1,0:T(8,128)(2,1)S(1)}, u32[]{:S(2)}, u32[]{:S(2)}) collective-permute-start(bf16[128,1024]{1,0:T(8,128)(2,1)S(1)} %get-tuple-element.28), channel_id=1, source_target_pairs={{0,2},{2,0},{4,6},{6,4},{8,10},{10,8},{12,14},{14,12},{1,3},{3,1},... | collective-permute-start | bytes 786440 | tf_op jit(solution)/shard_map/ppermute | solution.py:387
  11.8 1.6 %collective-permute-start.1 = (s32[2,8,128]{2,1,0:T(8,128)S(1)}, s32[2,8,128]{2,1,0:T(8,128)S(1)}, u32[]{:S(2)}, u32[]{:S(2)}) collective-permute-start(s32[2,8,128]{2,1,0:T(8,128)S(1)} %get-tuple-element.25.first_ref), channel_id=1, source_target_pairs={{0,4},{2,6},{4,0},{6,2},{8,12},{10,14},{12,8},{14,10},{1,5},{3,7},... | collective-permute-start | bytes 24584 | tf_op jit(solution)/shard_map/ppermute | solution.py:393
  13.4 2.1 %collective-permute-done.1.second_ref = s32[2,8,128]{2,1,0:T(8,128)S(1)} collective-permute-done((s32[2,8,128]{2,1,0:T(8,128)S(1)}, s32[2,8,128]{2,1,0:T(8,128)S(1)}, u32[]{:S(2)}, u32[]{:S(2)}) %collective-permute-start.1) | collective-permute-done | bytes 8224 | tf_op jit(solution)/shard_map/ppermute | solution.py:393
  15.5 0.0 collective-permute-done.2.refs_0_
  15.5 2.6 %collective-permute-start.3 = (s32[4,8,128]{2,1,0:T(8,128)S(1)}, s32[4,8,128]{2,1,0:T(8,128)S(1)}, u32[]{:S(2)}, u32[]{:S(2)}) collective-permute-start(s32[4,8,128]{2,1,0:T(8,128)S(1)} %get-tuple-element.26.first_ref), channel_id=1, source_target_pairs={{0,8},{2,10},{4,12},{6,14},{8,0},{10,2},{12,4},{14,6},{1,9},{3,11}... | collective-permute-start | bytes 49160 | tf_op jit(solution)/shard_map/ppermute | solution.py:393
  18.1 0.2 collective-permute-start.6
  18.3 0.0 collective-permute-done.4.refs_0_.xy_ref
  18.3 4.6 %collective-permute-done.3.second_ref = s32[4,8,128]{2,1,0:T(8,128)S(1)} collective-permute-done((s32[4,8,128]{2,1,0:T(8,128)S(1)}, s32[4,8,128]{2,1,0:T(8,128)S(1)}, u32[]{:S(2)}, u32[]{:S(2)}) %collective-permute-start.3) | collective-permute-done | bytes 16416 | tf_op jit(solution)/shard_map/ppermute | solution.py:393
  22.9 0.6 collective-permute-start.7
  23.5 0.0 collective-permute-start.5
  23.5 3.5 %shard_map.126 = (bf16[1024,2048]{1,0:T(8,128)(2,1)S(1)}, bf16[2048,1024]{1,0:T(8,128)(2,1)S(1)}) custom-call(bf16[1024,2048]{1,0:T(8,128)(2,1)} %bitcast.28, bf16[2048,1024]{1,0:T(8,128)(2,1)} %bitcast.30, s32[8,8,128]{2,1,0:T(8,128)S(1)} %get-tuple-element.29.refs_0_.low_ref), custom_call_target="tpu_custom_call" | custom-call | tf_op jit(solution)/shard_map/pallas_call | solution.py:160
  27.0 0.0 collective-permute-done.5.high_ref
  27.0 0.0 collective-permute-done.6.refs_0_
  27.0 0.0 copy-done.10
  27.0 0.0 copy-start.5
  27.0 1.1 %shard_map.127 = (s32[8,8,128]{2,1,0:T(8,128)S(1)}, bf16[128,1024]{1,0:T(8,128)(2,1)S(1)}) custom-call(s32[1]{0:T(128)} %bitcast.2.own_ref, s32[16]{0:T(128)S(1)} %copy-done.10, s32[8,8,128]{2,1,0:T(8,128)S(1)} %get-tuple-element.29.refs_0_.low_ref, s32[8,8,128]{2,1,0:T(8,128)S(1)} %collective-permute-done.5.high_ref, ...), custom_call_target="tpu_custom_call", output_to_operand_aliasing={{1}: (4, {})} | custom-call | tf_op jit(solution)/shard_map/pallas_call | solution.py:236
  28.1 0.1 collective-permute-start.12
  28.2 1.6 %collective-permute-start.11 = (bf16[128,1024]{1,0:T(8,128)(2,1)S(1)}, bf16[128,1024]{1,0:T(8,128)(2,1)S(1)}, u32[]{:S(2)}, u32[]{:S(2)}) collective-permute-start(bf16[128,1024]{1,0:T(8,128)(2,1)S(1)} %get-tuple-element.36.xz_ref), channel_id=1, source_target_pairs={{0,2},{2,0},{4,6},{6,4},{8,10},{10,8},{12,14},{14,12},{1,3},{3,1},... | collective-permute-start | bytes 786440 | tf_op jit(solution)/shard_map/ppermute | solution.py:387
  29.8 0.0 collective-permute-done.7.xy_ref
  29.8 0.0 collective-permute-done.8.refs_2_
  29.8 0.0 collective-permute-done.9.refs_3_
  29.8 0.0 copy-done.5
  29.8 5.8 %shard_map.128 = (bf16[128,1024]{1,0:T(8,128)(2,1)S(1)}, bf16[128,1024]{1,0:T(8,128)(2,1)S(1)}, bf16[1024,2048]{1,0:T(8,128)(2,1)S(1)}, bf16[2048,1024]{1,0:T(8,128)(2,1)S(1)}) custom-call(s32[1]{0:T(128)} %bitcast.2.own_ref, s32[8,8,128]{2,1,0:T(8,128)S(1)} %get-tuple-element.32.kept_ref, bf16[16,1024]{1,0:T(8,128)(2,1)S(1)} %bitcast.22, ...), custom_call_target="tpu_custom_call" | custom-call | flops 4294967296 | bytes 1048576 | tf_op jit(solution)/shard_map/pallas_call | solution.py:338
  35.6 0.6 collective-permute-start.10
  36.2 2.6 %collective-permute-done.12.refs_0_ = bf16[128,1024]{1,0:T(8,128)(2,1)S(1)} collective-permute-done((bf16[128,1024]{1,0:T(8,128)(2,1)S(1)}, bf16[128,1024]{1,0:T(8,128)(2,1)S(1)}, u32[]{:S(2)}, u32[]{:S(2)}) %collective-permute-start.12) | collective-permute-done | bytes 262176 | tf_op jit(solution)/shard_map/ppermute | solution.py:390
  38.7 1.5 %collective-permute-start.15 = (bf16[128,1024]{1,0:T(8,128)(2,1)S(1)}, bf16[128,1024]{1,0:T(8,128)(2,1)S(1)}, u32[]{:S(2)}, u32[]{:S(2)}) collective-permute-start(bf16[128,1024]{1,0:T(8,128)(2,1)S(1)} %shard_map.129.refs_5_.xz_ref), channel_id=1, source_target_pairs={{0,2},{2,0},{4,6},{6,4},{8,10},{10,8},{12,14},{14,12},{1,3},{3,1},... | collective-permute-start | bytes 786440 | tf_op jit(solution)/shard_map/ppermute | solution.py:387
  40.2 0.0 collective-permute-done.11.xy_ref
  40.2 4.7 %shard_map.130 = (bf16[128,1024]{1,0:T(8,128)(2,1)S(1)}, bf16[128,1024]{1,0:T(8,128)(2,1)S(1)}) custom-call(s32[1]{0:T(128)} %bitcast.2.own_ref, s32[8,8,128]{2,1,0:T(8,128)S(1)} %get-tuple-element.32.kept_ref, bf16[16,1024]{1,0:T(8,128)(2,1)S(1)} %bitcast.23, bf16[128,1024]{1,0:T(8,128)(2,1)S(1)} %get-tuple-element.36.xz_ref, ...), custom_call_target="tpu_custom_call" | custom-call | flops 4294967296 | bytes 1048576 | tf_op jit(solution)/shard_map/pallas_call | solution.py:338
  44.9 0.6 collective-permute-start.17
  45.5 0.0 collective-permute-done.10.second_ref
  45.5 0.1 shard_map.131
  45.6 3.3 %collective-permute-start.19 = (bf16[128,1024]{1,0:T(8,128)(2,1)S(1)}, bf16[128,1024]{1,0:T(8,128)(2,1)S(1)}, u32[]{:S(2)}, u32[]{:S(2)}) collective-permute-start(bf16[128,1024]{1,0:T(8,128)(2,1)S(1)} %get-tuple-element.42.refs_5_), channel_id=1, source_target_pairs={{0,12},{2,14},{4,0},{6,2},{8,4},{10,6},{12,8},{14,10},{1,13},{3,15... | collective-permute-start | bytes 786440 | tf_op jit(solution)/shard_map/ppermute | solution.py:390
  48.9 0.0 collective-permute-start.13
  48.9 1.5 %collective-permute-done.15.xy_ref = bf16[128,1024]{1,0:T(8,128)(2,1)S(1)} collective-permute-done((bf16[128,1024]{1,0:T(8,128)(2,1)S(1)}, bf16[128,1024]{1,0:T(8,128)(2,1)S(1)}, u32[]{:S(2)}, u32[]{:S(2)}) %collective-permute-start.15) | collective-permute-done | bytes 262176 | tf_op jit(solution)/shard_map/ppermute | solution.py:387
  50.4 4.7 %shard_map.132 = (bf16[128,1024]{1,0:T(8,128)(2,1)S(1)}, bf16[128,1024]{1,0:T(8,128)(2,1)S(1)}) custom-call(s32[1]{0:T(128)} %bitcast.2.own_ref, s32[8,8,128]{2,1,0:T(8,128)S(1)} %get-tuple-element.32.kept_ref, bf16[16,1024]{1,0:T(8,128)(2,1)S(1)} %bitcast.24, bf16[128,1024]{1,0:T(8,128)(2,1)S(1)} %shard_map.129.refs_5_.xz_ref, ...), custom_call_target="tpu_custom_call" | custom-call | flops 4294967296 | bytes 1048576 | tf_op jit(solution)/shard_map/pallas_call | solution.py:338
  55.1 0.6 collective-permute-start.16
  55.7 0.0 collective-permute-done.17.second_ref
  55.7 0.1 shard_map.133.refs_5_
  55.8 0.1 collective-permute-start.20
  55.8 0.0 copy-start.7
  55.9 0.0 copy-start.9
  55.9 0.1 collective-permute-start.14
  56.0 4.7 %shard_map.134 = (bf16[128,1024]{1,0:T(8,128)(2,1)S(1)}, bf16[128,1024]{1,0:T(8,128)(2,1)S(1)}) custom-call(s32[1]{0:T(128)} %bitcast.2.own_ref, s32[8,8,128]{2,1,0:T(8,128)S(1)} %get-tuple-element.32.kept_ref, bf16[16,1024]{1,0:T(8,128)(2,1)S(1)} %bitcast.25, bf16[128,1024]{1,0:T(8,128)(2,1)S(1)} %bitcast.19, ...), custom_call_target="tpu_custom_call" | custom-call | flops 4294967296 | bytes 1048576 | tf_op jit(solution)/shard_map/pallas_call | solution.py:338
  60.7 1.8 %collective-permute-done.16.second_ref = bf16[128,1024]{1,0:T(8,128)(2,1)S(1)} collective-permute-done((bf16[128,1024]{1,0:T(8,128)(2,1)S(1)}, bf16[128,1024]{1,0:T(8,128)(2,1)S(1)}, u32[]{:S(2)}, u32[]{:S(2)}) %collective-permute-start.16) | collective-permute-done | bytes 262176 | tf_op jit(solution)/shard_map/ppermute | solution.py:387
  62.4 0.5 collective-permute-start.18
  62.9 0.1 shard_map.135.rest_0_
  63.0 0.0 collective-permute-done.13.k_far
  63.0 3.6 %collective-permute-start.21 = (bf16[128,1024]{1,0:T(8,128)(2,1)S(1)}, bf16[128,1024]{1,0:T(8,128)(2,1)S(1)}, u32[]{:S(2)}, u32[]{:S(2)}) collective-permute-start(bf16[128,1024]{1,0:T(8,128)(2,1)S(1)} %shard_map.135.rest_0_), channel_id=1, source_target_pairs={{0,4},{2,6},{4,8},{6,10},{8,12},{10,14},{12,0},{14,2},{1,5},{3,7},... | collective-permute-start | bytes 786440 | tf_op jit(solution)/shard_map/ppermute | solution.py:390
  66.6 0.0 collective-permute-done.14.v_far
  66.7 1.6 %shard_map.136.rest_0_ = bf16[128,2048]{1,0:T(8,128)(2,1)} custom-call(s32[1]{0:T(128)} %bitcast.place_ref, bf16[128,2048]{1,0:T(8,128)(2,1)S(1)} %bitcast.15, bf16[128,2048]{1,0:T(8,128)(2,1)S(1)} %get-tuple-element.40.k_own, bf16[128,2048]{1,0:T(8,128)(2,1)S(1)} %collective-permute-done.13.k_far, bf16[128,2048]{1,0:T(8,128)(2,1)S(1)} %get-tuple-element.41.v_own, ...), custom_call_target="tpu_custom_call" | custom-call | flops 134217728 | bytes 1572864 | tf_op jit(solution)/shard_map/pallas_call | solution.py:67
  68.2 1.6 %shard_map.137 = bf16[128,2048]{1,0:T(8,128)(2,1)} custom-call(s32[1]{0:T(128)} %bitcast.place_ref, bf16[128,2048]{1,0:T(8,128)(2,1)S(1)} %bitcast.16, bf16[128,2048]{1,0:T(8,128)(2,1)S(1)} %get-tuple-element.40.k_own, bf16[128,2048]{1,0:T(8,128)(2,1)S(1)} %collective-permute-done.13.k_far, ...), custom_call_target="tpu_custom_call", output_to_operand_aliasing={{}: (9, {})} | custom-call | flops 134217728 | bytes 1572864 | tf_op jit(solution)/shard_map/pallas_call | solution.py:67
  69.8 0.0 collective-permute-done.18
  69.8 5.4 %collective-permute-done.20 = bf16[128,1024]{1,0:T(8,128)(2,1)S(1)} collective-permute-done((bf16[128,1024]{1,0:T(8,128)(2,1)S(1)}, bf16[128,1024]{1,0:T(8,128)(2,1)S(1)}, u32[]{:S(2)}, u32[]{:S(2)}) %collective-permute-start.20) | collective-permute-done | bytes 262176 | tf_op jit(solution)/shard_map/ppermute | solution.py:390
  75.2 0.0 collective-permute-done.19
  75.2 0.0 collective-permute-done.21
  75.2 0.9 %fusion = bf16[1,128,1024]{2,1,0:T(8,128)(2,1)} fusion(bf16[128,1024]{1,0:T(8,128)(2,1)S(1)} %collective-permute-done.21, bf16[128,1024]{1,0:T(8,128)(2,1)S(1)} %collective-permute-done.20, bf16[128,1024]{1,0:T(8,128)(2,1)S(1)} %collective-permute-done.19, bf16[128,1024]{1,0:T(8,128)(2,1)S(1)} %collective-permute-done.18, ...), kind=kLoop, calls=%fused_computation.1 | loop fusion | flops 1310720 | bytes 1572864 | tf_op jit(solution)/shard_map/broadcast_in_dim | solution.py:444
  (20 shorter events, 0.1 us)
Async XLA Ops:
  0.6 29.2 %collective-permute-start.8 = (bf16[1024,2048]{1,0:T(8,128)(2,1)}, bf16[1024,2048]{1,0:T(8,128)(2,1)}, u32[]{:S(2)}, u32[]{:S(2)}) collective-permute-start(bf16[1024,2048]{1,0:T(8,128)(2,1)} %bitcast.27), channel_id=1, source_target_pairs={{0,1},{1,0},{2,3},{3,2},{4,5},{5,4},{6,7},{7,6},{8,9},{9,8},{10,11... | collective-permute-start | bytes 12582920 | tf_op jit(solution)/shard_map/ppermute | solution.py:384
  1.1 28.7 %collective-permute-start.9 = (bf16[2048,1024]{1,0:T(8,128)(2,1)}, bf16[2048,1024]{1,0:T(8,128)(2,1)}, u32[]{:S(2)}, u32[]{:S(2)}) collective-permute-start(bf16[2048,1024]{1,0:T(8,128)(2,1)} %bitcast.29), channel_id=1, source_target_pairs={{0,1},{1,0},{2,3},{3,2},{4,5},{5,4},{6,7},{7,6},{8,9},{9,8},{10,11... | collective-permute-start | bytes 12582920 | tf_op jit(solution)/shard_map/ppermute | solution.py:384
  1.2 14.3 %collective-permute-start.2 = (bf16[128,1024]{1,0:T(8,128)(2,1)}, bf16[128,1024]{1,0:T(8,128)(2,1)S(1)}, u32[]{:S(2)}, u32[]{:S(2)}) collective-permute-start(bf16[128,1024]{1,0:T(8,128)(2,1)} %bitcast.17), channel_id=1, source_target_pairs={{0,4},{2,6},{4,8},{6,10},{8,12},{10,14},{12,0},{14,2},{1,5},{3,7},... | collective-permute-start | bytes 786440 | tf_op jit(solution)/shard_map/ppermute | solution.py:390
  4.2 0.7 copy-start.6
  4.9 0.7 copy-start.8
  5.6 3.7 %collective-permute-start = (s32[1,8,128]{2,1,0:T(8,128)S(1)}, s32[1,8,128]{2,1,0:T(8,128)S(1)}, u32[]{:S(2)}, u32[]{:S(2)}) collective-permute-start(s32[1,8,128]{2,1,0:T(8,128)S(1)} %shard_map.122.first_ref), channel_id=1, source_target_pairs={{0,2},{2,0},{4,6},{6,4},{8,10},{10,8},{12,14},{14,12},{1,3},{3,1},... | collective-permute-start | bytes 12296 | tf_op jit(solution)/shard_map/ppermute | solution.py:387
  9.3 1.0 %copy-start.1 = (bf16[1,128,1024]{2,1,0:T(8,128)(2,1)S(1)}, bf16[1,128,1024]{2,1,0:T(8,128)(2,1)}, u32[]{:S(2)}) copy-start(bf16[1,128,1024]{2,1,0:T(8,128)(2,1)} %param.14) | copy-start | bytes 786436
  10.2 8.1 %collective-permute-start.4 = (bf16[128,1024]{1,0:T(8,128)(2,1)S(1)}, bf16[128,1024]{1,0:T(8,128)(2,1)S(1)}, u32[]{:S(2)}, u32[]{:S(2)}) collective-permute-start(bf16[128,1024]{1,0:T(8,128)(2,1)S(1)} %get-tuple-element.28), channel_id=1, source_target_pairs={{0,2},{2,0},{4,6},{6,4},{8,10},{10,8},{12,14},{14,12},{1,3},{3,1},... | collective-permute-start | bytes 786440 | tf_op jit(solution)/shard_map/ppermute | solution.py:387
  11.8 3.7 %collective-permute-start.1 = (s32[2,8,128]{2,1,0:T(8,128)S(1)}, s32[2,8,128]{2,1,0:T(8,128)S(1)}, u32[]{:S(2)}, u32[]{:S(2)}) collective-permute-start(s32[2,8,128]{2,1,0:T(8,128)S(1)} %get-tuple-element.25.first_ref), channel_id=1, source_target_pairs={{0,4},{2,6},{4,0},{6,2},{8,12},{10,14},{12,8},{14,10},{1,5},{3,7},... | collective-permute-start | bytes 24584 | tf_op jit(solution)/shard_map/ppermute | solution.py:393
  15.5 7.4 %collective-permute-start.3 = (s32[4,8,128]{2,1,0:T(8,128)S(1)}, s32[4,8,128]{2,1,0:T(8,128)S(1)}, u32[]{:S(2)}, u32[]{:S(2)}) collective-permute-start(s32[4,8,128]{2,1,0:T(8,128)S(1)} %get-tuple-element.26.first_ref), channel_id=1, source_target_pairs={{0,8},{2,10},{4,12},{6,14},{8,0},{10,2},{12,4},{14,6},{1,9},{3,11}... | collective-permute-start | bytes 49160 | tf_op jit(solution)/shard_map/ppermute | solution.py:393
  18.1 8.9 %collective-permute-start.6 = (bf16[128,1024]{1,0:T(8,128)(2,1)S(1)}, bf16[128,1024]{1,0:T(8,128)(2,1)S(1)}, u32[]{:S(2)}, u32[]{:S(2)}) collective-permute-start(bf16[128,1024]{1,0:T(8,128)(2,1)S(1)} %get-tuple-element.27.rows_ref.xz_ref), channel_id=1, source_target_pairs={{0,4},{2,6},{4,8},{6,10},{8,12},{10,14},{12,0},{14,2},{1,5},{3,7},... | collective-permute-start | bytes 786440 | tf_op jit(solution)/shard_map/ppermute | solution.py:390
  22.9 6.9 %collective-permute-start.7 = (bf16[128,1024]{1,0:T(8,128)(2,1)S(1)}, bf16[128,1024]{1,0:T(8,128)(2,1)S(1)}, u32[]{:S(2)}, u32[]{:S(2)}) collective-permute-start(bf16[128,1024]{1,0:T(8,128)(2,1)S(1)} %get-tuple-element.33), channel_id=1, source_target_pairs={{0,2},{2,0},{4,6},{6,4},{8,10},{10,8},{12,14},{14,12},{1,3},{3,1},... | collective-permute-start | bytes 786440 | tf_op jit(solution)/shard_map/ppermute | solution.py:387
  23.5 3.5 %collective-permute-start.5 = (s32[8,8,128]{2,1,0:T(8,128)S(1)}, s32[8,8,128]{2,1,0:T(8,128)S(1)}, u32[]{:S(2)}, u32[]{:S(2)}) collective-permute-start(s32[8,8,128]{2,1,0:T(8,128)S(1)} %get-tuple-element.29.refs_0_.low_ref), channel_id=1, source_target_pairs={{0,1},{1,0},{2,3},{3,2},{4,5},{5,4},{6,7},{7,6},{8,9},{9,8},{10,11... | collective-permute-start | bytes 98312 | tf_op jit(solution)/shard_map/ppermute | solution.py:384
  23.5 3.5 %copy-start.10 = (s32[16]{0:T(128)S(1)}, s32[16]{0:T(128)}, u32[]{:S(2)}) copy-start(s32[16]{0:T(128)} %capacity_ref.1) | copy-start | bytes 196
  27.0 2.8 %copy-start.5 = (bf16[1024,16]{0,1:T(8,128)(2,1)S(1)}, bf16[1024,16]{0,1:T(8,128)(2,1)}, u32[]{:S(2)}) copy-start(bf16[1024,16]{0,1:T(8,128)(2,1)} %param.15) | copy-start | bytes 98308
  28.1 10.6 %collective-permute-start.12 = (bf16[128,1024]{1,0:T(8,128)(2,1)S(1)}, bf16[128,1024]{1,0:T(8,128)(2,1)S(1)}, u32[]{:S(2)}, u32[]{:S(2)}) collective-permute-start(bf16[128,1024]{1,0:T(8,128)(2,1)S(1)} %get-tuple-element.36.xz_ref), channel_id=1, source_target_pairs={{0,4},{2,6},{4,8},{6,10},{8,12},{10,14},{12,0},{14,2},{1,5},{3,7},... | collective-permute-start | bytes 786440 | tf_op jit(solution)/shard_map/ppermute | solution.py:390
  28.2 12.0 %collective-permute-start.11 = (bf16[128,1024]{1,0:T(8,128)(2,1)S(1)}, bf16[128,1024]{1,0:T(8,128)(2,1)S(1)}, u32[]{:S(2)}, u32[]{:S(2)}) collective-permute-start(bf16[128,1024]{1,0:T(8,128)(2,1)S(1)} %get-tuple-element.36.xz_ref), channel_id=1, source_target_pairs={{0,2},{2,0},{4,6},{6,4},{8,10},{10,8},{12,14},{14,12},{1,3},{3,1},... | collective-permute-start | bytes 786440 | tf_op jit(solution)/shard_map/ppermute | solution.py:387
  35.6 9.9 %collective-permute-start.10 = (bf16[128,1024]{1,0:T(8,128)(2,1)S(1)}, bf16[128,1024]{1,0:T(8,128)(2,1)S(1)}, u32[]{:S(2)}, u32[]{:S(2)}) collective-permute-start(bf16[128,1024]{1,0:T(8,128)(2,1)S(1)} %get-tuple-element.35), channel_id=1, source_target_pairs={{0,2},{2,0},{4,6},{6,4},{8,10},{10,8},{12,14},{14,12},{1,3},{3,1},... | collective-permute-start | bytes 786440 | tf_op jit(solution)/shard_map/ppermute | solution.py:387
  38.7 11.7 %collective-permute-start.15 = (bf16[128,1024]{1,0:T(8,128)(2,1)S(1)}, bf16[128,1024]{1,0:T(8,128)(2,1)S(1)}, u32[]{:S(2)}, u32[]{:S(2)}) collective-permute-start(bf16[128,1024]{1,0:T(8,128)(2,1)S(1)} %shard_map.129.refs_5_.xz_ref), channel_id=1, source_target_pairs={{0,2},{2,0},{4,6},{6,4},{8,10},{10,8},{12,14},{14,12},{1,3},{3,1},... | collective-permute-start | bytes 786440 | tf_op jit(solution)/shard_map/ppermute | solution.py:387
  40.2 5.3 %copy-start.3 = (bf16[1,128,2048]{2,1,0:T(8,128)(2,1)S(1)}, bf16[1,128,2048]{2,1,0:T(8,128)(2,1)}, u32[]{:S(2)}) copy-start(bf16[1,128,2048]{2,1,0:T(8,128)(2,1)} %param.12) | copy-start | bytes 1572868
  40.2 5.3 %copy-start.4 = (bf16[1,128,2048]{2,1,0:T(8,128)(2,1)S(1)}, bf16[1,128,2048]{2,1,0:T(8,128)(2,1)}, u32[]{:S(2)}) copy-start(bf16[1,128,2048]{2,1,0:T(8,128)(2,1)} %param.13) | copy-start | bytes 1572868
  44.9 10.7 %collective-permute-start.17 = (bf16[128,1024]{1,0:T(8,128)(2,1)S(1)}, bf16[128,1024]{1,0:T(8,128)(2,1)S(1)}, u32[]{:S(2)}, u32[]{:S(2)}) collective-permute-start(bf16[128,1024]{1,0:T(8,128)(2,1)S(1)} %get-tuple-element.45), channel_id=1, source_target_pairs={{0,2},{2,0},{4,6},{6,4},{8,10},{10,8},{12,14},{14,12},{1,3},{3,1},... | collective-permute-start | bytes 786440 | tf_op jit(solution)/shard_map/ppermute | solution.py:387
  45.6 29.6 %collective-permute-start.19 = (bf16[128,1024]{1,0:T(8,128)(2,1)S(1)}, bf16[128,1024]{1,0:T(8,128)(2,1)S(1)}, u32[]{:S(2)}, u32[]{:S(2)}) collective-permute-start(bf16[128,1024]{1,0:T(8,128)(2,1)S(1)} %get-tuple-element.42.refs_5_), channel_id=1, source_target_pairs={{0,12},{2,14},{4,0},{6,2},{8,4},{10,6},{12,8},{14,10},{1,13},{3,15... | collective-permute-start | bytes 786440 | tf_op jit(solution)/shard_map/ppermute | solution.py:390
  48.9 7.0 %copy-start.2 = (bf16[1,128,1024]{2,1,0:T(8,128)(2,1)S(1)}, bf16[1,128,1024]{2,1,0:T(8,128)(2,1)}, u32[]{:S(2)}) copy-start(bf16[1,128,1024]{2,1,0:T(8,128)(2,1)} %param.14) | copy-start | bytes 786436
  48.9 14.1 %collective-permute-start.13 = (bf16[128,2048]{1,0:T(8,128)(2,1)S(1)}, bf16[128,2048]{1,0:T(8,128)(2,1)S(1)}, u32[]{:S(2)}, u32[]{:S(2)}) collective-permute-start(bf16[128,2048]{1,0:T(8,128)(2,1)S(1)} %get-tuple-element.40.k_own), channel_id=1, source_target_pairs={{0,1},{1,0},{2,3},{3,2},{4,5},{5,4},{6,7},{7,6},{8,9},{9,8},{10,11... | collective-permute-start | bytes 1572872 | tf_op jit(solution)/shard_map/ppermute | solution.py:384
  55.1 7.3 %collective-permute-start.16 = (bf16[128,1024]{1,0:T(8,128)(2,1)S(1)}, bf16[128,1024]{1,0:T(8,128)(2,1)S(1)}, u32[]{:S(2)}, u32[]{:S(2)}) collective-permute-start(bf16[128,1024]{1,0:T(8,128)(2,1)S(1)} %get-tuple-element.44), channel_id=1, source_target_pairs={{0,2},{2,0},{4,6},{6,4},{8,10},{10,8},{12,14},{14,12},{1,3},{3,1},... | collective-permute-start | bytes 786440 | tf_op jit(solution)/shard_map/ppermute | solution.py:387
  55.8 19.5 %collective-permute-start.20 = (bf16[128,1024]{1,0:T(8,128)(2,1)S(1)}, bf16[128,1024]{1,0:T(8,128)(2,1)S(1)}, u32[]{:S(2)}, u32[]{:S(2)}) collective-permute-start(bf16[128,1024]{1,0:T(8,128)(2,1)S(1)} %shard_map.133.refs_5_), channel_id=1, source_target_pairs={{0,8},{2,10},{4,12},{6,14},{8,0},{10,2},{12,4},{14,6},{1,9},{3,11}... | collective-permute-start | bytes 786440 | tf_op jit(solution)/shard_map/ppermute | solution.py:390
  55.8 10.8 %copy-start = (bf16[1,128,2048]{2,1,0:T(8,128)(2,1)S(1)}, bf16[1,128,2048]{2,1,0:T(8,128)(2,1)}, u32[]{:S(2)}) copy-start(bf16[1,128,2048]{2,1,0:T(8,128)(2,1)} %param.11) | copy-start | bytes 1572868
  55.8 10.8 %copy-start.7 = (s32[1,128]{1,0:T(1,128)S(1)}, s32[1,128]{1,0:T(1,128)}, u32[]{:S(2)}) copy-start(s32[1,128]{1,0:T(1,128)} %doc_own.3) | copy-start | bytes 1540
  55.9 10.8 %copy-start.9 = (s32[1,128]{1,0:T(1,128)S(1)}, s32[1,128]{1,0:T(1,128)}, u32[]{:S(2)}) copy-start(s32[1,128]{1,0:T(1,128)} %ahead_ref.3) | copy-start | bytes 1540
  55.9 10.8 %collective-permute-start.14 = (bf16[128,2048]{1,0:T(8,128)(2,1)S(1)}, bf16[128,2048]{1,0:T(8,128)(2,1)S(1)}, u32[]{:S(2)}, u32[]{:S(2)}) collective-permute-start(bf16[128,2048]{1,0:T(8,128)(2,1)S(1)} %get-tuple-element.41.v_own), channel_id=1, source_target_pairs={{0,1},{1,0},{2,3},{3,2},{4,5},{5,4},{6,7},{7,6},{8,9},{9,8},{10,11... | collective-permute-start | bytes 1572872 | tf_op jit(solution)/shard_map/ppermute | solution.py:384
  62.4 7.4 %collective-permute-start.18 = (bf16[128,1024]{1,0:T(8,128)(2,1)S(1)}, bf16[128,1024]{1,0:T(8,128)(2,1)S(1)}, u32[]{:S(2)}, u32[]{:S(2)}) collective-permute-start(bf16[128,1024]{1,0:T(8,128)(2,1)S(1)} %get-tuple-element.47), channel_id=1, source_target_pairs={{0,2},{2,0},{4,6},{6,4},{8,10},{10,8},{12,14},{14,12},{1,3},{3,1},... | collective-permute-start | bytes 786440 | tf_op jit(solution)/shard_map/ppermute | solution.py:387
  63.0 12.2 %collective-permute-start.21 = (bf16[128,1024]{1,0:T(8,128)(2,1)S(1)}, bf16[128,1024]{1,0:T(8,128)(2,1)S(1)}, u32[]{:S(2)}, u32[]{:S(2)}) collective-permute-start(bf16[128,1024]{1,0:T(8,128)(2,1)S(1)} %shard_map.135.rest_0_), channel_id=1, source_target_pairs={{0,4},{2,6},{4,8},{6,10},{8,12},{10,14},{12,0},{14,2},{1,5},{3,7},... | collective-permute-start | bytes 786440 | tf_op jit(solution)/shard_map/ppermute | solution.py:390

commit v12 on v11

--- a/solution.py
+++ b/solution.py
@@ -78,35 +78,34 @@
     )(place, q, k_own, k_far, v_own, v_far, doc_own, doc_far, ahead, *extra)
 
 
-def pack_kernel(named_any, doc_any, table_ref, named_ref, doc_ref, sems):
+def pack_kernel(latent_any, named_any, rows_ref, table_ref, named_ref, sems):
     loads = [
         pltpu.make_async_copy(named_any, named_ref, sems.at[0]),
-        pltpu.make_async_copy(doc_any, doc_ref, sems.at[1]),
+        pltpu.make_async_copy(latent_any, rows_ref, sems.at[1]),
     ]
     for load in loads:
         load.start()
-    for load in loads:
-        load.wait()
+    loads[0].wait()
     for k in range(TOPK):
         table_ref[0, k : k + 1, :] = named_ref[k]
-    table_ref[0, TOPK : TOPK + 1, :] = doc_ref[...]
-    table_ref[0, TOPK + 1 :, :] = doc_ref[...]
-
-
-def pack(named, doc):
-    anywhere = pl.BlockSpec(memory_space=pl.ANY)
+    table_ref[0, TOPK:, :] = jnp.zeros((8 - TOPK, named_ref.shape[2]), jnp.int32)
+    loads[1].wait()
+
+
+def pack(latent, named):
+    hbm = pl.BlockSpec(memory_space=pltpu.HBM)
+    vmem = pl.BlockSpec(memory_space=pltpu.VMEM)
     return pl.pallas_call(
         pack_kernel,
-        out_shape=jax.ShapeDtypeStruct((1, 8, doc.shape[1]), jnp.int32),
-        in_specs=[anywhere] * 2,
-        out_specs=pl.BlockSpec(memory_space=pltpu.VMEM),
-        scratch_shapes=[
-            pltpu.VMEM(named.shape, jnp.int32),
-            pltpu.VMEM(doc.shape, jnp.int32),
-            pltpu.SemaphoreType.DMA((2,)),
+        out_shape=[
+            jax.ShapeDtypeStruct(latent.shape, latent.dtype),
+            jax.ShapeDtypeStruct((1, 8, named.shape[2]), jnp.int32),
         ],
+        in_specs=[hbm] * 2,
+        out_specs=[vmem] * 2,
+        scratch_shapes=[pltpu.VMEM(named.shape, jnp.int32), pltpu.SemaphoreType.DMA((2,))],
         compiler_params=pltpu.CompilerParams(vmem_limit_bytes=SMALL_VMEM),
-    )(named, doc)
+    )(latent, named)
 
 
 def join_kernel(first_ref, second_ref, *refs):
@@ -115,25 +114,28 @@
     refs[-1][count:] = second_ref[...]
 
 
-def copy_join_kernel(first_ref, second_ref, rows_ref, *refs):
+def copy_join_kernel(first_ref, second_ref, rows_ref, doc_ref, *refs):
     join_kernel(first_ref, second_ref, refs[-1])
+    refs[-1][0, TOPK : TOPK + 1, :] = doc_ref[...]
     refs[-2][...] = rows_ref[...]
 
 
-def join(first, second, passed=None, after=(), copy=False):
+def join(first, second, passed=None, after=(), doc=None):
     vmem = pl.BlockSpec(memory_space=pltpu.VMEM)
     anywhere = pl.BlockSpec(memory_space=pl.ANY)
     table = jax.ShapeDtypeStruct((2 * first.shape[0],) + first.shape[1:], first.dtype)
+    copy = doc is not None
     through = [] if passed is None else [passed]
     place = vmem if copy else anywhere
+    extra = through + ([doc] if copy else [])
     out = pl.pallas_call(
         copy_join_kernel if copy else join_kernel,
         out_shape=[jax.ShapeDtypeStruct(x.shape, x.dtype) for x in through] + [table],
-        in_specs=[vmem] * 2 + [place] * len(through) + [anywhere] * len(after),
+        in_specs=[vmem] * 2 + [place] * len(extra) + [anywhere] * len(after),
         out_specs=[place] * len(through) + [vmem],
         input_output_aliases={2: 0} if through and not copy else {},
         compiler_params=pltpu.CompilerParams(vmem_limit_bytes=SMALL_VMEM),
-    )(first, second, *through, *after)
+    )(first, second, *extra, *after)
     return out if through else out[0]
 
 
@@ -283,11 +285,11 @@
         )
 
     def ready(which, column):
+        if first and which == 1 and column == 0:
+            for index in range(WINDOW, len(chunks)):
+                load(index).start()
         if first and which > 1:
-            index = chunks.index((which, column))
-            load(index).wait()
-            if index + WINDOW < len(chunks):
-                load(index + WINDOW).start()
+            load(chunks.index((which, column))).wait()
 
     if first:
         for index in range(WINDOW):
@@ -396,13 +398,13 @@
     far_weights = [swap_core(expert_in[0]), swap_core(expert_out[0])]
 
     arriving = along(latent[0], 1)
-    table = pack(routes.transpose(2, 0, 1), segments)
-    rows, table = join(table, swap_side(table), passed=latent[0], copy=True)
+    rows, table = pack(latent[0], routes.transpose(2, 0, 1))
+    rows, table = join(table, swap_side(table), passed=rows)
     beside_own = swap_side(rows)
     arriving, table = join(table, flipped(table, 1), passed=arriving)
     flip = flipped(table, 2)
     chained = along(arriving, 1)
-    passed, table = join(table, flip, passed=arriving, copy=True, after=(beside_own,))
+    passed, table = join(table, flip, passed=arriving, after=(beside_own,), doc=segments)
     far_table = swap_core(table)
     from_side = [beside_own, swap_side(passed)]
     own_weights = load_weights(expert_in[0], expert_out[0], (table,))

time: 76.3 us -> 76.3 us (level)
  no operation moved by 1% of the time
where the time goes in v12:
time: 76.3 us; the launch traced here: 76.1 us
  Pallas kernels  27.9 us (37%)
  starting transfers between devices  24.1 us (32%)
  waiting for transfers between devices  19.9 us (26%)
  local copies, waits for them, and re-layouts  2.36 us (3%)
  other arithmetic  0.92 us (1%)
  between operations  0.85 us (1%)
    pallas_call x4, Pallas kernels, run_piece(): pl.pallas_call(functools.partial(expert_kernel, place, first), out_shape=...  19.8 us
    ppermute x6, starting transfers between devices, along(): lax.ppermute(x, 'expert', [(2 * z + y, 2 * ((z + step) % line) + y) for z...  10.3 us
    ppermute x9, starting transfers between devices, swap_side(): return lax.ppermute(x, 'expert', across)  9.01 us
    ppermute x6, waiting for transfers between devices, along(): lax.ppermute(x, 'expert', [(2 * z + y, 2 * ((z + step) % line) + y) for z...  7.94 us
    ppermute x2, waiting for transfers between devices, flipped(): lax.ppermute(x, 'expert', [(2 * z + y, 2 * (z ^ span) + y) for z, y in sp...  6.64 us
    ppermute x9, waiting for transfers between devices, swap_side(): return lax.ppermute(x, 'expert', across)  5.34 us
    ppermute x2, starting transfers between devices, flipped(): lax.ppermute(x, 'expert', [(2 * z + y, 2 * (z ^ span) + y) for z, y in sp...  4.17 us
    pallas_call x1, Pallas kernels, load_weights(): pl.pallas_call(load_kernel, out_shape=[pltpu.VMEM(w.shape, w.dtype) for w...  3.51 us
  transfers between devices with their start and end apart: 22, of which 7 were waited for; matrix products, arithmetic and copies ran while one was open for 0% of the time, Pallas kernels for 37%

profile of v12, /device:TPU:0, one launch (start us, length us, event | category | flops | bytes accessed | tf_op | source)
XLA Modules:
  0.0 76.1 jit_solution(11241866699586745710)
XLA Ops:
  0.6 0.5 collective-permute-start.8
  1.1 0.1 collective-permute-start.9
  1.2 3.0 %collective-permute-start.2 = (bf16[128,1024]{1,0:T(8,128)(2,1)}, bf16[128,1024]{1,0:T(8,128)(2,1)S(1)}, u32[]{:S(2)}, u32[]{:S(2)}) collective-permute-start(bf16[128,1024]{1,0:T(8,128)(2,1)} %bitcast.17), channel_id=1, source_target_pairs={{0,4},{2,6},{4,8},{6,10},{8,12},{10,14},{12,0},{14,2},{1,5},{3,7},... | collective-permute-start | bytes 786440 | tf_op jit(solution)/shard_map/ppermute | solution.py:392
  4.2 1.0 %copy-done.1 = bf16[1,128,1024]{2,1,0:T(8,128)(2,1)S(1)} copy-done((bf16[1,128,1024]{2,1,0:T(8,128)(2,1)S(1)}, bf16[1,128,1024]{2,1,0:T(8,128)(2,1)}, u32[]{:S(2)}) %copy-start.1) | copy-done | bytes 262168
  5.2 0.7 copy-done.8
  5.9 1.6 %collective-permute-start = (s32[1,8,128]{2,1,0:T(8,128)S(1)}, s32[1,8,128]{2,1,0:T(8,128)S(1)}, u32[]{:S(2)}, u32[]{:S(2)}) collective-permute-start(s32[1,8,128]{2,1,0:T(8,128)S(1)} %get-tuple-element.27.first_ref), channel_id=1, source_target_pairs={{0,2},{2,0},{4,6},{6,4},{8,10},{10,8},{12,14},{14,12},{1,3},{3,1},... | collective-permute-start | bytes 12296 | tf_op jit(solution)/shard_map/ppermute | solution.py:389
  7.5 2.1 %collective-permute-done.second_ref = s32[1,8,128]{2,1,0:T(8,128)S(1)} collective-permute-done((s32[1,8,128]{2,1,0:T(8,128)S(1)}, s32[1,8,128]{2,1,0:T(8,128)S(1)}, u32[]{:S(2)}, u32[]{:S(2)}) %collective-permute-start) | collective-permute-done | bytes 4128 | tf_op jit(solution)/shard_map/ppermute | solution.py:389
  9.6 1.5 %collective-permute-start.4 = (bf16[128,1024]{1,0:T(8,128)(2,1)S(1)}, bf16[128,1024]{1,0:T(8,128)(2,1)S(1)}, u32[]{:S(2)}, u32[]{:S(2)}) collective-permute-start(bf16[128,1024]{1,0:T(8,128)(2,1)S(1)} %get-tuple-element.32), channel_id=1, source_target_pairs={{0,2},{2,0},{4,6},{6,4},{8,10},{10,8},{12,14},{14,12},{1,3},{3,1},... | collective-permute-start | bytes 786440 | tf_op jit(solution)/shard_map/ppermute | solution.py:389
  11.1 1.6 %collective-permute-start.1 = (s32[2,8,128]{2,1,0:T(8,128)S(1)}, s32[2,8,128]{2,1,0:T(8,128)S(1)}, u32[]{:S(2)}, u32[]{:S(2)}) collective-permute-start(s32[2,8,128]{2,1,0:T(8,128)S(1)} %get-tuple-element.29.first_ref), channel_id=1, source_target_pairs={{0,4},{2,6},{4,0},{6,2},{8,12},{10,14},{12,8},{14,10},{1,5},{3,7},... | collective-permute-start | bytes 24584 | tf_op jit(solution)/shard_map/ppermute | solution.py:395
  12.7 2.1 %collective-permute-done.1.second_ref = s32[2,8,128]{2,1,0:T(8,128)S(1)} collective-permute-done((s32[2,8,128]{2,1,0:T(8,128)S(1)}, s32[2,8,128]{2,1,0:T(8,128)S(1)}, u32[]{:S(2)}, u32[]{:S(2)}) %collective-permute-start.1) | collective-permute-done | bytes 8224 | tf_op jit(solution)/shard_map/ppermute | solution.py:395
  14.8 0.0 collective-permute-done.2.refs_0_
  14.8 2.6 %collective-permute-start.3 = (s32[4,8,128]{2,1,0:T(8,128)S(1)}, s32[4,8,128]{2,1,0:T(8,128)S(1)}, u32[]{:S(2)}, u32[]{:S(2)}) collective-permute-start(s32[4,8,128]{2,1,0:T(8,128)S(1)} %get-tuple-element.30.first_ref), channel_id=1, source_target_pairs={{0,8},{2,10},{4,12},{6,14},{8,0},{10,2},{12,4},{14,6},{1,9},{3,11}... | collective-permute-start | bytes 49160 | tf_op jit(solution)/shard_map/ppermute | solution.py:395
  17.4 0.2 collective-permute-start.6
  17.6 0.0 collective-permute-done.4.refs_0_.xy_ref
  17.6 4.6 %collective-permute-done.3.second_ref = s32[4,8,128]{2,1,0:T(8,128)S(1)} collective-permute-done((s32[4,8,128]{2,1,0:T(8,128)S(1)}, s32[4,8,128]{2,1,0:T(8,128)S(1)}, u32[]{:S(2)}, u32[]{:S(2)}) %collective-permute-start.3) | collective-permute-done | bytes 16416 | tf_op jit(solution)/shard_map/ppermute | solution.py:395
  22.2 0.7 copy-done.6
  22.9 0.6 collective-permute-start.7
  23.4 0.0 collective-permute-start.5
  23.4 3.5 %shard_map.126 = (bf16[1024,2048]{1,0:T(8,128)(2,1)S(1)}, bf16[2048,1024]{1,0:T(8,128)(2,1)S(1)}) custom-call(bf16[1024,2048]{1,0:T(8,128)(2,1)} %bitcast.28, bf16[2048,1024]{1,0:T(8,128)(2,1)} %bitcast.30, s32[8,8,128]{2,1,0:T(8,128)S(1)} %get-tuple-element.33.refs_0_.low_ref), custom_call_target="tpu_custom_call" | custom-call | tf_op jit(solution)/shard_map/pallas_call | solution.py:162
  27.0 0.0 collective-permute-done.5.high_ref
  27.0 0.0 collective-permute-done.6.refs_0_
  27.0 0.0 copy-start.5
  27.0 1.1 %shard_map.127 = (s32[8,8,128]{2,1,0:T(8,128)S(1)}, bf16[128,1024]{1,0:T(8,128)(2,1)S(1)}) custom-call(s32[1]{0:T(128)} %bitcast.2.own_ref, s32[16]{0:T(128)S(1)} %copy-done.10, s32[8,8,128]{2,1,0:T(8,128)S(1)} %get-tuple-element.33.refs_0_.low_ref, s32[8,8,128]{2,1,0:T(8,128)S(1)} %collective-permute-done.5.high_ref, ...), custom_call_target="tpu_custom_call", output_to_operand_aliasing={{1}: (4, {})} | custom-call | tf_op jit(solution)/shard_map/pallas_call | solution.py:238
  28.1 0.1 collective-permute-start.12
  28.2 1.6 %collective-permute-start.11 = (bf16[128,1024]{1,0:T(8,128)(2,1)S(1)}, bf16[128,1024]{1,0:T(8,128)(2,1)S(1)}, u32[]{:S(2)}, u32[]{:S(2)}) collective-permute-start(bf16[128,1024]{1,0:T(8,128)(2,1)S(1)} %get-tuple-element.40.xz_ref), channel_id=1, source_target_pairs={{0,2},{2,0},{4,6},{6,4},{8,10},{10,8},{12,14},{14,12},{1,3},{3,1},... | collective-permute-start | bytes 786440 | tf_op jit(solution)/shard_map/ppermute | solution.py:389
  29.8 0.0 collective-permute-done.7.xy_ref
  29.8 0.0 collective-permute-done.8.refs_2_
  29.8 0.0 collective-permute-done.9.refs_3_
  29.8 5.8 %shard_map.128 = (bf16[128,1024]{1,0:T(8,128)(2,1)S(1)}, bf16[128,1024]{1,0:T(8,128)(2,1)S(1)}, bf16[1024,2048]{1,0:T(8,128)(2,1)S(1)}, bf16[2048,1024]{1,0:T(8,128)(2,1)S(1)}) custom-call(s32[1]{0:T(128)} %bitcast.2.own_ref, s32[8,8,128]{2,1,0:T(8,128)S(1)} %get-tuple-element.36.kept_ref, bf16[16,1024]{1,0:T(8,128)(2,1)S(1)} %bitcast.22, ...), custom_call_target="tpu_custom_call" | custom-call | flops 4294967296 | bytes 1048576 | tf_op jit(solution)/shard_map/pallas_call | solution.py:340
  35.6 0.6 collective-permute-start.10
  36.1 2.6 %collective-permute-done.12.refs_0_ = bf16[128,1024]{1,0:T(8,128)(2,1)S(1)} collective-permute-done((bf16[128,1024]{1,0:T(8,128)(2,1)S(1)}, bf16[128,1024]{1,0:T(8,128)(2,1)S(1)}, u32[]{:S(2)}, u32[]{:S(2)}) %collective-permute-start.12) | collective-permute-done | bytes 262176 | tf_op jit(solution)/shard_map/ppermute | solution.py:392
  38.7 1.5 %collective-permute-start.15 = (bf16[128,1024]{1,0:T(8,128)(2,1)S(1)}, bf16[128,1024]{1,0:T(8,128)(2,1)S(1)}, u32[]{:S(2)}, u32[]{:S(2)}) collective-permute-start(bf16[128,1024]{1,0:T(8,128)(2,1)S(1)} %shard_map.129.refs_5_.xz_ref), channel_id=1, source_target_pairs={{0,2},{2,0},{4,6},{6,4},{8,10},{10,8},{12,14},{14,12},{1,3},{3,1},... | collective-permute-start | bytes 786440 | tf_op jit(solution)/shard_map/ppermute | solution.py:389
  40.2 0.0 collective-permute-done.11.xy_ref
  40.2 4.7 %shard_map.130 = (bf16[128,1024]{1,0:T(8,128)(2,1)S(1)}, bf16[128,1024]{1,0:T(8,128)(2,1)S(1)}) custom-call(s32[1]{0:T(128)} %bitcast.2.own_ref, s32[8,8,128]{2,1,0:T(8,128)S(1)} %get-tuple-element.36.kept_ref, bf16[16,1024]{1,0:T(8,128)(2,1)S(1)} %bitcast.23, bf16[128,1024]{1,0:T(8,128)(2,1)S(1)} %get-tuple-element.40.xz_ref, ...), custom_call_target="tpu_custom_call" | custom-call | flops 4294967296 | bytes 1048576 | tf_op jit(solution)/shard_map/pallas_call | solution.py:340
  44.9 0.6 collective-permute-start.17
  45.5 0.0 collective-permute-done.10.second_ref
  45.5 0.0 copy-done.4
  45.5 0.1 shard_map.131
  45.6 3.3 %collective-permute-start.19 = (bf16[128,1024]{1,0:T(8,128)(2,1)S(1)}, bf16[128,1024]{1,0:T(8,128)(2,1)S(1)}, u32[]{:S(2)}, u32[]{:S(2)}) collective-permute-start(bf16[128,1024]{1,0:T(8,128)(2,1)S(1)} %get-tuple-element.46.refs_5_), channel_id=1, source_target_pairs={{0,12},{2,14},{4,0},{6,2},{8,4},{10,6},{12,8},{14,10},{1,13},{3,15... | collective-permute-start | bytes 786440 | tf_op jit(solution)/shard_map/ppermute | solution.py:392
  48.9 0.0 collective-permute-start.13
  48.9 1.5 %collective-permute-done.15.xy_ref = bf16[128,1024]{1,0:T(8,128)(2,1)S(1)} collective-permute-done((bf16[128,1024]{1,0:T(8,128)(2,1)S(1)}, bf16[128,1024]{1,0:T(8,128)(2,1)S(1)}, u32[]{:S(2)}, u32[]{:S(2)}) %collective-permute-start.15) | collective-permute-done | bytes 262176 | tf_op jit(solution)/shard_map/ppermute | solution.py:389
  50.4 4.7 %shard_map.132 = (bf16[128,1024]{1,0:T(8,128)(2,1)S(1)}, bf16[128,1024]{1,0:T(8,128)(2,1)S(1)}) custom-call(s32[1]{0:T(128)} %bitcast.2.own_ref, s32[8,8,128]{2,1,0:T(8,128)S(1)} %get-tuple-element.36.kept_ref, bf16[16,1024]{1,0:T(8,128)(2,1)S(1)} %bitcast.24, bf16[128,1024]{1,0:T(8,128)(2,1)S(1)} %shard_map.129.refs_5_.xz_ref, ...), custom_call_target="tpu_custom_call" | custom-call | flops 4294967296 | bytes 1048576 | tf_op jit(solution)/shard_map/pallas_call | solution.py:340
  55.1 0.6 collective-permute-start.16
  55.7 0.0 collective-permute-done.17.second_ref
  55.7 0.1 shard_map.133.refs_5_
  55.7 0.1 collective-permute-start.20
  55.8 0.0 copy-start
  55.8 0.0 copy-start.7
  55.8 0.0 copy-start.9
  55.8 0.1 collective-permute-start.14
  55.9 4.7 %shard_map.134 = (bf16[128,1024]{1,0:T(8,128)(2,1)S(1)}, bf16[128,1024]{1,0:T(8,128)(2,1)S(1)}) custom-call(s32[1]{0:T(128)} %bitcast.2.own_ref, s32[8,8,128]{2,1,0:T(8,128)S(1)} %get-tuple-element.36.kept_ref, bf16[16,1024]{1,0:T(8,128)(2,1)S(1)} %bitcast.25, bf16[128,1024]{1,0:T(8,128)(2,1)S(1)} %bitcast.19, ...), custom_call_target="tpu_custom_call" | custom-call | flops 4294967296 | bytes 1048576 | tf_op jit(solution)/shard_map/pallas_call | solution.py:340
  60.6 1.8 %collective-permute-done.16.second_ref = bf16[128,1024]{1,0:T(8,128)(2,1)S(1)} collective-permute-done((bf16[128,1024]{1,0:T(8,128)(2,1)S(1)}, bf16[128,1024]{1,0:T(8,128)(2,1)S(1)}, u32[]{:S(2)}, u32[]{:S(2)}) %collective-permute-start.16) | collective-permute-done | bytes 262176 | tf_op jit(solution)/shard_map/ppermute | solution.py:389
  62.4 0.5 collective-permute-start.18
  62.9 0.1 shard_map.135.rest_0_
  63.0 0.0 collective-permute-done.13.k_far
  63.0 3.6 %collective-permute-start.21 = (bf16[128,1024]{1,0:T(8,128)(2,1)S(1)}, bf16[128,1024]{1,0:T(8,128)(2,1)S(1)}, u32[]{:S(2)}, u32[]{:S(2)}) collective-permute-start(bf16[128,1024]{1,0:T(8,128)(2,1)S(1)} %shard_map.135.rest_0_), channel_id=1, source_target_pairs={{0,4},{2,6},{4,8},{6,10},{8,12},{10,14},{12,0},{14,2},{1,5},{3,7},... | collective-permute-start | bytes 786440 | tf_op jit(solution)/shard_map/ppermute | solution.py:392
  66.6 0.0 collective-permute-done.14.v_far
  66.6 1.6 %shard_map.136.rest_0_ = bf16[128,2048]{1,0:T(8,128)(2,1)} custom-call(s32[1]{0:T(128)} %bitcast.place_ref, bf16[128,2048]{1,0:T(8,128)(2,1)S(1)} %bitcast.15, bf16[128,2048]{1,0:T(8,128)(2,1)S(1)} %get-tuple-element.44.k_own, bf16[128,2048]{1,0:T(8,128)(2,1)S(1)} %collective-permute-done.13.k_far, bf16[128,2048]{1,0:T(8,128)(2,1)S(1)} %get-tuple-element.45.v_own, ...), custom_call_target="tpu_custom_call" | custom-call | flops 134217728 | bytes 1572864 | tf_op jit(solution)/shard_map/pallas_call | solution.py:67
  68.2 1.6 %shard_map.137 = bf16[128,2048]{1,0:T(8,128)(2,1)} custom-call(s32[1]{0:T(128)} %bitcast.place_ref, bf16[128,2048]{1,0:T(8,128)(2,1)S(1)} %bitcast.16, bf16[128,2048]{1,0:T(8,128)(2,1)S(1)} %get-tuple-element.44.k_own, bf16[128,2048]{1,0:T(8,128)(2,1)S(1)} %collective-permute-done.13.k_far, ...), custom_call_target="tpu_custom_call", output_to_operand_aliasing={{}: (9, {})} | custom-call | flops 134217728 | bytes 1572864 | tf_op jit(solution)/shard_map/pallas_call | solution.py:67
  69.8 0.0 collective-permute-done.18
  69.8 5.4 %collective-permute-done.20 = bf16[128,1024]{1,0:T(8,128)(2,1)S(1)} collective-permute-done((bf16[128,1024]{1,0:T(8,128)(2,1)S(1)}, bf16[128,1024]{1,0:T(8,128)(2,1)S(1)}, u32[]{:S(2)}, u32[]{:S(2)}) %collective-permute-start.20) | collective-permute-done | bytes 262176 | tf_op jit(solution)/shard_map/ppermute | solution.py:392
  75.2 0.0 collective-permute-done.19
  75.2 0.0 collective-permute-done.21
  75.2 0.9 %fusion = bf16[1,128,1024]{2,1,0:T(8,128)(2,1)} fusion(bf16[128,1024]{1,0:T(8,128)(2,1)S(1)} %collective-permute-done.21, bf16[128,1024]{1,0:T(8,128)(2,1)S(1)} %collective-permute-done.20, bf16[128,1024]{1,0:T(8,128)(2,1)S(1)} %collective-permute-done.19, bf16[128,1024]{1,0:T(8,128)(2,1)S(1)} %collective-permute-done.18, ...), kind=kLoop, calls=%fused_computation.1 | loop fusion | flops 1310720 | bytes 1572864 | tf_op jit(solution)/shard_map/broadcast_in_dim | solution.py:446
  (20 shorter events, 0.1 us)
Async XLA Ops:
  0.6 29.1 %collective-permute-start.8 = (bf16[1024,2048]{1,0:T(8,128)(2,1)}, bf16[1024,2048]{1,0:T(8,128)(2,1)}, u32[]{:S(2)}, u32[]{:S(2)}) collective-permute-start(bf16[1024,2048]{1,0:T(8,128)(2,1)} %bitcast.27), channel_id=1, source_target_pairs={{0,1},{1,0},{2,3},{3,2},{4,5},{5,4},{6,7},{7,6},{8,9},{9,8},{10,11... | collective-permute-start | bytes 12582920 | tf_op jit(solution)/shard_map/ppermute | solution.py:386
  1.1 28.6 %collective-permute-start.9 = (bf16[2048,1024]{1,0:T(8,128)(2,1)}, bf16[2048,1024]{1,0:T(8,128)(2,1)}, u32[]{:S(2)}, u32[]{:S(2)}) collective-permute-start(bf16[2048,1024]{1,0:T(8,128)(2,1)} %bitcast.29), channel_id=1, source_target_pairs={{0,1},{1,0},{2,3},{3,2},{4,5},{5,4},{6,7},{7,6},{8,9},{9,8},{10,11... | collective-permute-start | bytes 12582920 | tf_op jit(solution)/shard_map/ppermute | solution.py:386
  1.2 13.6 %collective-permute-start.2 = (bf16[128,1024]{1,0:T(8,128)(2,1)}, bf16[128,1024]{1,0:T(8,128)(2,1)S(1)}, u32[]{:S(2)}, u32[]{:S(2)}) collective-permute-start(bf16[128,1024]{1,0:T(8,128)(2,1)} %bitcast.17), channel_id=1, source_target_pairs={{0,4},{2,6},{4,8},{6,10},{8,12},{10,14},{12,0},{14,2},{1,5},{3,7},... | collective-permute-start | bytes 786440 | tf_op jit(solution)/shard_map/ppermute | solution.py:392
  4.2 1.0 %copy-start.1 = (bf16[1,128,1024]{2,1,0:T(8,128)(2,1)S(1)}, bf16[1,128,1024]{2,1,0:T(8,128)(2,1)}, u32[]{:S(2)}) copy-start(bf16[1,128,1024]{2,1,0:T(8,128)(2,1)} %param.14) | copy-start | bytes 786436
  5.2 0.7 copy-start.8
  5.9 3.7 %collective-permute-start = (s32[1,8,128]{2,1,0:T(8,128)S(1)}, s32[1,8,128]{2,1,0:T(8,128)S(1)}, u32[]{:S(2)}, u32[]{:S(2)}) collective-permute-start(s32[1,8,128]{2,1,0:T(8,128)S(1)} %get-tuple-element.27.first_ref), channel_id=1, source_target_pairs={{0,2},{2,0},{4,6},{6,4},{8,10},{10,8},{12,14},{14,12},{1,3},{3,1},... | collective-permute-start | bytes 12296 | tf_op jit(solution)/shard_map/ppermute | solution.py:389
  9.6 8.0 %collective-permute-start.4 = (bf16[128,1024]{1,0:T(8,128)(2,1)S(1)}, bf16[128,1024]{1,0:T(8,128)(2,1)S(1)}, u32[]{:S(2)}, u32[]{:S(2)}) collective-permute-start(bf16[128,1024]{1,0:T(8,128)(2,1)S(1)} %get-tuple-element.32), channel_id=1, source_target_pairs={{0,2},{2,0},{4,6},{6,4},{8,10},{10,8},{12,14},{14,12},{1,3},{3,1},... | collective-permute-start | bytes 786440 | tf_op jit(solution)/shard_map/ppermute | solution.py:389
  11.1 3.7 %collective-permute-start.1 = (s32[2,8,128]{2,1,0:T(8,128)S(1)}, s32[2,8,128]{2,1,0:T(8,128)S(1)}, u32[]{:S(2)}, u32[]{:S(2)}) collective-permute-start(s32[2,8,128]{2,1,0:T(8,128)S(1)} %get-tuple-element.29.first_ref), channel_id=1, source_target_pairs={{0,4},{2,6},{4,0},{6,2},{8,12},{10,14},{12,8},{14,10},{1,5},{3,7},... | collective-permute-start | bytes 24584 | tf_op jit(solution)/shard_map/ppermute | solution.py:395
  14.8 7.4 %collective-permute-start.3 = (s32[4,8,128]{2,1,0:T(8,128)S(1)}, s32[4,8,128]{2,1,0:T(8,128)S(1)}, u32[]{:S(2)}, u32[]{:S(2)}) collective-permute-start(s32[4,8,128]{2,1,0:T(8,128)S(1)} %get-tuple-element.30.first_ref), channel_id=1, source_target_pairs={{0,8},{2,10},{4,12},{6,14},{8,0},{10,2},{12,4},{14,6},{1,9},{3,11}... | collective-permute-start | bytes 49160 | tf_op jit(solution)/shard_map/ppermute | solution.py:395
  17.4 9.6 %collective-permute-start.6 = (bf16[128,1024]{1,0:T(8,128)(2,1)S(1)}, bf16[128,1024]{1,0:T(8,128)(2,1)S(1)}, u32[]{:S(2)}, u32[]{:S(2)}) collective-permute-start(bf16[128,1024]{1,0:T(8,128)(2,1)S(1)} %get-tuple-element.31.rows_ref.xz_ref), channel_id=1, source_target_pairs={{0,4},{2,6},{4,8},{6,10},{8,12},{10,14},{12,0},{14,2},{1,5},{3,7},... | collective-permute-start | bytes 786440 | tf_op jit(solution)/shard_map/ppermute | solution.py:392
  22.2 0.7 copy-start.6
  22.9 6.9 %collective-permute-start.7 = (bf16[128,1024]{1,0:T(8,128)(2,1)S(1)}, bf16[128,1024]{1,0:T(8,128)(2,1)S(1)}, u32[]{:S(2)}, u32[]{:S(2)}) collective-permute-start(bf16[128,1024]{1,0:T(8,128)(2,1)S(1)} %get-tuple-element.37), channel_id=1, source_target_pairs={{0,2},{2,0},{4,6},{6,4},{8,10},{10,8},{12,14},{14,12},{1,3},{3,1},... | collective-permute-start | bytes 786440 | tf_op jit(solution)/shard_map/ppermute | solution.py:389
  23.4 3.5 %collective-permute-start.5 = (s32[8,8,128]{2,1,0:T(8,128)S(1)}, s32[8,8,128]{2,1,0:T(8,128)S(1)}, u32[]{:S(2)}, u32[]{:S(2)}) collective-permute-start(s32[8,8,128]{2,1,0:T(8,128)S(1)} %get-tuple-element.33.refs_0_.low_ref), channel_id=1, source_target_pairs={{0,1},{1,0},{2,3},{3,2},{4,5},{5,4},{6,7},{7,6},{8,9},{9,8},{10,11... | collective-permute-start | bytes 98312 | tf_op jit(solution)/shard_map/ppermute | solution.py:386
  23.4 3.5 %copy-start.10 = (s32[16]{0:T(128)S(1)}, s32[16]{0:T(128)}, u32[]{:S(2)}) copy-start(s32[16]{0:T(128)} %capacity_ref.1) | copy-start | bytes 196
  27.0 2.8 %copy-start.5 = (bf16[1024,16]{0,1:T(8,128)(2,1)S(1)}, bf16[1024,16]{0,1:T(8,128)(2,1)}, u32[]{:S(2)}) copy-start(bf16[1024,16]{0,1:T(8,128)(2,1)} %param.15) | copy-start | bytes 98308
  28.1 10.6 %collective-permute-start.12 = (bf16[128,1024]{1,0:T(8,128)(2,1)S(1)}, bf16[128,1024]{1,0:T(8,128)(2,1)S(1)}, u32[]{:S(2)}, u32[]{:S(2)}) collective-permute-start(bf16[128,1024]{1,0:T(8,128)(2,1)S(1)} %get-tuple-element.40.xz_ref), channel_id=1, source_target_pairs={{0,4},{2,6},{4,8},{6,10},{8,12},{10,14},{12,0},{14,2},{1,5},{3,7},... | collective-permute-start | bytes 786440 | tf_op jit(solution)/shard_map/ppermute | solution.py:392
  28.2 12.0 %collective-permute-start.11 = (bf16[128,1024]{1,0:T(8,128)(2,1)S(1)}, bf16[128,1024]{1,0:T(8,128)(2,1)S(1)}, u32[]{:S(2)}, u32[]{:S(2)}) collective-permute-start(bf16[128,1024]{1,0:T(8,128)(2,1)S(1)} %get-tuple-element.40.xz_ref), channel_id=1, source_target_pairs={{0,2},{2,0},{4,6},{6,4},{8,10},{10,8},{12,14},{14,12},{1,3},{3,1},... | collective-permute-start | bytes 786440 | tf_op jit(solution)/shard_map/ppermute | solution.py:389
  35.6 9.9 %collective-permute-start.10 = (bf16[128,1024]{1,0:T(8,128)(2,1)S(1)}, bf16[128,1024]{1,0:T(8,128)(2,1)S(1)}, u32[]{:S(2)}, u32[]{:S(2)}) collective-permute-start(bf16[128,1024]{1,0:T(8,128)(2,1)S(1)} %get-tuple-element.39), channel_id=1, source_target_pairs={{0,2},{2,0},{4,6},{6,4},{8,10},{10,8},{12,14},{14,12},{1,3},{3,1},... | collective-permute-start | bytes 786440 | tf_op jit(solution)/shard_map/ppermute | solution.py:389
  38.7 11.7 %collective-permute-start.15 = (bf16[128,1024]{1,0:T(8,128)(2,1)S(1)}, bf16[128,1024]{1,0:T(8,128)(2,1)S(1)}, u32[]{:S(2)}, u32[]{:S(2)}) collective-permute-start(bf16[128,1024]{1,0:T(8,128)(2,1)S(1)} %shard_map.129.refs_5_.xz_ref), channel_id=1, source_target_pairs={{0,2},{2,0},{4,6},{6,4},{8,10},{10,8},{12,14},{14,12},{1,3},{3,1},... | collective-permute-start | bytes 786440 | tf_op jit(solution)/shard_map/ppermute | solution.py:389
  40.2 5.3 %copy-start.3 = (bf16[1,128,2048]{2,1,0:T(8,128)(2,1)S(1)}, bf16[1,128,2048]{2,1,0:T(8,128)(2,1)}, u32[]{:S(2)}) copy-start(bf16[1,128,2048]{2,1,0:T(8,128)(2,1)} %param.12) | copy-start | bytes 1572868
  40.2 5.3 %copy-start.4 = (bf16[1,128,2048]{2,1,0:T(8,128)(2,1)S(1)}, bf16[1,128,2048]{2,1,0:T(8,128)(2,1)}, u32[]{:S(2)}) copy-start(bf16[1,128,2048]{2,1,0:T(8,128)(2,1)} %param.13) | copy-start | bytes 1572868
  44.9 10.8 %collective-permute-start.17 = (bf16[128,1024]{1,0:T(8,128)(2,1)S(1)}, bf16[128,1024]{1,0:T(8,128)(2,1)S(1)}, u32[]{:S(2)}, u32[]{:S(2)}) collective-permute-start(bf16[128,1024]{1,0:T(8,128)(2,1)S(1)} %get-tuple-element.49), channel_id=1, source_target_pairs={{0,2},{2,0},{4,6},{6,4},{8,10},{10,8},{12,14},{14,12},{1,3},{3,1},... | collective-permute-start | bytes 786440 | tf_op jit(solution)/shard_map/ppermute | solution.py:389
  45.6 29.6 %collective-permute-start.19 = (bf16[128,1024]{1,0:T(8,128)(2,1)S(1)}, bf16[128,1024]{1,0:T(8,128)(2,1)S(1)}, u32[]{:S(2)}, u32[]{:S(2)}) collective-permute-start(bf16[128,1024]{1,0:T(8,128)(2,1)S(1)} %get-tuple-element.46.refs_5_), channel_id=1, source_target_pairs={{0,12},{2,14},{4,0},{6,2},{8,4},{10,6},{12,8},{14,10},{1,13},{3,15... | collective-permute-start | bytes 786440 | tf_op jit(solution)/shard_map/ppermute | solution.py:392
  48.9 7.0 %copy-start.2 = (bf16[1,128,1024]{2,1,0:T(8,128)(2,1)S(1)}, bf16[1,128,1024]{2,1,0:T(8,128)(2,1)}, u32[]{:S(2)}) copy-start(bf16[1,128,1024]{2,1,0:T(8,128)(2,1)} %param.14) | copy-start | bytes 786436
  48.9 14.1 %collective-permute-start.13 = (bf16[128,2048]{1,0:T(8,128)(2,1)S(1)}, bf16[128,2048]{1,0:T(8,128)(2,1)S(1)}, u32[]{:S(2)}, u32[]{:S(2)}) collective-permute-start(bf16[128,2048]{1,0:T(8,128)(2,1)S(1)} %get-tuple-element.44.k_own), channel_id=1, source_target_pairs={{0,1},{1,0},{2,3},{3,2},{4,5},{5,4},{6,7},{7,6},{8,9},{9,8},{10,11... | collective-permute-start | bytes 1572872 | tf_op jit(solution)/shard_map/ppermute | solution.py:386
  55.1 7.3 %collective-permute-start.16 = (bf16[128,1024]{1,0:T(8,128)(2,1)S(1)}, bf16[128,1024]{1,0:T(8,128)(2,1)S(1)}, u32[]{:S(2)}, u32[]{:S(2)}) collective-permute-start(bf16[128,1024]{1,0:T(8,128)(2,1)S(1)} %get-tuple-element.48), channel_id=1, source_target_pairs={{0,2},{2,0},{4,6},{6,4},{8,10},{10,8},{12,14},{14,12},{1,3},{3,1},... | collective-permute-start | bytes 786440 | tf_op jit(solution)/shard_map/ppermute | solution.py:389
  55.7 19.5 %collective-permute-start.20 = (bf16[128,1024]{1,0:T(8,128)(2,1)S(1)}, bf16[128,1024]{1,0:T(8,128)(2,1)S(1)}, u32[]{:S(2)}, u32[]{:S(2)}) collective-permute-start(bf16[128,1024]{1,0:T(8,128)(2,1)S(1)} %shard_map.133.refs_5_), channel_id=1, source_target_pairs={{0,8},{2,10},{4,12},{6,14},{8,0},{10,2},{12,4},{14,6},{1,9},{3,11}... | collective-permute-start | bytes 786440 | tf_op jit(solution)/shard_map/ppermute | solution.py:392
  55.8 10.8 %copy-start = (bf16[1,128,2048]{2,1,0:T(8,128)(2,1)S(1)}, bf16[1,128,2048]{2,1,0:T(8,128)(2,1)}, u32[]{:S(2)}) copy-start(bf16[1,128,2048]{2,1,0:T(8,128)(2,1)} %param.11) | copy-start | bytes 1572868
  55.8 10.8 %copy-start.7 = (s32[1,128]{1,0:T(1,128)S(1)}, s32[1,128]{1,0:T(1,128)}, u32[]{:S(2)}) copy-start(s32[1,128]{1,0:T(1,128)} %doc_own.3) | copy-start | bytes 1540
  55.8 10.8 %copy-start.9 = (s32[1,128]{1,0:T(1,128)S(1)}, s32[1,128]{1,0:T(1,128)}, u32[]{:S(2)}) copy-start(s32[1,128]{1,0:T(1,128)} %ahead_ref.3) | copy-start | bytes 1540
  55.8 10.7 %collective-permute-start.14 = (bf16[128,2048]{1,0:T(8,128)(2,1)S(1)}, bf16[128,2048]{1,0:T(8,128)(2,1)S(1)}, u32[]{:S(2)}, u32[]{:S(2)}) collective-permute-start(bf16[128,2048]{1,0:T(8,128)(2,1)S(1)} %get-tuple-element.45.v_own), channel_id=1, source_target_pairs={{0,1},{1,0},{2,3},{3,2},{4,5},{5,4},{6,7},{7,6},{8,9},{9,8},{10,11... | collective-permute-start | bytes 1572872 | tf_op jit(solution)/shard_map/ppermute | solution.py:386
  62.4 7.4 %collective-permute-start.18 = (bf16[128,1024]{1,0:T(8,128)(2,1)S(1)}, bf16[128,1024]{1,0:T(8,128)(2,1)S(1)}, u32[]{:S(2)}, u32[]{:S(2)}) collective-permute-start(bf16[128,1024]{1,0:T(8,128)(2,1)S(1)} %get-tuple-element.51), channel_id=1, source_target_pairs={{0,2},{2,0},{4,6},{6,4},{8,10},{10,8},{12,14},{14,12},{1,3},{3,1},... | collective-permute-start | bytes 786440 | tf_op jit(solution)/shard_map/ppermute | solution.py:389
  63.0 12.2 %collective-permute-start.21 = (bf16[128,1024]{1,0:T(8,128)(2,1)S(1)}, bf16[128,1024]{1,0:T(8,128)(2,1)S(1)}, u32[]{:S(2)}, u32[]{:S(2)}) collective-permute-start(bf16[128,1024]{1,0:T(8,128)(2,1)S(1)} %shard_map.135.rest_0_), channel_id=1, source_target_pairs={{0,4},{2,6},{4,8},{6,10},{8,12},{10,14},{12,0},{14,2},{1,5},{3,7},... | collective-permute-start | bytes 786440 | tf_op jit(solution)/shard_map/ppermute | solution.py:392
